TPU v7x, 32 devices: a whole 2x2x4 slice. The times are simulated.
32 devices in a mesh: groups: 2 (over y), space: 4 (over z), chan: 2 (over x), pipe: 2 (over core).
Axes of the slice: x: 2, y: 2, z: 4, core: 2. Of those that a mesh axis runs over, the one named last changes fastest.
Arguments:
- grid_latent: bfloat16 [32768, 512], P(('groups', 'space', 'pipe')), parts along dimension 0, may hold values from -6 to 6
- g2m_face: int32 [32768, 1], P(('groups', 'space', 'pipe')), parts along dimension 0, may hold values from 0 to 3; in each aligned block of 2048 rows (0 to 2047, 2048 to 4095, ...) at most 1024 rows name the same one
- g2m_node: int32 [32768], P(('groups', 'space', 'pipe')), parts along dimension 0, may hold values from 0 to 511
- mesh_latent: bfloat16 [4096, 512], P(('groups', 'space'), 'chan'), parts along dimension 0, may hold values from -6 to 6
- mesh_links: int32 [4096, 6], P(('groups', 'space'), 'pipe'), parts along dimension 0, may hold values from 0 to 2047, as said below
- w_enc: bfloat16 [512, 512], replicated, may hold values from -0.25 to 0.25
- w_send: bfloat16 [2, 512, 512], replicated, may hold values from -0.25 to 0.25
- w_recv: bfloat16 [2, 512, 512], replicated, may hold values from -0.25 to 0.25
- w_node: bfloat16 [2, 512, 512], replicated, may hold values from -0.25 to 0.25
- w_dec: bfloat16 [512, 512], replicated, may hold values from -0.25 to 0.25
- cotangent: bfloat16 [32768, 512], P(('groups', 'space', 'pipe'), 'chan'), parts along dimension 0, may hold values from -6 to 6
Outputs:
- mixed: bfloat16 [32768, 512], P(('groups', 'space', 'pipe'), 'chan'), parts along dimension 0
- grad_grid: bfloat16 [32768, 512], P(('groups', 'space', 'pipe'), 'chan'), parts along dimension 0
- grad_mesh: float32 [4096, 512], P(('groups', 'space'), 'chan'), parts along dimension 0
- grad_w_enc: float32 [1024, 512], P('groups', 'chan'), parts along dimension 0
- grad_w_send: float32 [4, 512, 512], P('groups', None, 'chan'), parts along dimension 0
- grad_w_recv: float32 [4, 512, 512], P('groups', None, 'chan'), parts along dimension 0
- grad_w_node: float32 [4, 512, 512], P('groups', None, 'chan'), parts along dimension 0
- grad_w_dec: float32 [1024, 512], P('groups', 'chan'), parts along dimension 0
There are 2 independent parts, one for each index of `groups`. A program takes and returns all parts, laid end to end along the dimension named above; an argument that names none is the same for every part. Nothing has to cross between parts.
Inputs may be any that keep to these rules, and one draw needn't show every extreme that they name: `g2m_face`: in each aligned block of 2048 rows (the rows of one device) no face block is named by more than 1024 rows, and in some such block a face block is named by exactly 1024 rows. `mesh_links`: each entry names a mesh node in the row's own block of 512 rows or in one of the two blocks beside it, the first and the last block counting as beside each other.
All inputs are finite; a program needn't handle non-finite values.
Results may differ from a plain program's by a relative error of at most 0.014.
Values may be sent and summed in bfloat16 or wider, within the bound.
No kernel may reach another device: no remote copies, remote signals or barrier semaphores. Data moves between devices by JAX's collectives and lax.ppermute only.
A program may use at most 128 MiB of HBM per device.

v0:
```python
import jax
import jax.numpy as jnp
from jax import lax
from jax.sharding import PartitionSpec as P


def extended_2(array, sides, width):
    for axis, dim in sides:
        size, length = (lax.axis_size(axis), array.shape[dim])
        up = [(i, (i + 1) % size) for i in range(size)]
        down = [(j, i) for i, j in up]
        last = lax.slice_in_dim(array, length - width, length, axis=dim)
        first = lax.slice_in_dim(array, 0, width, axis=dim)
        before = lax.ppermute(last, axis, up)
        after = lax.ppermute(first, axis, down)
        array = jnp.concatenate([before, array, after], axis=dim)
    return array


def from_behind(block, axis, distance):
    devices = range(lax.axis_size(axis))
    route = [((i - distance) % len(devices), i) for i in devices]
    return lax.ppermute(block, axis, route)


def silu_slope(values):
    sigmoid_v = jax.nn.sigmoid(values)
    return sigmoid_v * (1.0 + values * (1.0 - sigmoid_v))


def dot_plain(left, right):
    return jnp.dot(left, right, preferred_element_type=jnp.float32)


def dot_back(left, right):
    return lax.dot_general(
        left, right, (((1,), (1,)), ((), ())), preferred_element_type=jnp.float32
    )


def dot_left(left, right):
    return lax.dot_general(
        left, right, (((0,), (0,)), ((), ())), preferred_element_type=jnp.float32
    )


def mesh_wide(values):
    return lax.all_gather(values, "chan", axis=1, tiled=True)


def grad_wide(values):
    return lax.all_gather(values, "chan", axis=1, tiled=True)


def face_total(values):
    return lax.psum(values, "pipe")


def per_device(
    grid_latent,
    g2m_face,
    g2m_node,
    mesh_latent,
    mesh_links,
    w_enc,
    w_send,
    w_recv,
    w_node,
    w_dec,
    cotangent,
):
    face_count = lax.axis_size("space")
    pipe_count = lax.axis_size("pipe")
    grid_rows = grid_latent.shape[0]
    mesh_rows = mesh_latent.shape[0]
    narrow = mesh_latent.shape[1]
    col_start = lax.axis_index("chan") * narrow
    capacity = 2 * grid_rows // face_count
    slot_count = face_count * capacity
    mix_scale = (mesh_rows / (grid_rows * pipe_count)) ** 0.5
    layers = w_send.shape[0]

    def columns(weight):
        return lax.dynamic_slice_in_dim(weight, col_start, narrow, weight.ndim - 1)

    def row_block(weight):
        return lax.dynamic_slice_in_dim(weight, col_start, narrow, weight.ndim - 2)

    face_ids = g2m_face[:, 0]
    member = (face_ids[:, None] == jnp.arange(face_count, dtype=jnp.int32)[None, :]).astype(
        jnp.int32
    )
    slot_rank = jnp.sum(jnp.cumsum(member, axis=0) * member, axis=1) - 1
    slot_place = face_ids * capacity + slot_rank
    z_enc = dot_plain(grid_latent, columns(w_enc))
    enc_out = jax.nn.silu(z_enc).astype(jnp.bfloat16)
    send_vals = jnp.zeros((slot_count, narrow), jnp.bfloat16).at[slot_place].set(enc_out)
    send_ids = jnp.full((slot_count,), -1, jnp.int32).at[slot_place].set(g2m_node)
    recv_vals, recv_ids = (
        lax.all_to_all(send_vals, "space", split_axis=0, concat_axis=0, tiled=True),
        lax.all_to_all(send_ids, "space", split_axis=0, concat_axis=0, tiled=True),
    )
    picker = (recv_ids[None, :] == jnp.arange(mesh_rows, dtype=jnp.int32)[:, None]).astype(
        jnp.bfloat16
    )
    agg_first = face_total(dot_plain(picker, recv_vals))
    mesh_state = mesh_latent.astype(jnp.float32) + mix_scale * agg_first
    nbrs_all = mesh_links.shape[1] * pipe_count
    kept_nbrs = mesh_links.shape[1]
    owner_block = mesh_links // mesh_rows
    offset = (owner_block - lax.axis_index("space")) % face_count
    local_row = mesh_links % mesh_rows
    halo_spot = jnp.where(
        offset == 0,
        mesh_rows + local_row,
        jnp.where(offset == 1, 2 * mesh_rows + local_row, local_row),
    )
    flat_spot = halo_spot.reshape(-1)
    stored = []
    for step_index in range(layers):
        state_bf = mesh_state.astype(jnp.bfloat16)
        state_wide = mesh_wide(state_bf)
        send_p = dot_plain(state_wide, columns(w_send[step_index])).astype(jnp.bfloat16)
        recv_p = dot_plain(state_wide, columns(w_recv[step_index]))
        extended = extended_2(send_p, (("space", 0),), mesh_rows)
        pre_edge = (
            jnp.take(extended, flat_spot, axis=0)
            .reshape(mesh_rows, kept_nbrs, narrow)
            .astype(jnp.float32)
            + recv_p[:, None, :]
        )
        partial_value = jnp.sum(jax.nn.silu(pre_edge), axis=1) / nbrs_all
        partial_value = lax.psum(partial_value, "pipe")
        agg_b = partial_value.astype(jnp.bfloat16)
        agg_wide = lax.all_gather(agg_b, "chan", axis=1, tiled=True)
        mesh_state = mesh_state + dot_plain(agg_wide, columns(w_node[step_index]))
        stored.append((state_wide, pre_edge, agg_wide))
    last_b = mesh_state.astype(jnp.bfloat16)
    last_wide = mesh_wide(last_b)
    z_dec = dot_plain(last_wide, columns(w_dec))
    dec_out = jax.nn.silu(z_dec).astype(jnp.bfloat16)
    safe_ids = jnp.clip(recv_ids, 0, mesh_rows - 1)
    returned = lax.all_to_all(
        jnp.take(dec_out, safe_ids, axis=0), "space", split_axis=0, concat_axis=0, tiled=True
    )
    mixed = (
        columns(grid_latent).astype(jnp.float32)
        + jnp.take(returned, slot_place, axis=0).astype(jnp.float32)
    ).astype(jnp.bfloat16)
    send_cot = jnp.zeros((slot_count, narrow), jnp.bfloat16).at[slot_place].set(cotangent)
    recv_cot = lax.all_to_all(send_cot, "space", split_axis=0, concat_axis=0, tiled=True)
    back_dec = face_total(dot_plain(picker, recv_cot))
    dec_grad = (back_dec * silu_slope(z_dec)).astype(jnp.bfloat16)
    grad_w_dec = dot_left(last_wide, dec_grad)
    grad_state = dot_back(grad_wide(dec_grad), row_block(w_dec))
    send_list = [None] * layers
    recv_list = [None] * layers
    node_list = [None] * layers
    for step_index in reversed(range(layers)):
        state_wide, pre_edge, agg_wide = stored[step_index]
        grad_b = grad_state.astype(jnp.bfloat16)
        node_list[step_index] = dot_left(agg_wide, grad_b)
        back_agg = dot_back(grad_wide(grad_b), row_block(w_node[step_index]))
        back_pre = (back_agg / nbrs_all)[:, None, :] * silu_slope(pre_edge)
        back_recv = jnp.sum(back_pre, axis=1)
        spread = jax.ops.segment_sum(back_pre.reshape(-1, narrow), flat_spot, 3 * mesh_rows)
        from_above = from_behind(spread[:mesh_rows], "space", -1)
        from_below = from_behind(spread[2 * mesh_rows :], "space", 1)
        back_send = spread[mesh_rows : 2 * mesh_rows] + from_above + from_below
        back_send, back_recv = lax.psum((back_send, back_recv), "pipe")
        send_grad = back_send.astype(jnp.bfloat16)
        recv_grad = back_recv.astype(jnp.bfloat16)
        send_list[step_index] = dot_left(state_wide, send_grad)
        recv_list[step_index] = dot_left(state_wide, recv_grad)
        send_wide, recv_wide = (
            lax.all_gather(send_grad, "chan", axis=1, tiled=True),
            lax.all_gather(recv_grad, "chan", axis=1, tiled=True),
        )
        grad_state = (
            grad_state
            + dot_back(send_wide, row_block(w_send[step_index]))
            + dot_back(recv_wide, row_block(w_recv[step_index]))
        )
    enc_back = (mix_scale * grad_state).astype(jnp.bfloat16)
    returned_back = lax.all_to_all(
        jnp.take(enc_back, safe_ids, axis=0), "space", split_axis=0, concat_axis=0, tiled=True
    )
    enc_grad = (
        jnp.take(returned_back, slot_place, axis=0).astype(jnp.float32) * silu_slope(z_enc)
    ).astype(jnp.bfloat16)
    grad_w_enc = lax.psum(dot_left(grid_latent, enc_grad), ("space", "pipe"))
    cot_full = cotangent.astype(jnp.float32)
    grid_terms = dot_back(enc_grad, columns(w_enc))
    grad_grid = (
        cot_full + lax.psum_scatter(grid_terms, "chan", scatter_dimension=1, tiled=True)
    ).astype(jnp.bfloat16)
    grad_w_send, grad_w_recv, grad_w_node, grad_w_dec = lax.psum(
        (jnp.stack(send_list), jnp.stack(recv_list), jnp.stack(node_list), grad_w_dec), "space"
    )
    return (
        mixed,
        grad_grid,
        grad_state,
        grad_w_enc,
        grad_w_send,
        grad_w_recv,
        grad_w_node,
        grad_w_dec,
    )


def solution(mesh):
    in_specs = (
        P(("groups", "space", "pipe"), None),
        P(("groups", "space", "pipe"), None),
        P(("groups", "space", "pipe")),
        P(("groups", "space"), "chan"),
        P(("groups", "space"), "pipe"),
        P(),
        P(),
        P(),
        P(),
        P(),
        P(("groups", "space", "pipe"), "chan"),
    )
    out_specs = (
        P(("groups", "space", "pipe"), "chan"),
        P(("groups", "space", "pipe"), "chan"),
        P(("groups", "space"), "chan"),
        P("groups", "chan"),
        P("groups", None, "chan"),
        P("groups", None, "chan"),
        P("groups", None, "chan"),
        P("groups", "chan"),
    )
    return jax.shard_map(
        per_device, mesh=mesh, in_specs=in_specs, out_specs=out_specs, check_vma=False
    )
```

profile of v0, /device:TPU:0, one launch (start us, length us, event | category | flops | bytes accessed | tf_op | source)
XLA Modules:
  0.0 853.0 jit_solution(14841487224177264039)
XLA Ops:
  11.7 8.8 %scatter_custom_fusion = s32[4096]{0:T(1024)} fusion(s32[2048]{0:T(1024)S(1)} %bitcast.138, s32[2048]{0:T(1024)} %param.19, s32[]{:T(128)} %constant.119.clone.1), kind=kCustom, calls=%fused_computation.158 | custom fusion | bytes 16896 | tf_op jit(solution)/shard_map/scatter | solution.py:98
  20.5 6.3 all-to-all-start
  26.8 11.3 %scatter_custom_fusion.2 = bf16[4096,256]{1,0:T(8,128)(2,1)} fusion(s32[2048]{0:T(1024)S(1)} %bitcast.139, bf16[2048,256]{1,0:T(8,128)(2,1)} %param.27, bf16[]{:T(256)} %constant.122.clone.1), kind=kCustom, calls=%fused_computation.73 | custom fusion | bytes 2097664 | tf_op jit(solution)/shard_map/scatter | solution.py:150
  38.1 5.1 all-to-all-start.3
  43.2 4.1 multiply_convert_fusion.1
  49.6 11.3 %scatter_custom_fusion.1 = bf16[4096,256]{1,0:T(8,128)(2,1)} fusion(s32[2048]{0:T(1024)S(1)} %bitcast.140, bf16[2048,256]{1,0:T(8,128)(2,1)} %copy.27, bf16[]{:T(256)} %constant.122.clone.1), kind=kCustom, calls=%fused_computation.75 | custom fusion | bytes 2097664 | tf_op jit(solution)/shard_map/scatter | solution.py:97
  60.8 30.0 %all-to-all-done.3 = bf16[4,1024,256]{2,1,0:T(8,128)(2,1)S(1)} async-done(((bf16[4,1024,256]{2,1,0:T(8,128)(2,1)}), bf16[4,1024,256]{2,1,0:T(8,128)(2,1)S(1)}, u32[]{:S(2)}, u32[]{:S(2)}) %all-to-all-start.3) | async-done | bytes 2097184 | tf_op jit(solution)/shard_map/all_to_all | solution.py:151
  90.9 4.6 all-to-all-start.1
  98.6 44.6 %all-to-all-done.1 = bf16[4,1024,256]{2,1,0:T(8,128)(2,1)} async-done(((bf16[4,1024,256]{2,1,0:T(8,128)(2,1)}), bf16[4,1024,256]{2,1,0:T(8,128)(2,1)}, u32[]{:S(2)}, u32[]{:S(2)}) %all-to-all-start.1) | async-done | bytes 2097184 | tf_op jit(solution)/shard_map/all_to_all | solution.py:100
  143.2 3.8 fusion.1
  151.4 14.6 %all-reduce.16.cloned.1.call-done = (f32[512,256]{1,0:T(8,128)}, f32[512,256]{1,0:T(8,128)}) async-done(((f32[512,256]{1,0:T(8,128)}, f32[512,256]{1,0:T(8,128)}), (f32[512,256]{1,0:T(8,128)}, f32[512,256]{1,0:T(8,128)})) %all-reduce.16.cloned.1.call-update) | async-done | bytes 1048592 | tf_op jit(solution)/shard_map/psum | solution.py:56
  167.1 9.2 %all_gather.36 = bf16[512,512]{1,0:T(8,128)(2,1)S(1)} all-gather(bf16[512,256]{1,0:T(8,128)(2,1)S(1)} %fusion.37), channel_id=1, replica_groups=mesh['groups'=2,'space'=4,'chan'=2,'pipe'=2] {'chan'}, dimensions={1}, use_global_device_ids=true | all-gather | bytes 786432 | tf_op jit(solution)/shard_map/all_gather | solution.py:48
  180.6 6.4 collective-permute-done.1
  187.0 5.0 collective-permute-done
  192.1 4.8 gather_fusion
  205.0 5.6 all-reduce.17
  210.6 9.4 %all_gather.37 = bf16[512,512]{1,0:T(8,128)(2,1)S(1)} all-gather(bf16[512,256]{1,0:T(8,128)(2,1)S(1)} %all-reduce.17), channel_id=1, replica_groups=mesh['groups'=2,'space'=4,'chan'=2,'pipe'=2] {'chan'}, dimensions={1}, use_global_device_ids=true | all-gather | bytes 786432 | tf_op jit(solution)/shard_map/all_gather | solution.py:135
  222.4 8.4 all_gather.38
  247.5 5.4 gather_fusion.1
  259.2 3.9 multiply_reduce_fusion.2
  264.0 5.6 all-reduce.18
  269.6 9.4 %all_gather.39 = bf16[512,512]{1,0:T(8,128)(2,1)S(1)} all-gather(bf16[512,256]{1,0:T(8,128)(2,1)S(1)} %all-reduce.18), channel_id=1, replica_groups=mesh['groups'=2,'space'=4,'chan'=2,'pipe'=2] {'chan'}, dimensions={1}, use_global_device_ids=true | all-gather | bytes 786432 | tf_op jit(solution)/shard_map/all_gather | solution.py:135
  280.6 8.4 all_gather.40
  289.5 7.7 all_gather.41
  299.0 7.0 all_gather.42
  312.6 12.0 %scatter_custom_fusion.3 = f32[1536,256]{1,0:T(8,128)} fusion(s32[1536]{0:T(1024)S(1)} %reshape.100, f32[1536,256]{1,0:T(8,128)} %mul.121, f32[1536,256]{1,0:T(8,128)} %add.241, f32[]{:T(128)} %constant.123.clone.1, f32[]{:T(128)} %constant.132.clone.1, bf16[1536,256]{1,0:T(8,128)(2,1)} %gather_fusion.1, pred[1536]{0:T(1024)(128)(4,1)S(1)} %compare_and_fusion.2), kind=kCustom, calls=%fused_computation.41 | custom fusion | flops 4718592 | bytes 5507080 | tf_op jit(solution)/shard_map/scatter-add | solution.py:166
  330.7 4.8 multiply_reduce_fusion.1
  335.5 17.0 %gather_fusion.2 = bf16[4096,256]{1,0:T(8,128)(2,1)} fusion(bf16[512,256]{1,0:T(8,128)(2,1)S(1)} %get-tuple-element.56, s32[4096]{0:T(1024)S(1)} %fusion.74), kind=kCustom, calls=%fused_computation.1.clone | custom fusion | bytes 4210688 | tf_op jit(solution)/shard_map/jit(_take)/gather | solution.py:144
  354.9 7.1 all-reduce.19
  361.9 9.6 %all_gather.43 = bf16[512,512]{1,0:T(8,128)(2,1)S(1)} all-gather(bf16[512,256]{1,0:T(8,128)(2,1)} %get-tuple-element.41), channel_id=1, replica_groups=mesh['groups'=2,'space'=4,'chan'=2,'pipe'=2] {'chan'}, dimensions={1}, use_global_device_ids=true | all-gather | bytes 786432 | tf_op jit(solution)/shard_map/all_gather | solution.py:176
  371.5 8.4 all_gather.44
  383.3 7.5 all_gather.45
  393.7 3.8 mul.129
  397.6 12.1 %scatter_custom_fusion.4 = f32[1536,256]{1,0:T(8,128)} fusion(s32[1536]{0:T(1024)S(1)} %reshape.100, f32[1536,256]{1,0:T(8,128)} %mul.129, f32[1536,256]{1,0:T(8,128)} %add.250, f32[]{:T(128)} %constant.123.clone.1, f32[]{:T(128)} %constant.132.clone.1, bf16[1536,256]{1,0:T(8,128)(2,1)S(1)} %copy-done.13, pred[1536]{0:T(1024)(128)(4,1)S(1)} %compare_and_fusion.2), kind=kCustom, calls=%fused_computation.30 | custom fusion | flops 4718592 | bytes 5507080 | tf_op jit(solution)/shard_map/scatter-add | solution.py:166
  411.0 3.9 collective-permute-start.6
  417.8 9.4 %collective-permute-done.6 = f32[512,256]{1,0:T(8,128)S(1)} collective-permute-done((f32[512,256]{1,0:T(8,128)S(1)}, f32[512,256]{1,0:T(8,128)S(1)}, u32[]{:S(2)}, u32[]{:S(2)}) %collective-permute-start.6) | collective-permute-done | bytes 524320 | tf_op jit(solution)/shard_map/ppermute | solution.py:23
  427.2 8.7 %collective-permute-done.7 = f32[512,256]{1,0:T(8,128)S(1)} collective-permute-done((f32[512,256]{1,0:T(8,128)S(1)}, f32[512,256]{1,0:T(8,128)S(1)}, u32[]{:S(2)}, u32[]{:S(2)}) %collective-permute-start.7) | collective-permute-done | bytes 524320 | tf_op jit(solution)/shard_map/ppermute | solution.py:23
  437.1 6.4 all-reduce.20
  443.5 9.3 %all_gather.46 = bf16[512,512]{1,0:T(8,128)(2,1)S(1)} all-gather(bf16[512,256]{1,0:T(8,128)(2,1)S(1)} %get-tuple-element.39), channel_id=1, replica_groups=mesh['groups'=2,'space'=4,'chan'=2,'pipe'=2] {'chan'}, dimensions={1}, use_global_device_ids=true | all-gather | bytes 786432 | tf_op jit(solution)/shard_map/all_gather | solution.py:176
  452.8 8.4 all_gather.47
  463.6 17.0 %gather_fusion.4 = bf16[4096,256]{1,0:T(8,128)(2,1)} fusion(bf16[512,256]{1,0:T(8,128)(2,1)S(1)} %get-tuple-element.69, s32[4096]{0:T(1024)S(1)} %fusion.74), kind=kCustom, calls=%fused_computation.4.clone | custom fusion | bytes 4210688 | tf_op jit(solution)/shard_map/jit(_take)/gather | solution.py:186
  488.4 46.9 %all-to-all-done.4 = bf16[4,1024,256]{2,1,0:T(8,128)(2,1)S(1)} async-done(((bf16[4,1024,256]{2,1,0:T(8,128)(2,1)}), bf16[4,1024,256]{2,1,0:T(8,128)(2,1)S(1)}, u32[]{:S(2)}, u32[]{:S(2)}) %all-to-all-start.4) | async-done | bytes 2097184 | tf_op jit(solution)/shard_map/all_to_all | solution.py:185
  535.4 9.0 %gather_fusion.5 = bf16[2048,256]{1,0:T(8,128)(2,1)} fusion(bf16[4096,256]{1,0:T(8,128)(2,1)S(1)} %bitcast.125, s32[2048]{0:T(1024)S(1)} %get-tuple-element.57), kind=kCustom, calls=%fused_computation.5.clone | custom fusion | bytes 2105344 | tf_op jit(solution)/shard_map/jit(_take)/gather | solution.py:189
  567.8 45.2 %all-to-all-done.2 = bf16[4,1024,256]{2,1,0:T(8,128)(2,1)S(1)} async-done(((bf16[4,1024,256]{2,1,0:T(8,128)(2,1)}), bf16[4,1024,256]{2,1,0:T(8,128)(2,1)S(1)}, u32[]{:S(2)}, u32[]{:S(2)}) %all-to-all-start.2) | async-done | bytes 2097184 | tf_op jit(solution)/shard_map/all_to_all | solution.py:143
  612.9 9.0 %gather_fusion.3 = bf16[2048,256]{1,0:T(8,128)(2,1)} fusion(bf16[4096,256]{1,0:T(8,128)(2,1)S(1)} %bitcast.124, s32[2048]{0:T(1024)S(1)} %get-tuple-element.57), kind=kCustom, calls=%fused_computation.2.clone | custom fusion | bytes 2105344 | tf_op jit(solution)/shard_map/jit(_take)/gather | solution.py:148
  624.7 18.2 %all-reduce.12.cloned.1.call-done = f32[512,256]{0,1:T(8,128)} async-done(((f32[512,256]{0,1:T(8,128)}), f32[512,256]{0,1:T(8,128)}) %all-reduce.12.cloned.1.call-update) | async-done | bytes 524304 | tf_op jit(solution)/shard_map/psum | solution.py:191
  645.0 53.6 %reduce-scatter.2.cloned.1.call-done = f32[2048,256]{1,0:T(8,128)} async-done(((f32[2048,512]{1,0:T(8,128)}), f32[2048,256]{1,0:T(8,128)}) %reduce-scatter.2.cloned.1.call-update) | async-done | bytes 2097168 | tf_op jit(solution)/shard_map/reduce_scatter | solution.py:195
  701.4 139.5 %all-reduce.14.cloned.1.call-done = (f32[2,512,256]{2,1,0:T(8,128)}, f32[2,512,256]{2,1,0:T(8,128)}, f32[2,512,256]{2,1,0:T(8,128)}, f32[512,256]{1,0:T(8,128)}) async-done(((f32[2,512,256]{2,1,0:T(8,128)}, f32[2,512,256]{2,1,0:T(8,128)}, f32[2,512,256]{2,1,0:T(8,128)}, f32[512,256]{1,0:T(8,128)}), (f32[2,512,256]{2,1,0:T(8,128)}, f32[2,512,256]{2,1,0:T(8,128)}, f32[2,512,256]{2,1,0:T(8,128)}, ...) | async-done | bytes 3670032 | tf_op jit(solution)/shard_map/psum | solution.py:197
  (216 shorter events, 130.5 us)
Async XLA Ops:
  7.2 36.1 %copy-start = (bf16[512,512]{1,0:T(8,128)(2,1)S(1)}, bf16[512,512]{1,0:T(8,128)(2,1)}, u32[]{:S(2)}) copy-start(bf16[512,512]{1,0:T(8,128)(2,1)} %param.22) | copy-start | bytes 1572868
  20.5 17.6 %all-to-all-start = ((s32[4,1024,1]{1,2,0:T(1,128)}), s32[4,1024,1]{1,2,0:T(1,128)S(1)}, u32[]{:S(2)}, u32[]{:S(2)}) async-start(s32[4,1024,1]{1,2,0:T(1,128)} %bitcast.5), calls=%async_computation | async-start | bytes 32768 | tf_op jit(solution)/shard_map/all_to_all | solution.py:101
  38.1 52.7 %all-to-all-start.3 = ((bf16[4,1024,256]{2,1,0:T(8,128)(2,1)}), bf16[4,1024,256]{2,1,0:T(8,128)(2,1)S(1)}, u32[]{:S(2)}, u32[]{:S(2)}) async-start(bf16[4,1024,256]{2,1,0:T(8,128)(2,1)} %bitcast.18), calls=%async_computation.3 | async-start | bytes 4194304 | tf_op jit(solution)/shard_map/all_to_all | solution.py:151
  90.9 5.1 copy-start.55
  90.9 52.3 %all-to-all-start.1 = ((bf16[4,1024,256]{2,1,0:T(8,128)(2,1)}), bf16[4,1024,256]{2,1,0:T(8,128)(2,1)}, u32[]{:S(2)}, u32[]{:S(2)}) async-start(bf16[4,1024,256]{2,1,0:T(8,128)(2,1)} %bitcast.8), calls=%async_computation.1 | async-start | bytes 4194304 | tf_op jit(solution)/shard_map/all_to_all | solution.py:100
  95.5 70.5 %all-reduce.16.cloned.1.call-start = ((), (), s32[]{:S(2)}) async-start(), calls=%async_computation.9 | async-start | bytes 2097152 | tf_op jit(solution)/shard_map/psum | solution.py:56
  148.0 28.3 %copy-start.36 = (bf16[1,512,512]{2,1,0:T(8,128)(2,1)}, bf16[1,512,512]{2,1,0:T(8,128)(2,1)S(1)}, u32[]{:S(2)}) copy-start(bf16[1,512,512]{2,1,0:T(8,128)(2,1)S(1)} %get-tuple-element.54) | copy-start | bytes 1572868
  148.0 18.0 %copy-start.48 = (bf16[512,256]{1,0:T(8,128)(2,1)S(1)}, bf16[512,256]{1,0:T(8,128)(2,1)}, u32[]{:S(2)}) copy-start(bf16[512,256]{1,0:T(8,128)(2,1)} %param.20) | copy-start | bytes 786436
  150.3 30.0 %copy-start.27 = (bf16[1,512,512]{2,1,0:T(8,128)(2,1)}, bf16[1,512,512]{2,1,0:T(8,128)(2,1)S(1)}, u32[]{:S(2)}) copy-start(bf16[1,512,512]{2,1,0:T(8,128)(2,1)S(1)} %get-tuple-element.52) | copy-start | bytes 1572868
  176.3 10.7 %copy-start.2 = (bf16[512,512]{1,0:T(8,128)(2,1)}, bf16[512,512]{1,0:T(8,128)(2,1)S(1)}, u32[]{:S(2)}) copy-start(bf16[512,512]{1,0:T(8,128)(2,1)S(1)} %all_gather.36) | copy-start | bytes 1572868
  176.6 10.4 %collective-permute-start.1 = (bf16[512,256]{1,0:T(8,128)(2,1)S(1)}, bf16[512,256]{1,0:T(8,128)(2,1)S(1)}, u32[]{:S(2)}, u32[]{:S(2)}) collective-permute-start(bf16[512,256]{1,0:T(8,128)(2,1)S(1)} %convolution_convert_fusion.1), channel_id=1, source_target_pairs={{4,0},{8,4},{12,8},{0,12},{5,1},{9,5},{13,9},{1,13},{6,2},{10,6},{... | collective-permute-start | bytes 786440 | tf_op jit(solution)/shard_map/ppermute | solution.py:15
  180.3 11.8 %collective-permute-start = (bf16[512,256]{1,0:T(8,128)(2,1)S(1)}, bf16[512,256]{1,0:T(8,128)(2,1)S(1)}, u32[]{:S(2)}, u32[]{:S(2)}) collective-permute-start(bf16[512,256]{1,0:T(8,128)(2,1)S(1)} %convolution_convert_fusion.1), channel_id=1, source_target_pairs={{0,4},{4,8},{8,12},{12,0},{1,5},{5,9},{9,13},{13,1},{2,6},{6,10},{... | collective-permute-start | bytes 786440 | tf_op jit(solution)/shard_map/ppermute | solution.py:14
  180.6 21.2 %copy-start.6 = (f32[512,256]{1,0:T(8,128)}, f32[512,256]{1,0:T(8,128)S(1)}, u32[]{:S(2)}) copy-start(f32[512,256]{1,0:T(8,128)S(1)} %fusion.49) | copy-start | bytes 1572868
  204.2 15.9 %copy-start.25 = (f32[512,256]{1,0:T(8,128)S(1)}, f32[512,256]{1,0:T(8,128)}, u32[]{:S(2)}) copy-start(f32[512,256]{1,0:T(8,128)} %get-tuple-element.43) | copy-start | bytes 1572868
  210.6 20.2 %copy-start.37 = (bf16[1,512,512]{2,1,0:T(8,128)(2,1)S(1)}, bf16[1,512,512]{2,1,0:T(8,128)(2,1)}, u32[]{:S(2)}) copy-start(bf16[1,512,512]{2,1,0:T(8,128)(2,1)} %get-tuple-element.53) | copy-start | bytes 1572868
  220.0 11.1 %copy-start.17 = (bf16[512,512]{1,0:T(8,128)(2,1)}, bf16[512,512]{1,0:T(8,128)(2,1)S(1)}, u32[]{:S(2)}) copy-start(bf16[512,512]{1,0:T(8,128)(2,1)S(1)} %all_gather.37) | copy-start | bytes 1572868
  220.0 13.3 %copy-start.7 = (f32[512,256]{1,0:T(8,128)S(1)}, f32[512,256]{1,0:T(8,128)}, u32[]{:S(2)}) copy-start(f32[512,256]{1,0:T(8,128)} %copy-done.6) | copy-start | bytes 1572868
  230.8 8.1 copy-start.4
  231.1 7.8 copy-start.50
  231.1 15.2 %collective-permute-start.3 = (bf16[512,256]{1,0:T(8,128)(2,1)S(1)}, bf16[512,256]{1,0:T(8,128)(2,1)}, u32[]{:S(2)}, u32[]{:S(2)}) collective-permute-start(bf16[512,256]{1,0:T(8,128)(2,1)S(1)} %convolution_convert_fusion), channel_id=1, source_target_pairs={{4,0},{8,4},{12,8},{0,12},{5,1},{9,5},{13,9},{1,13},{6,2},{10,6},{... | collective-permute-start | bytes 786440 | tf_op jit(solution)/shard_map/ppermute | solution.py:15
  232.9 13.4 %collective-permute-start.2 = (bf16[512,256]{1,0:T(8,128)(2,1)S(1)}, bf16[512,256]{1,0:T(8,128)(2,1)}, u32[]{:S(2)}, u32[]{:S(2)}) collective-permute-start(bf16[512,256]{1,0:T(8,128)(2,1)S(1)} %convolution_convert_fusion), channel_id=1, source_target_pairs={{0,4},{4,8},{8,12},{12,0},{1,5},{5,9},{9,13},{13,1},{2,6},{6,10},{... | collective-permute-start | bytes 786440 | tf_op jit(solution)/shard_map/ppermute | solution.py:14
  269.6 19.5 %copy-start.54 = (bf16[512,512]{1,0:T(8,128)(2,1)S(1)}, bf16[512,512]{1,0:T(8,128)(2,1)}, u32[]{:S(2)}) copy-start(bf16[512,512]{1,0:T(8,128)(2,1)} %param.26) | copy-start | bytes 1572868
  269.6 19.5 %copy-start.56 = (f32[512,256]{1,0:T(8,128)S(1)}, f32[512,256]{1,0:T(8,128)}, u32[]{:S(2)}) copy-start(f32[512,256]{1,0:T(8,128)} %get-tuple-element.44) | copy-start | bytes 1572868
  279.0 10.5 %copy-start.19 = (bf16[512,512]{1,0:T(8,128)(2,1)}, bf16[512,512]{1,0:T(8,128)(2,1)S(1)}, u32[]{:S(2)}) copy-start(bf16[512,512]{1,0:T(8,128)(2,1)S(1)} %all_gather.39) | copy-start | bytes 1572868
  289.0 8.1 copy-start.29
  289.4 16.6 %copy-start.38 = (bf16[512,256]{1,0:T(8,128)(2,1)}, bf16[512,256]{1,0:T(8,128)(2,1)S(1)}, u32[]{:S(2)}) copy-start(bf16[512,256]{1,0:T(8,128)(2,1)S(1)} %get-tuple-element.55) | copy-start | bytes 786436
  289.5 16.6 %copy-start.34 = (bf16[1,512,512]{2,1,0:T(8,128)(2,1)S(1)}, bf16[1,512,512]{2,1,0:T(8,128)(2,1)}, u32[]{:S(2)}) copy-start(bf16[1,512,512]{2,1,0:T(8,128)(2,1)} %get-tuple-element.49) | copy-start | bytes 1572868
  324.6 6.1 copy-start.1
  327.0 25.6 %collective-permute-start.4 = (f32[512,256]{1,0:T(8,128)}, f32[512,256]{1,0:T(8,128)}, u32[]{:S(2)}, u32[]{:S(2)}) collective-permute-start(f32[512,256]{1,0:T(8,128)} %get-tuple-element.47), channel_id=1, source_target_pairs={{4,0},{8,4},{12,8},{0,12},{5,1},{9,5},{13,9},{1,13},{6,2},{10,6},{... | collective-permute-start | bytes 1572872 | tf_op jit(solution)/shard_map/ppermute | solution.py:23
  330.7 21.9 %collective-permute-start.5 = (f32[512,256]{1,0:T(8,128)}, f32[512,256]{1,0:T(8,128)}, u32[]{:S(2)}, u32[]{:S(2)}) collective-permute-start(f32[512,256]{1,0:T(8,128)} %get-tuple-element.48), channel_id=1, source_target_pairs={{12,0},{0,4},{4,8},{8,12},{13,1},{1,5},{5,9},{9,13},{14,2},{2,6},{... | collective-permute-start | bytes 1572872 | tf_op jit(solution)/shard_map/ppermute | solution.py:23
  361.9 20.7 %copy-start.40 = (bf16[512,256]{1,0:T(8,128)(2,1)}, bf16[512,256]{1,0:T(8,128)(2,1)S(1)}, u32[]{:S(2)}) copy-start(bf16[512,256]{1,0:T(8,128)(2,1)S(1)} %get-tuple-element.42) | copy-start | bytes 786436
  361.9 19.5 %copy-start.32 = (bf16[1,512,512]{2,1,0:T(8,128)(2,1)S(1)}, bf16[1,512,512]{2,1,0:T(8,128)(2,1)}, u32[]{:S(2)}) copy-start(bf16[1,512,512]{2,1,0:T(8,128)(2,1)} %get-tuple-element.51) | copy-start | bytes 1572868
  380.0 10.9 %copy-start.31 = (bf16[1,512,512]{2,1,0:T(8,128)(2,1)S(1)}, bf16[1,512,512]{2,1,0:T(8,128)(2,1)}, u32[]{:S(2)}) copy-start(bf16[1,512,512]{2,1,0:T(8,128)(2,1)} %get-tuple-element.50) | copy-start | bytes 1572868
  409.6 5.2 copy-start.8
  409.6 5.2 copy-start.15
  411.0 16.2 %collective-permute-start.6 = (f32[512,256]{1,0:T(8,128)S(1)}, f32[512,256]{1,0:T(8,128)S(1)}, u32[]{:S(2)}, u32[]{:S(2)}) collective-permute-start(f32[512,256]{1,0:T(8,128)S(1)} %get-tuple-element.45), channel_id=1, source_target_pairs={{4,0},{8,4},{12,8},{0,12},{5,1},{9,5},{13,9},{1,13},{6,2},{10,6},{... | collective-permute-start | bytes 1572872 | tf_op jit(solution)/shard_map/ppermute | solution.py:23
  414.9 21.0 %collective-permute-start.7 = (f32[512,256]{1,0:T(8,128)S(1)}, f32[512,256]{1,0:T(8,128)S(1)}, u32[]{:S(2)}, u32[]{:S(2)}) collective-permute-start(f32[512,256]{1,0:T(8,128)S(1)} %get-tuple-element.46), channel_id=1, source_target_pairs={{12,0},{0,4},{4,8},{8,12},{13,1},{1,5},{5,9},{9,13},{14,2},{2,6},{... | collective-permute-start | bytes 1572872 | tf_op jit(solution)/shard_map/ppermute | solution.py:23
  417.8 43.4 %copy-start.33 = (f32[512,256]{1,0:T(8,128)S(1)}, f32[512,256]{1,0:T(8,128)}, u32[]{:S(2)}) copy-start(f32[512,256]{1,0:T(8,128)} %get-tuple-element.68) | copy-start | bytes 1572868
  437.1 25.4 %copy-start.28 = (bf16[1,512,512]{2,1,0:T(8,128)(2,1)S(1)}, bf16[1,512,512]{2,1,0:T(8,128)(2,1)}, u32[]{:S(2)}) copy-start(bf16[1,512,512]{2,1,0:T(8,128)(2,1)} %copy-done.27) | copy-start | bytes 1572868
  443.5 17.7 %copy-start.43 = (bf16[512,256]{1,0:T(8,128)(2,1)}, bf16[512,256]{1,0:T(8,128)(2,1)S(1)}, u32[]{:S(2)}) copy-start(bf16[512,256]{1,0:T(8,128)(2,1)S(1)} %get-tuple-element.40) | copy-start | bytes 786436
  463.6 17.0 %copy-start.11 = (bf16[4096,256]{1,0:T(8,128)(2,1)S(1)}, bf16[4096,256]{1,0:T(8,128)(2,1)}, u32[]{:S(2)}) copy-start(bf16[4096,256]{1,0:T(8,128)(2,1)} %gather_fusion.2) | copy-start | bytes 6291460
  484.4 4.1 copy-start.53
  484.4 51.0 %all-to-all-start.4 = ((bf16[4,1024,256]{2,1,0:T(8,128)(2,1)}), bf16[4,1024,256]{2,1,0:T(8,128)(2,1)S(1)}, u32[]{:S(2)}, u32[]{:S(2)}) async-start(bf16[4,1024,256]{2,1,0:T(8,128)(2,1)} %bitcast.127), calls=%async_computation.4 | async-start | bytes 4194304 | tf_op jit(solution)/shard_map/all_to_all | solution.py:185
  488.1 154.8 %all-reduce.12.cloned.1.call-start = ((), (), s32[]{:S(2)}) async-start(), calls=%async_computation.7 | async-start | bytes 1048576 | tf_op jit(solution)/shard_map/psum | solution.py:191
  550.0 148.6 %reduce-scatter.2.cloned.1.call-start = ((), (), s32[]{:S(2)}) async-start(), calls=%async_computation.6 | async-start | bytes 6291456 | tf_op jit(solution)/shard_map/reduce_scatter | solution.py:195
  559.1 53.9 %all-to-all-start.2 = ((bf16[4,1024,256]{2,1,0:T(8,128)(2,1)}), bf16[4,1024,256]{2,1,0:T(8,128)(2,1)S(1)}, u32[]{:S(2)}, u32[]{:S(2)}) async-start(bf16[4,1024,256]{2,1,0:T(8,128)(2,1)} %bitcast.126), calls=%async_computation.2 | async-start | bytes 4194304 | tf_op jit(solution)/shard_map/all_to_all | solution.py:143
  562.8 278.1 %all-reduce.14.cloned.1.call-start = ((), (), s32[]{:S(2)}) async-start(), calls=%async_computation.8 | async-start | bytes 7340032 | tf_op jit(solution)/shard_map/psum | solution.py:197
  622.0 76.6 %copy-start.49 = (bf16[2048,256]{1,0:T(8,128)(2,1)S(1)}, bf16[2048,256]{1,0:T(8,128)(2,1)}, u32[]{:S(2)}) copy-start(bf16[2048,256]{1,0:T(8,128)(2,1)} %param.27) | copy-start | bytes 3145732
  (26 other events, 55.3 us)
Sparse Core Ops, SparseCore 0:
  147.2 18.7 all-reduce.15
  550.1 92.8 all-reduce.11
  645.2 53.2 reduce-scatter.1
  701.8 139.0 all-reduce.13
where the time goes:
time: 862 us; the launch traced here: 853 us
  waiting for transfers between devices  422 us (49%)
  local copies, waits for them, and re-layouts  147 us (17%)
  blocking collectives  127 us (15%)
  other arithmetic  70 us (8%)
  starting transfers between devices  37.8 us (4%)
  matrix products  33.4 us (4%)
  between operations  14.8 us (2%)
    psum x1, waiting for transfers between devices, per_device(): lax.psum((jnp.stack(send_list), jnp.stack(recv_list), jnp.stack(node_list...  140 us
    reduce_scatter x1, waiting for transfers between devices, per_device(): lax.psum_scatter(grid_terms, 'chan', scatter_dimension=1, tiled=True)  53.6 us
    all_to_all x1, waiting for transfers between devices, per_device(): lax.all_to_all(jnp.take(enc_back, safe_ids, axis=0), 'space', split_axis=...  46.9 us
    all_to_all x1, waiting for transfers between devices, per_device(): lax.all_to_all(jnp.take(dec_out, safe_ids, axis=0), 'space', split_axis=0...  45.2 us
    all_to_all x1, waiting for transfers between devices, per_device(): lax.all_to_all(send_vals, 'space', split_axis=0, concat_axis=0, tiled=True)  44.6 us
    all_to_all x1, waiting for transfers between devices, per_device(): lax.all_to_all(send_cot, 'space', split_axis=0, concat_axis=0, tiled=True)  30 us
    all_gather x3, blocking collectives, mesh_wide(): return lax.all_gather(values, 'chan', axis=1, tiled=True)  26 us
    scatter-add x2, other arithmetic, per_device(): jax.ops.segment_sum(back_pre.reshape(-1, narrow), flat_spot, 3 * mesh_rows)  24 us
  transfers between devices with their start and end apart: 17, of which 12 were waited for; matrix products, arithmetic and copies ran while one was open for 12% of the time, Pallas kernels for 0%

commit v1 on v0

v1 whole, which is shorter than its diff:
```python
import functools

import jax
import jax.numpy as jnp
from jax import lax
from jax.experimental import pallas as pl
from jax.experimental.pallas import tpu as pltpu
from jax.sharding import PartitionSpec as P

F32, BF16 = jnp.float32, jnp.bfloat16
FACE_AXES = ("chan", "pipe")


def shifted(block, axis, distance):
    count = lax.axis_size(axis)
    return lax.ppermute(block, axis, [((i + distance) % count, i) for i in range(count)])


def dot_plain(left, right):
    return jnp.dot(left, right, preferred_element_type=F32)


def dot_back(left, right):
    return lax.dot_general(left, right, (((1,), (1,)), ((), ())), preferred_element_type=F32)


def dot_left(left, right):
    return lax.dot_general(left, right, (((0,), (0,)), ((), ())), preferred_element_type=F32)


def slope_of(values, sigmoid_v):
    return sigmoid_v * (1.0 + values * (1.0 - sigmoid_v))


def one_hot(rows, ids):
    return jnp.where(rows == ids, 1.0, 0.0).astype(BF16)


def pick(values, index, width):
    out = values[:, :width]
    for j in range(1, values.shape[1] // width):
        out = jnp.where(index == j, values[:, j * width : (j + 1) * width], out)
    return out


def widen(parts):
    return jnp.concatenate([parts[j] for j in range(parts.shape[0])], axis=1)


def whole(shape):
    return pl.BlockSpec(shape, lambda i, sr: (0,) * len(shape))


def layer_of(shape, layer):
    return pl.BlockSpec((None,) + shape[1:], lambda i, sr: (layer, 0, 0))


def run(body, scalars, args, outs, scratch=(), flops=0, specs=None):
    specs = specs or {}
    return pl.pallas_call(
        body,
        out_shape=[jax.ShapeDtypeStruct(s, d) for s, d in outs],
        grid_spec=pltpu.PrefetchScalarGridSpec(
            num_scalar_prefetch=1,
            grid=(1,),
            in_specs=[specs.get(i, whole(a.shape)) for i, a in enumerate(args)],
            out_specs=[whole(s) for s, _ in outs],
            scratch_shapes=list(scratch),
        ),
        compiler_params=pltpu.CompilerParams(vmem_limit_bytes=56 * 1024 * 1024),
        cost_estimate=pl.CostEstimate(flops=flops, bytes_accessed=0, transcendentals=0),
    )(scalars, *args)


def rows_at(index, size):
    return pl.ds(pl.multiple_of(index * size, size), size)


def sum_by_node(sr, target, values, keep, give):
    mesh_all, width = keep.shape
    grid_rows = values.shape[0]
    size = 256

    def step(i, carry):
        ids = lax.broadcasted_iota(jnp.int32, (size, grid_rows), 0) + i * size
        total = dot_plain(one_hot(ids, target[...]), values[...])
        low, high = total[:, :width], total[:, width:]
        first = sr[1] == 0
        keep[rows_at(i, size), :] = jnp.where(first, low, high).astype(BF16)
        give[rows_at(i, size), :] = jnp.where(first, high, low).astype(BF16)
        return carry

    lax.fori_loop(0, mesh_all // size, step, 0)


def encode_body(sr, x, w, target, keep, give, enc):
    size = 512

    def step(i, carry):
        z = dot_plain(x[rows_at(i, size), :], w[...])
        enc[rows_at(i, size), :] = (z * jax.nn.sigmoid(z)).astype(BF16)
        return carry

    lax.fori_loop(0, x.shape[0] // size, step, 0)
    sum_by_node(sr, target, enc, keep, give)


def project(sr, state_b, w_send, w_recv, send_p, recv_p):
    width = send_p.shape[1]
    send_p[...] = dot_plain(state_b, pick(w_send[...], sr[2], width)).astype(BF16)
    recv_p[...] = dot_plain(state_b, pick(w_recv[...], sr[2], width))


def first_body(sr, parts, w_send, w_recv, state_b, send_p, recv_p):
    wide = widen(parts)
    state_b[...] = wide
    project(sr, wide, w_send, w_recv, send_p, recv_p)


def next_body(sr, agg, state, w_node, w_send, w_recv, agg_wide, new_state, state_b, send_p, recv_p):
    wide = widen(agg)
    agg_wide[...] = wide
    total = state[...].astype(F32) + dot_plain(wide, w_node[...])
    new_state[...] = total
    narrow = total.astype(BF16)
    state_b[...] = narrow
    project(sr, narrow, w_send, w_recv, send_p, recv_p)


def edge_body(sr, below, own, above, recv_p, spot, agg, slope, halo):
    mesh_rows = own.shape[0]
    halo[:mesh_rows, :] = below[...]
    halo[mesh_rows : 2 * mesh_rows, :] = own[...]
    halo[2 * mesh_rows :, :] = above[...]
    ids = lax.broadcasted_iota(jnp.int32, (mesh_rows, 3 * mesh_rows), 1)
    count = slope.shape[0]
    total = jnp.zeros(agg.shape, F32)
    for k in range(count):
        pre = dot_plain(one_hot(ids, spot[:, k : k + 1]), halo[...]) + recv_p[...]
        sigmoid_v = jax.nn.sigmoid(pre)
        total = total + pre * sigmoid_v
        slope[k] = slope_of(pre, sigmoid_v)
    agg[...] = (total / count).astype(BF16)


def edge_back(sr, grad_b, w_node, slope, spot, recv_grad, below, own, above, back):
    mesh_rows, width = recv_grad.shape
    count = slope.shape[0]
    w_rows = w_node[rows_at(sr[2], width), :]
    back_agg = dot_back(grad_b, w_rows) / count
    total = jnp.zeros(recv_grad.shape, F32)
    for k in range(count):
        term = back_agg * slope[k]
        total = total + term
        back[k * mesh_rows : (k + 1) * mesh_rows, :] = term.astype(BF16)
    recv_grad[...] = total.astype(BF16)
    size = 256
    ids = lax.broadcasted_iota(jnp.int32, (size, count * mesh_rows), 0)
    for place, out in enumerate((below, own, above)):
        for half in range(mesh_rows // size):
            first = place * mesh_rows + half * size
            spread = dot_plain(one_hot(ids + first, spot[...]), back[...])
            out[half * size : (half + 1) * size, :] = spread.astype(out.dtype)


def turn_body(
    sr, agg, state, w_node, w_dec, back_dec, slope, spot,
    agg_wide, last_b, dec_part, dec_grad, grad, grad_b, recv_grad, below, own, above, back,
):
    wide = widen(agg)
    agg_wide[...] = wide
    last = (state[...] + dot_plain(wide, w_node[...])).astype(BF16)
    last_b[...] = last
    z_dec = dot_plain(last, w_dec[...])
    sigmoid_v = jax.nn.sigmoid(z_dec)
    dec_part[...] = pick(z_dec * sigmoid_v, sr[2], dec_part.shape[1]).astype(BF16)
    back_wide = widen(back_dec).astype(F32)
    down = (back_wide * slope_of(z_dec, sigmoid_v)).astype(BF16)
    dec_grad[...] = down
    total = dot_back(down, w_dec[...])
    grad[...] = total
    narrow = total.astype(BF16)
    grad_b[...] = narrow
    edge_back(sr, narrow, w_node, slope, spot, recv_grad, below, own, above, back)


def through(grad, send_wide, recv_wide, w_send, w_recv):
    return grad[...] + dot_back(send_wide, w_send[...]) + dot_back(recv_wide, w_recv[...])


def back_body(
    sr, grad, send_parts, recv_parts, w_send, w_recv, w_node, slope, spot,
    send_out, recv_out, new_grad, grad_b, recv_grad, below, own, above, back,
):
    send_wide, recv_wide = widen(send_parts), widen(recv_parts)
    send_out[...] = send_wide
    recv_out[...] = recv_wide
    total = through(grad, send_wide, recv_wide, w_send, w_recv)
    new_grad[...] = total
    narrow = total.astype(BF16)
    grad_b[...] = narrow
    edge_back(sr, narrow, w_node, slope, spot, recv_grad, below, own, above, back)


def last_body(mix_scale, sr, grad, send_parts, recv_parts, w_send, w_recv, send_out, recv_out, grad_mesh, enc_part):
    send_wide, recv_wide = widen(send_parts), widen(recv_parts)
    send_out[...] = send_wide
    recv_out[...] = recv_wide
    total = through(grad, send_wide, recv_wide, w_send, w_recv)
    grad_mesh[...] = pick(total, sr[0], grad_mesh.shape[1])
    enc_part[...] = (mix_scale * pick(total, sr[2], enc_part.shape[1])).astype(BF16)


def two_halves(sr, mine, other):
    first = sr[1] == 0
    return (
        jnp.where(first, mine[...], other[...]),
        jnp.where(first, other[...], mine[...]),
    )


def fill_table(sr, table, column, mine, other):
    low, high = two_halves(sr, mine, other)
    width = low.shape[1]
    table[:, column : column + width] = low
    table[:, column + width : column + 2 * width] = high


def mixed_body(sr, x, target, mine, other, mixed, table):
    fill_table(sr, table, 0, mine, other)
    size = 256

    def step(i, carry):
        at = rows_at(i, size)
        ids = lax.broadcasted_iota(jnp.int32, (size, table.shape[0]), 1)
        got = dot_plain(one_hot(ids, target[at, :]), table[...])
        mixed[at, :] = (x[at, :].astype(F32) + got).astype(BF16)
        return carry

    lax.fori_loop(0, x.shape[0] // size, step, 0)


def enc_own_body(sr, x, w, target, mine, other, enc_grad, grad_keep, grad_give, table, total):
    fill_table(sr, table, 0, mine, other)
    size = 256
    total[...] = jnp.zeros(total.shape, F32)

    def step(i, carry):
        at = rows_at(i, size)
        ids = lax.broadcasted_iota(jnp.int32, (size, table.shape[0]), 1)
        got = dot_plain(one_hot(ids, target[at, :]), table[...])
        z = dot_plain(x[at, :], w[...])
        down = (got * slope_of(z, jax.nn.sigmoid(z))).astype(BF16)
        enc_grad[at, :] = down
        total[...] += dot_left(x[at, :], down)
        return carry

    lax.fori_loop(0, x.shape[0] // size, step, 0)
    half = grad_keep.shape[0]
    grad_keep[...] = total[rows_at(sr[1], half), :]
    grad_give[...] = total[rows_at(1 - sr[1], half), :].astype(BF16)


def enc_other_body(count, sr, x, target, cotangent, enc_grad, w_own, w_own_rows, *rest):
    w_cols, w_rows = rest[:count], rest[count : 2 * count]
    mine, other = rest[2 * count : 3 * count], rest[3 * count : 4 * count]
    grad_grid, table = rest[4 * count :]
    narrow = cotangent.shape[1]
    for j in range(count):
        fill_table(sr, table, j * narrow, mine[j], other[j])
    size = 256

    def step(i, carry):
        at = rows_at(i, size)
        ids = lax.broadcasted_iota(jnp.int32, (size, table.shape[0]), 1)
        got = dot_plain(one_hot(ids, target[at, :]), table[...])
        total = cotangent[at, :].astype(F32) + dot_back(enc_grad[at, :], w_own_rows[...])
        for j in range(count):
            z = dot_plain(x[at, :], w_cols[j][...])
            part = got[:, j * narrow : (j + 1) * narrow]
            down = (part * slope_of(z, jax.nn.sigmoid(z))).astype(BF16)
            total = total + dot_back(down, w_rows[j][...])
        grad_grid[at, :] = total.astype(BF16)
        return carry

    lax.fori_loop(0, x.shape[0] // size, step, 0)


def weight_body(pairs, sr, *refs):
    outs = refs[2 * pairs :]
    for i in range(pairs):
        left, right, out = refs[2 * i], refs[2 * i + 1], outs[i]
        rows, columns = out.shape
        out[...] = dot_left(pick(left[...], sr[1], rows), pick(right[...], sr[0], columns))


def per_device(
    grid_latent, g2m_face, g2m_node, mesh_latent, mesh_links,
    w_enc, w_send, w_recv, w_node, w_dec, cotangent,
):
    face_count = lax.axis_size("space")
    pipe_count = lax.axis_size("pipe")
    chan_count = lax.axis_size("chan")
    grid_rows, wide = grid_latent.shape
    mesh_rows, narrow = mesh_latent.shape
    part = narrow // pipe_count
    mesh_all = face_count * mesh_rows
    mix_scale = (mesh_rows / (grid_rows * pipe_count)) ** 0.5
    nbrs = mesh_links.shape[1] * pipe_count
    chan, pipe, face = (lax.axis_index(a) for a in ("chan", "pipe", "space"))
    scalars = jnp.stack(
        [chan, pipe, chan * pipe_count + pipe]
        + [(chan + j) % chan_count for j in range(1, chan_count)]
    ).astype(jnp.int32)

    target = ((g2m_face[:, 0] - face) % face_count) * mesh_rows + g2m_node
    target_row = target.reshape(1, grid_rows)
    target_col = target.reshape(grid_rows, 1)

    links = lax.all_gather(mesh_links, "pipe", axis=1, tiled=True)
    offset = (links // mesh_rows - face) % face_count
    local = links % mesh_rows
    spot = jnp.where(
        offset == 0, mesh_rows + local, jnp.where(offset == 1, 2 * mesh_rows + local, local)
    )
    spot_row = spot.T.reshape(1, nbrs * mesh_rows)

    def columns_at(place):
        return pl.BlockSpec((wide, narrow), lambda i, sr: (0, sr[place]))

    def to_owner(keep, give):
        mixed_sum = keep.astype(F32) + shifted(give, "pipe", 1).astype(F32)
        blocks = mixed_sum.astype(BF16).reshape(face_count, mesh_rows, part)
        total = blocks[0].astype(F32)
        for k in range(1, face_count):
            total = total + shifted(blocks[k], "space", -k).astype(F32)
        return total

    def face_wide(block):
        return lax.all_gather(block, FACE_AXES)

    def from_owners(block):
        parts = [block] + [shifted(block, "space", k) for k in range(1, face_count)]
        return jnp.concatenate(parts, axis=0)

    sums = [((mesh_all, part), BF16)] * 2
    sum_flops = 2 * mesh_all * grid_rows * narrow
    keep, give = run(
        encode_body, scalars, (grid_latent, w_enc, target_row), sums,
        scratch=[pltpu.VMEM((grid_rows, narrow), BF16)],
        flops=sum_flops + 2 * grid_rows * wide * narrow, specs={1: columns_at(0)},
    )
    mesh_part = lax.dynamic_slice_in_dim(mesh_latent, pipe * part, part, 1)
    state_part = mesh_part.astype(F32) + mix_scale * to_owner(keep, give)
    parts = face_wide(state_part.astype(BF16))

    keep, give = run(sum_by_node, scalars, (target_row, cotangent), sums, flops=sum_flops)
    back_dec = face_wide(to_owner(keep, give).astype(BF16))

    block = (mesh_rows, part)
    full = (mesh_rows, wide)
    edge_flops = 6 * mesh_rows * mesh_rows * nbrs * part
    layer_specs = lambda first, layer: {
        first: layer_of(w_send.shape, layer), first + 1: layer_of(w_recv.shape, layer)
    }

    def edges(send_p, recv_p):
        return run(
            edge_body, scalars,
            (shifted(send_p, "space", -1), send_p, shifted(send_p, "space", 1), recv_p, spot),
            [(block, BF16), ((nbrs,) + block, F32)],
            scratch=[pltpu.VMEM((3 * mesh_rows, part), BF16)], flops=edge_flops,
        )

    state_0, send_p, recv_p = run(
        first_body, scalars, (parts, w_send, w_recv),
        [(full, BF16), (block, BF16), (block, F32)], specs=layer_specs(1, 0),
        flops=4 * mesh_rows * wide * part,
    )
    agg, slope_0 = edges(send_p, recv_p)
    agg_0, state, state_1, send_p, recv_p = run(
        next_body, scalars, (face_wide(agg), state_0, w_node, w_send, w_recv),
        [(full, BF16), (full, F32), (full, BF16), (block, BF16), (block, F32)],
        specs={2: layer_of(w_node.shape, 0), **layer_specs(3, 1)},
        flops=2 * mesh_rows * wide * wide,
    )
    agg, slope_1 = edges(send_p, recv_p)
    back_outs = [(full, F32), (full, BF16), (block, BF16), (block, BF16), (block, F32), (block, BF16)]
    back_scratch = [pltpu.VMEM((nbrs * mesh_rows, part), BF16)]
    agg_1, last_b, dec_part, dec_grad, grad, grad_b, recv_grad, below, own, above = run(
        turn_body, scalars,
        (face_wide(agg), state, w_node, w_dec, back_dec, slope_1, spot_row),
        [(full, BF16), (full, BF16), (block, BF16), (full, BF16)] + back_outs,
        specs={2: layer_of(w_node.shape, 1)}, scratch=back_scratch,
        flops=edge_flops + 6 * mesh_rows * wide * wide,
    )

    def weights(*pairs):
        shape = (wide // pipe_count, narrow)
        return run(
            functools.partial(weight_body, len(pairs)), scalars,
            [a for pair in pairs for a in pair], [(shape, F32)] * len(pairs),
            flops=2 * mesh_rows * shape[0] * shape[1] * len(pairs),
        )

    def senders(below, own, above):
        return (
            own
            + shifted(below, "space", 1).astype(F32)
            + shifted(above, "space", -1).astype(F32)
        ).astype(BF16)

    grads_a = lax.psum(weights((last_b, dec_grad), (agg_1, grad_b)), "space")
    recv_parts = face_wide(recv_grad)
    send_parts = face_wide(senders(below, own, above))
    send_1, recv_1, grad, grad_b, recv_grad, below, own, above = run(
        back_body, scalars,
        (grad, send_parts, recv_parts, w_send, w_recv, w_node, slope_0, spot_row),
        [(full, BF16), (full, BF16)] + back_outs,
        specs={**layer_specs(3, 1), 5: layer_of(w_node.shape, 0)}, scratch=back_scratch,
        flops=edge_flops + 4 * mesh_rows * wide * wide,
    )
    grads_b = lax.psum(weights((state_1, send_1), (state_1, recv_1), (agg_0, grad_b)), "space")
    recv_parts = face_wide(recv_grad)
    send_parts = face_wide(senders(below, own, above))
    send_0, recv_0, grad_mesh, enc_part = run(
        functools.partial(last_body, mix_scale), scalars,
        (grad, send_parts, recv_parts, w_send, w_recv),
        [(full, BF16), (full, BF16), ((mesh_rows, narrow), F32), (block, BF16)],
        specs=layer_specs(3, 0), flops=4 * mesh_rows * wide * wide,
    )
    grads_c = lax.psum(weights((state_0, send_0), (state_0, recv_0)), "space")

    table = pltpu.VMEM((mesh_all, narrow), BF16)
    dec_mine = from_owners(dec_part)
    mixed, = run(
        mixed_body, scalars, (grid_latent, target_col, dec_mine, shifted(dec_mine, "pipe", 1)),
        [((grid_rows, narrow), BF16)], scratch=[table], flops=sum_flops,
        specs={0: pl.BlockSpec((grid_rows, narrow), lambda i, sr: (0, sr[0]))},
    )
    enc_mine = from_owners(enc_part)
    half = (wide // pipe_count, narrow)
    enc_grad, grad_keep, grad_give = run(
        enc_own_body, scalars,
        (grid_latent, w_enc, target_col, enc_mine, shifted(enc_mine, "pipe", 1)),
        [((grid_rows, narrow), BF16), (half, F32), (half, BF16)],
        scratch=[table, pltpu.VMEM((wide, narrow), F32)],
        flops=sum_flops + 4 * grid_rows * wide * narrow, specs={1: columns_at(0)},
    )
    half_sum = (grad_keep + shifted(grad_give, "pipe", 1).astype(F32)).astype(BF16)
    total = half_sum.astype(F32)
    for k in range(1, face_count):
        total = total + shifted(half_sum, "space", k).astype(F32)
    grad_w_enc = lax.all_gather(total, "pipe", axis=0, tiled=True)

    others = chan_count - 1
    other_mine = [shifted(enc_mine, "chan", j) for j in range(1, chan_count)]
    other_sib = [shifted(block_j, "pipe", 1) for block_j in other_mine]
    corner = lambda place: pl.BlockSpec((narrow, narrow), lambda i, sr: (sr[0], sr[place]))
    specs = {4: columns_at(0), 5: corner(0)}
    for j in range(others):
        specs[6 + j] = columns_at(3 + j)
        specs[6 + others + j] = corner(3 + j)
    grad_grid, = run(
        functools.partial(enc_other_body, others), scalars,
        (grid_latent, target_col, cotangent, enc_grad, w_enc, w_enc)
        + (w_enc,) * (2 * others) + tuple(other_mine) + tuple(other_sib),
        [((grid_rows, narrow), BF16)], specs=specs,
        scratch=[pltpu.VMEM((mesh_all, narrow * others), BF16)],
        flops=(sum_flops + 4 * grid_rows * wide * narrow) * others,
    )

    def rows_of(*blocks):
        return lax.all_gather(jnp.stack(blocks), "pipe", axis=1, tiled=True)

    grad_w_dec = lax.all_gather(grads_a[0], "pipe", axis=0, tiled=True)
    return (
        mixed,
        grad_grid,
        grad_mesh,
        grad_w_enc,
        rows_of(grads_c[0], grads_b[0]),
        rows_of(grads_c[1], grads_b[1]),
        rows_of(grads_b[2], grads_a[1]),
        grad_w_dec,
    )


def solution(mesh):
    nodes = ("groups", "space", "pipe")
    in_specs = (
        P(nodes, None), P(nodes, None), P(nodes), P(("groups", "space"), "chan"),
        P(("groups", "space"), "pipe"), P(), P(), P(), P(), P(), P(nodes, "chan"),
    )
    out_specs = (
        P(nodes, "chan"), P(nodes, "chan"), P(("groups", "space"), "chan"), P("groups", "chan"),
        P("groups", None, "chan"), P("groups", None, "chan"), P("groups", None, "chan"),
        P("groups", "chan"),
    )
    return jax.shard_map(
        per_device, mesh=mesh, in_specs=in_specs, out_specs=out_specs, check_vma=False
    )
```

time: 862 us -> 351 us (0.41)
  waiting for transfers between devices: 422 us -> 106 us
  local copies, waits for them, and re-layouts: 147 us -> 12 us
  Pallas kernels: 0 us -> 93.4 us
  other arithmetic: 70 us -> 8.34 us
  blocking collectives: 127 us -> 67.8 us
  matrix products: 33.4 us -> 0 us
  starting transfers between devices: 37.8 us -> 49 us
    all_to_all x5 -> x0, waiting for transfers between devices: 167 us -> none  [the longest x1 46.9 us: per_device(): lax.all_to_all(jnp.take(enc_back, safe_ids, axis=0), 'space', split_axis=...]
    pallas_call x0 -> x15, Pallas kernels: none -> 93.4 us  [run(): pl.pallas_call(body, out_shape=[jax.ShapeDtypeStruct(s, d) for s, d in ou...]
    psum x3 -> x1, waiting for transfers between devices: 172 us -> 80.7 us  [per_device(): lax.psum(weights((state_1, send_1), (state_1, recv_1), (agg_0, grad_b)),...]
    gather x7 -> x0, local copies, waits for them, and re-layouts: 63.7 us -> none  [the longest x1 17 us: per_device(): jnp.take(dec_out, safe_ids, axis=0)]
    reduce_scatter x1 -> x0, waiting for transfers between devices: 53.6 us -> none  [per_device(): lax.psum_scatter(grid_terms, 'chan', scatter_dimension=1, tiled=True)]
    ppermute x8 -> x30, starting transfers between devices: 13.5 us -> 48.8 us  [shifted(): lax.ppermute(block, axis, [((i + distance) % count, i) for i in range(cou...]
    all_gather x12 -> x11, blocking collectives: 103 us -> 67.8 us  [the longest x8 61.5 us: face_wide(): return lax.all_gather(block, FACE_AXES)]
    dot_general x26 -> x0, matrix products: 33.4 us -> none  [the longest x10 16.6 us: dot_plain(): return jnp.dot(left, right, preferred_element_type=jnp.float32)]
  transfers between devices with their start and end apart: 17 -> 34, of which waited for: 12 -> 9; matrix products, arithmetic and copies ran while one was open for 12% -> 2% of each run, Pallas kernels for 0% -> 13%
where the time goes in v1:
time: 351 us; the launch traced here: 350 us
  waiting for transfers between devices  106 us (30%)
  Pallas kernels  93.4 us (27%)
  blocking collectives  67.8 us (19%)
  starting transfers between devices  49 us (14%)
  between operations  14.1 us (4%)
  local copies, waits for them, and re-layouts  12 us (3%)
  other arithmetic  8.34 us (2%)
    pallas_call x15, Pallas kernels, run(): pl.pallas_call(body, out_shape=[jax.ShapeDtypeStruct(s, d) for s, d in ou...  93.4 us
    psum x1, waiting for transfers between devices, per_device(): lax.psum(weights((state_1, send_1), (state_1, recv_1), (agg_0, grad_b)),...  80.7 us
    all_gather x8, blocking collectives, face_wide(): return lax.all_gather(block, FACE_AXES)  61.5 us
    ppermute x30, starting transfers between devices, shifted(): lax.ppermute(block, axis, [((i + distance) % count, i) for i in range(cou...  48.8 us
    ppermute x30, waiting for transfers between devices, shifted(): lax.ppermute(block, axis, [((i + distance) % count, i) for i in range(cou...  24.9 us
    unnamed x74, local copies, waits for them, and re-layouts  10.4 us
  transfers between devices with their start and end apart: 34, of which 9 were waited for; matrix products, arithmetic and copies ran while one was open for 2% of the time, Pallas kernels for 13%

profile of v1, /device:TPU:0, one launch (start us, length us, event | category | flops | bytes accessed | tf_op | source)
XLA Modules:
  0.0 350.3 jit_solution(3506950440032847751)
XLA Ops:
  9.8 8.1 %shard_map.170 = (bf16[2048,128]{1,0:T(8,128)(2,1)}, bf16[2048,128]{1,0:T(8,128)(2,1)}) custom-call(s32[4]{0:T(128)} %pad_add_fusion.sr, bf16[2048,512]{1,0:T(8,128)(2,1)} %x.7, bf16[512,512]{1,0:T(8,128)(2,1)} %rest_1_.1, s32[1,2048]{1,0:T(1,128)} %bitcast.66), custom_call_target="tpu_custom_call" | custom-call | flops 2684354560 | tf_op jit(solution)/shard_map/pallas_call | solution.py:60
  18.4 6.4 %shard_map.175 = (bf16[2048,128]{1,0:T(8,128)(2,1)}, bf16[2048,128]{1,0:T(8,128)(2,1)}) custom-call(s32[4]{0:T(128)} %pad_add_fusion.sr, s32[1,2048]{1,0:T(1,128)} %bitcast.67, bf16[2048,256]{1,0:T(8,128)(2,1)} %cotangent.1), custom_call_target="tpu_custom_call" | custom-call | flops 2147483648 | tf_op jit(solution)/shard_map/pallas_call | solution.py:60
  24.8 1.9 all-gather.8
  29.4 2.9 collective-permute-start.1
  32.3 2.6 collective-permute-start.2
  36.7 2.8 collective-permute-start.11
  39.5 9.2 %collective-permute-start.9 = (bf16[512,128]{1,0:T(8,128)(2,1)S(1)}, bf16[512,128]{1,0:T(8,128)(2,1)S(1)}, u32[]{:S(2)}, u32[]{:S(2)}) collective-permute-start(bf16[512,128]{1,0:T(8,128)(2,1)S(1)} %get-tuple-element.111), channel_id=1, source_target_pairs={{12,0},{0,4},{4,8},{8,12},{13,1},{1,5},{5,9},{9,13},{14,2},{2,6},{... | collective-permute-start | bytes 393224 | tf_op jit(solution)/shard_map/ppermute | solution.py:16
  48.9 7.6 %all-gather = bf16[2048,128]{1,0:T(8,128)(2,1)} all-gather(bf16[512,128]{1,0:T(8,128)(2,1)S(1)} %add_convert_fusion.6), channel_id=2, replica_groups=mesh['groups'=2,'space'=4,'chan'=2,'pipe'=2] {'chan','pipe'}, dimensions={0}, use_global_device_ids=true | all-gather | bytes 655360 | tf_op jit(solution)/shard_map/all_gather | solution.py:340
  56.5 3.2 shard_map.171
  59.7 3.0 collective-permute-start.4
  62.8 2.9 collective-permute-start.5
  65.8 4.4 %collective-permute-done.4.below = bf16[512,128]{1,0:T(8,128)(2,1)S(1)} collective-permute-done((bf16[512,128]{1,0:T(8,128)(2,1)}, bf16[512,128]{1,0:T(8,128)(2,1)S(1)}, u32[]{:S(2)}, u32[]{:S(2)}) %collective-permute-start.4) | collective-permute-done | bytes 131104 | tf_op jit(solution)/shard_map/ppermute | solution.py:16
  71.9 6.0 %shard_map.172 = (bf16[512,128]{1,0:T(8,128)(2,1)}, f32[6,512,128]{2,1,0:T(8,128)}) custom-call(s32[4]{0:T(128)} %pad_add_fusion.sr, bf16[512,128]{1,0:T(8,128)(2,1)} %copy-done.26, bf16[512,128]{1,0:T(8,128)(2,1)} %get-tuple-element.58.own, bf16[512,128]{1,0:T(8,128)(2,1)} %copy-done.27, f32[512,128]{1,0:T(8,128)} %get-tuple-element.59.recv_p, ...), custom_call_target="tpu_custom_call" | custom-call | flops 1207959552 | tf_op jit(solution)/shard_map/pallas_call | solution.py:60
  77.9 7.5 %all-gather.1 = bf16[2048,128]{1,0:T(8,128)(2,1)} all-gather(bf16[512,128]{1,0:T(8,128)(2,1)} %get-tuple-element.60), channel_id=3, replica_groups=mesh['groups'=2,'space'=4,'chan'=2,'pipe'=2] {'chan','pipe'}, dimensions={0}, use_global_device_ids=true | all-gather | bytes 655360 | tf_op jit(solution)/shard_map/all_gather | solution.py:340
  85.4 4.1 %shard_map.173 = (bf16[512,512]{1,0:T(8,128)(2,1)}, f32[512,512]{1,0:T(8,128)}, bf16[512,512]{1,0:T(8,128)(2,1)}, bf16[512,128]{1,0:T(8,128)(2,1)}, f32[512,128]{1,0:T(8,128)}) custom-call(s32[4]{0:T(128)} %pad_add_fusion.sr, bf16[4,512,128]{2,1,0:T(8,128)(2,1)} %bitcast.53, bf16[512,512]{1,0:T(8,128)(2,1)} %get-tuple-element.61.state.refs_0_.refs_2_, ...), custom_call_target="tpu_custom_call" | custom-call | flops 268435456 | tf_op jit(solution)/shard_map/pallas_call | solution.py:60
  89.4 2.8 collective-permute-start.6
  93.2 7.3 %all-gather.3 = bf16[2048,128]{1,0:T(8,128)(2,1)} all-gather(bf16[512,128]{1,0:T(8,128)(2,1)S(1)} %add_convert_fusion.5), channel_id=5, replica_groups=mesh['groups'=2,'space'=4,'chan'=2,'pipe'=2] {'chan','pipe'}, dimensions={0}, use_global_device_ids=true | all-gather | bytes 655360 | tf_op jit(solution)/shard_map/all_gather | solution.py:340
  101.3 6.0 %shard_map.174 = (bf16[512,128]{1,0:T(8,128)(2,1)}, f32[6,512,128]{2,1,0:T(8,128)}) custom-call(s32[4]{0:T(128)} %pad_add_fusion.sr, bf16[512,128]{1,0:T(8,128)(2,1)} %copy-done.28, bf16[512,128]{1,0:T(8,128)(2,1)} %get-tuple-element.62.own, bf16[512,128]{1,0:T(8,128)(2,1)} %copy-done.29, f32[512,128]{1,0:T(8,128)} %get-tuple-element.63.recv_p, ...), custom_call_target="tpu_custom_call" | custom-call | flops 1207959552 | tf_op jit(solution)/shard_map/pallas_call | solution.py:60
  107.3 9.0 %all-gather.2 = bf16[2048,128]{1,0:T(8,128)(2,1)} all-gather(bf16[512,128]{1,0:T(8,128)(2,1)} %get-tuple-element.64), channel_id=4, replica_groups=mesh['groups'=2,'space'=4,'chan'=2,'pipe'=2] {'chan','pipe'}, dimensions={0}, use_global_device_ids=true | all-gather | bytes 655360 | tf_op jit(solution)/shard_map/all_gather | solution.py:340
  116.2 7.8 %shard_map.176 = (bf16[512,512]{1,0:T(8,128)(2,1)}, bf16[512,512]{1,0:T(8,128)(2,1)}, bf16[512,128]{1,0:T(8,128)(2,1)}, bf16[512,512]{1,0:T(8,128)(2,1)}, f32[51...) custom-call(s32[4]{0:T(128)} %pad_add_fusion.sr, ...), custom_call_target="tpu_custom_call" | custom-call | flops 2013265920 | tf_op jit(solution)/shard_map/pallas_call | solution.py:60
  124.1 1.7 collective-permute-start.16
  126.2 3.3 shard_map.184
  129.5 7.2 %all-gather.5 = bf16[2048,128]{1,0:T(8,128)(2,1)} all-gather(bf16[512,128]{1,0:T(8,128)(2,1)S(1)} %copy-done.14), channel_id=7, replica_groups=mesh['groups'=2,'space'=4,'chan'=2,'pipe'=2] {'chan','pipe'}, dimensions={0}, use_global_device_ids=true | all-gather | bytes 655360 | tf_op jit(solution)/shard_map/all_gather | solution.py:340
  136.7 7.7 %all-gather.4 = bf16[2048,128]{1,0:T(8,128)(2,1)} all-gather(bf16[512,128]{1,0:T(8,128)(2,1)S(1)} %add_convert_fusion.4), channel_id=6, replica_groups=mesh['groups'=2,'space'=4,'chan'=2,'pipe'=2] {'chan','pipe'}, dimensions={0}, use_global_device_ids=true | all-gather | bytes 655360 | tf_op jit(solution)/shard_map/all_gather | solution.py:340
  144.5 7.6 %shard_map.178 = (bf16[512,512]{1,0:T(8,128)(2,1)}, bf16[512,512]{1,0:T(8,128)(2,1)}, f32[512,512]{1,0:T(8,128)}, bf16[512,512]{1,0:T(8,128)(2,1)}, bf16[512,128...) custom-call(s32[4]{0:T(128)} %pad_add_fusion.sr, ...), custom_call_target="tpu_custom_call" | custom-call | flops 1744830464 | tf_op jit(solution)/shard_map/pallas_call | solution.py:60
  152.1 3.5 collective-permute-start.18
  155.6 3.9 %shard_map.183 = (f32[256,256]{1,0:T(8,128)}, f32[256,256]{1,0:T(8,128)}, f32[256,256]{1,0:T(8,128)}) custom-call(s32[4]{0:T(128)} %pad_add_fusion.sr, bf16[512,512]{1,0:T(8,128)(2,1)} %get-tuple-element.89.refs_0_.refs_2_, bf16[512,512]{1,0:T(8,128)(2,1)} %get-tuple-element.90.refs_1_, bf16[512,512]{1,0:T(8,128)(2,1)} %get-tuple-element.89.refs_0_.refs_2_, ...), custom_call_target="tpu_custom_call" | custom-call | flops 201326592 | tf_op jit(solution)/shard_map/pallas_call | solution.py:60
  159.5 7.4 %all-gather.7 = bf16[2048,128]{1,0:T(8,128)(2,1)} all-gather(bf16[512,128]{1,0:T(8,128)(2,1)S(1)} %copy-done.13), channel_id=9, replica_groups=mesh['groups'=2,'space'=4,'chan'=2,'pipe'=2] {'chan','pipe'}, dimensions={0}, use_global_device_ids=true | all-gather | bytes 655360 | tf_op jit(solution)/shard_map/all_gather | solution.py:340
  167.0 7.7 %all-gather.6 = bf16[2048,128]{1,0:T(8,128)(2,1)} all-gather(bf16[512,128]{1,0:T(8,128)(2,1)S(1)} %add_convert_fusion.3), channel_id=8, replica_groups=mesh['groups'=2,'space'=4,'chan'=2,'pipe'=2] {'chan','pipe'}, dimensions={0}, use_global_device_ids=true | all-gather | bytes 655360 | tf_op jit(solution)/shard_map/all_gather | solution.py:340
  174.7 4.1 %shard_map.179 = (bf16[512,512]{1,0:T(8,128)(2,1)}, bf16[512,512]{1,0:T(8,128)(2,1)}, f32[512,256]{1,0:T(8,128)}, bf16[512,128]{1,0:T(8,128)(2,1)}) custom-call(s32[4]{0:T(128)} %pad_add_fusion.sr, f32[512,512]{1,0:T(8,128)} %get-tuple-element.76.grad, bf16[4,512,128]{2,1,0:T(8,128)(2,1)} %bitcast.52, bf16[4,512,128]{2,1,0:T(8,128)(2,1)} %bitcast.50, ...), custom_call_target="tpu_custom_call" | custom-call | flops 536870912 | tf_op jit(solution)/shard_map/pallas_call | solution.py:60
  178.8 3.4 shard_map.182
  182.3 80.7 %all-reduce.3.cloned.1.call-done = (f32[1,256,256]{2,1,0:T(8,128)}, f32[1,256,256]{2,1,0:T(8,128)}, f32[1,256,256]{2,1,0:T(8,128)}, f32[1,256,256]{2,1,0:T(8,128...) async-done(((f32[1,256,256]{2,1,0:T(8,128)}, f32[1,256,256]{2,1,0:T(8,128)}, f32[1,256,256]{2,1,0:T(8,128)}, f32[1,256,256]{2,1,0:T(8,128)}, ...) | async-done | bytes 1835024 | tf_op jit(solution)/shard_map/psum | solution.py:423
  263.0 1.9 pad_maximum_fusion.2
  265.0 1.5 collective-permute-start.20
  266.7 1.8 collective-permute-start.22
  268.4 2.4 collective-permute-done.20
  270.9 7.4 %collective-permute-done.21 = bf16[512,128]{1,0:T(8,128)(2,1)S(1)} collective-permute-done((bf16[512,128]{1,0:T(8,128)(2,1)S(1)}, bf16[512,128]{1,0:T(8,128)(2,1)S(1)}, u32[]{:S(2)}, u32[]{:S(2)}) %collective-permute-start.21) | collective-permute-done | bytes 131104 | tf_op jit(solution)/shard_map/ppermute | solution.py:16
  282.8 2.3 collective-permute-start.14
  285.3 1.5 collective-permute-start.24
  286.8 7.2 %collective-permute-done.13 = bf16[512,128]{1,0:T(8,128)(2,1)S(1)} collective-permute-done((bf16[512,128]{1,0:T(8,128)(2,1)S(1)}, bf16[512,128]{1,0:T(8,128)(2,1)S(1)}, u32[]{:S(2)}, u32[]{:S(2)}) %collective-permute-start.13) | collective-permute-done | bytes 131104 | tf_op jit(solution)/shard_map/ppermute | solution.py:16
  295.0 10.9 %shard_map.180 = (bf16[2048,256]{1,0:T(8,128)(2,1)}, f32[256,256]{1,0:T(8,128)}, bf16[256,256]{1,0:T(8,128)(2,1)}) custom-call(s32[4]{0:T(128)} %pad_add_fusion.sr, bf16[2048,512]{1,0:T(8,128)(2,1)} %x.7, bf16[512,512]{1,0:T(8,128)(2,1)} %rest_1_.1, s32[2048,1]{1,0:T(8,128)} %copy.28.target, bf16[2048,128]{1,0:T(8,128)(2,1)} %copy-done.19, ...), custom_call_target="tpu_custom_call" | custom-call | flops 3221225472 | tf_op jit(solution)/shard_map/pallas_call | solution.py:60
  307.7 1.8 collective-permute-start.28
  309.5 1.9 collective-permute-start.29
  312.3 7.7 %shard_map.177 = bf16[2048,256]{1,0:T(8,128)(2,1)} custom-call(s32[4]{0:T(128)} %pad_add_fusion.sr, bf16[2048,512]{1,0:T(8,128)(2,1)} %x.7, s32[2048,1]{1,0:T(8,128)} %copy.28.target, bf16[2048,128]{1,0:T(8,128)(2,1)} %copy-done.20, bf16[2048,128]{1,0:T(8,128)(2,1)} %copy-done.24), custom_call_target="tpu_custom_call" | custom-call | flops 2147483648 | tf_op jit(solution)/shard_map/pallas_call | solution.py:60
  320.0 1.9 collective-permute-done.28
  322.0 2.2 all_gather.83
  324.9 10.9 %shard_map.181 = bf16[2048,256]{1,0:T(8,128)(2,1)} custom-call(s32[4]{0:T(128)} %pad_add_fusion.sr, bf16[2048,512]{1,0:T(8,128)(2,1)} %x.7, s32[2048,1]{1,0:T(8,128)} %copy.28.target, bf16[2048,256]{1,0:T(8,128)(2,1)} %cotangent.1, bf16[2048,256]{1,0:T(8,128)(2,1)} %get-tuple-element.82.enc_grad, bf16[512,512]{1,0:T(8,128)(2,1)} %rest_1_.1, ...), custom_call_target="tpu_custom_call" | custom-call | flops 3221225472 | tf_op jit(solution)/shard_map/pallas_call | solution.py:60
  335.8 2.2 all_gather.87
  (146 shorter events, 26.6 us)
Async XLA Ops:
  7.2 255.8 %all-reduce.3.cloned.1.call-start = ((), (), s32[]{:S(2)}) async-start(), calls=%async_computation.3 | async-start | bytes 3670016 | tf_op jit(solution)/shard_map/psum | solution.py:423
  17.9 11.2 %collective-permute-start = (bf16[2048,128]{1,0:T(8,128)(2,1)}, bf16[2048,128]{1,0:T(8,128)(2,1)S(1)}, u32[]{:S(2)}, u32[]{:S(2)}) collective-permute-start(bf16[2048,128]{1,0:T(8,128)(2,1)} %get-tuple-element.57), channel_id=1, source_target_pairs={{1,0},{0,1},{3,2},{2,3},{5,4},{4,5},{7,6},{6,7},{9,8},{8,9},{11,10... | collective-permute-start | bytes 1572872 | tf_op jit(solution)/shard_map/ppermute | solution.py:16
  24.8 11.5 %collective-permute-start.8 = (bf16[2048,128]{1,0:T(8,128)(2,1)}, bf16[2048,128]{1,0:T(8,128)(2,1)S(1)}, u32[]{:S(2)}, u32[]{:S(2)}) collective-permute-start(bf16[2048,128]{1,0:T(8,128)(2,1)} %get-tuple-element.67), channel_id=1, source_target_pairs={{1,0},{0,1},{3,2},{2,3},{5,4},{4,5},{7,6},{6,7},{9,8},{8,9},{11,10... | collective-permute-start | bytes 1572872 | tf_op jit(solution)/shard_map/ppermute | solution.py:16
  29.3 19.5 %copy-start.17 = (bf16[512,256]{1,0:T(8,128)(2,1)S(1)}, bf16[512,256]{1,0:T(8,128)(2,1)}, u32[]{:S(2)}) copy-start(bf16[512,256]{1,0:T(8,128)(2,1)} %param.14) | copy-start | bytes 786436
  29.4 10.2 %collective-permute-start.1 = (bf16[512,128]{1,0:T(8,128)(2,1)S(1)}, bf16[512,128]{1,0:T(8,128)(2,1)S(1)}, u32[]{:S(2)}, u32[]{:S(2)}) collective-permute-start(bf16[512,128]{1,0:T(8,128)(2,1)S(1)} %get-tuple-element.114), channel_id=1, source_target_pairs={{12,0},{0,4},{4,8},{8,12},{13,1},{1,5},{5,9},{9,13},{14,2},{2,6},{... | collective-permute-start | bytes 393224 | tf_op jit(solution)/shard_map/ppermute | solution.py:16
  32.3 16.5 %collective-permute-start.2 = (bf16[512,128]{1,0:T(8,128)(2,1)S(1)}, bf16[512,128]{1,0:T(8,128)(2,1)S(1)}, u32[]{:S(2)}, u32[]{:S(2)}) collective-permute-start(bf16[512,128]{1,0:T(8,128)(2,1)S(1)} %get-tuple-element.116), channel_id=1, source_target_pairs={{8,0},{12,4},{0,8},{4,12},{9,1},{13,5},{1,9},{5,13},{10,2},{14,6},... | collective-permute-start | bytes 393224 | tf_op jit(solution)/shard_map/ppermute | solution.py:16
  34.9 13.9 %collective-permute-start.3 = (bf16[512,128]{1,0:T(8,128)(2,1)S(1)}, bf16[512,128]{1,0:T(8,128)(2,1)S(1)}, u32[]{:S(2)}, u32[]{:S(2)}) collective-permute-start(bf16[512,128]{1,0:T(8,128)(2,1)S(1)} %get-tuple-element.115), channel_id=1, source_target_pairs={{4,0},{8,4},{12,8},{0,12},{5,1},{9,5},{13,9},{1,13},{6,2},{10,6},{... | collective-permute-start | bytes 393224 | tf_op jit(solution)/shard_map/ppermute | solution.py:16
  36.4 29.2 %collective-permute-start.10 = (bf16[512,128]{1,0:T(8,128)(2,1)S(1)}, bf16[512,128]{1,0:T(8,128)(2,1)S(1)}, u32[]{:S(2)}, u32[]{:S(2)}) collective-permute-start(bf16[512,128]{1,0:T(8,128)(2,1)S(1)} %get-tuple-element.113), channel_id=1, source_target_pairs={{8,0},{12,4},{0,8},{4,12},{9,1},{13,5},{1,9},{5,13},{10,2},{14,6},... | collective-permute-start | bytes 393224 | tf_op jit(solution)/shard_map/ppermute | solution.py:16
  36.7 29.0 %collective-permute-start.11 = (bf16[512,128]{1,0:T(8,128)(2,1)S(1)}, bf16[512,128]{1,0:T(8,128)(2,1)S(1)}, u32[]{:S(2)}, u32[]{:S(2)}) collective-permute-start(bf16[512,128]{1,0:T(8,128)(2,1)S(1)} %get-tuple-element.112), channel_id=1, source_target_pairs={{4,0},{8,4},{12,8},{0,12},{5,1},{9,5},{13,9},{1,13},{6,2},{10,6},{... | collective-permute-start | bytes 393224 | tf_op jit(solution)/shard_map/ppermute | solution.py:16
  39.5 26.1 %collective-permute-start.9 = (bf16[512,128]{1,0:T(8,128)(2,1)S(1)}, bf16[512,128]{1,0:T(8,128)(2,1)S(1)}, u32[]{:S(2)}, u32[]{:S(2)}) collective-permute-start(bf16[512,128]{1,0:T(8,128)(2,1)S(1)} %get-tuple-element.111), channel_id=1, source_target_pairs={{12,0},{0,4},{4,8},{8,12},{13,1},{1,5},{5,9},{9,13},{14,2},{2,6},{... | collective-permute-start | bytes 393224 | tf_op jit(solution)/shard_map/ppermute | solution.py:16
  59.7 10.5 %collective-permute-start.4 = (bf16[512,128]{1,0:T(8,128)(2,1)}, bf16[512,128]{1,0:T(8,128)(2,1)S(1)}, u32[]{:S(2)}, u32[]{:S(2)}) collective-permute-start(bf16[512,128]{1,0:T(8,128)(2,1)} %get-tuple-element.58.own), channel_id=1, source_target_pairs={{12,0},{0,4},{4,8},{8,12},{13,1},{1,5},{5,9},{9,13},{14,2},{2,6},{... | collective-permute-start | bytes 393224 | tf_op jit(solution)/shard_map/ppermute | solution.py:16
  62.8 8.5 %collective-permute-start.5 = (bf16[512,128]{1,0:T(8,128)(2,1)}, bf16[512,128]{1,0:T(8,128)(2,1)S(1)}, u32[]{:S(2)}, u32[]{:S(2)}) collective-permute-start(bf16[512,128]{1,0:T(8,128)(2,1)} %get-tuple-element.58.own), channel_id=1, source_target_pairs={{4,0},{8,4},{12,8},{0,12},{5,1},{9,5},{13,9},{1,13},{6,2},{10,6},{... | collective-permute-start | bytes 393224 | tf_op jit(solution)/shard_map/ppermute | solution.py:16
  89.4 11.2 %collective-permute-start.6 = (bf16[512,128]{1,0:T(8,128)(2,1)}, bf16[512,128]{1,0:T(8,128)(2,1)S(1)}, u32[]{:S(2)}, u32[]{:S(2)}) collective-permute-start(bf16[512,128]{1,0:T(8,128)(2,1)} %get-tuple-element.62.own), channel_id=1, source_target_pairs={{12,0},{0,4},{4,8},{8,12},{13,1},{1,5},{5,9},{9,13},{14,2},{2,6},{... | collective-permute-start | bytes 393224 | tf_op jit(solution)/shard_map/ppermute | solution.py:16
  92.2 8.4 %collective-permute-start.7 = (bf16[512,128]{1,0:T(8,128)(2,1)}, bf16[512,128]{1,0:T(8,128)(2,1)S(1)}, u32[]{:S(2)}, u32[]{:S(2)}) collective-permute-start(bf16[512,128]{1,0:T(8,128)(2,1)} %get-tuple-element.62.own), channel_id=1, source_target_pairs={{4,0},{8,4},{12,8},{0,12},{5,1},{9,5},{13,9},{1,13},{6,2},{10,6},{... | collective-permute-start | bytes 393224 | tf_op jit(solution)/shard_map/ppermute | solution.py:16
  124.1 12.6 %copy-start.7 = (f32[512,128]{1,0:T(8,128)S(1)}, f32[512,128]{1,0:T(8,128)}, u32[]{:S(2)}) copy-start(f32[512,128]{1,0:T(8,128)} %get-tuple-element.71) | copy-start | bytes 786436
  124.1 12.6 %collective-permute-start.16 = (bf16[512,128]{1,0:T(8,128)(2,1)}, bf16[512,128]{1,0:T(8,128)(2,1)S(1)}, u32[]{:S(2)}, u32[]{:S(2)}) collective-permute-start(bf16[512,128]{1,0:T(8,128)(2,1)} %get-tuple-element.72), channel_id=1, source_target_pairs={{4,0},{8,4},{12,8},{0,12},{5,1},{9,5},{13,9},{1,13},{6,2},{10,6},{... | collective-permute-start | bytes 393224 | tf_op jit(solution)/shard_map/ppermute | solution.py:16
  125.8 10.9 %collective-permute-start.17 = (bf16[512,128]{1,0:T(8,128)(2,1)}, bf16[512,128]{1,0:T(8,128)(2,1)S(1)}, u32[]{:S(2)}, u32[]{:S(2)}) collective-permute-start(bf16[512,128]{1,0:T(8,128)(2,1)} %get-tuple-element.73), channel_id=1, source_target_pairs={{12,0},{0,4},{4,8},{8,12},{13,1},{1,5},{5,9},{9,13},{14,2},{2,6},{... | collective-permute-start | bytes 393224 | tf_op jit(solution)/shard_map/ppermute | solution.py:16
  152.1 14.8 %collective-permute-start.18 = (bf16[512,128]{1,0:T(8,128)(2,1)}, bf16[512,128]{1,0:T(8,128)(2,1)S(1)}, u32[]{:S(2)}, u32[]{:S(2)}) collective-permute-start(bf16[512,128]{1,0:T(8,128)(2,1)} %get-tuple-element.78), channel_id=1, source_target_pairs={{4,0},{8,4},{12,8},{0,12},{5,1},{9,5},{13,9},{1,13},{6,2},{10,6},{... | collective-permute-start | bytes 393224 | tf_op jit(solution)/shard_map/ppermute | solution.py:16
  155.5 11.4 %collective-permute-start.19 = (bf16[512,128]{1,0:T(8,128)(2,1)}, bf16[512,128]{1,0:T(8,128)(2,1)S(1)}, u32[]{:S(2)}, u32[]{:S(2)}) collective-permute-start(bf16[512,128]{1,0:T(8,128)(2,1)} %get-tuple-element.79), channel_id=1, source_target_pairs={{12,0},{0,4},{4,8},{8,12},{13,1},{1,5},{5,9},{9,13},{14,2},{2,6},{... | collective-permute-start | bytes 393224 | tf_op jit(solution)/shard_map/ppermute | solution.py:16
  155.5 11.4 %copy-start.6 = (f32[512,128]{1,0:T(8,128)S(1)}, f32[512,128]{1,0:T(8,128)}, u32[]{:S(2)}) copy-start(f32[512,128]{1,0:T(8,128)} %get-tuple-element.77) | copy-start | bytes 786436
  182.2 82.8 %copy-start.16 = (bf16[512,128]{1,0:T(8,128)(2,1)S(1)}, bf16[512,128]{1,0:T(8,128)(2,1)}, u32[]{:S(2)}) copy-start(bf16[512,128]{1,0:T(8,128)(2,1)} %get-tuple-element.81) | copy-start | bytes 393220
  182.2 155.8 %all-gather.17.cloned.1.call-start = ((), (), s32[]{:S(2)}) async-start(), calls=%async_computation.2 | async-start | bytes 1572864 | tf_op jit(solution)/shard_map/all_gather | solution.py:474
  263.0 15.3 %copy-start.11 = (f32[1,256,256]{2,1,0:T(8,128)S(1)}, f32[1,256,256]{2,1,0:T(8,128)}, u32[]{:S(2)}) copy-start(f32[1,256,256]{2,1,0:T(8,128)} %get-tuple-element.106) | copy-start | bytes 786436
  263.0 15.3 %copy-start.12 = (f32[1,256,256]{2,1,0:T(8,128)S(1)}, f32[1,256,256]{2,1,0:T(8,128)}, u32[]{:S(2)}) copy-start(f32[1,256,256]{2,1,0:T(8,128)} %get-tuple-element.107) | copy-start | bytes 786436
  264.9 14.4 %copy-start.15 = (bf16[512,128]{1,0:T(8,128)(2,1)S(1)}, bf16[512,128]{1,0:T(8,128)(2,1)}, u32[]{:S(2)}) copy-start(bf16[512,128]{1,0:T(8,128)(2,1)} %get-tuple-element.69) | copy-start | bytes 393220
  264.9 15.7 %copy-start.18 = (s32[2048]{0:T(1024)S(1)}, s32[2048]{0:T(1024)}, u32[]{:S(2)}) copy-start(s32[2048]{0:T(1024)} %fusion.7) | copy-start | bytes 24580
  265.0 73.0 %all-gather.15.cloned.1.call-start = ((), (), s32[]{:S(2)}) async-start(), calls=%async_computation.1 | async-start | bytes 1572864 | tf_op jit(solution)/shard_map/all_gather | solution.py:474
  265.0 5.8 %collective-permute-start.20 = (bf16[512,128]{1,0:T(8,128)(2,1)S(1)}, bf16[512,128]{1,0:T(8,128)(2,1)S(1)}, u32[]{:S(2)}, u32[]{:S(2)}) collective-permute-start(bf16[512,128]{1,0:T(8,128)(2,1)S(1)} %copy-done.16), channel_id=1, source_target_pairs={{4,0},{8,4},{12,8},{0,12},{5,1},{9,5},{13,9},{1,13},{6,2},{10,6},{... | collective-permute-start | bytes 393224 | tf_op jit(solution)/shard_map/ppermute | solution.py:16
  266.5 11.7 %collective-permute-start.21 = (bf16[512,128]{1,0:T(8,128)(2,1)S(1)}, bf16[512,128]{1,0:T(8,128)(2,1)S(1)}, u32[]{:S(2)}, u32[]{:S(2)}) collective-permute-start(bf16[512,128]{1,0:T(8,128)(2,1)S(1)} %copy-done.16), channel_id=1, source_target_pairs={{8,0},{12,4},{0,8},{4,12},{9,1},{13,5},{1,9},{5,13},{10,2},{14,6},... | collective-permute-start | bytes 393224 | tf_op jit(solution)/shard_map/ppermute | solution.py:16
  266.7 12.6 %collective-permute-start.22 = (bf16[512,128]{1,0:T(8,128)(2,1)S(1)}, bf16[512,128]{1,0:T(8,128)(2,1)S(1)}, u32[]{:S(2)}, u32[]{:S(2)}) collective-permute-start(bf16[512,128]{1,0:T(8,128)(2,1)S(1)} %copy-done.16), channel_id=1, source_target_pairs={{12,0},{0,4},{4,8},{8,12},{13,1},{1,5},{5,9},{9,13},{14,2},{2,6},{... | collective-permute-start | bytes 393224 | tf_op jit(solution)/shard_map/ppermute | solution.py:16
  279.2 58.8 %all-gather.13.cloned.1.call-start = ((), (), s32[]{:S(2)}) async-start(), calls=%async_computation | async-start | bytes 1572864 | tf_op jit(solution)/shard_map/all_gather | solution.py:474
  279.3 14.9 %copy-start.19 = (bf16[2048,128]{1,0:T(8,128)(2,1)}, bf16[2048,128]{1,0:T(8,128)(2,1)S(1)}, u32[]{:S(2)}) copy-start(bf16[2048,128]{1,0:T(8,128)(2,1)S(1)} %constant_dynamic-update-slice_fusion.4.mine) | copy-start | bytes 1572868
  279.3 14.9 %collective-permute-start.23 = (bf16[2048,128]{1,0:T(8,128)(2,1)S(1)}, bf16[2048,128]{1,0:T(8,128)(2,1)S(1)}, u32[]{:S(2)}, u32[]{:S(2)}) collective-permute-start(bf16[2048,128]{1,0:T(8,128)(2,1)S(1)} %constant_dynamic-update-slice_fusion.4.mine), channel_id=1, source_target_pairs={{1,0},{0,1},{3,2},{2,3},{5,4},{4,5},{7,6},{6,7},{9,8},{8,9},{11,10... | collective-permute-start | bytes 1572872 | tf_op jit(solution)/shard_map/ppermute | solution.py:16
  279.4 5.9 %collective-permute-start.12 = (bf16[512,128]{1,0:T(8,128)(2,1)S(1)}, bf16[512,128]{1,0:T(8,128)(2,1)S(1)}, u32[]{:S(2)}, u32[]{:S(2)}) collective-permute-start(bf16[512,128]{1,0:T(8,128)(2,1)S(1)} %copy-done.15), channel_id=1, source_target_pairs={{4,0},{8,4},{12,8},{0,12},{5,1},{9,5},{13,9},{1,13},{6,2},{10,6},{... | collective-permute-start | bytes 393224 | tf_op jit(solution)/shard_map/ppermute | solution.py:16
  282.0 12.1 %collective-permute-start.13 = (bf16[512,128]{1,0:T(8,128)(2,1)S(1)}, bf16[512,128]{1,0:T(8,128)(2,1)S(1)}, u32[]{:S(2)}, u32[]{:S(2)}) collective-permute-start(bf16[512,128]{1,0:T(8,128)(2,1)S(1)} %copy-done.15), channel_id=1, source_target_pairs={{8,0},{12,4},{0,8},{4,12},{9,1},{13,5},{1,9},{5,13},{10,2},{14,6},... | collective-permute-start | bytes 393224 | tf_op jit(solution)/shard_map/ppermute | solution.py:16
  282.8 11.3 %collective-permute-start.14 = (bf16[512,128]{1,0:T(8,128)(2,1)S(1)}, bf16[512,128]{1,0:T(8,128)(2,1)S(1)}, u32[]{:S(2)}, u32[]{:S(2)}) collective-permute-start(bf16[512,128]{1,0:T(8,128)(2,1)S(1)} %copy-done.15), channel_id=1, source_target_pairs={{12,0},{0,4},{4,8},{8,12},{13,1},{1,5},{5,9},{9,13},{14,2},{2,6},{... | collective-permute-start | bytes 393224 | tf_op jit(solution)/shard_map/ppermute | solution.py:16
  285.3 21.2 %collective-permute-start.24 = (bf16[2048,128]{1,0:T(8,128)(2,1)S(1)}, bf16[2048,128]{1,0:T(8,128)(2,1)S(1)}, u32[]{:S(2)}, u32[]{:S(2)}) collective-permute-start(bf16[2048,128]{1,0:T(8,128)(2,1)S(1)} %constant_dynamic-update-slice_fusion.4.mine), channel_id=1, source_target_pairs={{2,0},{0,2},{3,1},{1,3},{6,4},{4,6},{7,5},{5,7},{10,8},{8,10},{11,... | collective-permute-start | bytes 1572872 | tf_op jit(solution)/shard_map/ppermute | solution.py:16
  294.1 11.9 %copy-start.20 = (bf16[2048,128]{1,0:T(8,128)(2,1)}, bf16[2048,128]{1,0:T(8,128)(2,1)S(1)}, u32[]{:S(2)}) copy-start(bf16[2048,128]{1,0:T(8,128)(2,1)S(1)} %constant_dynamic-update-slice_fusion.mine) | copy-start | bytes 1572868
  294.1 12.4 %copy-start.9 = (f32[1,256,256]{2,1,0:T(8,128)S(1)}, f32[1,256,256]{2,1,0:T(8,128)}, u32[]{:S(2)}) copy-start(f32[1,256,256]{2,1,0:T(8,128)} %get-tuple-element.104) | copy-start | bytes 786436
  294.1 12.4 %copy-start.10 = (f32[1,256,256]{2,1,0:T(8,128)S(1)}, f32[1,256,256]{2,1,0:T(8,128)}, u32[]{:S(2)}) copy-start(f32[1,256,256]{2,1,0:T(8,128)} %get-tuple-element.105) | copy-start | bytes 786436
  294.1 17.4 %collective-permute-start.15 = (bf16[2048,128]{1,0:T(8,128)(2,1)S(1)}, bf16[2048,128]{1,0:T(8,128)(2,1)S(1)}, u32[]{:S(2)}, u32[]{:S(2)}) collective-permute-start(bf16[2048,128]{1,0:T(8,128)(2,1)S(1)} %constant_dynamic-update-slice_fusion.mine), channel_id=1, source_target_pairs={{1,0},{0,1},{3,2},{2,3},{5,4},{4,5},{7,6},{6,7},{9,8},{8,9},{11,10... | collective-permute-start | bytes 1572872 | tf_op jit(solution)/shard_map/ppermute | solution.py:16
  306.0 1.7 collective-permute-start.26
  306.5 13.6 %copy-start.22 = (bf16[2048,128]{1,0:T(8,128)(2,1)}, bf16[2048,128]{1,0:T(8,128)(2,1)S(1)}, u32[]{:S(2)}) copy-start(bf16[2048,128]{1,0:T(8,128)(2,1)S(1)} %collective-permute-done.24.rest_2_) | copy-start | bytes 1572868
  306.5 17.7 %collective-permute-start.25 = (bf16[2048,128]{1,0:T(8,128)(2,1)S(1)}, bf16[2048,128]{1,0:T(8,128)(2,1)S(1)}, u32[]{:S(2)}, u32[]{:S(2)}) collective-permute-start(bf16[2048,128]{1,0:T(8,128)(2,1)S(1)} %collective-permute-done.24.rest_2_), channel_id=1, source_target_pairs={{1,0},{0,1},{3,2},{2,3},{5,4},{4,5},{7,6},{6,7},{9,8},{8,9},{11,10... | collective-permute-start | bytes 1572872 | tf_op jit(solution)/shard_map/ppermute | solution.py:16
  307.7 12.4 %collective-permute-start.27 = (bf16[256,256]{1,0:T(8,128)(2,1)S(1)}, bf16[256,256]{1,0:T(8,128)(2,1)S(1)}, u32[]{:S(2)}, u32[]{:S(2)}) collective-permute-start(bf16[256,256]{1,0:T(8,128)(2,1)S(1)} %add_convert_fusion.2), channel_id=1, source_target_pairs={{4,0},{8,4},{12,8},{0,12},{5,1},{9,5},{13,9},{1,13},{6,2},{10,6},{... | collective-permute-start | bytes 393224 | tf_op jit(solution)/shard_map/ppermute | solution.py:16
  307.7 14.1 %collective-permute-start.28 = (bf16[256,256]{1,0:T(8,128)(2,1)S(1)}, bf16[256,256]{1,0:T(8,128)(2,1)S(1)}, u32[]{:S(2)}, u32[]{:S(2)}) collective-permute-start(bf16[256,256]{1,0:T(8,128)(2,1)S(1)} %add_convert_fusion.2), channel_id=1, source_target_pairs={{8,0},{12,4},{0,8},{4,12},{9,1},{13,5},{1,9},{5,13},{10,2},{14,6},... | collective-permute-start | bytes 393224 | tf_op jit(solution)/shard_map/ppermute | solution.py:16
  309.5 12.4 %collective-permute-start.29 = (bf16[256,256]{1,0:T(8,128)(2,1)S(1)}, bf16[256,256]{1,0:T(8,128)(2,1)S(1)}, u32[]{:S(2)}, u32[]{:S(2)}) collective-permute-start(bf16[256,256]{1,0:T(8,128)(2,1)S(1)} %add_convert_fusion.2), channel_id=1, source_target_pairs={{12,0},{0,4},{4,8},{8,12},{13,1},{1,5},{5,9},{9,13},{14,2},{2,6},{... | collective-permute-start | bytes 393224 | tf_op jit(solution)/shard_map/ppermute | solution.py:16
  324.9 10.9 %copy-start.5 = (f32[256,256]{1,0:T(8,128)S(1)}, f32[256,256]{1,0:T(8,128)}, u32[]{:S(2)}) copy-start(f32[256,256]{1,0:T(8,128)} %get-tuple-element.110) | copy-start | bytes 786436
  (16 other events, 42.1 us)
Sparse Core Ops, SparseCore 0:
  182.3 80.6 all-reduce.2
  265.1 7.8 all-gather.16
  279.3 7.5 all-gather.14
  307.6 8.1 all-gather.12

commit v2 on v1

v2 whole, which is shorter than its diff:
```python
import functools

import jax
import jax.numpy as jnp
from jax import lax
from jax.experimental import pallas as pl
from jax.experimental.pallas import tpu as pltpu
from jax.sharding import PartitionSpec as P

F32, BF16 = jnp.float32, jnp.bfloat16
FACE_AXES = ("chan", "pipe")


def shifted(block, axis, distance):
    count = lax.axis_size(axis)
    return lax.ppermute(block, axis, [((i + distance) % count, i) for i in range(count)])


def dot_plain(left, right):
    return jnp.dot(left, right, preferred_element_type=F32)


def dot_back(left, right):
    return lax.dot_general(left, right, (((1,), (1,)), ((), ())), preferred_element_type=F32)


def dot_left(left, right):
    return lax.dot_general(left, right, (((0,), (0,)), ((), ())), preferred_element_type=F32)


def slope_of(values, sigmoid_v):
    return sigmoid_v * (1.0 + values * (1.0 - sigmoid_v))


def one_hot(rows, ids):
    return jnp.where(rows == ids, 1.0, 0.0).astype(BF16)


def pick(values, index, width):
    out = values[:, :width]
    for j in range(1, values.shape[1] // width):
        out = jnp.where(index == j, values[:, j * width : (j + 1) * width], out)
    return out


def widen(parts):
    return jnp.concatenate([parts[j] for j in range(parts.shape[0])], axis=1)


def some_of(parts, index, count):
    return jnp.concatenate([parts[index * count + j] for j in range(count)], axis=1)


def whole(shape):
    return pl.BlockSpec(shape, lambda i, sr: (0,) * len(shape))


def layer_of(shape, layer):
    return pl.BlockSpec((None,) + shape[1:], lambda i, sr: (layer, 0, 0))


def run(body, scalars, args, outs, scratch=(), flops=0, specs=None):
    specs = specs or {}
    return pl.pallas_call(
        body,
        out_shape=[jax.ShapeDtypeStruct(s, d) for s, d in outs],
        grid_spec=pltpu.PrefetchScalarGridSpec(
            num_scalar_prefetch=1,
            grid=(1,),
            in_specs=[specs.get(i, whole(a.shape)) for i, a in enumerate(args)],
            out_specs=[whole(s) for s, _ in outs],
            scratch_shapes=list(scratch),
        ),
        compiler_params=pltpu.CompilerParams(vmem_limit_bytes=56 * 1024 * 1024),
        cost_estimate=pl.CostEstimate(flops=flops, bytes_accessed=0, transcendentals=0),
    )(scalars, *args)


def rows_at(index, size):
    return pl.ds(pl.multiple_of(index * size, size), size)


def sum_by_node(sr, target, values, keep, give):
    mesh_all, width = keep.shape
    grid_rows = values.shape[0]
    size = 512

    def step(i, carry):
        ids = lax.broadcasted_iota(jnp.int32, (size, grid_rows), 0) + i * size
        total = dot_plain(one_hot(ids, target[...]), values[...])
        low, high = total[:, :width], total[:, width:]
        first = sr[1] == 0
        keep[rows_at(i, size), :] = jnp.where(first, low, high).astype(BF16)
        give[rows_at(i, size), :] = jnp.where(first, high, low).astype(BF16)
        return carry

    lax.fori_loop(0, mesh_all // size, step, 0)


def encode_body(sr, x, w, target, keep, give, enc):
    size = 512

    def step(i, carry):
        z = dot_plain(x[rows_at(i, size), :], w[...])
        enc[rows_at(i, size), :] = (z * jax.nn.sigmoid(z)).astype(BF16)
        return carry

    lax.fori_loop(0, x.shape[0] // size, step, 0)
    sum_by_node(sr, target, enc, keep, give)


def project(sr, state_b, w_send, w_recv, send_p, recv_p):
    width = send_p.shape[1]
    send_p[...] = dot_plain(state_b, own_columns(sr, w_send, width)).astype(BF16)
    recv_p[...] = dot_plain(state_b, own_columns(sr, w_recv, width))


def own_columns(sr, w, width):
    return w[...] if w.shape[1] == width else pick(w[...], sr[2], width)


def first_body(sr, parts, w_send, w_recv, send_p, recv_p):
    project(sr, widen(parts), w_send, w_recv, send_p, recv_p)


def next_body(sr, agg, state, w_node, w_send, w_recv, new_state, send_p, recv_p):
    total = widen(state).astype(F32) + dot_plain(widen(agg), w_node[...])
    new_state[...] = total
    project(sr, total.astype(BF16), w_send, w_recv, send_p, recv_p)


def edge_body(sr, below, own, above, recv_p, spot, agg, slope, halo):
    mesh_rows, width = own.shape
    middle, half = mesh_rows // 2, 3 * mesh_rows // 2
    halo[:mesh_rows, :width] = below[...]
    halo[mesh_rows:, :width] = own[:middle, :]
    halo[:middle, width:] = own[middle:, :]
    halo[middle:, width:] = above[...]
    ids = lax.broadcasted_iota(jnp.int32, (mesh_rows, half), 1)
    count = slope.shape[0]
    total = jnp.zeros(agg.shape, F32)
    for k in range(count):
        place = spot[:, k : k + 1]
        right = place >= half
        both = dot_plain(one_hot(ids, jnp.where(right, place - half, place)), halo[...])
        pre = jnp.where(right, both[:, width:], both[:, :width]) + recv_p[...]
        sigmoid_v = jax.nn.sigmoid(pre)
        total = total + pre * sigmoid_v
        slope[k] = slope_of(pre, sigmoid_v).astype(BF16)
    agg[...] = (total / count).astype(BF16)


def edge_back(sr, grad_b, w_node, slope, spot, spot_row, recv_grad, below, own, above, back):
    mesh_rows, width = recv_grad.shape
    middle, half = mesh_rows // 2, 3 * mesh_rows // 2
    count = slope.shape[0]
    back_agg = dot_back(grad_b, w_node[rows_at(sr[2], width), :]) / count
    total = jnp.zeros(recv_grad.shape, F32)
    for k in range(count):
        term = back_agg * slope[k].astype(F32)
        total = total + term
        right = spot[:, k : k + 1] >= half
        rows = slice(k * mesh_rows, (k + 1) * mesh_rows)
        back[rows, :width] = jnp.where(right, 0.0, term).astype(BF16)
        back[rows, width:] = jnp.where(right, term, 0.0).astype(BF16)
    recv_grad[...] = total.astype(BF16)
    place = spot_row[...]
    place = jnp.where(place >= half, place - half, place)
    ids = lax.broadcasted_iota(jnp.int32, (half, count * mesh_rows), 0)
    spread = dot_plain(one_hot(ids, place), back[...])
    below[...] = spread[:mesh_rows, :width].astype(BF16)
    own[:middle, :] = spread[mesh_rows:, :width]
    own[middle:, :] = spread[:middle, width:]
    above[...] = spread[middle:, width:].astype(BF16)


def turn_body(
    sr, agg, state, w_node, w_dec, back_dec, slope, spot, spot_row,
    last_b, dec_part, dec_grad, grad, recv_grad, below, own, above, back,
):
    last = (state[...] + dot_plain(widen(agg), w_node[...])).astype(BF16)
    last_b[...] = last
    z_dec = dot_plain(last, w_dec[...])
    sigmoid_v = jax.nn.sigmoid(z_dec)
    dec_part[...] = pick(z_dec * sigmoid_v, sr[2], dec_part.shape[1]).astype(BF16)
    down = (widen(back_dec).astype(F32) * slope_of(z_dec, sigmoid_v)).astype(BF16)
    dec_grad[...] = down
    total = dot_back(down, w_dec[...])
    grad[...] = total
    edge_back(sr, total.astype(BF16), w_node, slope, spot, spot_row, recv_grad, below, own, above, back)


def through(grad, send_parts, recv_parts, w_send, w_recv):
    return (
        grad[...]
        + dot_back(widen(send_parts), w_send[...])
        + dot_back(widen(recv_parts), w_recv[...])
    )


def back_body(
    sr, grad, send_parts, recv_parts, w_send, w_recv, w_node, slope, spot, spot_row,
    new_grad, recv_grad, below, own, above, back,
):
    total = through(grad, send_parts, recv_parts, w_send, w_recv)
    new_grad[...] = total
    edge_back(sr, total.astype(BF16), w_node, slope, spot, spot_row, recv_grad, below, own, above, back)


def last_body(mix_scale, sr, grad, send_parts, recv_parts, w_send, w_recv, grad_mesh, enc_part, enc_all):
    total = through(grad, send_parts, recv_parts, w_send, w_recv)
    grad_mesh[...] = pick(total, sr[0], grad_mesh.shape[1])
    scaled = (mix_scale * total).astype(BF16)
    enc_part[...] = pick(scaled, sr[2], enc_part.shape[1])
    enc_all[...] = scaled


def put_pair(sr, table, row, column, mine, other):
    first = sr[1] == 0
    rows, width = mine.shape
    at = slice(row, row + rows)
    table[at, column : column + width] = jnp.where(first, mine[...], other[...])
    table[at, column + width : column + 2 * width] = jnp.where(first, other[...], mine[...])


def node_values(target, at, table):
    ids = lax.broadcasted_iota(jnp.int32, (table.shape[0], at.size), 0)
    return dot_left(one_hot(ids, target[:, at]), table[...])


def mixed_body(sr, x, x_own, w, target, mine, other, mixed, slope, table):
    put_pair(sr, table, 0, 0, mine, other)
    size = 512

    def step(i, carry):
        at = rows_at(i, size)
        got = node_values(target, at, table)
        mixed[at, :] = (x_own[at, :].astype(F32) + got).astype(BF16)
        z = dot_plain(x[at, :], w[...])
        slope[at, :] = slope_of(z, jax.nn.sigmoid(z)).astype(BF16)
        return carry

    lax.fori_loop(0, x.shape[0] // size, step, 0)


def enc_own_body(count, sr, x, target, slope, *rest):
    mine, other = rest[:count], rest[count : 2 * count]
    enc_grad, grad_keep, grad_give, table, total = rest[2 * count :]
    mesh_rows = mine[0].shape[0]
    for k in range(count):
        put_pair(sr, table, k * mesh_rows, 0, mine[k], other[k])
    size = 512
    total[...] = jnp.zeros(total.shape, F32)

    def step(i, carry):
        at = rows_at(i, size)
        down = (node_values(target, at, table) * slope[at, :].astype(F32)).astype(BF16)
        enc_grad[at, :] = down
        total[...] += dot_left(x[at, :], down)
        return carry

    lax.fori_loop(0, x.shape[0] // size, step, 0)
    half = grad_keep.shape[0]
    grad_keep[...] = total[rows_at(sr[1], half), :]
    grad_give[...] = total[rows_at(1 - sr[1], half), :].astype(BF16)


def enc_other_body(faces, count, sr, target, cotangent, enc_grad, w_own_rows, enc_all, *rest):
    slopes, w_rows = rest[:count], rest[count : 2 * count]
    blocks = rest[2 * count : -2]
    grad_grid, table = rest[-2:]
    grid_rows, narrow = cotangent.shape
    width, mesh_rows = narrow // 2, enc_all.shape[0]
    for j in range(count):
        own = pick(enc_all[...], sr[4 + j], narrow)
        table[:mesh_rows, j * narrow : (j + 1) * narrow] = own
        for k in range(1, faces):
            mine, other = blocks[2 * (j * (faces - 1) + k - 1) :][:2]
            put_pair(sr, table, k * mesh_rows, j * narrow, mine, other)
    size = 512

    def step(i, carry):
        at = rows_at(i, size)
        got = node_values(target, at, table)
        total = cotangent[at, :].astype(F32) + dot_back(enc_grad[at, :], w_own_rows[...])
        for j in range(count):
            part = got[:, j * narrow : (j + 1) * narrow]
            down = (part * slopes[j][at, :].astype(F32)).astype(BF16)
            total = total + dot_back(down, w_rows[j][...])
        grad_grid[at, :] = total.astype(BF16)
        return carry

    lax.fori_loop(0, grid_rows // size, step, 0)


def weight_body(kinds, sr, *refs):
    out = refs[-1]
    rows = out.shape[0] // len(kinds)
    narrow = out.shape[1]

    def half_of(ref, index, width):
        if len(ref.shape) == 3:
            return some_of(ref, index, width // ref.shape[2])
        return pick(ref[...].astype(BF16), index, width)

    for i, (left, right) in enumerate(kinds):
        product = dot_left(half_of(refs[left], sr[1], rows), half_of(refs[right], sr[0], narrow))
        out[i * rows : (i + 1) * rows, :] = product.astype(BF16)


def write_body(places, sr, *refs):
    count = len(places)
    outs = refs[2 * count :]
    for i, items in enumerate(places):
        mine, other = refs[i], refs[count + i]
        rows = mine.shape[0] // len(items)
        for j, (out, layer) in enumerate(items):
            ref = outs[out] if layer is None else outs[out].at[layer]
            at = slice(j * rows, (j + 1) * rows)
            ref[rows_at(sr[1], rows), :] = mine[at, :].astype(F32)
            ref[rows_at(1 - sr[1], rows), :] = other[at, :].astype(F32)


def per_device(
    grid_latent, g2m_face, g2m_node, mesh_latent, mesh_links,
    w_enc, w_send, w_recv, w_node, w_dec, cotangent,
):
    face_count = lax.axis_size("space")
    pipe_count = lax.axis_size("pipe")
    chan_count = lax.axis_size("chan")
    grid_rows, wide = grid_latent.shape
    mesh_rows, narrow = mesh_latent.shape
    part = narrow // pipe_count
    mesh_all = face_count * mesh_rows
    others = chan_count - 1
    mix_scale = (mesh_rows / (grid_rows * pipe_count)) ** 0.5
    nbrs = mesh_links.shape[1] * pipe_count
    chan, pipe, face = (lax.axis_index(a) for a in ("chan", "pipe", "space"))
    scalars = jnp.stack(
        [chan, pipe, chan * pipe_count + pipe, face]
        + [(chan + j) % chan_count for j in range(1, chan_count)]
    ).astype(jnp.int32)
    target = ((g2m_face[:, 0] - face) % face_count) * mesh_rows + g2m_node
    target = target.reshape(1, grid_rows)

    def columns_at(place):
        return pl.BlockSpec((wide, narrow), lambda i, sr: (0, sr[place]))

    def both_cores(keep, give):
        total = keep.astype(F32) + shifted(give, "pipe", 1).astype(F32)
        return list(total.astype(BF16).reshape(face_count, mesh_rows, part))

    def to_owner(blocks):
        total = blocks[0].astype(F32)
        for k in range(1, face_count):
            total = total + shifted(blocks[k], "space", -k).astype(F32)
        return total

    def face_wide(block):
        return lax.all_gather(block, FACE_AXES)

    def from_owners(block):
        return [block] + [shifted(block, "space", k) for k in range(1, face_count)]

    sums = [((mesh_all, part), BF16)] * 2
    sum_flops = 2 * mesh_all * grid_rows * narrow
    keep, give = run(
        encode_body, scalars, (grid_latent, w_enc, target), sums,
        scratch=[pltpu.VMEM((grid_rows, narrow), BF16)],
        flops=sum_flops + 2 * grid_rows * wide * narrow, specs={1: columns_at(0)},
    )
    blocks, cotangent_late, links = lax.optimization_barrier(
        (both_cores(keep, give), cotangent, mesh_links)
    )
    mesh_part = lax.dynamic_slice_in_dim(mesh_latent, pipe * part, part, 1)
    state_part = mesh_part.astype(F32) + mix_scale * to_owner(blocks)
    state_0 = face_wide(state_part.astype(BF16))

    links = jnp.concatenate([links, shifted(links, "pipe", 1)], axis=1)
    offset = (links // mesh_rows - face) % face_count
    local = links % mesh_rows
    spot = jnp.where(
        offset == 0, mesh_rows + local, jnp.where(offset == 1, 2 * mesh_rows + local, local)
    )
    spot_row = spot.T.reshape(1, nbrs * mesh_rows)

    keep, give = run(sum_by_node, scalars, (target, cotangent_late), sums, flops=sum_flops)
    back_blocks = both_cores(keep, give)

    block = (mesh_rows, part)
    full = (mesh_rows, wide)
    edge_flops = 6 * mesh_rows * mesh_rows * nbrs * part

    def own_part(layer):
        if part % 128:
            return layer_of(w_send.shape, layer)
        return pl.BlockSpec((None, wide, part), lambda i, sr: (layer, 0, sr[2]))

    def neighbours(send_p):
        return shifted(send_p, "space", -1), shifted(send_p, "space", 1)

    def edges(send_p, recv_p, below, above):
        return run(
            edge_body, scalars, (below, send_p, above, recv_p, spot),
            [(block, BF16), ((nbrs,) + block, BF16)],
            scratch=[pltpu.VMEM((3 * mesh_rows // 2, 2 * part), BF16)], flops=edge_flops,
        )

    send_p, recv_p = run(
        first_body, scalars, (state_0, w_send, w_recv), [(block, BF16), (block, F32)],
        specs={1: own_part(0), 2: own_part(0)}, flops=4 * mesh_rows * wide * part,
    )
    below, above, back_blocks = lax.optimization_barrier((*neighbours(send_p), back_blocks))
    agg, slope_0 = edges(send_p, recv_p, below, above)
    agg_0 = face_wide(agg)
    state_1, send_p, recv_p = run(
        next_body, scalars, (agg_0, state_0, w_node, w_send, w_recv),
        [(full, F32), (block, BF16), (block, F32)],
        specs={2: layer_of(w_node.shape, 0), 3: own_part(1), 4: own_part(1)},
        flops=2 * mesh_rows * wide * wide,
    )
    back_dec = face_wide(to_owner(back_blocks).astype(BF16))
    agg, slope_1 = edges(send_p, recv_p, *neighbours(send_p))
    agg_1 = face_wide(agg)
    back_outs = [(full, F32), (block, BF16), (block, BF16), (block, F32), (block, BF16)]
    back_scratch = [pltpu.VMEM((nbrs * mesh_rows, 2 * part), BF16)]
    last_b, dec_part, dec_grad, grad_2, recv_grad, below, own, above = run(
        turn_body, scalars,
        (agg_1, state_1, w_node, w_dec, back_dec, slope_1, spot, spot_row),
        [(full, BF16), (block, BF16), (full, BF16)] + back_outs,
        specs={2: layer_of(w_node.shape, 1)}, scratch=back_scratch,
        flops=edge_flops + 6 * mesh_rows * wide * wide,
    )

    half = wide // pipe_count

    def weights(args, kinds):
        return run(
            functools.partial(weight_body, kinds), scalars, args,
            [((half * len(kinds), narrow), BF16)],
            flops=2 * mesh_rows * half * narrow * len(kinds),
        )[0]

    def senders(below, own, above):
        return (own + below.astype(F32) + above.astype(F32)).astype(BF16)

    sums_a = weights((last_b, dec_grad, agg_1, grad_2), ((0, 1), (2, 3)))
    recv_1 = face_wide(recv_grad)
    below, above = shifted(below, "space", 1), shifted(above, "space", -1)
    below, above, dec_part = lax.optimization_barrier((below, above, dec_part))
    send_1 = face_wide(senders(below, own, above))
    layer_specs = lambda first, layer: {
        first: layer_of(w_send.shape, layer), first + 1: layer_of(w_recv.shape, layer)
    }
    grad_1, recv_grad, below, own, above = run(
        back_body, scalars,
        (grad_2, send_1, recv_1, w_send, w_recv, w_node, slope_0, spot, spot_row), back_outs,
        specs={**layer_specs(3, 1), 5: layer_of(w_node.shape, 0)}, scratch=back_scratch,
        flops=edge_flops + 4 * mesh_rows * wide * wide,
    )
    sums_b = weights((state_1, send_1, recv_1, agg_0, grad_1), ((0, 1), (0, 2), (3, 4)))
    recv_0 = face_wide(recv_grad)
    below, above = shifted(below, "space", 1), shifted(above, "space", -1)
    send_0 = face_wide(senders(below, own, above))
    grad_mesh, enc_part, enc_all = run(
        functools.partial(last_body, mix_scale), scalars,
        (grad_1, send_0, recv_0, w_send, w_recv),
        [((mesh_rows, narrow), F32), (block, BF16), (full, BF16)],
        specs=layer_specs(3, 0), flops=4 * mesh_rows * wide * wide,
    )
    sums_c = weights((state_0, send_0, recv_0), ((0, 1), (0, 2)))

    dec_mine = jnp.concatenate(from_owners(dec_part), axis=0)
    mixed, slope_enc = run(
        mixed_body, scalars,
        (grid_latent, grid_latent, w_enc, target, dec_mine, shifted(dec_mine, "pipe", 1)),
        [((grid_rows, narrow), BF16), ((grid_rows, wide), BF16)],
        scratch=[pltpu.VMEM((mesh_all, narrow), BF16)],
        flops=sum_flops + 2 * grid_rows * wide * wide,
        specs={1: pl.BlockSpec((grid_rows, narrow), lambda i, sr: (0, sr[0]))},
    )
    enc_mine = from_owners(enc_part)
    enc_other = [shifted(piece, "pipe", 1) for piece in enc_mine]
    grid_columns = lambda place: pl.BlockSpec((grid_rows, narrow), lambda i, sr: (0, sr[place]))
    enc_grad, grad_keep, grad_give = run(
        functools.partial(enc_own_body, face_count), scalars,
        (grid_latent, target, slope_enc, *enc_mine, *enc_other),
        [((grid_rows, narrow), BF16), ((half, narrow), F32), ((half, narrow), BF16)],
        scratch=[pltpu.VMEM((mesh_all, narrow), BF16), pltpu.VMEM((wide, narrow), F32)],
        flops=sum_flops + 2 * grid_rows * wide * narrow, specs={2: grid_columns(0)},
    )
    half_sum = (grad_keep + shifted(grad_give, "pipe", 1).astype(F32)).astype(BF16)
    total = half_sum.astype(F32)
    for k in range(1, face_count):
        total = total + shifted(half_sum, "space", k).astype(F32)
    grad_w_enc = lax.all_gather(total, "pipe", axis=0, tiled=True)

    pieces = []
    for j in range(1, chan_count):
        for k in range(1, face_count):
            piece = shifted(enc_mine[k], "chan", j)
            pieces += [piece, shifted(piece, "pipe", 1)]
    corner = lambda place: pl.BlockSpec((narrow, narrow), lambda i, sr: (sr[0], sr[place]))
    specs = {3: corner(0)}
    for j in range(others):
        specs[5 + j] = grid_columns(4 + j)
        specs[5 + others + j] = corner(4 + j)
    grad_grid, = run(
        functools.partial(enc_other_body, face_count, others), scalars,
        (target, cotangent, enc_grad, w_enc, enc_all)
        + (slope_enc,) * others + (w_enc,) * others + tuple(pieces),
        [((grid_rows, narrow), BF16)], specs=specs,
        scratch=[pltpu.VMEM((mesh_all, narrow * others), BF16)],
        flops=(sum_flops + 4 * grid_rows * narrow * narrow) * others,
    )

    sums_all = lax.psum((sums_a, sums_b, sums_c), "space")
    layers = w_send.shape[0]
    layer_shape = ((layers, wide, narrow), F32)
    grad_w_send, grad_w_recv, grad_w_node, grad_w_dec = run(
        functools.partial(
            write_body, (((3, None), (2, 1)), ((0, 1), (1, 1), (2, 0)), ((0, 0), (1, 0)))
        ),
        scalars, (*sums_all, *(shifted(a, "pipe", 1) for a in sums_all)),
        [layer_shape] * 3 + [((wide, narrow), F32)],
    )
    return (
        mixed,
        grad_grid,
        grad_mesh,
        grad_w_enc,
        grad_w_send,
        grad_w_recv,
        grad_w_node,
        grad_w_dec,
    )


def solution(mesh):
    nodes = ("groups", "space", "pipe")
    in_specs = (
        P(nodes, None), P(nodes, None), P(nodes), P(("groups", "space"), "chan"),
        P(("groups", "space"), "pipe"), P(), P(), P(), P(), P(), P(nodes, "chan"),
    )
    out_specs = (
        P(nodes, "chan"), P(nodes, "chan"), P(("groups", "space"), "chan"), P("groups", "chan"),
        P("groups", None, "chan"), P("groups", None, "chan"), P("groups", None, "chan"),
        P("groups", "chan"),
    )
    return jax.shard_map(
        per_device, mesh=mesh, in_specs=in_specs, out_specs=out_specs, check_vma=False
    )
```

time: 351 us -> 261 us (0.74)
  waiting for transfers between devices: 106 us -> 36.8 us
  starting transfers between devices: 49 us -> 41.5 us
  Pallas kernels: 93.4 us -> 87.5 us
  local copies, waits for them, and re-layouts: 12 us -> 6.49 us
    psum x1, waiting for transfers between devices: 80.7 us -> 27.1 us  [per_device(): sums_all = lax.psum((sums_a, sums_b, sums_c), 'space')]
    ppermute x30 -> x41, waiting for transfers between devices: 24.9 us -> 9.7 us  [shifted(): lax.ppermute(block, axis, [((i + distance) % count, i) for i in range(cou...]
    ppermute x30 -> x41, starting transfers between devices: 48.8 us -> 41.5 us  [shifted(): lax.ppermute(block, axis, [((i + distance) % count, i) for i in range(cou...]
    pallas_call x15 -> x16, Pallas kernels: 93.4 us -> 87.5 us  [run(): pl.pallas_call(body, out_shape=[jax.ShapeDtypeStruct(s, d) for s, d in ou...]
    unnamed x74 -> x63, local copies, waits for them, and re-layouts: 10.4 us -> 5.55 us
    another operation x4 -> x0, other arithmetic: 4.24 us -> none  [the longest x3 3.62 us: rows_of(): return lax.all_gather(jnp.stack(blocks), 'pipe', axis=1, tiled=True)]
    all_gather x2 -> x0, blocking collectives: 4.1 us -> none  [the longest x1 2.17 us: per_device(): grad_w_dec = lax.all_gather(grads_a[0], 'pipe', axis=0, tiled=True)]
  transfers between devices with their start and end apart: 34 -> 42, of which waited for: 9 -> 6; matrix products, arithmetic and copies ran while one was open for 2% -> 2% of each run, Pallas kernels for 13% -> 25%
where the time goes in v2:
time: 261 us
  Pallas kernels  87.5 us (34%)
  blocking collectives  65.8 us (25%)
  starting transfers between devices  41.5 us (16%)
  waiting for transfers between devices  36.8 us (14%)
  between operations  14.4 us (6%)
  other arithmetic  8.04 us (3%)
  local copies, waits for them, and re-layouts  6.49 us (2%)
    pallas_call x16, Pallas kernels, run(): pl.pallas_call(body, out_shape=[jax.ShapeDtypeStruct(s, d) for s, d in ou...  87.5 us
    all_gather x8, blocking collectives, face_wide(): return lax.all_gather(block, FACE_AXES)  63.5 us
    ppermute x41, starting transfers between devices, shifted(): lax.ppermute(block, axis, [((i + distance) % count, i) for i in range(cou...  41.5 us
    psum x1, waiting for transfers between devices, per_device(): sums_all = lax.psum((sums_a, sums_b, sums_c), 'space')  27.1 us
    ppermute x41, waiting for transfers between devices, shifted(): lax.ppermute(block, axis, [((i + distance) % count, i) for i in range(cou...  9.7 us
    unnamed x63, local copies, waits for them, and re-layouts  5.55 us
  transfers between devices with their start and end apart: 42, of which 6 were waited for; matrix products, arithmetic and copies ran while one was open for 2% of the time, Pallas kernels for 25%

profile of v2, /device:TPU:0, one launch (start us, length us, event | category | flops | bytes accessed | tf_op | source)
XLA Modules:
  0.0 260.5 jit_solution(16747147281997233678)
XLA Ops:
  7.9 1.3 fusion.6
  9.8 7.4 %shard_map.170 = (bf16[2048,128]{1,0:T(8,128)(2,1)}, bf16[2048,128]{1,0:T(8,128)(2,1)}) custom-call(s32[5]{0:T(128)} %stack.23.sr, bf16[2048,512]{1,0:T(8,128)(2,1)} %x.5, bf16[512,512]{1,0:T(8,128)(2,1)} %rest_1_.1, s32[1,2048]{1,0:T(1,128)} %bitcast.40), custom_call_target="tpu_custom_call" | custom-call | flops 2684354560 | tf_op jit(solution)/shard_map/pallas_call | solution.py:64
  17.7 1.7 collective-permute-done
  19.4 1.2 add_convert_fusion.1
  21.1 2.7 %collective-permute-start.1 = (bf16[512,128]{1,0:T(8,128)(2,1)S(1)}, bf16[512,128]{1,0:T(8,128)(2,1)S(1)}, u32[]{:S(2)}, u32[]{:S(2)}) collective-permute-start(bf16[512,128]{1,0:T(8,128)(2,1)S(1)} %get-tuple-element.64), channel_id=1, source_target_pairs={{12,0},{0,4},{4,8},{8,12},{13,1},{1,5},{5,9},{9,13},{14,2},{2,6},{... | collective-permute-start | bytes 393224 | tf_op jit(solution)/shard_map/ppermute | solution.py:16
  23.8 2.6 collective-permute-start.2
  26.4 1.3 collective-permute-start.3
  27.8 5.7 %shard_map.172 = (bf16[2048,128]{1,0:T(8,128)(2,1)}, bf16[2048,128]{1,0:T(8,128)(2,1)}) custom-call(s32[5]{0:T(128)} %stack.23.sr, s32[1,2048]{1,0:T(1,128)} %bitcast.41, bf16[2048,256]{1,0:T(8,128)(2,1)} %cotangent.1), custom_call_target="tpu_custom_call" | custom-call | flops 2147483648 | tf_op jit(solution)/shard_map/pallas_call | solution.py:64
  33.7 1.1 fusion.2.spot
  36.0 7.9 %all-gather = bf16[2048,128]{1,0:T(8,128)(2,1)} all-gather(bf16[512,128]{1,0:T(8,128)(2,1)S(1)} %add_convert_fusion.6), channel_id=2, replica_groups=mesh['groups'=2,'space'=4,'chan'=2,'pipe'=2] {'chan','pipe'}, dimensions={0}, use_global_device_ids=true | all-gather | bytes 655360 | tf_op jit(solution)/shard_map/all_gather | solution.py:360
  43.9 2.9 %shard_map.171 = (bf16[512,128]{1,0:T(8,128)(2,1)}, f32[512,128]{1,0:T(8,128)}) custom-call(s32[5]{0:T(128)} %stack.23.sr, bf16[4,512,128]{2,1,0:T(8,128)(2,1)} %bitcast.20, bf16[2,512,512]{2,1,0:T(8,128)(2,1)} %w_send.7, bf16[2,512,512]{2,1,0:T(8,128)(2,1)} %w_recv.7), custom_call_target="tpu_custom_call" | custom-call | flops 134217728 | tf_op jit(solution)/shard_map/pallas_call | solution.py:64
  46.8 3.8 %collective-permute-start.5 = (bf16[512,128]{1,0:T(8,128)(2,1)}, bf16[512,128]{1,0:T(8,128)(2,1)S(1)}, u32[]{:S(2)}, u32[]{:S(2)}) collective-permute-start(bf16[512,128]{1,0:T(8,128)(2,1)} %get-tuple-element.67.own), channel_id=1, source_target_pairs={{4,0},{8,4},{12,8},{0,12},{5,1},{9,5},{13,9},{1,13},{6,2},{10,6},{... | collective-permute-start | bytes 393224 | tf_op jit(solution)/shard_map/ppermute | solution.py:16
  50.8 4.0 %collective-permute-done.5.above = bf16[512,128]{1,0:T(8,128)(2,1)S(1)} collective-permute-done((bf16[512,128]{1,0:T(8,128)(2,1)}, bf16[512,128]{1,0:T(8,128)(2,1)S(1)}, u32[]{:S(2)}, u32[]{:S(2)}) %collective-permute-start.5) | collective-permute-done | bytes 131104 | tf_op jit(solution)/shard_map/ppermute | solution.py:16
  54.8 3.3 %collective-permute-done.4.below = bf16[512,128]{1,0:T(8,128)(2,1)S(1)} collective-permute-done((bf16[512,128]{1,0:T(8,128)(2,1)}, bf16[512,128]{1,0:T(8,128)(2,1)S(1)}, u32[]{:S(2)}, u32[]{:S(2)}) %collective-permute-start.4) | collective-permute-done | bytes 131104 | tf_op jit(solution)/shard_map/ppermute | solution.py:16
  58.1 1.3 collective-permute-start.10
  60.0 2.5 collective-permute-start.12
  62.4 4.5 %shard_map.173 = (bf16[512,128]{1,0:T(8,128)(2,1)}, bf16[6,512,128]{2,1,0:T(8,128)(2,1)}) custom-call(s32[5]{0:T(128)} %stack.23.sr, bf16[512,128]{1,0:T(8,128)(2,1)} %copy-done.24, bf16[512,128]{1,0:T(8,128)(2,1)} %get-tuple-element.67.own, bf16[512,128]{1,0:T(8,128)(2,1)} %copy-done.23, f32[512,128]{1,0:T(8,128)} %get-tuple-element.73.recv_p, ...), custom_call_target="tpu_custom_call" | custom-call | flops 1207959552 | tf_op jit(solution)/shard_map/pallas_call | solution.py:64
  67.0 8.0 %all-gather.1 = bf16[2048,128]{1,0:T(8,128)(2,1)} all-gather(bf16[512,128]{1,0:T(8,128)(2,1)} %get-tuple-element.75), channel_id=3, replica_groups=mesh['groups'=2,'space'=4,'chan'=2,'pipe'=2] {'chan','pipe'}, dimensions={0}, use_global_device_ids=true | all-gather | bytes 655360 | tf_op jit(solution)/shard_map/all_gather | solution.py:360
  74.9 3.6 %shard_map.174 = (f32[512,512]{1,0:T(8,128)}, bf16[512,128]{1,0:T(8,128)(2,1)}, f32[512,128]{1,0:T(8,128)}) custom-call(s32[5]{0:T(128)} %stack.23.sr, bf16[4,512,128]{2,1,0:T(8,128)(2,1)} %bitcast.23, bf16[4,512,128]{2,1,0:T(8,128)(2,1)} %bitcast.21, bf16[2,512,512]{2,1,0:T(8,128)(2,1)} %w_node.5, bf16[2,512,512]{2,1,0:T(8,128)(2,1)} %w_send.7, ...), custom_call_target="tpu_custom_call" | custom-call | flops 268435456 | tf_op jit(solution)/shard_map/pallas_call | solution.py:64
  79.5 1.1 collective-permute-start.8
  80.7 7.2 %all-gather.3 = bf16[2048,128]{1,0:T(8,128)(2,1)} all-gather(bf16[512,128]{1,0:T(8,128)(2,1)S(1)} %add_convert_fusion.5), channel_id=5, replica_groups=mesh['groups'=2,'space'=4,'chan'=2,'pipe'=2] {'chan','pipe'}, dimensions={0}, use_global_device_ids=true | all-gather | bytes 655360 | tf_op jit(solution)/shard_map/all_gather | solution.py:360
  88.6 4.5 %shard_map.175 = (bf16[512,128]{1,0:T(8,128)(2,1)}, bf16[6,512,128]{2,1,0:T(8,128)(2,1)}) custom-call(s32[5]{0:T(128)} %stack.23.sr, bf16[512,128]{1,0:T(8,128)(2,1)} %copy-done.28, bf16[512,128]{1,0:T(8,128)(2,1)} %get-tuple-element.76.own, bf16[512,128]{1,0:T(8,128)(2,1)} %copy-done.26, f32[512,128]{1,0:T(8,128)} %get-tuple-element.77.recv_p, ...), custom_call_target="tpu_custom_call" | custom-call | flops 1207959552 | tf_op jit(solution)/shard_map/pallas_call | solution.py:64
  93.1 8.9 %all-gather.2 = bf16[2048,128]{1,0:T(8,128)(2,1)} all-gather(bf16[512,128]{1,0:T(8,128)(2,1)} %get-tuple-element.78), channel_id=4, replica_groups=mesh['groups'=2,'space'=4,'chan'=2,'pipe'=2] {'chan','pipe'}, dimensions={0}, use_global_device_ids=true | all-gather | bytes 655360 | tf_op jit(solution)/shard_map/all_gather | solution.py:360
  102.0 7.0 %shard_map.176 = (bf16[512,512]{1,0:T(8,128)(2,1)}, bf16[512,128]{1,0:T(8,128)(2,1)}, bf16[512,512]{1,0:T(8,128)(2,1)}, f32[512,512]{1,0:T(8,128)}, bf16[512,128...) custom-call(s32[5]{0:T(128)} %stack.23.sr, ...), custom_call_target="tpu_custom_call" | custom-call | flops 2013265920 | tf_op jit(solution)/shard_map/pallas_call | solution.py:64
  108.9 3.0 %collective-permute-start.13 = (bf16[512,128]{1,0:T(8,128)(2,1)}, bf16[512,128]{1,0:T(8,128)(2,1)S(1)}, u32[]{:S(2)}, u32[]{:S(2)}) collective-permute-start(bf16[512,128]{1,0:T(8,128)(2,1)} %get-tuple-element.85), channel_id=1, source_target_pairs={{4,0},{8,4},{12,8},{0,12},{5,1},{9,5},{13,9},{1,13},{6,2},{10,6},{... | collective-permute-start | bytes 393224 | tf_op jit(solution)/shard_map/ppermute | solution.py:16
  111.9 8.4 %all-gather.5 = bf16[2048,128]{1,0:T(8,128)(2,1)} all-gather(bf16[512,128]{1,0:T(8,128)(2,1)} %get-tuple-element.95), channel_id=7, replica_groups=mesh['groups'=2,'space'=4,'chan'=2,'pipe'=2] {'chan','pipe'}, dimensions={0}, use_global_device_ids=true | all-gather | bytes 655360 | tf_op jit(solution)/shard_map/all_gather | solution.py:360
  120.7 3.8 %collective-permute-start.16 = (bf16[512,128]{1,0:T(8,128)(2,1)}, bf16[512,128]{1,0:T(8,128)(2,1)S(1)}, u32[]{:S(2)}, u32[]{:S(2)}) collective-permute-start(bf16[512,128]{1,0:T(8,128)(2,1)} %get-tuple-element.88), channel_id=1, source_target_pairs={{8,0},{12,4},{0,8},{4,12},{9,1},{13,5},{1,9},{5,13},{10,2},{14,6},... | collective-permute-start | bytes 393224 | tf_op jit(solution)/shard_map/ppermute | solution.py:16
  125.5 7.2 %all-gather.4 = bf16[2048,128]{1,0:T(8,128)(2,1)} all-gather(bf16[512,128]{1,0:T(8,128)(2,1)S(1)} %add_convert_fusion.4), channel_id=6, replica_groups=mesh['groups'=2,'space'=4,'chan'=2,'pipe'=2] {'chan','pipe'}, dimensions={0}, use_global_device_ids=true | all-gather | bytes 655360 | tf_op jit(solution)/shard_map/all_gather | solution.py:360
  132.7 6.8 %shard_map.178 = (f32[512,512]{1,0:T(8,128)}, bf16[512,128]{1,0:T(8,128)(2,1)}, bf16[512,128]{1,0:T(8,128)(2,1)}, f32[512,128]{1,0:T(8,128)}, bf16[512,128]{1,0:T(8,128)(2,1)}) custom-call(s32[5]{0:T(128)} %stack.23.sr, f32[512,512]{1,0:T(8,128)} %get-tuple-element.91.grad.refs_3_, bf16[4,512,128]{2,1,0:T(8,128)(2,1)} %bitcast.31, ...), custom_call_target="tpu_custom_call" | custom-call | flops 1744830464 | tf_op jit(solution)/shard_map/pallas_call | solution.py:64
  139.5 1.5 collective-permute-start.19
  141.6 8.4 %all-gather.7 = bf16[2048,128]{1,0:T(8,128)(2,1)} all-gather(bf16[512,128]{1,0:T(8,128)(2,1)} %get-tuple-element.101), channel_id=9, replica_groups=mesh['groups'=2,'space'=4,'chan'=2,'pipe'=2] {'chan','pipe'}, dimensions={0}, use_global_device_ids=true | all-gather | bytes 655360 | tf_op jit(solution)/shard_map/all_gather | solution.py:360
  151.6 7.6 %all-gather.6 = bf16[2048,128]{1,0:T(8,128)(2,1)} all-gather(bf16[512,128]{1,0:T(8,128)(2,1)S(1)} %add_convert_fusion.3), channel_id=8, replica_groups=mesh['groups'=2,'space'=4,'chan'=2,'pipe'=2] {'chan','pipe'}, dimensions={0}, use_global_device_ids=true | all-gather | bytes 655360 | tf_op jit(solution)/shard_map/all_gather | solution.py:360
  159.1 4.3 %shard_map.179 = (f32[512,256]{1,0:T(8,128)}, bf16[512,128]{1,0:T(8,128)(2,1)}, bf16[512,512]{1,0:T(8,128)(2,1)}) custom-call(s32[5]{0:T(128)} %stack.23.sr, f32[512,512]{1,0:T(8,128)} %get-tuple-element.97.grad.refs_4_, bf16[4,512,128]{2,1,0:T(8,128)(2,1)} %bitcast.27, bf16[4,512,128]{2,1,0:T(8,128)(2,1)} %bitcast.25, bf16[2,512,512]{2,1,0:T(8,128)(2,1)} %w_send.7, ...), custom_call_target="tpu_custom_call" | custom-call | flops 536870912 | tf_op jit(solution)/shard_map/pallas_call | solution.py:64
  163.4 1.7 collective-permute-start.23
  165.1 1.9 collective-permute-start.22
  167.8 3.4 %shard_map.182 = bf16[512,256]{1,0:T(8,128)(2,1)} custom-call(s32[5]{0:T(128)} %stack.23.sr, bf16[512,512]{1,0:T(8,128)(2,1)} %get-tuple-element.108.refs_0_, bf16[512,512]{1,0:T(8,128)(2,1)} %get-tuple-element.109.refs_1_, bf16[4,512,128]{2,1,0:T(8,128)(2,1)} %bitcast.34, f32[512,512]{1,0:T(8,128)} %get-tuple-element.91.grad.refs_3_), custom_call_target="tpu_custom_call" | custom-call | flops 134217728 | tf_op jit(solution)/shard_map/pallas_call | solution.py:64
  171.2 4.0 %shard_map.183 = bf16[768,256]{1,0:T(8,128)(2,1)} custom-call(s32[5]{0:T(128)} %stack.23.sr, f32[512,512]{1,0:T(8,128)} %get-tuple-element.79.state.refs_0_, bf16[4,512,128]{2,1,0:T(8,128)(2,1)} %bitcast.32, bf16[4,512,128]{2,1,0:T(8,128)(2,1)} %bitcast.30, bf16[4,512,128]{2,1,0:T(8,128)(2,1)} %bitcast.24, f32[512,512]{1,0:T(8,128)} %get-tuple-element.97.grad.refs_4_), custom_call_target="tpu_custom_call" | custom-call | flops 201326592 | tf_op jit(solution)/shard_map/pallas_call | solution.py:64
  175.2 3.1 %shard_map.184 = bf16[512,256]{1,0:T(8,128)(2,1)} custom-call(s32[5]{0:T(128)} %stack.23.sr, bf16[4,512,128]{2,1,0:T(8,128)(2,1)} %bitcast.22, bf16[4,512,128]{2,1,0:T(8,128)(2,1)} %bitcast.28, bf16[4,512,128]{2,1,0:T(8,128)(2,1)} %bitcast.26), custom_call_target="tpu_custom_call" | custom-call | flops 134217728 | tf_op jit(solution)/shard_map/pallas_call | solution.py:64
  178.3 1.1 collective-permute-start.32
  180.8 9.3 %shard_map.177 = (bf16[2048,256]{1,0:T(8,128)(2,1)}, bf16[2048,512]{1,0:T(8,128)(2,1)}) custom-call(s32[5]{0:T(128)} %stack.23.sr, bf16[2048,512]{1,0:T(8,128)(2,1)} %x.5, bf16[2048,512]{1,0:T(8,128)(2,1)} %x.5, bf16[512,512]{1,0:T(8,128)(2,1)} %rest_1_.1, s32[1,2048]{1,0:T(1,128)} %bitcast.42, bf16[2048,128]{1,0:T(8,128)(2,1)} %copy-done.8, ...), custom_call_target="tpu_custom_call" | custom-call | flops 3221225472 | tf_op jit(solution)/shard_map/pallas_call | solution.py:64
  191.0 1.2 collective-permute-start.28
  192.9 8.7 %shard_map.180 = (bf16[2048,256]{1,0:T(8,128)(2,1)}, f32[256,256]{1,0:T(8,128)}, bf16[256,256]{1,0:T(8,128)(2,1)}) custom-call(s32[5]{0:T(128)} %stack.23.sr, bf16[2048,512]{1,0:T(8,128)(2,1)} %x.5, s32[1,2048]{1,0:T(1,128)} %bitcast.43, bf16[2048,512]{1,0:T(8,128)(2,1)} %get-tuple-element.90.slope.rest_0_, bf16[512,128]{1,0:T(8,128)(2,1)} %get-tuple-element.102.rest_0_, ...), custom_call_target="tpu_custom_call" | custom-call | flops 2684354560 | tf_op jit(solution)/shard_map/pallas_call | solution.py:64
  204.1 1.1 collective-permute-start.37
  206.3 2.1 collective-permute-start.35
  208.4 27.1 %all-reduce.3.cloned.1.call-done = (bf16[512,256]{1,0:T(8,128)(2,1)}, bf16[768,256]{1,0:T(8,128)(2,1)}, bf16[512,256]{1,0:T(8,128)(2,1)}) async-done(((bf16[512,256]{1,0:T(8,128)(2,1)}, bf16[768,256]{1,0:T(8,128)(2,1)}, bf16[512,256]{1,0:T(8,128)(2,1)}), (bf16[512,256]{1,0:T(8,128)(2,1)}, bf16[768,256]{1,0:T(8,128)(2,1)}, bf16[512,256]{1,0:T(8,128)(2,1)})) %all-reduce.3.cloned.1.call-update) | async-done | bytes 917520 | tf_op jit(solution)/shard_map/psum | solution.py:517
  236.2 8.2 %shard_map.181 = bf16[2048,256]{1,0:T(8,128)(2,1)} custom-call(s32[5]{0:T(128)} %stack.23.sr, s32[1,2048]{1,0:T(1,128)} %bitcast.44, bf16[2048,256]{1,0:T(8,128)(2,1)} %cotangent.1, bf16[2048,256]{1,0:T(8,128)(2,1)} %get-tuple-element.103.enc_grad, bf16[512,512]{1,0:T(8,128)(2,1)} %rest_1_.1, bf16[512,512]{1,0:T(8,128)(2,1)} %get-tuple-element.104.enc_all, ...), custom_call_target="tpu_custom_call" | custom-call | flops 2684354560 | tf_op jit(solution)/shard_map/pallas_call | solution.py:64
  245.0 2.2 all_gather.67
  248.8 4.1 %shard_map.185 = (f32[2,512,256]{2,1,0:T(8,128)}, f32[2,512,256]{2,1,0:T(8,128)}, f32[2,512,256]{2,1,0:T(8,128)}, f32[512,256]{1,0:T(8,128)}) custom-call(s32[5]{0:T(128)} %stack.23.sr, bf16[512,256]{1,0:T(8,128)(2,1)} %get-tuple-element.114.refs_0_, bf16[768,256]{1,0:T(8,128)(2,1)} %get-tuple-element.115.refs_1_, ...), custom_call_target="tpu_custom_call" | custom-call | tf_op jit(solution)/shard_map/pallas_call | solution.py:64
  (144 shorter events, 20.5 us)
Async XLA Ops:
  7.2 228.3 %all-reduce.3.cloned.1.call-start = ((), (), s32[]{:S(2)}) async-start(), calls=%async_computation | async-start | bytes 1835008 | tf_op jit(solution)/shard_map/psum | solution.py:517
  17.2 2.2 collective-permute-start
  20.7 12.8 %collective-permute-start.7 = (s32[512,3]{0,1:T(4,128)S(1)}, s32[512,3]{0,1:T(4,128)S(1)}, u32[]{:S(2)}, u32[]{:S(2)}) collective-permute-start(s32[512,3]{0,1:T(4,128)S(1)} %copy-done.9), channel_id=1, source_target_pairs={{1,0},{0,1},{3,2},{2,3},{5,4},{4,5},{7,6},{6,7},{9,8},{8,9},{11,10... | collective-permute-start | bytes 18440 | tf_op jit(solution)/shard_map/ppermute | solution.py:16
  21.1 14.7 %collective-permute-start.1 = (bf16[512,128]{1,0:T(8,128)(2,1)S(1)}, bf16[512,128]{1,0:T(8,128)(2,1)S(1)}, u32[]{:S(2)}, u32[]{:S(2)}) collective-permute-start(bf16[512,128]{1,0:T(8,128)(2,1)S(1)} %get-tuple-element.64), channel_id=1, source_target_pairs={{12,0},{0,4},{4,8},{8,12},{13,1},{1,5},{5,9},{9,13},{14,2},{2,6},{... | collective-permute-start | bytes 393224 | tf_op jit(solution)/shard_map/ppermute | solution.py:16
  23.8 12.0 %collective-permute-start.2 = (bf16[512,128]{1,0:T(8,128)(2,1)S(1)}, bf16[512,128]{1,0:T(8,128)(2,1)S(1)}, u32[]{:S(2)}, u32[]{:S(2)}) collective-permute-start(bf16[512,128]{1,0:T(8,128)(2,1)S(1)} %get-tuple-element.65), channel_id=1, source_target_pairs={{8,0},{12,4},{0,8},{4,12},{9,1},{13,5},{1,9},{5,13},{10,2},{14,6},... | collective-permute-start | bytes 393224 | tf_op jit(solution)/shard_map/ppermute | solution.py:16
  26.4 9.4 %collective-permute-start.3 = (bf16[512,128]{1,0:T(8,128)(2,1)S(1)}, bf16[512,128]{1,0:T(8,128)(2,1)S(1)}, u32[]{:S(2)}, u32[]{:S(2)}) collective-permute-start(bf16[512,128]{1,0:T(8,128)(2,1)S(1)} %get-tuple-element.66), channel_id=1, source_target_pairs={{4,0},{8,4},{12,8},{0,12},{5,1},{9,5},{13,9},{1,13},{6,2},{10,6},{... | collective-permute-start | bytes 393224 | tf_op jit(solution)/shard_map/ppermute | solution.py:16
  33.5 17.1 %collective-permute-start.6 = (bf16[2048,128]{1,0:T(8,128)(2,1)}, bf16[2048,128]{1,0:T(8,128)(2,1)S(1)}, u32[]{:S(2)}, u32[]{:S(2)}) collective-permute-start(bf16[2048,128]{1,0:T(8,128)(2,1)} %get-tuple-element.70), channel_id=1, source_target_pairs={{1,0},{0,1},{3,2},{2,3},{5,4},{4,5},{7,6},{6,7},{9,8},{8,9},{11,10... | collective-permute-start | bytes 1572872 | tf_op jit(solution)/shard_map/ppermute | solution.py:16
  46.8 8.0 %collective-permute-start.5 = (bf16[512,128]{1,0:T(8,128)(2,1)}, bf16[512,128]{1,0:T(8,128)(2,1)S(1)}, u32[]{:S(2)}, u32[]{:S(2)}) collective-permute-start(bf16[512,128]{1,0:T(8,128)(2,1)} %get-tuple-element.67.own), channel_id=1, source_target_pairs={{4,0},{8,4},{12,8},{0,12},{5,1},{9,5},{13,9},{1,13},{6,2},{10,6},{... | collective-permute-start | bytes 393224 | tf_op jit(solution)/shard_map/ppermute | solution.py:16
  50.6 7.5 %collective-permute-start.4 = (bf16[512,128]{1,0:T(8,128)(2,1)}, bf16[512,128]{1,0:T(8,128)(2,1)S(1)}, u32[]{:S(2)}, u32[]{:S(2)}) collective-permute-start(bf16[512,128]{1,0:T(8,128)(2,1)} %get-tuple-element.67.own), channel_id=1, source_target_pairs={{12,0},{0,4},{4,8},{8,12},{13,1},{1,5},{5,9},{9,13},{14,2},{2,6},{... | collective-permute-start | bytes 393224 | tf_op jit(solution)/shard_map/ppermute | solution.py:16
  58.1 22.5 %collective-permute-start.10 = (bf16[512,128]{1,0:T(8,128)(2,1)S(1)}, bf16[512,128]{1,0:T(8,128)(2,1)S(1)}, u32[]{:S(2)}, u32[]{:S(2)}) collective-permute-start(bf16[512,128]{1,0:T(8,128)(2,1)S(1)} %get-tuple-element.81), channel_id=1, source_target_pairs={{12,0},{0,4},{4,8},{8,12},{13,1},{1,5},{5,9},{9,13},{14,2},{2,6},{... | collective-permute-start | bytes 393224 | tf_op jit(solution)/shard_map/ppermute | solution.py:16
  59.4 21.1 %collective-permute-start.11 = (bf16[512,128]{1,0:T(8,128)(2,1)S(1)}, bf16[512,128]{1,0:T(8,128)(2,1)S(1)}, u32[]{:S(2)}, u32[]{:S(2)}) collective-permute-start(bf16[512,128]{1,0:T(8,128)(2,1)S(1)} %get-tuple-element.82), channel_id=1, source_target_pairs={{8,0},{12,4},{0,8},{4,12},{9,1},{13,5},{1,9},{5,13},{10,2},{14,6},... | collective-permute-start | bytes 393224 | tf_op jit(solution)/shard_map/ppermute | solution.py:16
  60.0 20.6 %collective-permute-start.12 = (bf16[512,128]{1,0:T(8,128)(2,1)S(1)}, bf16[512,128]{1,0:T(8,128)(2,1)S(1)}, u32[]{:S(2)}, u32[]{:S(2)}) collective-permute-start(bf16[512,128]{1,0:T(8,128)(2,1)S(1)} %get-tuple-element.83), channel_id=1, source_target_pairs={{4,0},{8,4},{12,8},{0,12},{5,1},{9,5},{13,9},{1,13},{6,2},{10,6},{... | collective-permute-start | bytes 393224 | tf_op jit(solution)/shard_map/ppermute | solution.py:16
  78.5 9.3 %collective-permute-start.9 = (bf16[512,128]{1,0:T(8,128)(2,1)}, bf16[512,128]{1,0:T(8,128)(2,1)S(1)}, u32[]{:S(2)}, u32[]{:S(2)}) collective-permute-start(bf16[512,128]{1,0:T(8,128)(2,1)} %get-tuple-element.76.own), channel_id=1, source_target_pairs={{4,0},{8,4},{12,8},{0,12},{5,1},{9,5},{13,9},{1,13},{6,2},{10,6},{... | collective-permute-start | bytes 393224 | tf_op jit(solution)/shard_map/ppermute | solution.py:16
  79.5 8.4 %collective-permute-start.8 = (bf16[512,128]{1,0:T(8,128)(2,1)}, bf16[512,128]{1,0:T(8,128)(2,1)S(1)}, u32[]{:S(2)}, u32[]{:S(2)}) collective-permute-start(bf16[512,128]{1,0:T(8,128)(2,1)} %get-tuple-element.76.own), channel_id=1, source_target_pairs={{12,0},{0,4},{4,8},{8,12},{13,1},{1,5},{5,9},{9,13},{14,2},{2,6},{... | collective-permute-start | bytes 393224 | tf_op jit(solution)/shard_map/ppermute | solution.py:16
  108.9 11.4 %collective-permute-start.13 = (bf16[512,128]{1,0:T(8,128)(2,1)}, bf16[512,128]{1,0:T(8,128)(2,1)S(1)}, u32[]{:S(2)}, u32[]{:S(2)}) collective-permute-start(bf16[512,128]{1,0:T(8,128)(2,1)} %get-tuple-element.85), channel_id=1, source_target_pairs={{4,0},{8,4},{12,8},{0,12},{5,1},{9,5},{13,9},{1,13},{6,2},{10,6},{... | collective-permute-start | bytes 393224 | tf_op jit(solution)/shard_map/ppermute | solution.py:16
  111.9 8.5 %collective-permute-start.14 = (bf16[512,128]{1,0:T(8,128)(2,1)}, bf16[512,128]{1,0:T(8,128)(2,1)S(1)}, u32[]{:S(2)}, u32[]{:S(2)}) collective-permute-start(bf16[512,128]{1,0:T(8,128)(2,1)} %get-tuple-element.86), channel_id=1, source_target_pairs={{12,0},{0,4},{4,8},{8,12},{13,1},{1,5},{5,9},{9,13},{14,2},{2,6},{... | collective-permute-start | bytes 393224 | tf_op jit(solution)/shard_map/ppermute | solution.py:16
  120.4 29.7 %collective-permute-start.17 = (bf16[512,128]{1,0:T(8,128)(2,1)}, bf16[512,128]{1,0:T(8,128)(2,1)S(1)}, u32[]{:S(2)}, u32[]{:S(2)}) collective-permute-start(bf16[512,128]{1,0:T(8,128)(2,1)} %get-tuple-element.88), channel_id=1, source_target_pairs={{12,0},{0,4},{4,8},{8,12},{13,1},{1,5},{5,9},{9,13},{14,2},{2,6},{... | collective-permute-start | bytes 393224 | tf_op jit(solution)/shard_map/ppermute | solution.py:16
  120.7 29.3 %collective-permute-start.16 = (bf16[512,128]{1,0:T(8,128)(2,1)}, bf16[512,128]{1,0:T(8,128)(2,1)S(1)}, u32[]{:S(2)}, u32[]{:S(2)}) collective-permute-start(bf16[512,128]{1,0:T(8,128)(2,1)} %get-tuple-element.88), channel_id=1, source_target_pairs={{8,0},{12,4},{0,8},{4,12},{9,1},{13,5},{1,9},{5,13},{10,2},{14,6},... | collective-permute-start | bytes 393224 | tf_op jit(solution)/shard_map/ppermute | solution.py:16
  124.5 25.5 %collective-permute-start.15 = (bf16[512,128]{1,0:T(8,128)(2,1)}, bf16[512,128]{1,0:T(8,128)(2,1)S(1)}, u32[]{:S(2)}, u32[]{:S(2)}) collective-permute-start(bf16[512,128]{1,0:T(8,128)(2,1)} %get-tuple-element.88), channel_id=1, source_target_pairs={{4,0},{8,4},{12,8},{0,12},{5,1},{9,5},{13,9},{1,13},{6,2},{10,6},{... | collective-permute-start | bytes 393224 | tf_op jit(solution)/shard_map/ppermute | solution.py:16
  132.7 17.3 %copy-start.6 = (bf16[512,128]{1,0:T(8,128)(2,1)S(1)}, bf16[512,128]{1,0:T(8,128)(2,1)}, u32[]{:S(2)}) copy-start(bf16[512,128]{1,0:T(8,128)(2,1)} %get-tuple-element.88) | copy-start | bytes 393220
  139.5 11.0 %collective-permute-start.19 = (bf16[512,128]{1,0:T(8,128)(2,1)}, bf16[512,128]{1,0:T(8,128)(2,1)S(1)}, u32[]{:S(2)}, u32[]{:S(2)}) collective-permute-start(bf16[512,128]{1,0:T(8,128)(2,1)} %get-tuple-element.99), channel_id=1, source_target_pairs={{4,0},{8,4},{12,8},{0,12},{5,1},{9,5},{13,9},{1,13},{6,2},{10,6},{... | collective-permute-start | bytes 393224 | tf_op jit(solution)/shard_map/ppermute | solution.py:16
  141.0 9.6 %collective-permute-start.20 = (bf16[512,128]{1,0:T(8,128)(2,1)}, bf16[512,128]{1,0:T(8,128)(2,1)S(1)}, u32[]{:S(2)}, u32[]{:S(2)}) collective-permute-start(bf16[512,128]{1,0:T(8,128)(2,1)} %get-tuple-element.100), channel_id=1, source_target_pairs={{12,0},{0,4},{4,8},{8,12},{13,1},{1,5},{5,9},{9,13},{14,2},{2,6},{... | collective-permute-start | bytes 393224 | tf_op jit(solution)/shard_map/ppermute | solution.py:16
  150.1 29.8 %collective-permute-start.18 = (bf16[2048,128]{1,0:T(8,128)(2,1)S(1)}, bf16[2048,128]{1,0:T(8,128)(2,1)S(1)}, u32[]{:S(2)}, u32[]{:S(2)}) collective-permute-start(bf16[2048,128]{1,0:T(8,128)(2,1)S(1)} %constant_dynamic-update-slice_fusion.mine), channel_id=1, source_target_pairs={{1,0},{0,1},{3,2},{2,3},{5,4},{4,5},{7,6},{6,7},{9,8},{8,9},{11,10... | collective-permute-start | bytes 1572872 | tf_op jit(solution)/shard_map/ppermute | solution.py:16
  163.4 14.9 %collective-permute-start.23 = (bf16[512,128]{1,0:T(8,128)(2,1)}, bf16[512,128]{1,0:T(8,128)(2,1)S(1)}, u32[]{:S(2)}, u32[]{:S(2)}) collective-permute-start(bf16[512,128]{1,0:T(8,128)(2,1)} %get-tuple-element.102.rest_0_), channel_id=1, source_target_pairs={{12,0},{0,4},{4,8},{8,12},{13,1},{1,5},{5,9},{9,13},{14,2},{2,6},{... | collective-permute-start | bytes 393224 | tf_op jit(solution)/shard_map/ppermute | solution.py:16
  165.1 14.3 %collective-permute-start.22 = (bf16[512,128]{1,0:T(8,128)(2,1)}, bf16[512,128]{1,0:T(8,128)(2,1)S(1)}, u32[]{:S(2)}, u32[]{:S(2)}) collective-permute-start(bf16[512,128]{1,0:T(8,128)(2,1)} %get-tuple-element.102.rest_0_), channel_id=1, source_target_pairs={{8,0},{12,4},{0,8},{4,12},{9,1},{13,5},{1,9},{5,13},{10,2},{14,6},... | collective-permute-start | bytes 393224 | tf_op jit(solution)/shard_map/ppermute | solution.py:16
  167.0 12.7 %collective-permute-start.21 = (bf16[512,128]{1,0:T(8,128)(2,1)}, bf16[512,128]{1,0:T(8,128)(2,1)S(1)}, u32[]{:S(2)}, u32[]{:S(2)}) collective-permute-start(bf16[512,128]{1,0:T(8,128)(2,1)} %get-tuple-element.102.rest_0_), channel_id=1, source_target_pairs={{4,0},{8,4},{12,8},{0,12},{5,1},{9,5},{13,9},{1,13},{6,2},{10,6},{... | collective-permute-start | bytes 393224 | tf_op jit(solution)/shard_map/ppermute | solution.py:16
  175.2 14.9 %collective-permute-start.24 = (bf16[512,128]{1,0:T(8,128)(2,1)S(1)}, bf16[512,128]{1,0:T(8,128)(2,1)S(1)}, u32[]{:S(2)}, u32[]{:S(2)}) collective-permute-start(bf16[512,128]{1,0:T(8,128)(2,1)S(1)} %copy-done.15), channel_id=1, source_target_pairs={{1,0},{0,1},{3,2},{2,3},{5,4},{4,5},{7,6},{6,7},{9,8},{8,9},{11,10... | collective-permute-start | bytes 393224 | tf_op jit(solution)/shard_map/ppermute | solution.py:16
  178.3 23.2 %collective-permute-start.32 = (bf16[512,128]{1,0:T(8,128)(2,1)S(1)}, bf16[512,128]{1,0:T(8,128)(2,1)S(1)}, u32[]{:S(2)}, u32[]{:S(2)}) collective-permute-start(bf16[512,128]{1,0:T(8,128)(2,1)S(1)} %collective-permute-done.23.rest_3_), channel_id=1, source_target_pairs={{2,0},{0,2},{3,1},{1,3},{6,4},{4,6},{7,5},{5,7},{10,8},{8,10},{11,... | collective-permute-start | bytes 393224 | tf_op jit(solution)/shard_map/ppermute | solution.py:16
  179.5 11.6 %collective-permute-start.27 = (bf16[512,128]{1,0:T(8,128)(2,1)S(1)}, bf16[512,128]{1,0:T(8,128)(2,1)S(1)}, u32[]{:S(2)}, u32[]{:S(2)}) collective-permute-start(bf16[512,128]{1,0:T(8,128)(2,1)S(1)} %collective-permute-done.23.rest_3_), channel_id=1, source_target_pairs={{1,0},{0,1},{3,2},{2,3},{5,4},{4,5},{7,6},{6,7},{9,8},{8,9},{11,10... | collective-permute-start | bytes 393224 | tf_op jit(solution)/shard_map/ppermute | solution.py:16
  179.7 12.5 %collective-permute-start.26 = (bf16[512,128]{1,0:T(8,128)(2,1)S(1)}, bf16[512,128]{1,0:T(8,128)(2,1)S(1)}, u32[]{:S(2)}, u32[]{:S(2)}) collective-permute-start(bf16[512,128]{1,0:T(8,128)(2,1)S(1)} %collective-permute-done.22.rest_2_), channel_id=1, source_target_pairs={{1,0},{0,1},{3,2},{2,3},{5,4},{4,5},{7,6},{6,7},{9,8},{8,9},{11,10... | collective-permute-start | bytes 393224 | tf_op jit(solution)/shard_map/ppermute | solution.py:16
  180.0 12.2 %collective-permute-start.25 = (bf16[512,128]{1,0:T(8,128)(2,1)S(1)}, bf16[512,128]{1,0:T(8,128)(2,1)S(1)}, u32[]{:S(2)}, u32[]{:S(2)}) collective-permute-start(bf16[512,128]{1,0:T(8,128)(2,1)S(1)} %collective-permute-done.21.rest_1_), channel_id=1, source_target_pairs={{1,0},{0,1},{3,2},{2,3},{5,4},{4,5},{7,6},{6,7},{9,8},{8,9},{11,10... | collective-permute-start | bytes 393224 | tf_op jit(solution)/shard_map/ppermute | solution.py:16
  190.1 12.0 %collective-permute-start.30 = (bf16[512,128]{1,0:T(8,128)(2,1)S(1)}, bf16[512,128]{1,0:T(8,128)(2,1)S(1)}, u32[]{:S(2)}, u32[]{:S(2)}) collective-permute-start(bf16[512,128]{1,0:T(8,128)(2,1)S(1)} %collective-permute-done.22.rest_2_), channel_id=1, source_target_pairs={{2,0},{0,2},{3,1},{1,3},{6,4},{4,6},{7,5},{5,7},{10,8},{8,10},{11,... | collective-permute-start | bytes 393224 | tf_op jit(solution)/shard_map/ppermute | solution.py:16
  191.0 11.2 %collective-permute-start.28 = (bf16[512,128]{1,0:T(8,128)(2,1)S(1)}, bf16[512,128]{1,0:T(8,128)(2,1)S(1)}, u32[]{:S(2)}, u32[]{:S(2)}) collective-permute-start(bf16[512,128]{1,0:T(8,128)(2,1)S(1)} %collective-permute-done.21.rest_1_), channel_id=1, source_target_pairs={{2,0},{0,2},{3,1},{1,3},{6,4},{4,6},{7,5},{5,7},{10,8},{8,10},{11,... | collective-permute-start | bytes 393224 | tf_op jit(solution)/shard_map/ppermute | solution.py:16
  201.6 1.6 collective-permute-start.34
  201.6 34.0 %copy-start.11 = (bf16[512,128]{1,0:T(8,128)(2,1)}, bf16[512,128]{1,0:T(8,128)(2,1)S(1)}, u32[]{:S(2)}) copy-start(bf16[512,128]{1,0:T(8,128)(2,1)S(1)} %collective-permute-done.32.rest_6_) | copy-start | bytes 393220
  201.6 4.7 %collective-permute-start.33 = (bf16[512,128]{1,0:T(8,128)(2,1)S(1)}, bf16[512,128]{1,0:T(8,128)(2,1)S(1)}, u32[]{:S(2)}, u32[]{:S(2)}) collective-permute-start(bf16[512,128]{1,0:T(8,128)(2,1)S(1)} %collective-permute-done.32.rest_6_), channel_id=1, source_target_pairs={{1,0},{0,1},{3,2},{2,3},{5,4},{4,5},{7,6},{6,7},{9,8},{8,9},{11,10... | collective-permute-start | bytes 393224 | tf_op jit(solution)/shard_map/ppermute | solution.py:16
  202.1 33.5 %copy-start.16 = (bf16[512,128]{1,0:T(8,128)(2,1)}, bf16[512,128]{1,0:T(8,128)(2,1)S(1)}, u32[]{:S(2)}) copy-start(bf16[512,128]{1,0:T(8,128)(2,1)S(1)} %collective-permute-done.30.rest_4_) | copy-start | bytes 393220
  202.1 6.3 %collective-permute-start.31 = (bf16[512,128]{1,0:T(8,128)(2,1)S(1)}, bf16[512,128]{1,0:T(8,128)(2,1)S(1)}, u32[]{:S(2)}, u32[]{:S(2)}) collective-permute-start(bf16[512,128]{1,0:T(8,128)(2,1)S(1)} %collective-permute-done.30.rest_4_), channel_id=1, source_target_pairs={{1,0},{0,1},{3,2},{2,3},{5,4},{4,5},{7,6},{6,7},{9,8},{8,9},{11,10... | collective-permute-start | bytes 393224 | tf_op jit(solution)/shard_map/ppermute | solution.py:16
  202.2 33.4 %copy-start.17 = (bf16[512,128]{1,0:T(8,128)(2,1)}, bf16[512,128]{1,0:T(8,128)(2,1)S(1)}, u32[]{:S(2)}) copy-start(bf16[512,128]{1,0:T(8,128)(2,1)S(1)} %collective-permute-done.28.rest_2_) | copy-start | bytes 393220
  202.2 33.4 %collective-permute-start.29 = (bf16[512,128]{1,0:T(8,128)(2,1)S(1)}, bf16[512,128]{1,0:T(8,128)(2,1)S(1)}, u32[]{:S(2)}, u32[]{:S(2)}) collective-permute-start(bf16[512,128]{1,0:T(8,128)(2,1)S(1)} %collective-permute-done.28.rest_2_), channel_id=1, source_target_pairs={{1,0},{0,1},{3,2},{2,3},{5,4},{4,5},{7,6},{6,7},{9,8},{8,9},{11,10... | collective-permute-start | bytes 393224 | tf_op jit(solution)/shard_map/ppermute | solution.py:16
  204.1 40.7 %collective-permute-start.37 = (bf16[256,256]{1,0:T(8,128)(2,1)S(1)}, bf16[256,256]{1,0:T(8,128)(2,1)S(1)}, u32[]{:S(2)}, u32[]{:S(2)}) collective-permute-start(bf16[256,256]{1,0:T(8,128)(2,1)S(1)} %add_convert_fusion.2), channel_id=1, source_target_pairs={{12,0},{0,4},{4,8},{8,12},{13,1},{1,5},{5,9},{9,13},{14,2},{2,6},{... | collective-permute-start | bytes 393224 | tf_op jit(solution)/shard_map/ppermute | solution.py:16
  205.2 39.7 %collective-permute-start.36 = (bf16[256,256]{1,0:T(8,128)(2,1)S(1)}, bf16[256,256]{1,0:T(8,128)(2,1)S(1)}, u32[]{:S(2)}, u32[]{:S(2)}) collective-permute-start(bf16[256,256]{1,0:T(8,128)(2,1)S(1)} %add_convert_fusion.2), channel_id=1, source_target_pairs={{8,0},{12,4},{0,8},{4,12},{9,1},{13,5},{1,9},{5,13},{10,2},{14,6},... | collective-permute-start | bytes 393224 | tf_op jit(solution)/shard_map/ppermute | solution.py:16
  206.3 29.3 %copy-start.19 = (bf16[512,128]{1,0:T(8,128)(2,1)}, bf16[512,128]{1,0:T(8,128)(2,1)S(1)}, u32[]{:S(2)}) copy-start(bf16[512,128]{1,0:T(8,128)(2,1)S(1)} %collective-permute-done.33.rest_7_) | copy-start | bytes 393220
  206.3 38.6 %collective-permute-start.35 = (bf16[256,256]{1,0:T(8,128)(2,1)S(1)}, bf16[256,256]{1,0:T(8,128)(2,1)S(1)}, u32[]{:S(2)}, u32[]{:S(2)}) collective-permute-start(bf16[256,256]{1,0:T(8,128)(2,1)S(1)} %add_convert_fusion.2), channel_id=1, source_target_pairs={{4,0},{8,4},{12,8},{0,12},{5,1},{9,5},{13,9},{1,13},{6,2},{10,6},{... | collective-permute-start | bytes 393224 | tf_op jit(solution)/shard_map/ppermute | solution.py:16
  208.4 27.2 %copy-start.20 = (bf16[512,128]{1,0:T(8,128)(2,1)}, bf16[512,128]{1,0:T(8,128)(2,1)S(1)}, u32[]{:S(2)}) copy-start(bf16[512,128]{1,0:T(8,128)(2,1)S(1)} %collective-permute-done.31.rest_5_) | copy-start | bytes 393220
  235.5 11.8 %collective-permute-start.39 = (bf16[768,256]{1,0:T(8,128)(2,1)}, bf16[768,256]{1,0:T(8,128)(2,1)S(1)}, u32[]{:S(2)}, u32[]{:S(2)}) collective-permute-start(bf16[768,256]{1,0:T(8,128)(2,1)} %get-tuple-element.115.refs_1_), channel_id=1, source_target_pairs={{1,0},{0,1},{3,2},{2,3},{5,4},{4,5},{7,6},{6,7},{9,8},{8,9},{11,10... | collective-permute-start | bytes 1179656 | tf_op jit(solution)/shard_map/ppermute | solution.py:16
  244.4 2.8 %collective-permute-start.38 = (bf16[512,256]{1,0:T(8,128)(2,1)S(1)}, bf16[512,256]{1,0:T(8,128)(2,1)S(1)}, u32[]{:S(2)}, u32[]{:S(2)}) collective-permute-start(bf16[512,256]{1,0:T(8,128)(2,1)S(1)} %copy-done.2), channel_id=1, source_target_pairs={{1,0},{0,1},{3,2},{2,3},{5,4},{4,5},{7,6},{6,7},{9,8},{8,9},{11,10... | collective-permute-start | bytes 786440 | tf_op jit(solution)/shard_map/ppermute | solution.py:16
  244.8 2.4 collective-permute-start.40
  (23 other events, 129.0 us)
Sparse Core Ops, SparseCore 0:
  178.4 57.0 all-reduce.2

commit v3 on v2

v3 whole, which is shorter than its diff:
```python
import functools

import jax
import jax.numpy as jnp
from jax import lax
from jax.experimental import pallas as pl
from jax.experimental.pallas import tpu as pltpu
from jax.sharding import PartitionSpec as P

F32, BF16 = jnp.float32, jnp.bfloat16
FACE_AXES = ("chan", "pipe")


def shifted(block, axis, distance):
    count = lax.axis_size(axis)
    return lax.ppermute(block, axis, [((i + distance) % count, i) for i in range(count)])


def dot_plain(left, right):
    return jnp.dot(left, right, preferred_element_type=F32)


def dot_back(left, right):
    return lax.dot_general(left, right, (((1,), (1,)), ((), ())), preferred_element_type=F32)


def dot_left(left, right):
    return lax.dot_general(left, right, (((0,), (0,)), ((), ())), preferred_element_type=F32)


def slope_of(values, sigmoid_v):
    return sigmoid_v * (1.0 + values * (1.0 - sigmoid_v))


def one_hot(rows, ids):
    return jnp.where(rows == ids, 1.0, 0.0).astype(BF16)


def pick(values, index, width):
    out = values[:, :width]
    for j in range(1, values.shape[1] // width):
        out = jnp.where(index == j, values[:, j * width : (j + 1) * width], out)
    return out


def in_order(first, mine, other):
    return jnp.where(first, mine, other), jnp.where(first, other, mine)


def widen(parts):
    chan, first = lax.axis_index("chan"), lax.axis_index("pipe") == 0
    count = len(parts) // 2
    pairs = [
        jnp.concatenate(in_order(first, parts[2 * j][...], parts[2 * j + 1][...]), axis=1)
        for j in range(count)
    ]
    out = []
    for place in range(count):
        block = pairs[0]
        for j in range(1, count):
            block = jnp.where(lax.rem(chan + j, count) == place, pairs[j], block)
        out.append(block)
    return jnp.concatenate(out, axis=1)


def own_quarter():
    return lax.axis_index("chan") * lax.axis_size("pipe") + lax.axis_index("pipe")


def run(body, args, outs, scratch=(), flops=0, vmem=17, hbm=()):
    args = [pltpu.with_memory_space_constraint(a, pltpu.VMEM) for a in args]
    return pl.pallas_call(
        body,
        out_shape=[
            jax.ShapeDtypeStruct(s, d) if i in hbm else pltpu.VMEM(s, d)
            for i, (s, d) in enumerate(outs)
        ],
        in_specs=[pl.BlockSpec(memory_space=pltpu.VMEM)] * len(args),
        out_specs=[pl.BlockSpec(memory_space=pltpu.VMEM)] * len(outs),
        scratch_shapes=list(scratch),
        compiler_params=pltpu.CompilerParams(vmem_limit_bytes=vmem * 1024 * 1024),
        cost_estimate=pl.CostEstimate(flops=flops, bytes_accessed=0, transcendentals=0),
    )(*args)


def rows_at(index, size):
    return pl.ds(pl.multiple_of(index * size, size), size)


def table_rows(mesh_rows, face_ids, node_ids):
    count = lax.axis_size("space")
    turned = face_ids - lax.axis_index("space")
    return jnp.where(turned < 0, turned + count, turned) * mesh_rows + node_ids


def sum_by_node(mesh_rows, face_ids, node_ids, values, keep, give):
    mesh_all, width = keep.shape
    grid_rows = values.shape[0]
    size = 512
    first = lax.axis_index("pipe") == 0
    target = table_rows(mesh_rows, face_ids[...], node_ids[...])

    def step(i, carry):
        ids = lax.broadcasted_iota(jnp.int32, (size, grid_rows), 0) + i * size
        total = dot_plain(one_hot(ids, target), values[...])
        mine, other = in_order(first, total[:, :width], total[:, width:])
        keep[rows_at(i, size), :] = mine.astype(BF16)
        give[rows_at(i, size), :] = other.astype(BF16)
        return carry

    lax.fori_loop(0, mesh_all // size, step, 0)


def encode_body(mesh_rows, x, w, face_ids, node_ids, keep, give, enc):
    size = 512
    columns = pick(w[...], lax.axis_index("chan"), enc.shape[1])

    def step(i, carry):
        z = dot_plain(x[rows_at(i, size), :], columns)
        enc[rows_at(i, size), :] = (z * jax.nn.sigmoid(z)).astype(BF16)
        return carry

    lax.fori_loop(0, x.shape[0] // size, step, 0)
    sum_by_node(mesh_rows, face_ids, node_ids, enc, keep, give)


def join_body(keep, got, *outs):
    rows = outs[0].shape[0]
    for k, out in enumerate(outs):
        at = slice(k * rows, (k + 1) * rows)
        out[...] = (keep[at, :].astype(F32) + got[at, :].astype(F32)).astype(BF16)


def add_all(parts):
    total = parts[0][...].astype(F32)
    for ref in parts[1:]:
        total = total + ref[...].astype(F32)
    return total


def add_body(*refs):
    refs[-1][...] = add_all(refs[:-1]).astype(refs[-1].dtype)


def state_body(mix_scale, mesh, *refs):
    own = pick(mesh[...], lax.axis_index("pipe"), refs[-1].shape[1]).astype(F32)
    refs[-1][...] = (own + mix_scale * add_all(refs[:-1])).astype(BF16)


def project(layer, state_b, w_send, w_recv, send_p, recv_p):
    width, quarter = send_p.shape[1], own_quarter()
    send_p[...] = dot_plain(state_b, pick(w_send[layer], quarter, width)).astype(BF16)
    recv_p[...] = dot_plain(state_b, pick(w_recv[layer], quarter, width))


def first_body(w_send, w_recv, *refs):
    state_0, send_p, recv_p = refs[-3:]
    wide = widen(refs[:-3])
    state_0[...] = wide
    project(0, wide, w_send, w_recv, send_p, recv_p)


def next_body(state, w_node, w_send, w_recv, *refs):
    agg_wide, new_state, send_p, recv_p = refs[-4:]
    wide = widen(refs[:-4])
    agg_wide[...] = wide
    total = state[...].astype(F32) + dot_plain(wide, w_node[0])
    new_state[...] = total
    project(1, total.astype(BF16), w_send, w_recv, send_p, recv_p)


def edge_body(below, own, above, recv_p, spot, agg, slope, halo):
    mesh_rows, width = own.shape
    middle, half = mesh_rows // 2, 3 * mesh_rows // 2
    halo[:mesh_rows, :width] = below[...]
    halo[mesh_rows:, :width] = own[:middle, :]
    halo[:middle, width:] = own[middle:, :]
    halo[middle:, width:] = above[...]
    ids = lax.broadcasted_iota(jnp.int32, (mesh_rows, half), 1)
    count = slope.shape[0]
    total = jnp.zeros(agg.shape, F32)
    for k in range(count):
        place = spot[:, k : k + 1]
        right = place >= half
        both = dot_plain(one_hot(ids, jnp.where(right, place - half, place)), halo[...])
        pre = jnp.where(right, both[:, width:], both[:, :width]) + recv_p[...]
        sigmoid_v = jax.nn.sigmoid(pre)
        total = total + pre * sigmoid_v
        slope[k] = slope_of(pre, sigmoid_v).astype(BF16)
    agg[...] = (total / count).astype(BF16)


def edge_back(grad_b, w_node, slope, spot, spot_row, recv_grad, below, own, above, back):
    mesh_rows, width = recv_grad.shape
    middle, half = mesh_rows // 2, 3 * mesh_rows // 2
    count = slope.shape[0]
    back_agg = dot_back(grad_b, w_node[rows_at(own_quarter(), width), :]) / count
    total = jnp.zeros(recv_grad.shape, F32)
    for k in range(count):
        term = back_agg * slope[k].astype(F32)
        total = total + term
        right = spot[:, k : k + 1] >= half
        rows = slice(k * mesh_rows, (k + 1) * mesh_rows)
        back[rows, :width] = jnp.where(right, 0.0, term).astype(BF16)
        back[rows, width:] = jnp.where(right, term, 0.0).astype(BF16)
    recv_grad[...] = total.astype(BF16)
    place = spot_row[...]
    place = jnp.where(place >= half, place - half, place)
    ids = lax.broadcasted_iota(jnp.int32, (half, count * mesh_rows), 0)
    spread = dot_plain(one_hot(ids, place), back[...])
    below[...] = spread[:mesh_rows, :width].astype(BF16)
    own[:middle, :] = spread[mesh_rows:, :width]
    own[middle:, :] = spread[:middle, width:]
    above[...] = spread[middle:, width:].astype(BF16)


def turn_body(count, state, w_node, w_dec, slope, spot, spot_row, *refs):
    agg, back_dec = refs[:count], refs[count : 2 * count]
    agg_wide, last_b, dec_part, dec_grad, grad = refs[2 * count : 2 * count + 5]
    wide = widen(agg)
    agg_wide[...] = wide
    last = (state[...] + dot_plain(wide, w_node[1])).astype(BF16)
    last_b[...] = last
    z_dec = dot_plain(last, w_dec[...])
    sigmoid_v = jax.nn.sigmoid(z_dec)
    dec_part[...] = pick(z_dec * sigmoid_v, own_quarter(), dec_part.shape[1]).astype(BF16)
    down = (widen(back_dec).astype(F32) * slope_of(z_dec, sigmoid_v)).astype(BF16)
    dec_grad[...] = down
    total = dot_back(down, w_dec[...])
    grad[...] = total
    edge_back(total.astype(BF16), w_node.at[1], slope, spot, spot_row, *refs[2 * count + 5 :])


def through(layer, grad, w_send, w_recv, send_parts, recv_parts, send_wide, recv_wide):
    send, recv = widen(send_parts), widen(recv_parts)
    send_wide[...] = send
    recv_wide[...] = recv
    return grad[...] + dot_back(send, w_send[layer]) + dot_back(recv, w_recv[layer])


def back_body(count, grad, w_send, w_recv, w_node, slope, spot, spot_row, *refs):
    send_parts, recv_parts = refs[:count], refs[count : 2 * count]
    send_wide, recv_wide, new_grad = refs[2 * count : 2 * count + 3]
    total = through(1, grad, w_send, w_recv, send_parts, recv_parts, send_wide, recv_wide)
    new_grad[...] = total
    edge_back(total.astype(BF16), w_node.at[0], slope, spot, spot_row, *refs[2 * count + 3 :])


def last_body(count, mix_scale, grad, w_send, w_recv, *refs):
    send_parts, recv_parts = refs[:count], refs[count : 2 * count]
    send_wide, recv_wide, grad_mesh, enc_part, enc_all = refs[2 * count :]
    total = through(0, grad, w_send, w_recv, send_parts, recv_parts, send_wide, recv_wide)
    grad_mesh[...] = pick(total, lax.axis_index("chan"), grad_mesh.shape[1])
    scaled = (mix_scale * total).astype(BF16)
    enc_part[...] = pick(scaled, own_quarter(), enc_part.shape[1])
    enc_all[...] = scaled


def put_pair(table, row, column, mine, other):
    rows, width = mine.shape
    low, high = in_order(lax.axis_index("pipe") == 0, mine[...], other[...])
    table[row : row + rows, column : column + width] = low
    table[row : row + rows, column + width : column + 2 * width] = high


def node_values(target, at, table):
    ids = lax.broadcasted_iota(jnp.int32, (table.shape[0], at.size), 0)
    return dot_left(one_hot(ids, target[:, at]), table[...])


def mixed_body(count, x, w, face_ids, node_ids, *refs):
    mine, other = refs[:count], refs[count : 2 * count]
    mixed, slope, table, target = refs[2 * count :]
    mesh_rows = mine[0].shape[0]
    for k in range(count):
        put_pair(table, k * mesh_rows, 0, mine[k], other[k])
    target[...] = table_rows(mesh_rows, face_ids[...], node_ids[...])
    size = 512
    chan = lax.axis_index("chan")

    def step(i, carry):
        at = rows_at(i, size)
        got = node_values(target, at, table)
        rows = x[at, :]
        mixed[at, :] = (pick(rows, chan, mixed.shape[1]).astype(F32) + got).astype(BF16)
        z = dot_plain(rows, w[...])
        slope[at, :] = slope_of(z, jax.nn.sigmoid(z)).astype(BF16)
        return carry

    lax.fori_loop(0, x.shape[0] // size, step, 0)


def enc_own_body(count, x, face_ids, node_ids, slope, *refs):
    mine, other = refs[:count], refs[count : 2 * count]
    enc_grad, grad_keep, grad_give, table, target, total = refs[2 * count :]
    mesh_rows = mine[0].shape[0]
    for k in range(count):
        put_pair(table, k * mesh_rows, 0, mine[k], other[k])
    target[...] = table_rows(mesh_rows, face_ids[...], node_ids[...])
    size = 512
    chan, pipe = lax.axis_index("chan"), lax.axis_index("pipe")
    total[...] = jnp.zeros(total.shape, F32)

    def step(i, carry):
        at = rows_at(i, size)
        own = pick(slope[at, :], chan, enc_grad.shape[1]).astype(F32)
        down = (node_values(target, at, table) * own).astype(BF16)
        enc_grad[at, :] = down
        total[...] += dot_left(x[at, :], down)
        return carry

    lax.fori_loop(0, x.shape[0] // size, step, 0)
    half = grad_keep.shape[0]
    grad_keep[...] = total[rows_at(pipe, half), :]
    grad_give[...] = total[rows_at(1 - pipe, half), :].astype(BF16)


def enc_other_body(faces, count, face_ids, node_ids, cotangent, enc_grad, enc_all, slope, w, *refs):
    blocks = refs[:-3]
    grad_grid, table, target = refs[-3:]
    grid_rows, narrow = cotangent.shape
    mesh_rows = enc_all.shape[0]
    chan = lax.axis_index("chan")
    for j in range(count):
        other = lax.rem(chan + 1 + j, count + 1)
        columns = slice(j * narrow, (j + 1) * narrow)
        table[:mesh_rows, columns] = pick(enc_all[...], other, narrow)
        for k in range(1, faces):
            mine, sibling = blocks[2 * (j * (faces - 1) + k - 1) :][:2]
            put_pair(table, k * mesh_rows, j * narrow, mine, sibling)
    target[...] = table_rows(mesh_rows, face_ids[...], node_ids[...])
    size = 512
    w_rows = w[rows_at(chan, narrow), :]
    own_block = pick(w_rows, chan, narrow)

    def step(i, carry):
        at = rows_at(i, size)
        got = node_values(target, at, table)
        total = cotangent[at, :].astype(F32) + dot_back(enc_grad[at, :], own_block)
        for j in range(count):
            other = lax.rem(chan + 1 + j, count + 1)
            part = got[:, j * narrow : (j + 1) * narrow]
            down = (part * pick(slope[at, :], other, narrow).astype(F32)).astype(BF16)
            total = total + dot_back(down, pick(w_rows, other, narrow))
        grad_grid[at, :] = total.astype(BF16)
        return carry

    lax.fori_loop(0, grid_rows // size, step, 0)


def weight_body(kinds, count, *refs):
    outs, table = refs[-count - 1 : -1], refs[-1]
    rows = table.shape[0] // len(kinds)
    narrow = table.shape[1]
    chan, pipe, face = (lax.axis_index(a) for a in ("chan", "pipe", "space"))
    for i, (left, right) in enumerate(kinds):
        one = pick(refs[left][...].astype(BF16), pipe, rows)
        two = pick(refs[right][...].astype(BF16), chan, narrow)
        table[i * rows : (i + 1) * rows, :] = dot_left(one, two).astype(BF16)
    size = outs[0].shape[0]
    for k, out in enumerate(outs):
        out[...] = table[rows_at(lax.rem(face + k, count), size), :]


def write_body(places, count, *refs):
    groups = len(places)
    outs, table = refs[2 * groups * count : -1], refs[-1]
    pipe, face = lax.axis_index("pipe"), lax.axis_index("space")
    for side in range(2):
        for i, items in enumerate(places):
            pieces = refs[(side * groups + i) * count :][:count]
            size = pieces[0].shape[0]
            for k in range(count):
                table[rows_at(lax.rem(face + k, count), size), :] = pieces[k][...]
            rows = size * count // len(items)
            half = pipe if side == 0 else 1 - pipe
            for j, (out, layer) in enumerate(items):
                ref = outs[out] if layer is None else outs[out].at[layer]
                ref[rows_at(half, rows), :] = table[j * rows : (j + 1) * rows, :].astype(F32)


def halves_body(mine, other, out):
    rows = mine.shape[0]
    pipe = lax.axis_index("pipe")
    out[rows_at(pipe, rows), :] = mine[...]
    out[rows_at(1 - pipe, rows), :] = other[...]


def per_device(
    grid_latent, g2m_face, g2m_node, mesh_latent, mesh_links,
    w_enc, w_send, w_recv, w_node, w_dec, cotangent,
):
    tie = lax.optimization_barrier
    faces = lax.axis_size("space")
    pipe_count = lax.axis_size("pipe")
    chan_count = lax.axis_size("chan")
    grid_rows, wide = grid_latent.shape
    mesh_rows, narrow = mesh_latent.shape
    part = narrow // pipe_count
    mesh_all = faces * mesh_rows
    mix_scale = (mesh_rows / (grid_rows * pipe_count)) ** 0.5
    nbrs = mesh_links.shape[1] * pipe_count
    face = lax.axis_index("space")
    ids = (g2m_face.reshape(1, grid_rows), g2m_node.reshape(1, grid_rows))
    grid_vmem = 14 + mesh_all // 512

    def on(body, *fixed):
        return functools.partial(body, *fixed)

    def over_faces(blocks, step):
        return [shifted(b, "space", step * k) for k, b in enumerate(blocks) if k > 0]

    def face_parts(block):
        out = []
        for j in range(chan_count):
            mine = shifted(block, "chan", j) if j else block
            out += [mine, shifted(mine, "pipe", 1)]
        return out

    def add(parts, kind=BF16):
        return run(add_body, parts, [(parts[0].shape, kind)])[0]

    block = (mesh_rows, part)
    full = (mesh_rows, wide)
    half = wide // pipe_count
    sums = [((mesh_all, part), BF16)] * 2
    sum_flops = 2 * mesh_all * grid_rows * narrow
    edge_flops = 6 * mesh_rows * mesh_rows * nbrs * part
    parts_count = 2 * chan_count

    def join(keep, give):
        return run(join_body, (keep, shifted(give, "pipe", 1)), [(block, BF16)] * faces)

    keep, give = run(
        on(encode_body, mesh_rows), (grid_latent, w_enc, *ids), sums,
        scratch=[pltpu.VMEM((grid_rows, narrow), BF16)],
        flops=sum_flops + 2 * grid_rows * wide * narrow, vmem=grid_vmem,
    )
    *blocks, cotangent_late, links = tie((*join(keep, give), cotangent, mesh_links))
    state_part, = run(
        on(state_body, mix_scale), (mesh_latent, blocks[0], *over_faces(blocks, -1)),
        [(block, BF16)],
    )

    links = jnp.concatenate([links, shifted(links, "pipe", 1)], axis=1)
    offset = (links // mesh_rows - face) % faces
    local = links % mesh_rows
    spot = jnp.where(
        offset == 0, mesh_rows + local, jnp.where(offset == 1, 2 * mesh_rows + local, local)
    )
    spot_row = spot.T.reshape(1, nbrs * mesh_rows)
    keep, give = run(
        on(sum_by_node, mesh_rows), (*ids, cotangent_late), sums, flops=sum_flops, vmem=grid_vmem
    )
    keep, give, spot, spot_row, state_part = tie((keep, give, spot, spot_row, state_part))

    def edges(send_p, recv_p, below, above):
        return run(
            edge_body, (below, send_p, above, recv_p, spot),
            [(block, BF16), ((nbrs,) + block, BF16)],
            scratch=[pltpu.VMEM((3 * mesh_rows // 2, 2 * part), BF16)], flops=edge_flops,
        )

    def neighbours(send_p):
        return shifted(send_p, "space", -1), shifted(send_p, "space", 1)

    state_0, send_p, recv_p = run(
        first_body, (w_send, w_recv, *face_parts(state_part)),
        [(full, BF16), (block, BF16), (block, F32)], flops=4 * mesh_rows * wide * part,
    )
    below, above, *back_blocks = tie((*neighbours(send_p), *join(keep, give)))
    back_got = over_faces(back_blocks, -1)
    agg, slope_0 = edges(send_p, recv_p, below, above)
    agg_0, state_1, send_p, recv_p = run(
        next_body, (state_0, w_node, w_send, w_recv, *face_parts(agg)),
        [(full, BF16), (full, F32), (block, BF16), (block, F32)],
        flops=2 * mesh_rows * wide * wide,
    )
    send_p, *back_got = tie((send_p, *back_got))
    below, above = neighbours(send_p)
    back_parts = face_parts(add([back_blocks[0], *back_got]))
    below, above, *back_parts = tie((below, above, *back_parts))
    agg, slope_1 = edges(send_p, recv_p, below, above)
    back_outs = [(full, F32), (block, BF16), (block, BF16), (block, F32), (block, BF16)]
    back_scratch = [pltpu.VMEM((nbrs * mesh_rows, 2 * part), BF16)]
    agg_1, last_b, dec_part, dec_grad, grad_2, recv_grad, below, own, above = run(
        on(turn_body, parts_count),
        (state_1, w_node, w_dec, slope_1, spot, spot_row, *face_parts(agg), *back_parts),
        [(full, BF16), (full, BF16), (block, BF16), (full, BF16)] + back_outs,
        scratch=back_scratch, flops=edge_flops + 6 * mesh_rows * wide * wide,
    )

    def weights(args, kinds):
        rows = half * len(kinds)
        return run(
            on(weight_body, kinds, faces), args, [((rows // faces, narrow), BF16)] * faces,
            scratch=[pltpu.VMEM((rows, narrow), BF16)], flops=2 * mesh_rows * rows * narrow,
        )

    def from_owners(piece):
        return [piece] + [shifted(piece, "space", k) for k in range(1, faces)]

    recv_parts = face_parts(recv_grad)
    pieces_a = weights((last_b, dec_grad, agg_1, grad_2), ((0, 1), (2, 3)))
    below, above = shifted(below, "space", 1), shifted(above, "space", -1)
    below, above, dec_part, *rest = tie((below, above, dec_part, *pieces_a, *recv_parts))
    pieces_a, recv_parts = rest[:faces], rest[faces:]
    got_a = over_faces(pieces_a, -1)
    dec_mine = from_owners(dec_part)
    outs = run(
        on(back_body, parts_count),
        (grad_2, w_send, w_recv, w_node, slope_0, spot, spot_row)
        + (*face_parts(add([own, below, above])), *recv_parts),
        [(full, BF16), (full, BF16)] + back_outs,
        scratch=back_scratch, flops=edge_flops + 4 * mesh_rows * wide * wide,
    )
    outs = tie((*outs, *got_a, *dec_mine[1:]))
    send_1, recv_1, grad_1, recv_grad, below, own, above = outs[:7]
    got_a, dec_mine = outs[7 : 6 + faces], [dec_mine[0], *outs[6 + faces :]]

    recv_parts = face_parts(recv_grad)
    pieces_b = weights((state_1, send_1, recv_1, agg_0, grad_1), ((0, 1), (0, 2), (3, 4)))
    sum_a = add([pieces_a[0], *got_a])
    below, above = shifted(below, "space", 1), shifted(above, "space", -1)
    below, above, sum_a, *rest = tie((below, above, sum_a, *pieces_b, *recv_parts))
    pieces_b, recv_parts = rest[:faces], rest[faces:]
    all_a = from_owners(sum_a)
    got_b = over_faces(pieces_b, -1)
    outs = run(
        on(last_body, parts_count, mix_scale),
        (grad_1, w_send, w_recv, *face_parts(add([own, below, above])), *recv_parts),
        [(full, BF16), (full, BF16), ((mesh_rows, narrow), F32), (block, BF16), (full, BF16)],
        flops=4 * mesh_rows * wide * wide,
    )
    outs = tie((*outs, *all_a[1:], *got_b))
    send_0, recv_0, grad_mesh, enc_part, enc_all = outs[:5]
    all_a, got_b = [all_a[0], *outs[5 : 4 + faces]], outs[4 + faces :]

    enc_mine = from_owners(enc_part)
    pieces_c = weights((state_0, send_0, recv_0), ((0, 1), (0, 2)))
    sum_b = add([pieces_b[0], *got_b])
    table = [pltpu.VMEM((mesh_all, narrow), BF16), pltpu.VMEM((1, grid_rows), jnp.int32)]
    mixed, slope_enc = run(
        on(mixed_body, faces),
        (grid_latent, w_enc, *ids, *dec_mine, *(shifted(b, "pipe", 1) for b in dec_mine)),
        [((grid_rows, narrow), BF16), ((grid_rows, wide), BF16)], scratch=table,
        flops=sum_flops + 2 * grid_rows * wide * wide, vmem=grid_vmem,
    )
    outs = tie((*enc_mine[1:], slope_enc, sum_b, *pieces_c))
    enc_mine = [enc_mine[0], *outs[: faces - 1]]
    slope_enc, sum_b, *pieces_c = outs[faces - 1 :]
    got_c = over_faces(pieces_c, -1)
    all_b = from_owners(sum_b)
    enc_grad, grad_keep, grad_give = run(
        on(enc_own_body, faces),
        (grid_latent, *ids, slope_enc, *enc_mine, *(shifted(b, "pipe", 1) for b in enc_mine)),
        [((grid_rows, narrow), BF16), ((half, narrow), F32), ((half, narrow), BF16)],
        scratch=table + [pltpu.VMEM((wide, narrow), F32)],
        flops=sum_flops + 2 * grid_rows * wide * narrow, vmem=grid_vmem,
    )
    outs = tie((enc_grad, grad_keep, grad_give, *got_c))
    enc_grad, grad_keep, grad_give, *got_c = outs
    half_sum, = run(
        add_body, (grad_keep, shifted(grad_give, "pipe", 1)), [((half, narrow), BF16)]
    )
    total = add(from_owners(half_sum), F32)
    grad_w_enc, = run(
        halves_body, (total, shifted(total, "pipe", 1)), [((wide, narrow), F32)], hbm=(0,)
    )
    all_c = from_owners(add([pieces_c[0], *got_c]))

    pieces = []
    for j in range(1, chan_count):
        for k in range(1, faces):
            piece = shifted(enc_mine[k], "chan", j)
            pieces += [piece, shifted(piece, "pipe", 1)]
    others = chan_count - 1
    grad_grid, = run(
        on(enc_other_body, faces, others),
        (*ids, cotangent, enc_grad, enc_all, slope_enc, w_enc, *pieces),
        [((grid_rows, narrow), BF16)],
        scratch=[pltpu.VMEM((mesh_all, narrow * others), BF16), table[1]],
        flops=(sum_flops + 4 * grid_rows * narrow * narrow) * others, vmem=grid_vmem + 4, hbm=(0,),
    )
    groups = (*all_a, *all_b, *all_c)
    layer_shape = ((w_send.shape[0], wide, narrow), F32)
    places = (((3, None), (2, 1)), ((0, 1), (1, 1), (2, 0)), ((0, 0), (1, 0)))
    grad_w_send, grad_w_recv, grad_w_node, grad_w_dec = run(
        on(write_body, places, faces), (*groups, *(shifted(b, "pipe", 1) for b in groups)),
        [layer_shape] * 3 + [((wide, narrow), F32)], hbm=(0, 1, 2, 3),
        scratch=[pltpu.VMEM((3 * half, narrow), BF16)],
    )
    return (
        mixed,
        grad_grid,
        grad_mesh,
        grad_w_enc,
        grad_w_send,
        grad_w_recv,
        grad_w_node,
        grad_w_dec,
    )


def solution(mesh):
    nodes = ("groups", "space", "pipe")
    in_specs = (
        P(nodes, None), P(nodes, None), P(nodes), P(("groups", "space"), "chan"),
        P(("groups", "space"), "pipe"), P(), P(), P(), P(), P(), P(nodes, "chan"),
    )
    out_specs = (
        P(nodes, "chan"), P(nodes, "chan"), P(("groups", "space"), "chan"), P("groups", "chan"),
        P("groups", None, "chan"), P("groups", None, "chan"), P("groups", None, "chan"),
        P("groups", "chan"),
    )
    return jax.shard_map(
        per_device, mesh=mesh, in_specs=in_specs, out_specs=out_specs, check_vma=False
    )
```

time: 261 us -> 244 us (0.935)
  waiting for transfers between devices: 36.8 us -> 106 us
  blocking collectives: 65.8 us -> 0 us
  Pallas kernels: 87.5 us -> 39.1 us
  starting transfers between devices: 41.5 us -> 80.8 us
  between operations: 14.4 us -> 1.04 us
  local copies, waits for them, and re-layouts: 6.49 us -> 10.6 us
  other arithmetic: 8.04 us -> 4.82 us
    ppermute x41 -> x96, waiting for transfers between devices: 9.7 us -> 106 us  [shifted(): lax.ppermute(block, axis, [((i + distance) % count, i) for i in range(cou...]
    all_gather x9 -> x0, blocking collectives: 65.8 us -> none  [the longest x8 63.5 us: face_wide(): return lax.all_gather(block, FACE_AXES)]
    pallas_call x16 -> x28, Pallas kernels: 87.5 us -> 39.1 us  [run(): pl.pallas_call(body, out_shape=[jax.ShapeDtypeStruct(s, d) if i in hbm el...]
    ppermute x41 -> x96, starting transfers between devices: 41.5 us -> 80.8 us  [shifted(): lax.ppermute(block, axis, [((i + distance) % count, i) for i in range(cou...]
    psum x1 -> x0, waiting for transfers between devices: 27.1 us -> none  [per_device(): sums_all = lax.psum((sums_a, sums_b, sums_c), 'space')]
    convert_element_type x7 -> x0, other arithmetic: 4.49 us -> none  [the longest x2 2.01 us: senders(): return (own + below.astype(F32) + above.astype(F32)).astype(BF16)]
    unnamed x63 -> x35, local copies, waits for them, and re-layouts: 5.55 us -> 7.35 us
  transfers between devices with their start and end apart: 42 -> 96, of which waited for: 6 -> 36; matrix products, arithmetic and copies ran while one was open for 2% -> 4% of each run, Pallas kernels for 25% -> 11%
where the time goes in v3:
time: 244 us; the launch traced here: 243 us
  waiting for transfers between devices  106 us (43%)
  starting transfers between devices  80.8 us (33%)
  Pallas kernels  39.1 us (16%)
  local copies, waits for them, and re-layouts  10.6 us (4%)
  other arithmetic  4.82 us (2%)
    ppermute x96, waiting for transfers between devices, shifted(): lax.ppermute(block, axis, [((i + distance) % count, i) for i in range(cou...  106 us
    ppermute x96, starting transfers between devices, shifted(): lax.ppermute(block, axis, [((i + distance) % count, i) for i in range(cou...  80.8 us
    pallas_call x28, Pallas kernels, run(): pl.pallas_call(body, out_shape=[jax.ShapeDtypeStruct(s, d) if i in hbm el...  39.1 us
    unnamed x35, local copies, waits for them, and re-layouts  7.35 us
  transfers between devices with their start and end apart: 96, of which 36 were waited for; matrix products, arithmetic and copies ran while one was open for 4% of the time, Pallas kernels for 11%

profile of v3, /device:TPU:0, one launch (start us, length us, event | category | flops | bytes accessed | tf_op | source)
XLA Modules:
  0.0 242.6 jit_solution(11378633975140337234)
XLA Ops:
  4.7 4.1 %shard_map.170 = (bf16[2048,128]{1,0:T(8,128)(2,1)S(1)}, bf16[2048,128]{1,0:T(8,128)(2,1)S(1)}) custom-call(bf16[2048,512]{1,0:T(8,128)(2,1)S(1)} %copy-done.4, bf16[512,512]{1,0:T(8,128)(2,1)S(1)} %copy-done.9, s32[1,2048]{1,0:T(1,128)S(1)} %bitcast.9, s32[1,2048]{1,0:T(1,128)S(1)} %bitcast.14), custom_call_target="tpu_custom_call" | custom-call | flops 2684354560 | tf_op jit(solution)/shard_map/pallas_call | solution.py:72
  12.0 2.7 %collective-permute-start.2 = (bf16[512,128]{1,0:T(8,128)(2,1)}, bf16[512,128]{1,0:T(8,128)(2,1)S(1)}, u32[]{:S(2)}, u32[]{:S(2)}) collective-permute-start(bf16[512,128]{1,0:T(8,128)(2,1)} %get-tuple-element.172), channel_id=1, source_target_pairs={{12,0},{0,4},{4,8},{8,12},{13,1},{1,5},{5,9},{9,13},{14,2},{2,6},{... | collective-permute-start | bytes 393224 | tf_op jit(solution)/shard_map/ppermute | solution.py:16
  14.7 2.6 %collective-permute-start.3 = (bf16[512,128]{1,0:T(8,128)(2,1)}, bf16[512,128]{1,0:T(8,128)(2,1)S(1)}, u32[]{:S(2)}, u32[]{:S(2)}) collective-permute-start(bf16[512,128]{1,0:T(8,128)(2,1)} %get-tuple-element.173), channel_id=1, source_target_pairs={{8,0},{12,4},{0,8},{4,12},{9,1},{13,5},{1,9},{5,13},{10,2},{14,6},... | collective-permute-start | bytes 393224 | tf_op jit(solution)/shard_map/ppermute | solution.py:16
  18.6 2.9 %shard_map.172 = (bf16[2048,128]{1,0:T(8,128)(2,1)S(1)}, bf16[2048,128]{1,0:T(8,128)(2,1)S(1)}) custom-call(s32[1,2048]{1,0:T(1,128)S(1)} %bitcast.10, s32[1,2048]{1,0:T(1,128)S(1)} %bitcast.15, bf16[2048,256]{1,0:T(8,128)(2,1)S(1)} %copy-done.6), custom_call_target="tpu_custom_call" | custom-call | flops 2147483648 | tf_op jit(solution)/shard_map/pallas_call | solution.py:72
  25.3 2.0 fusion.4
  33.1 4.2 %collective-permute-done.6.refs_2_ = bf16[512,128]{1,0:T(8,128)(2,1)S(1)} collective-permute-done((bf16[512,128]{1,0:T(8,128)(2,1)S(1)}, bf16[512,128]{1,0:T(8,128)(2,1)S(1)}, u32[]{:S(2)}, u32[]{:S(2)}) %collective-permute-start.6) | collective-permute-done | bytes 131104 | tf_op jit(solution)/shard_map/ppermute | solution.py:16
  41.3 6.2 %collective-permute-done.9.above = bf16[512,128]{1,0:T(8,128)(2,1)S(1)} collective-permute-done((bf16[512,128]{1,0:T(8,128)(2,1)S(1)}, bf16[512,128]{1,0:T(8,128)(2,1)S(1)}, u32[]{:S(2)}, u32[]{:S(2)}) %collective-permute-start.9) | collective-permute-done | bytes 131104 | tf_op jit(solution)/shard_map/ppermute | solution.py:16
  50.8 3.5 %collective-permute-done.12.refs_2_ = bf16[512,128]{1,0:T(8,128)(2,1)S(1)} collective-permute-done((bf16[512,128]{1,0:T(8,128)(2,1)S(1)}, bf16[512,128]{1,0:T(8,128)(2,1)S(1)}, u32[]{:S(2)}, u32[]{:S(2)}) %collective-permute-start.12) | collective-permute-done | bytes 131104 | tf_op jit(solution)/shard_map/ppermute | solution.py:16
  56.5 2.6 %collective-permute-start.16 = (bf16[512,128]{1,0:T(8,128)(2,1)S(1)}, bf16[512,128]{1,0:T(8,128)(2,1)S(1)}, u32[]{:S(2)}, u32[]{:S(2)}) collective-permute-start(bf16[512,128]{1,0:T(8,128)(2,1)S(1)} %get-tuple-element.193), channel_id=1, source_target_pairs={{4,0},{8,4},{12,8},{0,12},{5,1},{9,5},{13,9},{1,13},{6,2},{10,6},{... | collective-permute-start | bytes 393224 | tf_op jit(solution)/shard_map/ppermute | solution.py:16
  59.8 2.8 %collective-permute-done.14.refs_1_ = bf16[512,128]{1,0:T(8,128)(2,1)S(1)} collective-permute-done((bf16[512,128]{1,0:T(8,128)(2,1)S(1)}, bf16[512,128]{1,0:T(8,128)(2,1)S(1)}, u32[]{:S(2)}, u32[]{:S(2)}) %collective-permute-start.14) | collective-permute-done | bytes 131104 | tf_op jit(solution)/shard_map/ppermute | solution.py:16
  62.6 5.2 %collective-permute-done.15.refs_2_ = bf16[512,128]{1,0:T(8,128)(2,1)S(1)} collective-permute-done((bf16[512,128]{1,0:T(8,128)(2,1)S(1)}, bf16[512,128]{1,0:T(8,128)(2,1)S(1)}, u32[]{:S(2)}, u32[]{:S(2)}) %collective-permute-start.15) | collective-permute-done | bytes 131104 | tf_op jit(solution)/shard_map/ppermute | solution.py:16
  69.4 3.6 %collective-permute-start.18 = (bf16[512,128]{1,0:T(8,128)(2,1)S(1)}, bf16[512,128]{1,0:T(8,128)(2,1)S(1)}, u32[]{:S(2)}, u32[]{:S(2)}) collective-permute-start(bf16[512,128]{1,0:T(8,128)(2,1)S(1)} %get-tuple-element.194.own), channel_id=1, source_target_pairs={{4,0},{8,4},{12,8},{0,12},{5,1},{9,5},{13,9},{1,13},{6,2},{10,6},{... | collective-permute-start | bytes 393224 | tf_op jit(solution)/shard_map/ppermute | solution.py:16
  73.2 3.6 %collective-permute-done.18.above = bf16[512,128]{1,0:T(8,128)(2,1)S(1)} collective-permute-done((bf16[512,128]{1,0:T(8,128)(2,1)S(1)}, bf16[512,128]{1,0:T(8,128)(2,1)S(1)}, u32[]{:S(2)}, u32[]{:S(2)}) %collective-permute-start.18) | collective-permute-done | bytes 131104 | tf_op jit(solution)/shard_map/ppermute | solution.py:16
  76.8 3.6 %collective-permute-done.17.below = bf16[512,128]{1,0:T(8,128)(2,1)S(1)} collective-permute-done((bf16[512,128]{1,0:T(8,128)(2,1)S(1)}, bf16[512,128]{1,0:T(8,128)(2,1)S(1)}, u32[]{:S(2)}, u32[]{:S(2)}) %collective-permute-start.17) | collective-permute-done | bytes 131104 | tf_op jit(solution)/shard_map/ppermute | solution.py:16
  82.8 4.4 %collective-permute-done.23.refs_2_ = bf16[512,128]{1,0:T(8,128)(2,1)S(1)} collective-permute-done((bf16[512,128]{1,0:T(8,128)(2,1)S(1)}, bf16[512,128]{1,0:T(8,128)(2,1)S(1)}, u32[]{:S(2)}, u32[]{:S(2)}) %collective-permute-start.23) | collective-permute-done | bytes 131104 | tf_op jit(solution)/shard_map/ppermute | solution.py:16
  88.6 3.4 %shard_map.180 = (bf16[512,512]{1,0:T(8,128)(2,1)S(1)}, bf16[512,512]{1,0:T(8,128)(2,1)S(1)}, bf16[512,128]{1,0:T(8,128)(2,1)S(1)}, bf16[512,512]{1,0:T(8,128)(2...) custom-call(f32[512,512]{1,0:T(8,128)S(1)} %get-tuple-element.189.st, ...), custom_call_target="tpu_custom_call" | custom-call | flops 2013265920 | tf_op jit(solution)/shard_map/pallas_call | solution.py:72
  94.7 3.0 %collective-permute-done.28.refs_6_ = bf16[512,128]{1,0:T(8,128)(2,1)S(1)} collective-permute-done((bf16[512,128]{1,0:T(8,128)(2,1)S(1)}, bf16[512,128]{1,0:T(8,128)(2,1)S(1)}, u32[]{:S(2)}, u32[]{:S(2)}) %collective-permute-start.28) | collective-permute-done | bytes 131104 | tf_op jit(solution)/shard_map/ppermute | solution.py:16
  98.6 3.9 %collective-permute-done.26.refs_2_ = bf16[512,128]{1,0:T(8,128)(2,1)S(1)} collective-permute-done((bf16[512,128]{1,0:T(8,128)(2,1)S(1)}, bf16[512,128]{1,0:T(8,128)(2,1)S(1)}, u32[]{:S(2)}, u32[]{:S(2)}) %collective-permute-start.26) | collective-permute-done | bytes 131104 | tf_op jit(solution)/shard_map/ppermute | solution.py:16
  104.1 3.6 %collective-permute-done.31.refs_2_ = bf16[512,128]{1,0:T(8,128)(2,1)S(1)} collective-permute-done((bf16[512,128]{1,0:T(8,128)(2,1)S(1)}, bf16[512,128]{1,0:T(8,128)(2,1)S(1)}, u32[]{:S(2)}, u32[]{:S(2)}) %collective-permute-start.31) | collective-permute-done | bytes 131104 | tf_op jit(solution)/shard_map/ppermute | solution.py:16
  109.9 2.2 collective-permute-start.37
  112.1 2.4 collective-permute-done.33.refs_1_
  114.5 4.4 %collective-permute-start.35 = (bf16[128,256]{1,0:T(8,128)(2,1)S(1)}, bf16[128,256]{1,0:T(8,128)(2,1)S(1)}, u32[]{:S(2)}, u32[]{:S(2)}) collective-permute-start(bf16[128,256]{1,0:T(8,128)(2,1)S(1)} %get-tuple-element.239), channel_id=1, source_target_pairs={{4,0},{8,4},{12,8},{0,12},{5,1},{9,5},{13,9},{1,13},{6,2},{10,6},{... | collective-permute-start | bytes 196616 | tf_op jit(solution)/shard_map/ppermute | solution.py:16
  118.9 3.0 %shard_map.183 = (bf16[512,512]{1,0:T(8,128)(2,1)S(1)}, bf16[512,512]{1,0:T(8,128)(2,1)S(1)}, f32[512,512]{1,0:T(8,128)S(1)}, bf16[512,128]{1,0:T(8,128)(2,1)S(1...) custom-call(f32[512,512]{1,0:T(8,128)S(1)} %get-tuple-element.215.refs_3_.grad, ...), custom_call_target="tpu_custom_call" | custom-call | flops 1744830464 | tf_op jit(solution)/shard_map/pallas_call | solution.py:72
  121.9 6.3 %collective-permute-done.34.refs_2_ = bf16[128,256]{1,0:T(8,128)(2,1)S(1)} collective-permute-done((bf16[128,256]{1,0:T(8,128)(2,1)S(1)}, bf16[128,256]{1,0:T(8,128)(2,1)S(1)}, u32[]{:S(2)}, u32[]{:S(2)}) %collective-permute-start.34) | collective-permute-done | bytes 65568 | tf_op jit(solution)/shard_map/ppermute | solution.py:16
  129.8 2.0 collective-permute-start.43
  135.8 3.5 %collective-permute-done.44.refs_2_ = bf16[512,128]{1,0:T(8,128)(2,1)S(1)} collective-permute-done((bf16[512,128]{1,0:T(8,128)(2,1)S(1)}, bf16[512,128]{1,0:T(8,128)(2,1)S(1)}, u32[]{:S(2)}, u32[]{:S(2)}) %collective-permute-start.44) | collective-permute-done | bytes 131104 | tf_op jit(solution)/shard_map/ppermute | solution.py:16
  140.0 4.4 %collective-permute-done.49.refs_2_ = bf16[512,128]{1,0:T(8,128)(2,1)S(1)} collective-permute-done((bf16[512,128]{1,0:T(8,128)(2,1)S(1)}, bf16[512,128]{1,0:T(8,128)(2,1)S(1)}, u32[]{:S(2)}, u32[]{:S(2)}) %collective-permute-start.49) | collective-permute-done | bytes 131104 | tf_op jit(solution)/shard_map/ppermute | solution.py:16
  147.1 2.8 %collective-permute-start.51 = (bf16[128,256]{1,0:T(8,128)(2,1)S(1)}, bf16[128,256]{1,0:T(8,128)(2,1)S(1)}, u32[]{:S(2)}, u32[]{:S(2)}) collective-permute-start(bf16[128,256]{1,0:T(8,128)(2,1)S(1)} %shard_map.185.refs_0_), channel_id=1, source_target_pairs={{4,0},{8,4},{12,8},{0,12},{5,1},{9,5},{13,9},{1,13},{6,2},{10,6},{... | collective-permute-start | bytes 196616 | tf_op jit(solution)/shard_map/ppermute | solution.py:16
  151.0 2.7 %collective-permute-done.52.refs_2_ = bf16[128,256]{1,0:T(8,128)(2,1)S(1)} collective-permute-done((bf16[128,256]{1,0:T(8,128)(2,1)S(1)}, bf16[128,256]{1,0:T(8,128)(2,1)S(1)}, u32[]{:S(2)}, u32[]{:S(2)}) %collective-permute-start.52) | collective-permute-done | bytes 65568 | tf_op jit(solution)/shard_map/ppermute | solution.py:16
  153.7 1.9 collective-permute-start.54
  158.7 2.4 %collective-permute-done.54.refs_1_ = bf16[192,256]{1,0:T(8,128)(2,1)S(1)} collective-permute-done((bf16[192,256]{1,0:T(8,128)(2,1)S(1)}, bf16[192,256]{1,0:T(8,128)(2,1)S(1)}, u32[]{:S(2)}, u32[]{:S(2)}) %collective-permute-start.54) | collective-permute-done | bytes 98336 | tf_op jit(solution)/shard_map/ppermute | solution.py:16
  161.1 3.8 %collective-permute-done.55.refs_2_ = bf16[192,256]{1,0:T(8,128)(2,1)S(1)} collective-permute-done((bf16[192,256]{1,0:T(8,128)(2,1)S(1)}, bf16[192,256]{1,0:T(8,128)(2,1)S(1)}, u32[]{:S(2)}, u32[]{:S(2)}) %collective-permute-start.55) | collective-permute-done | bytes 98336 | tf_op jit(solution)/shard_map/ppermute | solution.py:16
  165.0 2.6 %collective-permute-start.59 = (bf16[512,128]{1,0:T(8,128)(2,1)S(1)}, bf16[512,128]{1,0:T(8,128)(2,1)S(1)}, u32[]{:S(2)}, u32[]{:S(2)}) collective-permute-start(bf16[512,128]{1,0:T(8,128)(2,1)S(1)} %get-tuple-element.275.refs_0_), channel_id=1, source_target_pairs={{12,0},{0,4},{4,8},{8,12},{13,1},{1,5},{5,9},{9,13},{14,2},{2,6},{... | collective-permute-start | bytes 393224 | tf_op jit(solution)/shard_map/ppermute | solution.py:16
  170.4 2.8 %collective-permute-done.59.refs_3_ = bf16[512,128]{1,0:T(8,128)(2,1)S(1)} collective-permute-done((bf16[512,128]{1,0:T(8,128)(2,1)S(1)}, bf16[512,128]{1,0:T(8,128)(2,1)S(1)}, u32[]{:S(2)}, u32[]{:S(2)}) %collective-permute-start.59) | collective-permute-done | bytes 131104 | tf_op jit(solution)/shard_map/ppermute | solution.py:16
  173.2 5.2 %collective-permute-done.58.refs_2_ = bf16[512,128]{1,0:T(8,128)(2,1)S(1)} collective-permute-done((bf16[512,128]{1,0:T(8,128)(2,1)S(1)}, bf16[512,128]{1,0:T(8,128)(2,1)S(1)}, u32[]{:S(2)}, u32[]{:S(2)}) %collective-permute-start.58) | collective-permute-done | bytes 131104 | tf_op jit(solution)/shard_map/ppermute | solution.py:16
  178.9 4.4 %shard_map.184 = (bf16[2048,256]{1,0:T(8,128)(2,1)S(1)}, bf16[2048,512]{1,0:T(8,128)(2,1)S(1)}) custom-call(bf16[2048,512]{1,0:T(8,128)(2,1)S(1)} %copy-done.5, bf16[512,512]{1,0:T(8,128)(2,1)S(1)} %copy-done.10, s32[1,2048]{1,0:T(1,128)S(1)} %bitcast.11, s32[1,2048]{1,0:T(1,128)S(1)} %bitcast.16, bf16[512,128]{1,0:T(8,128)(2,1)S(1)} %get-tuple-element.221.refs_0_, ...), custom_call_target="tpu_custom_call" | custom-call | flops 3221225472 | tf_op jit(solution)/shard_map/pallas_call | solution.py:72
  183.9 2.8 %collective-permute-start.64 = (bf16[128,256]{1,0:T(8,128)(2,1)S(1)}, bf16[128,256]{1,0:T(8,128)(2,1)S(1)}, u32[]{:S(2)}, u32[]{:S(2)}) collective-permute-start(bf16[128,256]{1,0:T(8,128)(2,1)S(1)} %get-tuple-element.294), channel_id=1, source_target_pairs={{12,0},{0,4},{4,8},{8,12},{13,1},{1,5},{5,9},{9,13},{14,2},{2,6},{... | collective-permute-start | bytes 196616 | tf_op jit(solution)/shard_map/ppermute | solution.py:16
  190.0 3.0 %collective-permute-done.65.refs_2_ = bf16[128,256]{1,0:T(8,128)(2,1)S(1)} collective-permute-done((bf16[128,256]{1,0:T(8,128)(2,1)S(1)}, bf16[128,256]{1,0:T(8,128)(2,1)S(1)}, u32[]{:S(2)}, u32[]{:S(2)}) %collective-permute-start.65) | collective-permute-done | bytes 65568 | tf_op jit(solution)/shard_map/ppermute | solution.py:16
  194.6 2.7 %collective-permute-done.66.refs_3_ = bf16[128,256]{1,0:T(8,128)(2,1)S(1)} collective-permute-done((bf16[128,256]{1,0:T(8,128)(2,1)S(1)}, bf16[128,256]{1,0:T(8,128)(2,1)S(1)}, u32[]{:S(2)}, u32[]{:S(2)}) %collective-permute-start.66) | collective-permute-done | bytes 65568 | tf_op jit(solution)/shard_map/ppermute | solution.py:16
  197.3 4.1 %collective-permute-start.79 = (bf16[192,256]{1,0:T(8,128)(2,1)S(1)}, bf16[192,256]{1,0:T(8,128)(2,1)S(1)}, u32[]{:S(2)}, u32[]{:S(2)}) collective-permute-start(bf16[192,256]{1,0:T(8,128)(2,1)S(1)} %shard_map.189.refs_4_), channel_id=1, source_target_pairs={{8,0},{12,4},{0,8},{4,12},{9,1},{13,5},{1,9},{5,13},{10,2},{14,6},... | collective-permute-start | bytes 294920 | tf_op jit(solution)/shard_map/ppermute | solution.py:16
  203.5 5.0 %shard_map.191 = (bf16[2048,256]{1,0:T(8,128)(2,1)S(1)}, f32[256,256]{1,0:T(8,128)S(1)}, bf16[256,256]{1,0:T(8,128)(2,1)S(1)}) custom-call(bf16[2048,512]{1,0:T(8,128)(2,1)S(1)} %copy-done.5, s32[1,2048]{1,0:T(1,128)S(1)} %bitcast.12, s32[1,2048]{1,0:T(1,128)S(1)} %bitcast.17, bf16[2048,512]{1,0:T(8,128)(2,1)S(1)} %get-tuple-element.287.slope, ...), custom_call_target="tpu_custom_call" | custom-call | flops 2684354560 | tf_op jit(solution)/shard_map/pallas_call | solution.py:72
  210.1 3.4 %collective-permute-done.71.refs_4_ = bf16[512,128]{1,0:T(8,128)(2,1)S(1)} collective-permute-done((bf16[512,128]{1,0:T(8,128)(2,1)S(1)}, bf16[512,128]{1,0:T(8,128)(2,1)S(1)}, u32[]{:S(2)}, u32[]{:S(2)}) %collective-permute-start.71) | collective-permute-done | bytes 131104 | tf_op jit(solution)/shard_map/ppermute | solution.py:16
  213.5 2.0 collective-permute-start.83
  215.6 2.4 %collective-permute-start.76 = (bf16[256,256]{1,0:T(8,128)(2,1)S(1)}, bf16[256,256]{1,0:T(8,128)(2,1)S(1)}, u32[]{:S(2)}, u32[]{:S(2)}) collective-permute-start(bf16[256,256]{1,0:T(8,128)(2,1)S(1)} %shard_map.193.refs_0_), channel_id=1, source_target_pairs={{12,0},{0,4},{4,8},{8,12},{13,1},{1,5},{5,9},{9,13},{14,2},{2,6},{... | collective-permute-start | bytes 393224 | tf_op jit(solution)/shard_map/ppermute | solution.py:16
  218.8 2.6 %collective-permute-start.81 = (bf16[128,256]{1,0:T(8,128)(2,1)S(1)}, bf16[128,256]{1,0:T(8,128)(2,1)S(1)}, u32[]{:S(2)}, u32[]{:S(2)}) collective-permute-start(bf16[128,256]{1,0:T(8,128)(2,1)S(1)} %shard_map.196.refs_8_), channel_id=1, source_target_pairs={{4,0},{8,4},{12,8},{0,12},{5,1},{9,5},{13,9},{1,13},{6,2},{10,6},{... | collective-permute-start | bytes 196616 | tf_op jit(solution)/shard_map/ppermute | solution.py:16
  222.4 6.1 %collective-permute-done.82.refs_10_ = bf16[128,256]{1,0:T(8,128)(2,1)S(1)} collective-permute-done((bf16[128,256]{1,0:T(8,128)(2,1)S(1)}, bf16[128,256]{1,0:T(8,128)(2,1)S(1)}, u32[]{:S(2)}, u32[]{:S(2)}) %collective-permute-start.82) | collective-permute-done | bytes 65568 | tf_op jit(solution)/shard_map/ppermute | solution.py:16
  234.4 2.2 shard_map.197
  236.6 5.1 %shard_map.192 = bf16[2048,256]{1,0:T(8,128)(2,1)} custom-call(s32[1,2048]{1,0:T(1,128)S(1)} %bitcast.13, s32[1,2048]{1,0:T(1,128)S(1)} %bitcast.18, bf16[2048,256]{1,0:T(8,128)(2,1)S(1)} %copy-done.7, bf16[2048,256]{1,0:T(8,128)(2,1)S(1)} %get-tuple-element.297.enc_grad, bf16[512,512]{1,0:T(8,128)(2,1)S(1)} %get-tuple-element.298.enc_all, ...), custom_call_target="tpu_custom_call" | custom-call | flops 2684354560 | tf_op jit(solution)/shard_map/pallas_call | solution.py:72
  (212 shorter events, 75.5 us)
Async XLA Ops:
  11.6 10.7 %collective-permute-start.1 = (s32[512,3]{0,1:T(4,128)}, s32[512,3]{0,1:T(4,128)S(1)}, u32[]{:S(2)}, u32[]{:S(2)}) collective-permute-start(s32[512,3]{0,1:T(4,128)} %param.15), channel_id=1, source_target_pairs={{1,0},{0,1},{3,2},{2,3},{5,4},{4,5},{7,6},{6,7},{9,8},{8,9},{11,10... | collective-permute-start | bytes 18440 | tf_op jit(solution)/shard_map/ppermute | solution.py:16
  12.0 19.1 %collective-permute-start.2 = (bf16[512,128]{1,0:T(8,128)(2,1)}, bf16[512,128]{1,0:T(8,128)(2,1)S(1)}, u32[]{:S(2)}, u32[]{:S(2)}) collective-permute-start(bf16[512,128]{1,0:T(8,128)(2,1)} %get-tuple-element.172), channel_id=1, source_target_pairs={{12,0},{0,4},{4,8},{8,12},{13,1},{1,5},{5,9},{9,13},{14,2},{2,6},{... | collective-permute-start | bytes 393224 | tf_op jit(solution)/shard_map/ppermute | solution.py:16
  14.7 16.4 %collective-permute-start.3 = (bf16[512,128]{1,0:T(8,128)(2,1)}, bf16[512,128]{1,0:T(8,128)(2,1)S(1)}, u32[]{:S(2)}, u32[]{:S(2)}) collective-permute-start(bf16[512,128]{1,0:T(8,128)(2,1)} %get-tuple-element.173), channel_id=1, source_target_pairs={{8,0},{12,4},{0,8},{4,12},{9,1},{13,5},{1,9},{5,13},{10,2},{14,6},... | collective-permute-start | bytes 393224 | tf_op jit(solution)/shard_map/ppermute | solution.py:16
  17.3 13.8 %collective-permute-start.4 = (bf16[512,128]{1,0:T(8,128)(2,1)S(1)}, bf16[512,128]{1,0:T(8,128)(2,1)S(1)}, u32[]{:S(2)}, u32[]{:S(2)}) collective-permute-start(bf16[512,128]{1,0:T(8,128)(2,1)S(1)} %get-tuple-element.174), channel_id=1, source_target_pairs={{4,0},{8,4},{12,8},{0,12},{5,1},{9,5},{13,9},{1,13},{6,2},{10,6},{... | collective-permute-start | bytes 393224 | tf_op jit(solution)/shard_map/ppermute | solution.py:16
  31.3 9.9 %collective-permute-start.10 = (bf16[2048,128]{1,0:T(8,128)(2,1)}, bf16[2048,128]{1,0:T(8,128)(2,1)S(1)}, u32[]{:S(2)}, u32[]{:S(2)}) collective-permute-start(bf16[2048,128]{1,0:T(8,128)(2,1)} %copy-done.11), channel_id=1, source_target_pairs={{1,0},{0,1},{3,2},{2,3},{5,4},{4,5},{7,6},{6,7},{9,8},{8,9},{11,10... | collective-permute-start | bytes 1572872 | tf_op jit(solution)/shard_map/ppermute | solution.py:16
  39.1 8.4 %collective-permute-start.9 = (bf16[512,128]{1,0:T(8,128)(2,1)S(1)}, bf16[512,128]{1,0:T(8,128)(2,1)S(1)}, u32[]{:S(2)}, u32[]{:S(2)}) collective-permute-start(bf16[512,128]{1,0:T(8,128)(2,1)S(1)} %get-tuple-element.177.own), channel_id=1, source_target_pairs={{4,0},{8,4},{12,8},{0,12},{5,1},{9,5},{13,9},{1,13},{6,2},{10,6},{... | collective-permute-start | bytes 393224 | tf_op jit(solution)/shard_map/ppermute | solution.py:16
  50.8 8.2 %collective-permute-start.11 = (bf16[512,128]{1,0:T(8,128)(2,1)S(1)}, bf16[512,128]{1,0:T(8,128)(2,1)S(1)}, u32[]{:S(2)}, u32[]{:S(2)}) collective-permute-start(bf16[512,128]{1,0:T(8,128)(2,1)S(1)} %get-tuple-element.188.refs_0_), channel_id=1, source_target_pairs={{1,0},{0,1},{3,2},{2,3},{5,4},{4,5},{7,6},{6,7},{9,8},{8,9},{11,10... | collective-permute-start | bytes 393224 | tf_op jit(solution)/shard_map/ppermute | solution.py:16
  54.3 8.2 %collective-permute-start.14 = (bf16[512,128]{1,0:T(8,128)(2,1)S(1)}, bf16[512,128]{1,0:T(8,128)(2,1)S(1)}, u32[]{:S(2)}, u32[]{:S(2)}) collective-permute-start(bf16[512,128]{1,0:T(8,128)(2,1)S(1)} %get-tuple-element.191), channel_id=1, source_target_pairs={{12,0},{0,4},{4,8},{8,12},{13,1},{1,5},{5,9},{9,13},{14,2},{2,6},{... | collective-permute-start | bytes 393224 | tf_op jit(solution)/shard_map/ppermute | solution.py:16
  55.0 12.7 %collective-permute-start.15 = (bf16[512,128]{1,0:T(8,128)(2,1)S(1)}, bf16[512,128]{1,0:T(8,128)(2,1)S(1)}, u32[]{:S(2)}, u32[]{:S(2)}) collective-permute-start(bf16[512,128]{1,0:T(8,128)(2,1)S(1)} %get-tuple-element.192), channel_id=1, source_target_pairs={{8,0},{12,4},{0,8},{4,12},{9,1},{13,5},{1,9},{5,13},{10,2},{14,6},... | collective-permute-start | bytes 393224 | tf_op jit(solution)/shard_map/ppermute | solution.py:16
  56.5 11.3 %collective-permute-start.16 = (bf16[512,128]{1,0:T(8,128)(2,1)S(1)}, bf16[512,128]{1,0:T(8,128)(2,1)S(1)}, u32[]{:S(2)}, u32[]{:S(2)}) collective-permute-start(bf16[512,128]{1,0:T(8,128)(2,1)S(1)} %get-tuple-element.193), channel_id=1, source_target_pairs={{4,0},{8,4},{12,8},{0,12},{5,1},{9,5},{13,9},{1,13},{6,2},{10,6},{... | collective-permute-start | bytes 393224 | tf_op jit(solution)/shard_map/ppermute | solution.py:16
  92.6 9.8 %collective-permute-start.27 = (bf16[512,128]{1,0:T(8,128)(2,1)S(1)}, bf16[512,128]{1,0:T(8,128)(2,1)S(1)}, u32[]{:S(2)}, u32[]{:S(2)}) collective-permute-start(bf16[512,128]{1,0:T(8,128)(2,1)S(1)} %get-tuple-element.226.refs_4_), channel_id=1, source_target_pairs={{1,0},{0,1},{3,2},{2,3},{5,4},{4,5},{7,6},{6,7},{9,8},{8,9},{11,10... | collective-permute-start | bytes 393224 | tf_op jit(solution)/shard_map/ppermute | solution.py:16
  94.2 8.3 %collective-permute-start.26 = (bf16[512,128]{1,0:T(8,128)(2,1)S(1)}, bf16[512,128]{1,0:T(8,128)(2,1)S(1)}, u32[]{:S(2)}, u32[]{:S(2)}) collective-permute-start(bf16[512,128]{1,0:T(8,128)(2,1)S(1)} %get-tuple-element.210), channel_id=1, source_target_pairs={{12,0},{0,4},{4,8},{8,12},{13,1},{1,5},{5,9},{9,13},{14,2},{2,6},{... | collective-permute-start | bytes 393224 | tf_op jit(solution)/shard_map/ppermute | solution.py:16
  104.1 10.4 %collective-permute-start.30 = (bf16[512,128]{1,0:T(8,128)(2,1)S(1)}, bf16[512,128]{1,0:T(8,128)(2,1)S(1)}, u32[]{:S(2)}, u32[]{:S(2)}) collective-permute-start(bf16[512,128]{1,0:T(8,128)(2,1)S(1)} %shard_map.182.refs_0_), channel_id=1, source_target_pairs={{1,0},{0,1},{3,2},{2,3},{5,4},{4,5},{7,6},{6,7},{9,8},{8,9},{11,10... | collective-permute-start | bytes 393224 | tf_op jit(solution)/shard_map/ppermute | solution.py:16
  108.2 20.0 %collective-permute-start.38 = (bf16[512,128]{1,0:T(8,128)(2,1)S(1)}, bf16[512,128]{1,0:T(8,128)(2,1)S(1)}, u32[]{:S(2)}, u32[]{:S(2)}) collective-permute-start(bf16[512,128]{1,0:T(8,128)(2,1)S(1)} %get-tuple-element.221.refs_0_), channel_id=1, source_target_pairs={{12,0},{0,4},{4,8},{8,12},{13,1},{1,5},{5,9},{9,13},{14,2},{2,6},{... | collective-permute-start | bytes 393224 | tf_op jit(solution)/shard_map/ppermute | solution.py:16
  109.9 18.3 %collective-permute-start.37 = (bf16[512,128]{1,0:T(8,128)(2,1)S(1)}, bf16[512,128]{1,0:T(8,128)(2,1)S(1)}, u32[]{:S(2)}, u32[]{:S(2)}) collective-permute-start(bf16[512,128]{1,0:T(8,128)(2,1)S(1)} %get-tuple-element.221.refs_0_), channel_id=1, source_target_pairs={{8,0},{12,4},{0,8},{4,12},{9,1},{13,5},{1,9},{5,13},{10,2},{14,6},... | collective-permute-start | bytes 393224 | tf_op jit(solution)/shard_map/ppermute | solution.py:16
  114.5 13.7 %collective-permute-start.36 = (bf16[512,128]{1,0:T(8,128)(2,1)S(1)}, bf16[512,128]{1,0:T(8,128)(2,1)S(1)}, u32[]{:S(2)}, u32[]{:S(2)}) collective-permute-start(bf16[512,128]{1,0:T(8,128)(2,1)S(1)} %get-tuple-element.221.refs_0_), channel_id=1, source_target_pairs={{4,0},{8,4},{12,8},{0,12},{5,1},{9,5},{13,9},{1,13},{6,2},{10,6},{... | collective-permute-start | bytes 393224 | tf_op jit(solution)/shard_map/ppermute | solution.py:16
  114.5 13.7 %collective-permute-start.34 = (bf16[128,256]{1,0:T(8,128)(2,1)S(1)}, bf16[128,256]{1,0:T(8,128)(2,1)S(1)}, u32[]{:S(2)}, u32[]{:S(2)}) collective-permute-start(bf16[128,256]{1,0:T(8,128)(2,1)S(1)} %get-tuple-element.238), channel_id=1, source_target_pairs={{8,0},{12,4},{0,8},{4,12},{9,1},{13,5},{1,9},{5,13},{10,2},{14,6},... | collective-permute-start | bytes 196616 | tf_op jit(solution)/shard_map/ppermute | solution.py:16
  114.5 13.7 %collective-permute-start.35 = (bf16[128,256]{1,0:T(8,128)(2,1)S(1)}, bf16[128,256]{1,0:T(8,128)(2,1)S(1)}, u32[]{:S(2)}, u32[]{:S(2)}) collective-permute-start(bf16[128,256]{1,0:T(8,128)(2,1)S(1)} %get-tuple-element.239), channel_id=1, source_target_pairs={{4,0},{8,4},{12,8},{0,12},{5,1},{9,5},{13,9},{1,13},{6,2},{10,6},{... | collective-permute-start | bytes 196616 | tf_op jit(solution)/shard_map/ppermute | solution.py:16
  129.8 9.6 %collective-permute-start.45 = (bf16[512,128]{1,0:T(8,128)(2,1)S(1)}, bf16[512,128]{1,0:T(8,128)(2,1)S(1)}, u32[]{:S(2)}, u32[]{:S(2)}) collective-permute-start(bf16[512,128]{1,0:T(8,128)(2,1)S(1)} %get-tuple-element.262.refs_4_), channel_id=1, source_target_pairs={{1,0},{0,1},{3,2},{2,3},{5,4},{4,5},{7,6},{6,7},{9,8},{8,9},{11,10... | collective-permute-start | bytes 393224 | tf_op jit(solution)/shard_map/ppermute | solution.py:16
  140.0 15.5 %collective-permute-start.48 = (bf16[512,128]{1,0:T(8,128)(2,1)S(1)}, bf16[512,128]{1,0:T(8,128)(2,1)S(1)}, u32[]{:S(2)}, u32[]{:S(2)}) collective-permute-start(bf16[512,128]{1,0:T(8,128)(2,1)S(1)} %shard_map.187.refs_0_), channel_id=1, source_target_pairs={{1,0},{0,1},{3,2},{2,3},{5,4},{4,5},{7,6},{6,7},{9,8},{8,9},{11,10... | collective-permute-start | bytes 393224 | tf_op jit(solution)/shard_map/ppermute | solution.py:16
  144.5 12.8 %collective-permute-start.50 = (bf16[512,128]{1,0:T(8,128)(2,1)S(1)}, bf16[512,128]{1,0:T(8,128)(2,1)S(1)}, u32[]{:S(2)}, u32[]{:S(2)}) collective-permute-start(bf16[512,128]{1,0:T(8,128)(2,1)S(1)} %collective-permute-done.49.refs_2_), channel_id=1, source_target_pairs={{1,0},{0,1},{3,2},{2,3},{5,4},{4,5},{7,6},{6,7},{9,8},{8,9},{11,10... | collective-permute-start | bytes 393224 | tf_op jit(solution)/shard_map/ppermute | solution.py:16
  151.0 16.6 %collective-permute-start.39 = (bf16[512,128]{1,0:T(8,128)(2,1)S(1)}, bf16[512,128]{1,0:T(8,128)(2,1)S(1)}, u32[]{:S(2)}, u32[]{:S(2)}) collective-permute-start(bf16[512,128]{1,0:T(8,128)(2,1)S(1)} %get-tuple-element.221.refs_0_), channel_id=1, source_target_pairs={{1,0},{0,1},{3,2},{2,3},{5,4},{4,5},{7,6},{6,7},{9,8},{8,9},{11,10... | collective-permute-start | bytes 393224 | tf_op jit(solution)/shard_map/ppermute | solution.py:16
  153.6 14.5 %collective-permute-start.40 = (bf16[512,128]{1,0:T(8,128)(2,1)S(1)}, bf16[512,128]{1,0:T(8,128)(2,1)S(1)}, u32[]{:S(2)}, u32[]{:S(2)}) collective-permute-start(bf16[512,128]{1,0:T(8,128)(2,1)S(1)} %collective-permute-done.36.refs_1_), channel_id=1, source_target_pairs={{1,0},{0,1},{3,2},{2,3},{5,4},{4,5},{7,6},{6,7},{9,8},{8,9},{11,10... | collective-permute-start | bytes 393224 | tf_op jit(solution)/shard_map/ppermute | solution.py:16
  155.6 9.4 %collective-permute-start.55 = (bf16[192,256]{1,0:T(8,128)(2,1)S(1)}, bf16[192,256]{1,0:T(8,128)(2,1)S(1)}, u32[]{:S(2)}, u32[]{:S(2)}) collective-permute-start(bf16[192,256]{1,0:T(8,128)(2,1)S(1)} %get-tuple-element.273), channel_id=1, source_target_pairs={{8,0},{12,4},{0,8},{4,12},{9,1},{13,5},{1,9},{5,13},{10,2},{14,6},... | collective-permute-start | bytes 294920 | tf_op jit(solution)/shard_map/ppermute | solution.py:16
  161.1 8.8 %collective-permute-start.41 = (bf16[512,128]{1,0:T(8,128)(2,1)S(1)}, bf16[512,128]{1,0:T(8,128)(2,1)S(1)}, u32[]{:S(2)}, u32[]{:S(2)}) collective-permute-start(bf16[512,128]{1,0:T(8,128)(2,1)S(1)} %collective-permute-done.37.refs_2_), channel_id=1, source_target_pairs={{1,0},{0,1},{3,2},{2,3},{5,4},{4,5},{7,6},{6,7},{9,8},{8,9},{11,10... | collective-permute-start | bytes 393224 | tf_op jit(solution)/shard_map/ppermute | solution.py:16
  165.0 8.2 %collective-permute-start.59 = (bf16[512,128]{1,0:T(8,128)(2,1)S(1)}, bf16[512,128]{1,0:T(8,128)(2,1)S(1)}, u32[]{:S(2)}, u32[]{:S(2)}) collective-permute-start(bf16[512,128]{1,0:T(8,128)(2,1)S(1)} %get-tuple-element.275.refs_0_), channel_id=1, source_target_pairs={{12,0},{0,4},{4,8},{8,12},{13,1},{1,5},{5,9},{9,13},{14,2},{2,6},{... | collective-permute-start | bytes 393224 | tf_op jit(solution)/shard_map/ppermute | solution.py:16
  167.5 10.9 %collective-permute-start.58 = (bf16[512,128]{1,0:T(8,128)(2,1)S(1)}, bf16[512,128]{1,0:T(8,128)(2,1)S(1)}, u32[]{:S(2)}, u32[]{:S(2)}) collective-permute-start(bf16[512,128]{1,0:T(8,128)(2,1)S(1)} %get-tuple-element.275.refs_0_), channel_id=1, source_target_pairs={{8,0},{12,4},{0,8},{4,12},{9,1},{13,5},{1,9},{5,13},{10,2},{14,6},... | collective-permute-start | bytes 393224 | tf_op jit(solution)/shard_map/ppermute | solution.py:16
  168.1 10.3 %collective-permute-start.57 = (bf16[512,128]{1,0:T(8,128)(2,1)S(1)}, bf16[512,128]{1,0:T(8,128)(2,1)S(1)}, u32[]{:S(2)}, u32[]{:S(2)}) collective-permute-start(bf16[512,128]{1,0:T(8,128)(2,1)S(1)} %get-tuple-element.275.refs_0_), channel_id=1, source_target_pairs={{4,0},{8,4},{12,8},{0,12},{5,1},{9,5},{13,9},{1,13},{6,2},{10,6},{... | collective-permute-start | bytes 393224 | tf_op jit(solution)/shard_map/ppermute | solution.py:16
  169.9 13.9 %collective-permute-start.84 = (bf16[128,256]{1,0:T(8,128)(2,1)S(1)}, bf16[128,256]{1,0:T(8,128)(2,1)S(1)}, u32[]{:S(2)}, u32[]{:S(2)}) collective-permute-start(bf16[128,256]{1,0:T(8,128)(2,1)S(1)} %shard_map.185.refs_0_), channel_id=1, source_target_pairs={{1,0},{0,1},{3,2},{2,3},{5,4},{4,5},{7,6},{6,7},{9,8},{8,9},{11,10... | collective-permute-start | bytes 196616 | tf_op jit(solution)/shard_map/ppermute | solution.py:16
  169.9 18.7 %collective-permute-start.60 = (bf16[512,128]{1,0:T(8,128)(2,1)S(1)}, bf16[512,128]{1,0:T(8,128)(2,1)S(1)}, u32[]{:S(2)}, u32[]{:S(2)}) collective-permute-start(bf16[512,128]{1,0:T(8,128)(2,1)S(1)} %get-tuple-element.275.refs_0_), channel_id=1, source_target_pairs={{1,0},{0,1},{3,2},{2,3},{5,4},{4,5},{7,6},{6,7},{9,8},{8,9},{11,10... | collective-permute-start | bytes 393224 | tf_op jit(solution)/shard_map/ppermute | solution.py:16
  173.2 13.5 %collective-permute-start.85 = (bf16[128,256]{1,0:T(8,128)(2,1)S(1)}, bf16[128,256]{1,0:T(8,128)(2,1)S(1)}, u32[]{:S(2)}, u32[]{:S(2)}) collective-permute-start(bf16[128,256]{1,0:T(8,128)(2,1)S(1)} %collective-permute-done.51.refs_1_), channel_id=1, source_target_pairs={{1,0},{0,1},{3,2},{2,3},{5,4},{4,5},{7,6},{6,7},{9,8},{8,9},{11,10... | collective-permute-start | bytes 196616 | tf_op jit(solution)/shard_map/ppermute | solution.py:16
  178.4 9.7 %collective-permute-start.86 = (bf16[128,256]{1,0:T(8,128)(2,1)S(1)}, bf16[128,256]{1,0:T(8,128)(2,1)S(1)}, u32[]{:S(2)}, u32[]{:S(2)}) collective-permute-start(bf16[128,256]{1,0:T(8,128)(2,1)S(1)} %collective-permute-done.52.refs_2_), channel_id=1, source_target_pairs={{1,0},{0,1},{3,2},{2,3},{5,4},{4,5},{7,6},{6,7},{9,8},{8,9},{11,10... | collective-permute-start | bytes 196616 | tf_op jit(solution)/shard_map/ppermute | solution.py:16
  178.4 9.7 %collective-permute-start.87 = (bf16[128,256]{1,0:T(8,128)(2,1)S(1)}, bf16[128,256]{1,0:T(8,128)(2,1)S(1)}, u32[]{:S(2)}, u32[]{:S(2)}) collective-permute-start(bf16[128,256]{1,0:T(8,128)(2,1)S(1)} %collective-permute-done.53.refs_3_), channel_id=1, source_target_pairs={{1,0},{0,1},{3,2},{2,3},{5,4},{4,5},{7,6},{6,7},{9,8},{8,9},{11,10... | collective-permute-start | bytes 196616 | tf_op jit(solution)/shard_map/ppermute | solution.py:16
  188.1 13.3 %collective-permute-start.61 = (bf16[512,128]{1,0:T(8,128)(2,1)S(1)}, bf16[512,128]{1,0:T(8,128)(2,1)S(1)}, u32[]{:S(2)}, u32[]{:S(2)}) collective-permute-start(bf16[512,128]{1,0:T(8,128)(2,1)S(1)} %collective-permute-done.57.refs_1_), channel_id=1, source_target_pairs={{1,0},{0,1},{3,2},{2,3},{5,4},{4,5},{7,6},{6,7},{9,8},{8,9},{11,10... | collective-permute-start | bytes 393224 | tf_op jit(solution)/shard_map/ppermute | solution.py:16
  188.1 13.3 %collective-permute-start.62 = (bf16[512,128]{1,0:T(8,128)(2,1)S(1)}, bf16[512,128]{1,0:T(8,128)(2,1)S(1)}, u32[]{:S(2)}, u32[]{:S(2)}) collective-permute-start(bf16[512,128]{1,0:T(8,128)(2,1)S(1)} %collective-permute-done.58.refs_2_), channel_id=1, source_target_pairs={{1,0},{0,1},{3,2},{2,3},{5,4},{4,5},{7,6},{6,7},{9,8},{8,9},{11,10... | collective-permute-start | bytes 393224 | tf_op jit(solution)/shard_map/ppermute | solution.py:16
  188.6 13.4 %collective-permute-start.63 = (bf16[512,128]{1,0:T(8,128)(2,1)S(1)}, bf16[512,128]{1,0:T(8,128)(2,1)S(1)}, u32[]{:S(2)}, u32[]{:S(2)}) collective-permute-start(bf16[512,128]{1,0:T(8,128)(2,1)S(1)} %collective-permute-done.59.refs_3_), channel_id=1, source_target_pairs={{1,0},{0,1},{3,2},{2,3},{5,4},{4,5},{7,6},{6,7},{9,8},{8,9},{11,10... | collective-permute-start | bytes 393224 | tf_op jit(solution)/shard_map/ppermute | solution.py:16
  197.3 11.2 %collective-permute-start.80 = (bf16[192,256]{1,0:T(8,128)(2,1)S(1)}, bf16[192,256]{1,0:T(8,128)(2,1)S(1)}, u32[]{:S(2)}, u32[]{:S(2)}) collective-permute-start(bf16[192,256]{1,0:T(8,128)(2,1)S(1)} %shard_map.189.refs_4_), channel_id=1, source_target_pairs={{12,0},{0,4},{4,8},{8,12},{13,1},{1,5},{5,9},{9,13},{14,2},{2,6},{... | collective-permute-start | bytes 294920 | tf_op jit(solution)/shard_map/ppermute | solution.py:16
  197.3 11.8 %collective-permute-start.79 = (bf16[192,256]{1,0:T(8,128)(2,1)S(1)}, bf16[192,256]{1,0:T(8,128)(2,1)S(1)}, u32[]{:S(2)}, u32[]{:S(2)}) collective-permute-start(bf16[192,256]{1,0:T(8,128)(2,1)S(1)} %shard_map.189.refs_4_), channel_id=1, source_target_pairs={{8,0},{12,4},{0,8},{4,12},{9,1},{13,5},{1,9},{5,13},{10,2},{14,6},... | collective-permute-start | bytes 294920 | tf_op jit(solution)/shard_map/ppermute | solution.py:16
  201.4 8.2 %collective-permute-start.67 = (bf16[512,128]{1,0:T(8,128)(2,1)S(1)}, bf16[512,128]{1,0:T(8,128)(2,1)S(1)}, u32[]{:S(2)}, u32[]{:S(2)}) collective-permute-start(bf16[512,128]{1,0:T(8,128)(2,1)S(1)} %collective-permute-done.57.refs_1_), channel_id=1, source_target_pairs={{2,0},{0,2},{3,1},{1,3},{6,4},{4,6},{7,5},{5,7},{10,8},{8,10},{11,... | collective-permute-start | bytes 393224 | tf_op jit(solution)/shard_map/ppermute | solution.py:16
  209.7 8.3 %collective-permute-start.89 = (bf16[192,256]{1,0:T(8,128)(2,1)S(1)}, bf16[192,256]{1,0:T(8,128)(2,1)S(1)}, u32[]{:S(2)}, u32[]{:S(2)}) collective-permute-start(bf16[192,256]{1,0:T(8,128)(2,1)S(1)} %collective-permute-done.78.refs_5_), channel_id=1, source_target_pairs={{1,0},{0,1},{3,2},{2,3},{5,4},{4,5},{7,6},{6,7},{9,8},{8,9},{11,10... | collective-permute-start | bytes 294920 | tf_op jit(solution)/shard_map/ppermute | solution.py:16
  213.5 7.9 %collective-permute-start.83 = (bf16[128,256]{1,0:T(8,128)(2,1)S(1)}, bf16[128,256]{1,0:T(8,128)(2,1)S(1)}, u32[]{:S(2)}, u32[]{:S(2)}) collective-permute-start(bf16[128,256]{1,0:T(8,128)(2,1)S(1)} %shard_map.196.refs_8_), channel_id=1, source_target_pairs={{12,0},{0,4},{4,8},{8,12},{13,1},{1,5},{5,9},{9,13},{14,2},{2,6},{... | collective-permute-start | bytes 196616 | tf_op jit(solution)/shard_map/ppermute | solution.py:16
  215.5 13.0 %collective-permute-start.82 = (bf16[128,256]{1,0:T(8,128)(2,1)S(1)}, bf16[128,256]{1,0:T(8,128)(2,1)S(1)}, u32[]{:S(2)}, u32[]{:S(2)}) collective-permute-start(bf16[128,256]{1,0:T(8,128)(2,1)S(1)} %shard_map.196.refs_8_), channel_id=1, source_target_pairs={{8,0},{12,4},{0,8},{4,12},{9,1},{13,5},{1,9},{5,13},{10,2},{14,6},... | collective-permute-start | bytes 196616 | tf_op jit(solution)/shard_map/ppermute | solution.py:16
  215.6 14.3 %collective-permute-start.76 = (bf16[256,256]{1,0:T(8,128)(2,1)S(1)}, bf16[256,256]{1,0:T(8,128)(2,1)S(1)}, u32[]{:S(2)}, u32[]{:S(2)}) collective-permute-start(bf16[256,256]{1,0:T(8,128)(2,1)S(1)} %shard_map.193.refs_0_), channel_id=1, source_target_pairs={{12,0},{0,4},{4,8},{8,12},{13,1},{1,5},{5,9},{9,13},{14,2},{2,6},{... | collective-permute-start | bytes 393224 | tf_op jit(solution)/shard_map/ppermute | solution.py:16
  218.0 13.2 %collective-permute-start.75 = (bf16[256,256]{1,0:T(8,128)(2,1)S(1)}, bf16[256,256]{1,0:T(8,128)(2,1)S(1)}, u32[]{:S(2)}, u32[]{:S(2)}) collective-permute-start(bf16[256,256]{1,0:T(8,128)(2,1)S(1)} %shard_map.193.refs_0_), channel_id=1, source_target_pairs={{8,0},{12,4},{0,8},{4,12},{9,1},{13,5},{1,9},{5,13},{10,2},{14,6},... | collective-permute-start | bytes 393224 | tf_op jit(solution)/shard_map/ppermute | solution.py:16
  218.8 9.6 %collective-permute-start.81 = (bf16[128,256]{1,0:T(8,128)(2,1)S(1)}, bf16[128,256]{1,0:T(8,128)(2,1)S(1)}, u32[]{:S(2)}, u32[]{:S(2)}) collective-permute-start(bf16[128,256]{1,0:T(8,128)(2,1)S(1)} %shard_map.196.refs_8_), channel_id=1, source_target_pairs={{4,0},{8,4},{12,8},{0,12},{5,1},{9,5},{13,9},{1,13},{6,2},{10,6},{... | collective-permute-start | bytes 196616 | tf_op jit(solution)/shard_map/ppermute | solution.py:16
  221.4 10.6 %collective-permute-start.74 = (bf16[256,256]{1,0:T(8,128)(2,1)S(1)}, bf16[256,256]{1,0:T(8,128)(2,1)S(1)}, u32[]{:S(2)}, u32[]{:S(2)}) collective-permute-start(bf16[256,256]{1,0:T(8,128)(2,1)S(1)} %shard_map.193.refs_0_), channel_id=1, source_target_pairs={{4,0},{8,4},{12,8},{0,12},{5,1},{9,5},{13,9},{1,13},{6,2},{10,6},{... | collective-permute-start | bytes 393224 | tf_op jit(solution)/shard_map/ppermute | solution.py:16
  228.4 8.1 %collective-permute-start.68 = (bf16[512,128]{1,0:T(8,128)(2,1)S(1)}, bf16[512,128]{1,0:T(8,128)(2,1)S(1)}, u32[]{:S(2)}, u32[]{:S(2)}) collective-permute-start(bf16[512,128]{1,0:T(8,128)(2,1)S(1)} %collective-permute-done.67.refs_0_), channel_id=1, source_target_pairs={{1,0},{0,1},{3,2},{2,3},{5,4},{4,5},{7,6},{6,7},{9,8},{8,9},{11,10... | collective-permute-start | bytes 393224 | tf_op jit(solution)/shard_map/ppermute | solution.py:16
  232.5 9.3 %collective-permute-start.77 = (f32[256,256]{1,0:T(8,128)S(1)}, f32[256,256]{1,0:T(8,128)S(1)}, u32[]{:S(2)}, u32[]{:S(2)}) collective-permute-start(f32[256,256]{1,0:T(8,128)S(1)} %shard_map.194.mine), channel_id=1, source_target_pairs={{1,0},{0,1},{3,2},{2,3},{5,4},{4,5},{7,6},{6,7},{9,8},{8,9},{11,10... | collective-permute-start | bytes 786440 | tf_op jit(solution)/shard_map/ppermute | solution.py:16
  (64 other events, 466.1 us)

commit v4 on v3

--- a/solution.py
+++ b/solution.py
@@ -67,8 +67,11 @@
     return lax.axis_index("chan") * lax.axis_size("pipe") + lax.axis_index("pipe")
 
 
-def run(body, args, outs, scratch=(), flops=0, vmem=17, hbm=()):
-    args = [pltpu.with_memory_space_constraint(a, pltpu.VMEM) for a in args]
+def run(body, args, outs, scratch=(), flops=0, vmem=17, hbm=(), loads=()):
+    args = [
+        pltpu.with_memory_space_constraint(a, pltpu.HBM if i in loads else pltpu.VMEM)
+        for i, a in enumerate(args)
+    ]
     return pl.pallas_call(
         body,
         out_shape=[
@@ -167,6 +170,31 @@
     total = state[...].astype(F32) + dot_plain(wide, w_node[0])
     new_state[...] = total
     project(1, total.astype(BF16), w_send, w_recv, send_p, recv_p)
+
+
+def spot_body(mine, other, spot, spot_row):
+    count, mesh_rows = mine.shape
+    faces = lax.axis_size("space")
+    spare = jnp.zeros((spot.shape[1] - 2 * count, mesh_rows), jnp.int32)
+    links = jnp.concatenate([mine[...], other[...], spare], axis=0)
+    owner = lax.div(links, mesh_rows)
+    local = links - owner * mesh_rows
+    step = owner - lax.axis_index("space")
+    step = jnp.where(step < 0, step + faces, step)
+    place = jnp.where(step == 0, mesh_rows, jnp.where(step == 1, 2 * mesh_rows, 0)) + local
+    spot[...] = place.T
+    for k in range(2 * count):
+        spot_row[:, k * mesh_rows : (k + 1) * mesh_rows] = place[k : k + 1, :]
+
+
+def stack_body(*refs):
+    rows = refs[0].shape[0]
+    for k, ref in enumerate(refs[:-1]):
+        refs[-1][k * rows : (k + 1) * rows, :] = ref[...]
+
+
+def pick_body(values, out):
+    out[...] = pick(values[...], lax.axis_index("chan"), out.shape[1])
 
 
 def edge_body(below, own, above, recv_p, spot, agg, slope, halo):
@@ -246,11 +274,11 @@
     edge_back(total.astype(BF16), w_node.at[0], slope, spot, spot_row, *refs[2 * count + 3 :])
 
 
-def last_body(count, mix_scale, grad, w_send, w_recv, *refs):
+def last_body(count, mix_scale, grad_1, w_send, w_recv, *refs):
     send_parts, recv_parts = refs[:count], refs[count : 2 * count]
-    send_wide, recv_wide, grad_mesh, enc_part, enc_all = refs[2 * count :]
-    total = through(0, grad, w_send, w_recv, send_parts, recv_parts, send_wide, recv_wide)
-    grad_mesh[...] = pick(total, lax.axis_index("chan"), grad_mesh.shape[1])
+    send_wide, recv_wide, grad, enc_part, enc_all = refs[2 * count :]
+    total = through(0, grad_1, w_send, w_recv, send_parts, recv_parts, send_wide, recv_wide)
+    grad[...] = total
     scaled = (mix_scale * total).astype(BF16)
     enc_part[...] = pick(scaled, own_quarter(), enc_part.shape[1])
     enc_all[...] = scaled
@@ -268,12 +296,9 @@
     return dot_left(one_hot(ids, target[:, at]), table[...])
 
 
-def mixed_body(count, x, w, face_ids, node_ids, *refs):
-    mine, other = refs[:count], refs[count : 2 * count]
-    mixed, slope, table, target = refs[2 * count :]
-    mesh_rows = mine[0].shape[0]
-    for k in range(count):
-        put_pair(table, k * mesh_rows, 0, mine[k], other[k])
+def mixed_body(x, w, face_ids, node_ids, mine, other, mixed, slope, table, target):
+    put_pair(table, 0, 0, mine, other)
+    mesh_rows = mine.shape[0] // lax.axis_size("space")
     target[...] = table_rows(mesh_rows, face_ids[...], node_ids[...])
     size = 512
     chan = lax.axis_index("chan")
@@ -290,15 +315,16 @@
     lax.fori_loop(0, x.shape[0] // size, step, 0)
 
 
-def enc_own_body(count, x, face_ids, node_ids, slope, *refs):
-    mine, other = refs[:count], refs[count : 2 * count]
-    enc_grad, grad_keep, grad_give, table, target, total = refs[2 * count :]
-    mesh_rows = mine[0].shape[0]
-    for k in range(count):
-        put_pair(table, k * mesh_rows, 0, mine[k], other[k])
+def enc_own_body(
+    x, face_ids, node_ids, slope, enc_all, mine, other,
+    enc_grad, grad_keep, grad_give, table, target, total,
+):
+    mesh_rows = enc_all.shape[0]
+    chan, pipe = lax.axis_index("chan"), lax.axis_index("pipe")
+    table[:mesh_rows, :] = pick(enc_all[...], chan, table.shape[1])
+    put_pair(table, mesh_rows, 0, mine, other)
     target[...] = table_rows(mesh_rows, face_ids[...], node_ids[...])
     size = 512
-    chan, pipe = lax.axis_index("chan"), lax.axis_index("pipe")
     total[...] = jnp.zeros(total.shape, F32)
 
     def step(i, carry):
@@ -315,7 +341,7 @@
     grad_give[...] = total[rows_at(1 - pipe, half), :].astype(BF16)
 
 
-def enc_other_body(faces, count, face_ids, node_ids, cotangent, enc_grad, enc_all, slope, w, *refs):
+def enc_other_body(count, face_ids, node_ids, cotangent, enc_grad, enc_all, slope, w, *refs):
     blocks = refs[:-3]
     grad_grid, table, target = refs[-3:]
     grid_rows, narrow = cotangent.shape
@@ -325,9 +351,7 @@
         other = lax.rem(chan + 1 + j, count + 1)
         columns = slice(j * narrow, (j + 1) * narrow)
         table[:mesh_rows, columns] = pick(enc_all[...], other, narrow)
-        for k in range(1, faces):
-            mine, sibling = blocks[2 * (j * (faces - 1) + k - 1) :][:2]
-            put_pair(table, k * mesh_rows, j * narrow, mine, sibling)
+        put_pair(table, mesh_rows, j * narrow, blocks[2 * j], blocks[2 * j + 1])
     target[...] = table_rows(mesh_rows, face_ids[...], node_ids[...])
     size = 512
     w_rows = w[rows_at(chan, narrow), :]
@@ -348,42 +372,56 @@
     lax.fori_loop(0, grid_rows // size, step, 0)
 
 
-def weight_body(kinds, count, *refs):
-    outs, table = refs[-count - 1 : -1], refs[-1]
+def cut_by_face(table, outs):
+    count, size = len(outs), outs[0].shape[0]
+    face = lax.axis_index("space")
+    for k, out in enumerate(outs):
+        out[...] = table[rows_at(lax.rem(face + k, count), size), :].astype(out.dtype)
+
+
+def weight_body(kinds, *refs):
+    outs, table = refs[-1 - lax.axis_size("space") : -1], refs[-1]
     rows = table.shape[0] // len(kinds)
-    narrow = table.shape[1]
-    chan, pipe, face = (lax.axis_index(a) for a in ("chan", "pipe", "space"))
+    chan, pipe = lax.axis_index("chan"), lax.axis_index("pipe")
     for i, (left, right) in enumerate(kinds):
         one = pick(refs[left][...].astype(BF16), pipe, rows)
-        two = pick(refs[right][...].astype(BF16), chan, narrow)
+        two = pick(refs[right][...].astype(BF16), chan, table.shape[1])
         table[i * rows : (i + 1) * rows, :] = dot_left(one, two).astype(BF16)
-    size = outs[0].shape[0]
-    for k, out in enumerate(outs):
-        out[...] = table[rows_at(lax.rem(face + k, count), size), :]
-
-
-def write_body(places, count, *refs):
-    groups = len(places)
-    outs, table = refs[2 * groups * count : -1], refs[-1]
+    cut_by_face(table, outs)
+
+
+def cores_body(keep, got, *refs):
+    refs[-1][...] = keep[...] + got[...].astype(F32)
+    cut_by_face(refs[-1], refs[:-1])
+
+
+def stack_all_body(*refs):
+    row = 0
+    for ref in refs[:-1]:
+        rows = ref.shape[0]
+        refs[-1][row : row + rows, :] = ref[...]
+        row += rows
+
+
+def write_body(places, *refs):
+    count = lax.axis_size("space")
+    outs, tables = refs[2 * count : -len(places)], refs[-len(places) :]
     pipe, face = lax.axis_index("pipe"), lax.axis_index("space")
     for side in range(2):
-        for i, items in enumerate(places):
-            pieces = refs[(side * groups + i) * count :][:count]
-            size = pieces[0].shape[0]
-            for k in range(count):
-                table[rows_at(lax.rem(face + k, count), size), :] = pieces[k][...]
-            rows = size * count // len(items)
-            half = pipe if side == 0 else 1 - pipe
+        half = pipe if side == 0 else 1 - pipe
+        for k in range(count):
+            piece = refs[side * count + k]
+            block = lax.rem(face + k, count)
+            row = 0
+            for table in tables:
+                size = table.shape[0] // count
+                table[rows_at(block, size), :] = piece[row : row + size, :]
+                row += size
+        for table, items in zip(tables, places):
+            rows = table.shape[0] // len(items)
             for j, (out, layer) in enumerate(items):
-                ref = outs[out] if layer is None else outs[out].at[layer]
-                ref[rows_at(half, rows), :] = table[j * rows : (j + 1) * rows, :].astype(F32)
-
-
-def halves_body(mine, other, out):
-    rows = mine.shape[0]
-    pipe = lax.axis_index("pipe")
-    out[rows_at(pipe, rows), :] = mine[...]
-    out[rows_at(1 - pipe, rows), :] = other[...]
+                to = outs[out] if layer is None else outs[out].at[layer]
+                to[rows_at(half, rows), :] = table[j * rows : (j + 1) * rows, :].astype(F32)
 
 
 def per_device(
@@ -400,7 +438,6 @@
     mesh_all = faces * mesh_rows
     mix_scale = (mesh_rows / (grid_rows * pipe_count)) ** 0.5
     nbrs = mesh_links.shape[1] * pipe_count
-    face = lax.axis_index("space")
     ids = (g2m_face.reshape(1, grid_rows), g2m_node.reshape(1, grid_rows))
     grid_vmem = 14 + mesh_all // 512
 
@@ -431,28 +468,33 @@
     def join(keep, give):
         return run(join_body, (keep, shifted(give, "pipe", 1)), [(block, BF16)] * faces)
 
+    def neighbours(send_p):
+        return shifted(send_p, "space", -1), shifted(send_p, "space", 1)
+
+    def stack(blocks):
+        rows, columns = blocks[0].shape
+        return run(stack_body, blocks, [((len(blocks) * rows, columns), blocks[0].dtype)])[0]
+
     keep, give = run(
         on(encode_body, mesh_rows), (grid_latent, w_enc, *ids), sums,
-        scratch=[pltpu.VMEM((grid_rows, narrow), BF16)],
+        scratch=[pltpu.VMEM((grid_rows, narrow), BF16)], loads=(0, 1, 2, 3),
         flops=sum_flops + 2 * grid_rows * wide * narrow, vmem=grid_vmem,
     )
-    *blocks, cotangent_late, links = tie((*join(keep, give), cotangent, mesh_links))
+    *blocks, cotangent_late, links = tie((*join(keep, give), cotangent, mesh_links.T))
     state_part, = run(
         on(state_body, mix_scale), (mesh_latent, blocks[0], *over_faces(blocks, -1)),
         [(block, BF16)],
     )
-
-    links = jnp.concatenate([links, shifted(links, "pipe", 1)], axis=1)
-    offset = (links // mesh_rows - face) % faces
-    local = links % mesh_rows
-    spot = jnp.where(
-        offset == 0, mesh_rows + local, jnp.where(offset == 1, 2 * mesh_rows + local, local)
-    )
-    spot_row = spot.T.reshape(1, nbrs * mesh_rows)
+    spot, spot_row = run(
+        spot_body, (links, shifted(links, "pipe", 1)),
+        [((mesh_rows, 8), jnp.int32), ((1, nbrs * mesh_rows), jnp.int32)],
+    )
     keep, give = run(
-        on(sum_by_node, mesh_rows), (*ids, cotangent_late), sums, flops=sum_flops, vmem=grid_vmem
-    )
-    keep, give, spot, spot_row, state_part = tie((keep, give, spot, spot_row, state_part))
+        on(sum_by_node, mesh_rows), (*ids, cotangent_late), sums, flops=sum_flops,
+        vmem=grid_vmem, loads=(2,),
+    )
+    back_blocks = join(keep, give)
+    *parts, spot, spot_row = tie((*face_parts(state_part), spot, spot_row))
 
     def edges(send_p, recv_p, below, above):
         return run(
@@ -461,25 +503,19 @@
             scratch=[pltpu.VMEM((3 * mesh_rows // 2, 2 * part), BF16)], flops=edge_flops,
         )
 
-    def neighbours(send_p):
-        return shifted(send_p, "space", -1), shifted(send_p, "space", 1)
-
     state_0, send_p, recv_p = run(
-        first_body, (w_send, w_recv, *face_parts(state_part)),
+        first_body, (w_send, w_recv, *parts),
         [(full, BF16), (block, BF16), (block, F32)], flops=4 * mesh_rows * wide * part,
     )
-    below, above, *back_blocks = tie((*neighbours(send_p), *join(keep, give)))
-    back_got = over_faces(back_blocks, -1)
+    below, above, *back_blocks = tie((*neighbours(send_p), *back_blocks))
     agg, slope_0 = edges(send_p, recv_p, below, above)
     agg_0, state_1, send_p, recv_p = run(
         next_body, (state_0, w_node, w_send, w_recv, *face_parts(agg)),
         [(full, BF16), (full, F32), (block, BF16), (block, F32)],
         flops=2 * mesh_rows * wide * wide,
     )
-    send_p, *back_got = tie((send_p, *back_got))
-    below, above = neighbours(send_p)
-    back_parts = face_parts(add([back_blocks[0], *back_got]))
-    below, above, *back_parts = tie((below, above, *back_parts))
+    back_own = add([back_blocks[0], *over_faces(back_blocks, -1)])
+    below, above, *back_parts = tie((*neighbours(send_p), *face_parts(back_own)))
     agg, slope_1 = edges(send_p, recv_p, below, above)
     back_outs = [(full, F32), (block, BF16), (block, BF16), (block, F32), (block, BF16)]
     back_scratch = [pltpu.VMEM((nbrs * mesh_rows, 2 * part), BF16)]
@@ -492,103 +528,90 @@
 
     def weights(args, kinds):
         rows = half * len(kinds)
-        return run(
-            on(weight_body, kinds, faces), args, [((rows // faces, narrow), BF16)] * faces,
+        pieces = run(
+            on(weight_body, kinds), args, [((rows // faces, narrow), BF16)] * faces,
             scratch=[pltpu.VMEM((rows, narrow), BF16)], flops=2 * mesh_rows * rows * narrow,
         )
+        return add([pieces[0], *over_faces(pieces, -1)])
 
     def from_owners(piece):
         return [piece] + [shifted(piece, "space", k) for k in range(1, faces)]
 
     recv_parts = face_parts(recv_grad)
-    pieces_a = weights((last_b, dec_grad, agg_1, grad_2), ((0, 1), (2, 3)))
+    sums_a = weights((last_b, dec_grad, agg_1, grad_2), ((0, 1), (2, 3)))
     below, above = shifted(below, "space", 1), shifted(above, "space", -1)
-    below, above, dec_part, *rest = tie((below, above, dec_part, *pieces_a, *recv_parts))
-    pieces_a, recv_parts = rest[:faces], rest[faces:]
-    got_a = over_faces(pieces_a, -1)
-    dec_mine = from_owners(dec_part)
-    outs = run(
+    below, above, dec_part, *recv_parts = tie((below, above, dec_part, *recv_parts))
+    send_parts = face_parts(add([own, below, above]))
+    send_1, recv_1, grad_1, recv_grad, below, own, above = run(
         on(back_body, parts_count),
-        (grad_2, w_send, w_recv, w_node, slope_0, spot, spot_row)
-        + (*face_parts(add([own, below, above])), *recv_parts),
+        (grad_2, w_send, w_recv, w_node, slope_0, spot, spot_row, *send_parts, *recv_parts),
         [(full, BF16), (full, BF16)] + back_outs,
         scratch=back_scratch, flops=edge_flops + 4 * mesh_rows * wide * wide,
     )
-    outs = tie((*outs, *got_a, *dec_mine[1:]))
-    send_1, recv_1, grad_1, recv_grad, below, own, above = outs[:7]
-    got_a, dec_mine = outs[7 : 6 + faces], [dec_mine[0], *outs[6 + faces :]]
 
     recv_parts = face_parts(recv_grad)
-    pieces_b = weights((state_1, send_1, recv_1, agg_0, grad_1), ((0, 1), (0, 2), (3, 4)))
-    sum_a = add([pieces_a[0], *got_a])
+    sums_b = weights((state_1, send_1, recv_1, agg_0, grad_1), ((0, 1), (0, 2), (3, 4)))
+    dec_mine = stack(from_owners(dec_part))
+    dec_other = shifted(dec_mine, "pipe", 1)
     below, above = shifted(below, "space", 1), shifted(above, "space", -1)
-    below, above, sum_a, *rest = tie((below, above, sum_a, *pieces_b, *recv_parts))
-    pieces_b, recv_parts = rest[:faces], rest[faces:]
-    all_a = from_owners(sum_a)
-    got_b = over_faces(pieces_b, -1)
-    outs = run(
-        on(last_body, parts_count, mix_scale),
-        (grad_1, w_send, w_recv, *face_parts(add([own, below, above])), *recv_parts),
-        [(full, BF16), (full, BF16), ((mesh_rows, narrow), F32), (block, BF16), (full, BF16)],
+    below, above, sums_a, dec_other, *recv_parts = tie(
+        (below, above, sums_a, dec_other, *recv_parts)
+    )
+    send_parts = face_parts(add([own, below, above]))
+    send_0, recv_0, grad_0, enc_part, enc_all = run(
+        on(last_body, parts_count, mix_scale), (grad_1, w_send, w_recv, *send_parts, *recv_parts),
+        [(full, BF16), (full, BF16), (full, F32), (block, BF16), (full, BF16)],
         flops=4 * mesh_rows * wide * wide,
     )
-    outs = tie((*outs, *all_a[1:], *got_b))
-    send_0, recv_0, grad_mesh, enc_part, enc_all = outs[:5]
-    all_a, got_b = [all_a[0], *outs[5 : 4 + faces]], outs[4 + faces :]
-
-    enc_mine = from_owners(enc_part)
-    pieces_c = weights((state_0, send_0, recv_0), ((0, 1), (0, 2)))
-    sum_b = add([pieces_b[0], *got_b])
+
+    enc_got = from_owners(enc_part)[1:]
+    sums_c = weights((state_0, send_0, recv_0), ((0, 1), (0, 2)))
+    grad_mesh, = run(pick_body, (grad_0,), [((mesh_rows, narrow), F32)], hbm=(0,))
     table = [pltpu.VMEM((mesh_all, narrow), BF16), pltpu.VMEM((1, grid_rows), jnp.int32)]
     mixed, slope_enc = run(
-        on(mixed_body, faces),
-        (grid_latent, w_enc, *ids, *dec_mine, *(shifted(b, "pipe", 1) for b in dec_mine)),
-        [((grid_rows, narrow), BF16), ((grid_rows, wide), BF16)], scratch=table,
+        mixed_body, (grid_latent, w_enc, *ids, dec_mine, dec_other),
+        [((grid_rows, narrow), BF16), ((grid_rows, wide), BF16)], scratch=table, hbm=(0,),
         flops=sum_flops + 2 * grid_rows * wide * wide, vmem=grid_vmem,
     )
-    outs = tie((*enc_mine[1:], slope_enc, sum_b, *pieces_c))
-    enc_mine = [enc_mine[0], *outs[: faces - 1]]
-    slope_enc, sum_b, *pieces_c = outs[faces - 1 :]
-    got_c = over_faces(pieces_c, -1)
-    all_b = from_owners(sum_b)
+    *enc_got, slope_enc, grad_mesh = tie((*enc_got, slope_enc, grad_mesh))
+    enc_mine = stack(enc_got)
     enc_grad, grad_keep, grad_give = run(
-        on(enc_own_body, faces),
-        (grid_latent, *ids, slope_enc, *enc_mine, *(shifted(b, "pipe", 1) for b in enc_mine)),
+        enc_own_body,
+        (grid_latent, *ids, slope_enc, enc_all, enc_mine, shifted(enc_mine, "pipe", 1)),
         [((grid_rows, narrow), BF16), ((half, narrow), F32), ((half, narrow), BF16)],
         scratch=table + [pltpu.VMEM((wide, narrow), F32)],
         flops=sum_flops + 2 * grid_rows * wide * narrow, vmem=grid_vmem,
     )
-    outs = tie((enc_grad, grad_keep, grad_give, *got_c))
-    enc_grad, grad_keep, grad_give, *got_c = outs
-    half_sum, = run(
-        add_body, (grad_keep, shifted(grad_give, "pipe", 1)), [((half, narrow), BF16)]
-    )
-    total = add(from_owners(half_sum), F32)
-    grad_w_enc, = run(
-        halves_body, (total, shifted(total, "pipe", 1)), [((wide, narrow), F32)], hbm=(0,)
-    )
-    all_c = from_owners(add([pieces_c[0], *got_c]))
-
-    pieces = []
-    for j in range(1, chan_count):
-        for k in range(1, faces):
-            piece = shifted(enc_mine[k], "chan", j)
-            pieces += [piece, shifted(piece, "pipe", 1)]
+    enc_grad, grad_keep, grad_give, sums_b = tie((enc_grad, grad_keep, grad_give, sums_b))
+    sums_g = run(
+        cores_body, (grad_keep, shifted(grad_give, "pipe", 1)),
+        [((half // faces, narrow), BF16)] * faces, scratch=[pltpu.VMEM((half, narrow), F32)],
+    )
+    sums_g = add([sums_g[0], *over_faces(sums_g, -1)])
+    sums_all = (sums_a, sums_b, sums_c, sums_g)
+    reduced, = run(
+        stack_all_body, sums_all, [((sum(a.shape[0] for a in sums_all), narrow), BF16)]
+    )
+    reduced = from_owners(reduced)
+    reduced_other = [shifted(piece, "pipe", 1) for piece in reduced]
     others = chan_count - 1
+    pieces = face_parts(enc_mine)[2:]
     grad_grid, = run(
-        on(enc_other_body, faces, others),
+        on(enc_other_body, others),
         (*ids, cotangent, enc_grad, enc_all, slope_enc, w_enc, *pieces),
-        [((grid_rows, narrow), BF16)],
+        [((grid_rows, narrow), BF16)], loads=(2,),
         scratch=[pltpu.VMEM((mesh_all, narrow * others), BF16), table[1]],
         flops=(sum_flops + 4 * grid_rows * narrow * narrow) * others, vmem=grid_vmem + 4, hbm=(0,),
     )
-    groups = (*all_a, *all_b, *all_c)
+    *reduced_other, grad_grid = tie((*reduced_other, grad_grid))
     layer_shape = ((w_send.shape[0], wide, narrow), F32)
-    places = (((3, None), (2, 1)), ((0, 1), (1, 1), (2, 0)), ((0, 0), (1, 0)))
-    grad_w_send, grad_w_recv, grad_w_node, grad_w_dec = run(
-        on(write_body, places, faces), (*groups, *(shifted(b, "pipe", 1) for b in groups)),
-        [layer_shape] * 3 + [((wide, narrow), F32)], hbm=(0, 1, 2, 3),
-        scratch=[pltpu.VMEM((3 * half, narrow), BF16)],
+    places = (
+        ((3, None), (2, 1)), ((0, 1), (1, 1), (2, 0)), ((0, 0), (1, 0)), ((4, None),),
+    )
+    grad_w_send, grad_w_recv, grad_w_node, grad_w_dec, grad_w_enc = run(
+        on(write_body, places), (*reduced, *reduced_other),
+        [layer_shape] * 3 + [((wide, narrow), F32)] * 2, hbm=(0, 1, 2, 3, 4),
+        scratch=[pltpu.VMEM((half * len(items), narrow), BF16) for items in places],
     )
     return (
         mixed,

time: 244 us -> 217 us (0.89)
  local copies, waits for them, and re-layouts: 10.6 us -> 0.05 us
  starting transfers between devices: 80.8 us -> 71.4 us
  waiting for transfers between devices: 106 us -> 97 us
  Pallas kernels: 39.1 us -> 44.2 us
  other arithmetic: 4.82 us -> 0 us
    ppermute x96 -> x71, starting transfers between devices: 80.8 us -> 71.4 us  [shifted(): lax.ppermute(block, axis, [((i + distance) % count, i) for i in range(cou...]
    ppermute x96 -> x71, waiting for transfers between devices: 106 us -> 97 us  [shifted(): lax.ppermute(block, axis, [((i + distance) % count, i) for i in range(cou...]
    unnamed x35 -> x20, local copies, waits for them, and re-layouts: 7.35 us -> 0.05 us
    pallas_call x28 -> x32, Pallas kernels: 39.1 us -> 44.2 us  [run(): pl.pallas_call(body, out_shape=[jax.ShapeDtypeStruct(s, d) if i in hbm el...]
  transfers between devices with their start and end apart: 96 -> 71, of which waited for: 36 -> 33; matrix products, arithmetic and copies ran while one was open for 4% -> 0% of each run, Pallas kernels for 11% -> 14%
where the time goes in v4:
time: 217 us; the launch traced here: 214 us
  waiting for transfers between devices  97 us (45%)
  starting transfers between devices  71.4 us (33%)
  Pallas kernels  44.2 us (20%)
    ppermute x71, waiting for transfers between devices, shifted(): lax.ppermute(block, axis, [((i + distance) % count, i) for i in range(cou...  97 us
    ppermute x71, starting transfers between devices, shifted(): lax.ppermute(block, axis, [((i + distance) % count, i) for i in range(cou...  71.4 us
    pallas_call x32, Pallas kernels, run(): pl.pallas_call(body, out_shape=[jax.ShapeDtypeStruct(s, d) if i in hbm el...  44.2 us
  transfers between devices with their start and end apart: 71, of which 33 were waited for; matrix products, arithmetic and copies ran while one was open for 0% of the time, Pallas kernels for 14%

profile of v4, /device:TPU:0, one launch (start us, length us, event | category | flops | bytes accessed | tf_op | source)
XLA Modules:
  0.0 213.7 jit_solution(13615170997753340470)
XLA Ops:
  0.7 5.9 %shard_map.170 = (bf16[2048,128]{1,0:T(8,128)(2,1)S(1)}, bf16[2048,128]{1,0:T(8,128)(2,1)S(1)}) custom-call(bf16[2048,512]{1,0:T(8,128)(2,1)} %x.5, bf16[512,512]{1,0:T(8,128)(2,1)} %w.5, s32[1,2048]{1,0:T(1,128)} %bitcast.5, s32[1,2048]{1,0:T(1,128)} %bitcast.10), custom_call_target="tpu_custom_call" | custom-call | flops 2684354560 | tf_op jit(solution)/shard_map/pallas_call | solution.py:75
  8.8 3.0 %collective-permute-start.1 = (bf16[512,128]{1,0:T(8,128)(2,1)S(1)}, bf16[512,128]{1,0:T(8,128)(2,1)S(1)}, u32[]{:S(2)}, u32[]{:S(2)}) collective-permute-start(bf16[512,128]{1,0:T(8,128)(2,1)S(1)} %get-tuple-element.140), channel_id=1, source_target_pairs={{12,0},{0,4},{4,8},{8,12},{13,1},{1,5},{5,9},{9,13},{14,2},{2,6},{... | collective-permute-start | bytes 393224 | tf_op jit(solution)/shard_map/ppermute | solution.py:16
  11.8 2.6 %collective-permute-start.2 = (bf16[512,128]{1,0:T(8,128)(2,1)S(1)}, bf16[512,128]{1,0:T(8,128)(2,1)S(1)}, u32[]{:S(2)}, u32[]{:S(2)}) collective-permute-start(bf16[512,128]{1,0:T(8,128)(2,1)S(1)} %get-tuple-element.141), channel_id=1, source_target_pairs={{8,0},{12,4},{0,8},{4,12},{9,1},{13,5},{1,9},{5,13},{10,2},{14,6},... | collective-permute-start | bytes 393224 | tf_op jit(solution)/shard_map/ppermute | solution.py:16
  15.7 4.1 %shard_map.175 = (bf16[2048,128]{1,0:T(8,128)(2,1)S(1)}, bf16[2048,128]{1,0:T(8,128)(2,1)S(1)}) custom-call(s32[1,2048]{1,0:T(1,128)S(1)} %bitcast.6, s32[1,2048]{1,0:T(1,128)S(1)} %bitcast.11, bf16[2048,256]{1,0:T(8,128)(2,1)} %cotangent.1), custom_call_target="tpu_custom_call" | custom-call | flops 2147483648 | tf_op jit(solution)/shard_map/pallas_call | solution.py:75
  19.9 3.4 %collective-permute-done.2.refs_2_ = bf16[512,128]{1,0:T(8,128)(2,1)S(1)} collective-permute-done((bf16[512,128]{1,0:T(8,128)(2,1)S(1)}, bf16[512,128]{1,0:T(8,128)(2,1)S(1)}, u32[]{:S(2)}, u32[]{:S(2)}) %collective-permute-start.2) | collective-permute-done | bytes 131104 | tf_op jit(solution)/shard_map/ppermute | solution.py:16
  25.0 3.8 %collective-permute-done.5.refs_2_ = bf16[512,128]{1,0:T(8,128)(2,1)S(1)} collective-permute-done((bf16[512,128]{1,0:T(8,128)(2,1)S(1)}, bf16[512,128]{1,0:T(8,128)(2,1)S(1)}, u32[]{:S(2)}, u32[]{:S(2)}) %collective-permute-start.5) | collective-permute-done | bytes 131104 | tf_op jit(solution)/shard_map/ppermute | solution.py:16
  30.9 4.0 %collective-permute-start.9 = (bf16[512,128]{1,0:T(8,128)(2,1)S(1)}, bf16[512,128]{1,0:T(8,128)(2,1)S(1)}, u32[]{:S(2)}, u32[]{:S(2)}) collective-permute-start(bf16[512,128]{1,0:T(8,128)(2,1)S(1)} %get-tuple-element.151.own), channel_id=1, source_target_pairs={{4,0},{8,4},{12,8},{0,12},{5,1},{9,5},{13,9},{1,13},{6,2},{10,6},{... | collective-permute-start | bytes 393224 | tf_op jit(solution)/shard_map/ppermute | solution.py:16
  35.0 3.8 %collective-permute-done.9.above = bf16[512,128]{1,0:T(8,128)(2,1)S(1)} collective-permute-done((bf16[512,128]{1,0:T(8,128)(2,1)S(1)}, bf16[512,128]{1,0:T(8,128)(2,1)S(1)}, u32[]{:S(2)}, u32[]{:S(2)}) %collective-permute-start.9) | collective-permute-done | bytes 131104 | tf_op jit(solution)/shard_map/ppermute | solution.py:16
  38.8 3.5 %collective-permute-done.8.below = bf16[512,128]{1,0:T(8,128)(2,1)S(1)} collective-permute-done((bf16[512,128]{1,0:T(8,128)(2,1)S(1)}, bf16[512,128]{1,0:T(8,128)(2,1)S(1)}, u32[]{:S(2)}, u32[]{:S(2)}) %collective-permute-start.8) | collective-permute-done | bytes 131104 | tf_op jit(solution)/shard_map/ppermute | solution.py:16
  44.3 2.6 %collective-permute-start.18 = (bf16[512,128]{1,0:T(8,128)(2,1)S(1)}, bf16[512,128]{1,0:T(8,128)(2,1)S(1)}, u32[]{:S(2)}, u32[]{:S(2)}) collective-permute-start(bf16[512,128]{1,0:T(8,128)(2,1)S(1)} %get-tuple-element.169), channel_id=1, source_target_pairs={{4,0},{8,4},{12,8},{0,12},{5,1},{9,5},{13,9},{1,13},{6,2},{10,6},{... | collective-permute-start | bytes 393224 | tf_op jit(solution)/shard_map/ppermute | solution.py:16
  50.6 3.7 %collective-permute-done.17.refs_2_ = bf16[512,128]{1,0:T(8,128)(2,1)S(1)} collective-permute-done((bf16[512,128]{1,0:T(8,128)(2,1)S(1)}, bf16[512,128]{1,0:T(8,128)(2,1)S(1)}, u32[]{:S(2)}, u32[]{:S(2)}) %collective-permute-start.17) | collective-permute-done | bytes 131104 | tf_op jit(solution)/shard_map/ppermute | solution.py:16
  56.5 3.3 %collective-permute-done.20.refs_6_ = bf16[512,128]{1,0:T(8,128)(2,1)S(1)} collective-permute-done((bf16[512,128]{1,0:T(8,128)(2,1)S(1)}, bf16[512,128]{1,0:T(8,128)(2,1)S(1)}, u32[]{:S(2)}, u32[]{:S(2)}) %collective-permute-start.20) | collective-permute-done | bytes 131104 | tf_op jit(solution)/shard_map/ppermute | solution.py:16
  60.6 3.8 %collective-permute-start.15 = (bf16[512,128]{1,0:T(8,128)(2,1)S(1)}, bf16[512,128]{1,0:T(8,128)(2,1)S(1)}, u32[]{:S(2)}, u32[]{:S(2)}) collective-permute-start(bf16[512,128]{1,0:T(8,128)(2,1)S(1)} %get-tuple-element.165.own), channel_id=1, source_target_pairs={{4,0},{8,4},{12,8},{0,12},{5,1},{9,5},{13,9},{1,13},{6,2},{10,6},{... | collective-permute-start | bytes 393224 | tf_op jit(solution)/shard_map/ppermute | solution.py:16
  64.4 3.8 %collective-permute-done.15.above = bf16[512,128]{1,0:T(8,128)(2,1)S(1)} collective-permute-done((bf16[512,128]{1,0:T(8,128)(2,1)S(1)}, bf16[512,128]{1,0:T(8,128)(2,1)S(1)}, u32[]{:S(2)}, u32[]{:S(2)}) %collective-permute-start.15) | collective-permute-done | bytes 131104 | tf_op jit(solution)/shard_map/ppermute | solution.py:16
  68.2 3.7 %collective-permute-done.14.below = bf16[512,128]{1,0:T(8,128)(2,1)S(1)} collective-permute-done((bf16[512,128]{1,0:T(8,128)(2,1)S(1)}, bf16[512,128]{1,0:T(8,128)(2,1)S(1)}, u32[]{:S(2)}, u32[]{:S(2)}) %collective-permute-start.14) | collective-permute-done | bytes 131104 | tf_op jit(solution)/shard_map/ppermute | solution.py:16
  71.9 1.8 shard_map.180
  75.3 3.5 %collective-permute-done.23.refs_2_ = bf16[512,128]{1,0:T(8,128)(2,1)S(1)} collective-permute-done((bf16[512,128]{1,0:T(8,128)(2,1)S(1)}, bf16[512,128]{1,0:T(8,128)(2,1)S(1)}, u32[]{:S(2)}, u32[]{:S(2)}) %collective-permute-start.23) | collective-permute-done | bytes 131104 | tf_op jit(solution)/shard_map/ppermute | solution.py:16
  80.1 3.5 %shard_map.181 = (bf16[512,512]{1,0:T(8,128)(2,1)S(1)}, bf16[512,512]{1,0:T(8,128)(2,1)S(1)}, bf16[512,128]{1,0:T(8,128)(2,1)S(1)}, bf16[512,512]{1,0:T(8,128)(2...) custom-call(f32[512,512]{1,0:T(8,128)S(1)} %get-tuple-element.164.st, ...), custom_call_target="tpu_custom_call" | custom-call | flops 2013265920 | tf_op jit(solution)/shard_map/pallas_call | solution.py:75
  85.1 1.8 collective-permute-start.25
  87.2 2.0 collective-permute-done.28.refs_6_
  89.2 1.9 collective-permute-done.25.refs_1_
  91.0 4.5 %collective-permute-done.26.refs_2_ = bf16[512,128]{1,0:T(8,128)(2,1)S(1)} collective-permute-done((bf16[512,128]{1,0:T(8,128)(2,1)S(1)}, bf16[512,128]{1,0:T(8,128)(2,1)S(1)}, u32[]{:S(2)}, u32[]{:S(2)}) %collective-permute-start.26) | collective-permute-done | bytes 131104 | tf_op jit(solution)/shard_map/ppermute | solution.py:16
  96.4 2.2 %collective-permute-start.31 = (bf16[512,128]{1,0:T(8,128)(2,1)S(1)}, bf16[512,128]{1,0:T(8,128)(2,1)S(1)}, u32[]{:S(2)}, u32[]{:S(2)}) collective-permute-start(bf16[512,128]{1,0:T(8,128)(2,1)S(1)} %get-tuple-element.184.refs_0_), channel_id=1, source_target_pairs={{8,0},{12,4},{0,8},{4,12},{9,1},{13,5},{1,9},{5,13},{10,2},{14,6},... | collective-permute-start | bytes 393224 | tf_op jit(solution)/shard_map/ppermute | solution.py:16
  100.9 3.7 %collective-permute-done.32.refs_3_ = bf16[512,128]{1,0:T(8,128)(2,1)S(1)} collective-permute-done((bf16[512,128]{1,0:T(8,128)(2,1)S(1)}, bf16[512,128]{1,0:T(8,128)(2,1)S(1)}, u32[]{:S(2)}, u32[]{:S(2)}) %collective-permute-start.32) | collective-permute-done | bytes 131104 | tf_op jit(solution)/shard_map/ppermute | solution.py:16
  104.5 4.2 %collective-permute-done.31.refs_2_ = bf16[512,128]{1,0:T(8,128)(2,1)S(1)} collective-permute-done((bf16[512,128]{1,0:T(8,128)(2,1)S(1)}, bf16[512,128]{1,0:T(8,128)(2,1)S(1)}, u32[]{:S(2)}, u32[]{:S(2)}) %collective-permute-start.31) | collective-permute-done | bytes 131104 | tf_op jit(solution)/shard_map/ppermute | solution.py:16
  108.8 3.1 %shard_map.184 = (bf16[512,512]{1,0:T(8,128)(2,1)S(1)}, bf16[512,512]{1,0:T(8,128)(2,1)S(1)}, f32[512,512]{1,0:T(8,128)S(1)}, bf16[512,128]{1,0:T(8,128)(2,1)S(1...) custom-call(f32[512,512]{1,0:T(8,128)S(1)} %get-tuple-element.185.grad.refs_3_, ...), custom_call_target="tpu_custom_call" | custom-call | flops 1744830464 | tf_op jit(solution)/shard_map/pallas_call | solution.py:75
  113.9 2.4 %collective-permute-start.38 = (bf16[128,256]{1,0:T(8,128)(2,1)S(1)}, bf16[128,256]{1,0:T(8,128)(2,1)S(1)}, u32[]{:S(2)}, u32[]{:S(2)}) collective-permute-start(bf16[128,256]{1,0:T(8,128)(2,1)S(1)} %get-tuple-element.200), channel_id=1, source_target_pairs={{12,0},{0,4},{4,8},{8,12},{13,1},{1,5},{5,9},{9,13},{14,2},{2,6},{... | collective-permute-start | bytes 196616 | tf_op jit(solution)/shard_map/ppermute | solution.py:16
  118.7 1.9 collective-permute-done.38.refs_1_
  120.7 2.3 %collective-permute-done.39.refs_2_ = bf16[128,256]{1,0:T(8,128)(2,1)S(1)} collective-permute-done((bf16[128,256]{1,0:T(8,128)(2,1)S(1)}, bf16[128,256]{1,0:T(8,128)(2,1)S(1)}, u32[]{:S(2)}, u32[]{:S(2)}) %collective-permute-start.39) | collective-permute-done | bytes 65568 | tf_op jit(solution)/shard_map/ppermute | solution.py:16
  122.9 2.5 %collective-permute-start.36 = (bf16[512,128]{1,0:T(8,128)(2,1)S(1)}, bf16[512,128]{1,0:T(8,128)(2,1)S(1)}, u32[]{:S(2)}, u32[]{:S(2)}) collective-permute-start(bf16[512,128]{1,0:T(8,128)(2,1)S(1)} %get-tuple-element.194), channel_id=1, source_target_pairs={{4,0},{8,4},{12,8},{0,12},{5,1},{9,5},{13,9},{1,13},{6,2},{10,6},{... | collective-permute-start | bytes 393224 | tf_op jit(solution)/shard_map/ppermute | solution.py:16
  125.5 3.7 %collective-permute-done.36.refs_1_ = bf16[512,128]{1,0:T(8,128)(2,1)S(1)} collective-permute-done((bf16[512,128]{1,0:T(8,128)(2,1)S(1)}, bf16[512,128]{1,0:T(8,128)(2,1)S(1)}, u32[]{:S(2)}, u32[]{:S(2)}) %collective-permute-start.36) | collective-permute-done | bytes 131104 | tf_op jit(solution)/shard_map/ppermute | solution.py:16
  129.2 2.9 %collective-permute-done.37.refs_2_ = bf16[512,128]{1,0:T(8,128)(2,1)S(1)} collective-permute-done((bf16[512,128]{1,0:T(8,128)(2,1)S(1)}, bf16[512,128]{1,0:T(8,128)(2,1)S(1)}, u32[]{:S(2)}, u32[]{:S(2)}) %collective-permute-start.37) | collective-permute-done | bytes 131104 | tf_op jit(solution)/shard_map/ppermute | solution.py:16
  132.8 4.4 %collective-permute-done.46.refs_2_ = bf16[512,128]{1,0:T(8,128)(2,1)S(1)} collective-permute-done((bf16[512,128]{1,0:T(8,128)(2,1)S(1)}, bf16[512,128]{1,0:T(8,128)(2,1)S(1)}, u32[]{:S(2)}, u32[]{:S(2)}) %collective-permute-start.46) | collective-permute-done | bytes 131104 | tf_op jit(solution)/shard_map/ppermute | solution.py:16
  140.6 2.6 %collective-permute-start.48 = (bf16[512,128]{1,0:T(8,128)(2,1)S(1)}, bf16[512,128]{1,0:T(8,128)(2,1)S(1)}, u32[]{:S(2)}, u32[]{:S(2)}) collective-permute-start(bf16[512,128]{1,0:T(8,128)(2,1)S(1)} %get-tuple-element.215), channel_id=1, source_target_pairs={{4,0},{8,4},{12,8},{0,12},{5,1},{9,5},{13,9},{1,13},{6,2},{10,6},{... | collective-permute-start | bytes 393224 | tf_op jit(solution)/shard_map/ppermute | solution.py:16
  143.3 5.5 %shard_map.187 = (bf16[2048,256]{1,0:T(8,128)(2,1)}, bf16[2048,512]{1,0:T(8,128)(2,1)S(1)}) custom-call(bf16[2048,512]{1,0:T(8,128)(2,1)S(1)} %copy-done.5, bf16[512,512]{1,0:T(8,128)(2,1)S(1)} %copy-done.7, s32[1,2048]{1,0:T(1,128)S(1)} %bitcast.7, s32[1,2048]{1,0:T(1,128)S(1)} %bitcast.12, bf16[2048,128]{1,0:T(8,128)(2,1)S(1)} %shard_map.182.mine, ...), custom_call_target="tpu_custom_call" | custom-call | flops 3221225472 | tf_op jit(solution)/shard_map/pallas_call | solution.py:75
  149.6 2.8 %collective-permute-done.49.refs_1_ = bf16[512,128]{1,0:T(8,128)(2,1)S(1)} collective-permute-done((bf16[512,128]{1,0:T(8,128)(2,1)S(1)}, bf16[512,128]{1,0:T(8,128)(2,1)S(1)}, u32[]{:S(2)}, u32[]{:S(2)}) %collective-permute-start.49) | collective-permute-done | bytes 131104 | tf_op jit(solution)/shard_map/ppermute | solution.py:16
  153.0 2.6 %collective-permute-start.52 = (bf16[192,256]{1,0:T(8,128)(2,1)S(1)}, bf16[192,256]{1,0:T(8,128)(2,1)S(1)}, u32[]{:S(2)}, u32[]{:S(2)}) collective-permute-start(bf16[192,256]{1,0:T(8,128)(2,1)S(1)} %get-tuple-element.230), channel_id=1, source_target_pairs={{12,0},{0,4},{4,8},{8,12},{13,1},{1,5},{5,9},{9,13},{14,2},{2,6},{... | collective-permute-start | bytes 294920 | tf_op jit(solution)/shard_map/ppermute | solution.py:16
  156.3 1.8 collective-permute-start.54
  158.6 1.9 collective-permute-done.52.refs_1_
  160.6 3.8 %collective-permute-done.53.refs_2_ = bf16[192,256]{1,0:T(8,128)(2,1)S(1)} collective-permute-done((bf16[192,256]{1,0:T(8,128)(2,1)S(1)}, bf16[192,256]{1,0:T(8,128)(2,1)S(1)}, u32[]{:S(2)}, u32[]{:S(2)}) %collective-permute-start.53) | collective-permute-done | bytes 98336 | tf_op jit(solution)/shard_map/ppermute | solution.py:16
  164.4 5.0 %shard_map.192 = (bf16[2048,256]{1,0:T(8,128)(2,1)S(1)}, f32[256,256]{1,0:T(8,128)S(1)}, bf16[256,256]{1,0:T(8,128)(2,1)S(1)}) custom-call(bf16[2048,512]{1,0:T(8,128)(2,1)S(1)} %copy-done.5, s32[1,2048]{1,0:T(1,128)S(1)} %bitcast.8, s32[1,2048]{1,0:T(1,128)S(1)} %bitcast.13, bf16[2048,512]{1,0:T(8,128)(2,1)S(1)} %get-tuple-element.218.slope, ...), custom_call_target="tpu_custom_call" | custom-call | flops 2684354560 | tf_op jit(solution)/shard_map/pallas_call | solution.py:75
  170.4 2.6 %collective-permute-start.55 = (bf16[128,256]{1,0:T(8,128)(2,1)S(1)}, bf16[128,256]{1,0:T(8,128)(2,1)S(1)}, u32[]{:S(2)}, u32[]{:S(2)}) collective-permute-start(bf16[128,256]{1,0:T(8,128)(2,1)S(1)} %get-tuple-element.237), channel_id=1, source_target_pairs={{12,0},{0,4},{4,8},{8,12},{13,1},{1,5},{5,9},{9,13},{14,2},{2,6},{... | collective-permute-start | bytes 196616 | tf_op jit(solution)/shard_map/ppermute | solution.py:16
  179.4 3.6 %collective-permute-start.61 = (bf16[64,256]{1,0:T(8,128)(2,1)S(1)}, bf16[64,256]{1,0:T(8,128)(2,1)S(1)}, u32[]{:S(2)}, u32[]{:S(2)}) collective-permute-start(bf16[64,256]{1,0:T(8,128)(2,1)S(1)} %get-tuple-element.245), channel_id=1, source_target_pairs={{4,0},{8,4},{12,8},{0,12},{5,1},{9,5},{13,9},{1,13},{6,2},{10,6},{... | collective-permute-start | bytes 98312 | tf_op jit(solution)/shard_map/ppermute | solution.py:16
  185.0 4.8 %collective-permute-start.65 = (bf16[512,256]{1,0:T(8,128)(2,1)S(1)}, bf16[512,256]{1,0:T(8,128)(2,1)S(1)}, u32[]{:S(2)}, u32[]{:S(2)}) collective-permute-start(bf16[512,256]{1,0:T(8,128)(2,1)S(1)} %shard_map.199.refs_0_), channel_id=1, source_target_pairs={{8,0},{12,4},{0,8},{4,12},{9,1},{13,5},{1,9},{5,13},{10,2},{14,6},... | collective-permute-start | bytes 786440 | tf_op jit(solution)/shard_map/ppermute | solution.py:16
  189.8 6.7 %collective-permute-done.67.refs_3_ = bf16[512,256]{1,0:T(8,128)(2,1)S(1)} collective-permute-done((bf16[512,256]{1,0:T(8,128)(2,1)S(1)}, bf16[512,256]{1,0:T(8,128)(2,1)S(1)}, u32[]{:S(2)}, u32[]{:S(2)}) %collective-permute-start.67) | collective-permute-done | bytes 262176 | tf_op jit(solution)/shard_map/ppermute | solution.py:16
  196.5 8.1 %collective-permute-done.65.refs_2_ = bf16[512,256]{1,0:T(8,128)(2,1)S(1)} collective-permute-done((bf16[512,256]{1,0:T(8,128)(2,1)S(1)}, bf16[512,256]{1,0:T(8,128)(2,1)S(1)}, u32[]{:S(2)}, u32[]{:S(2)}) %collective-permute-start.65) | collective-permute-done | bytes 262176 | tf_op jit(solution)/shard_map/ppermute | solution.py:16
  205.1 6.3 %shard_map.200 = bf16[2048,256]{1,0:T(8,128)(2,1)} custom-call(s32[1,2048]{1,0:T(1,128)S(1)} %bitcast.9, s32[1,2048]{1,0:T(1,128)S(1)} %bitcast.14, bf16[2048,256]{1,0:T(8,128)(2,1)} %cotangent.1, bf16[2048,256]{1,0:T(8,128)(2,1)S(1)} %get-tuple-element.246.enc_grad, bf16[512,512]{1,0:T(8,128)(2,1)S(1)} %get-tuple-element.219.enc_all, ...), custom_call_target="tpu_custom_call" | custom-call | flops 2684354560 | tf_op jit(solution)/shard_map/pallas_call | solution.py:75
  211.5 2.2 %shard_map.201 = (f32[2,512,256]{2,1,0:T(8,128)}, f32[2,512,256]{2,1,0:T(8,128)}, f32[2,512,256]{2,1,0:T(8,128)}, f32[512,256]{1,0:T(8,128)}, f32[512,256]{1,0:T(8,128)}) custom-call(bf16[512,256]{1,0:T(8,128)(2,1)S(1)} %shard_map.199.refs_0_, bf16[512,256]{1,0:T(8,128)(2,1)S(1)} %collective-permute-done.63.refs_1_, ...), custom_call_target="tpu_custom_call" | custom-call | tf_op jit(solution)/shard_map/pallas_call | solution.py:75
  (146 shorter events, 44.8 us)
Async XLA Ops:
  8.8 11.1 %collective-permute-start.1 = (bf16[512,128]{1,0:T(8,128)(2,1)S(1)}, bf16[512,128]{1,0:T(8,128)(2,1)S(1)}, u32[]{:S(2)}, u32[]{:S(2)}) collective-permute-start(bf16[512,128]{1,0:T(8,128)(2,1)S(1)} %get-tuple-element.140), channel_id=1, source_target_pairs={{12,0},{0,4},{4,8},{8,12},{13,1},{1,5},{5,9},{9,13},{14,2},{2,6},{... | collective-permute-start | bytes 393224 | tf_op jit(solution)/shard_map/ppermute | solution.py:16
  11.8 11.5 %collective-permute-start.2 = (bf16[512,128]{1,0:T(8,128)(2,1)S(1)}, bf16[512,128]{1,0:T(8,128)(2,1)S(1)}, u32[]{:S(2)}, u32[]{:S(2)}) collective-permute-start(bf16[512,128]{1,0:T(8,128)(2,1)S(1)} %get-tuple-element.141), channel_id=1, source_target_pairs={{8,0},{12,4},{0,8},{4,12},{9,1},{13,5},{1,9},{5,13},{10,2},{14,6},... | collective-permute-start | bytes 393224 | tf_op jit(solution)/shard_map/ppermute | solution.py:16
  14.4 8.9 %collective-permute-start.3 = (bf16[512,128]{1,0:T(8,128)(2,1)S(1)}, bf16[512,128]{1,0:T(8,128)(2,1)S(1)}, u32[]{:S(2)}, u32[]{:S(2)}) collective-permute-start(bf16[512,128]{1,0:T(8,128)(2,1)S(1)} %get-tuple-element.142), channel_id=1, source_target_pairs={{4,0},{8,4},{12,8},{0,12},{5,1},{9,5},{13,9},{1,13},{6,2},{10,6},{... | collective-permute-start | bytes 393224 | tf_op jit(solution)/shard_map/ppermute | solution.py:16
  19.8 15.1 %collective-permute-start.10 = (bf16[2048,128]{1,0:T(8,128)(2,1)S(1)}, bf16[2048,128]{1,0:T(8,128)(2,1)S(1)}, u32[]{:S(2)}, u32[]{:S(2)}) collective-permute-start(bf16[2048,128]{1,0:T(8,128)(2,1)S(1)} %get-tuple-element.154), channel_id=1, source_target_pairs={{1,0},{0,1},{3,2},{2,3},{5,4},{4,5},{7,6},{6,7},{9,8},{8,9},{11,10... | collective-permute-start | bytes 1572872 | tf_op jit(solution)/shard_map/ppermute | solution.py:16
  30.9 7.9 %collective-permute-start.9 = (bf16[512,128]{1,0:T(8,128)(2,1)S(1)}, bf16[512,128]{1,0:T(8,128)(2,1)S(1)}, u32[]{:S(2)}, u32[]{:S(2)}) collective-permute-start(bf16[512,128]{1,0:T(8,128)(2,1)S(1)} %get-tuple-element.151.own), channel_id=1, source_target_pairs={{4,0},{8,4},{12,8},{0,12},{5,1},{9,5},{13,9},{1,13},{6,2},{10,6},{... | collective-permute-start | bytes 393224 | tf_op jit(solution)/shard_map/ppermute | solution.py:16
  34.9 7.4 %collective-permute-start.8 = (bf16[512,128]{1,0:T(8,128)(2,1)S(1)}, bf16[512,128]{1,0:T(8,128)(2,1)S(1)}, u32[]{:S(2)}, u32[]{:S(2)}) collective-permute-start(bf16[512,128]{1,0:T(8,128)(2,1)S(1)} %get-tuple-element.151.own), channel_id=1, source_target_pairs={{12,0},{0,4},{4,8},{8,12},{13,1},{1,5},{5,9},{9,13},{14,2},{2,6},{... | collective-permute-start | bytes 393224 | tf_op jit(solution)/shard_map/ppermute | solution.py:16
  42.3 8.3 %collective-permute-start.16 = (bf16[512,128]{1,0:T(8,128)(2,1)S(1)}, bf16[512,128]{1,0:T(8,128)(2,1)S(1)}, u32[]{:S(2)}, u32[]{:S(2)}) collective-permute-start(bf16[512,128]{1,0:T(8,128)(2,1)S(1)} %get-tuple-element.167), channel_id=1, source_target_pairs={{12,0},{0,4},{4,8},{8,12},{13,1},{1,5},{5,9},{9,13},{14,2},{2,6},{... | collective-permute-start | bytes 393224 | tf_op jit(solution)/shard_map/ppermute | solution.py:16
  43.5 10.8 %collective-permute-start.17 = (bf16[512,128]{1,0:T(8,128)(2,1)S(1)}, bf16[512,128]{1,0:T(8,128)(2,1)S(1)}, u32[]{:S(2)}, u32[]{:S(2)}) collective-permute-start(bf16[512,128]{1,0:T(8,128)(2,1)S(1)} %get-tuple-element.168), channel_id=1, source_target_pairs={{8,0},{12,4},{0,8},{4,12},{9,1},{13,5},{1,9},{5,13},{10,2},{14,6},... | collective-permute-start | bytes 393224 | tf_op jit(solution)/shard_map/ppermute | solution.py:16
  44.3 10.0 %collective-permute-start.18 = (bf16[512,128]{1,0:T(8,128)(2,1)S(1)}, bf16[512,128]{1,0:T(8,128)(2,1)S(1)}, u32[]{:S(2)}, u32[]{:S(2)}) collective-permute-start(bf16[512,128]{1,0:T(8,128)(2,1)S(1)} %get-tuple-element.169), channel_id=1, source_target_pairs={{4,0},{8,4},{12,8},{0,12},{5,1},{9,5},{13,9},{1,13},{6,2},{10,6},{... | collective-permute-start | bytes 393224 | tf_op jit(solution)/shard_map/ppermute | solution.py:16
  48.7 7.2 %collective-permute-start.12 = (bf16[512,128]{1,0:T(8,128)(2,1)S(1)}, bf16[512,128]{1,0:T(8,128)(2,1)S(1)}, u32[]{:S(2)}, u32[]{:S(2)}) collective-permute-start(bf16[512,128]{1,0:T(8,128)(2,1)S(1)} %get-tuple-element.163.refs_0_), channel_id=1, source_target_pairs={{2,0},{0,2},{3,1},{1,3},{6,4},{4,6},{7,5},{5,7},{10,8},{8,10},{11,... | collective-permute-start | bytes 393224 | tf_op jit(solution)/shard_map/ppermute | solution.py:16
  56.5 7.9 %collective-permute-start.19 = (bf16[512,128]{1,0:T(8,128)(2,1)S(1)}, bf16[512,128]{1,0:T(8,128)(2,1)S(1)}, u32[]{:S(2)}, u32[]{:S(2)}) collective-permute-start(bf16[512,128]{1,0:T(8,128)(2,1)S(1)} %shard_map.179.refs_4_), channel_id=1, source_target_pairs={{1,0},{0,1},{3,2},{2,3},{5,4},{4,5},{7,6},{6,7},{9,8},{8,9},{11,10... | collective-permute-start | bytes 393224 | tf_op jit(solution)/shard_map/ppermute | solution.py:16
  60.6 7.7 %collective-permute-start.15 = (bf16[512,128]{1,0:T(8,128)(2,1)S(1)}, bf16[512,128]{1,0:T(8,128)(2,1)S(1)}, u32[]{:S(2)}, u32[]{:S(2)}) collective-permute-start(bf16[512,128]{1,0:T(8,128)(2,1)S(1)} %get-tuple-element.165.own), channel_id=1, source_target_pairs={{4,0},{8,4},{12,8},{0,12},{5,1},{9,5},{13,9},{1,13},{6,2},{10,6},{... | collective-permute-start | bytes 393224 | tf_op jit(solution)/shard_map/ppermute | solution.py:16
  64.4 7.5 %collective-permute-start.14 = (bf16[512,128]{1,0:T(8,128)(2,1)S(1)}, bf16[512,128]{1,0:T(8,128)(2,1)S(1)}, u32[]{:S(2)}, u32[]{:S(2)}) collective-permute-start(bf16[512,128]{1,0:T(8,128)(2,1)S(1)} %get-tuple-element.165.own), channel_id=1, source_target_pairs={{12,0},{0,4},{4,8},{8,12},{13,1},{1,5},{5,9},{9,13},{14,2},{2,6},{... | collective-permute-start | bytes 393224 | tf_op jit(solution)/shard_map/ppermute | solution.py:16
  85.1 10.5 %collective-permute-start.27 = (bf16[512,128]{1,0:T(8,128)(2,1)S(1)}, bf16[512,128]{1,0:T(8,128)(2,1)S(1)}, u32[]{:S(2)}, u32[]{:S(2)}) collective-permute-start(bf16[512,128]{1,0:T(8,128)(2,1)S(1)} %get-tuple-element.190.refs_4_), channel_id=1, source_target_pairs={{1,0},{0,1},{3,2},{2,3},{5,4},{4,5},{7,6},{6,7},{9,8},{8,9},{11,10... | collective-permute-start | bytes 393224 | tf_op jit(solution)/shard_map/ppermute | solution.py:16
  87.0 8.6 %collective-permute-start.26 = (bf16[512,128]{1,0:T(8,128)(2,1)S(1)}, bf16[512,128]{1,0:T(8,128)(2,1)S(1)}, u32[]{:S(2)}, u32[]{:S(2)}) collective-permute-start(bf16[512,128]{1,0:T(8,128)(2,1)S(1)} %get-tuple-element.181), channel_id=1, source_target_pairs={{12,0},{0,4},{4,8},{8,12},{13,1},{1,5},{5,9},{9,13},{14,2},{2,6},{... | collective-permute-start | bytes 393224 | tf_op jit(solution)/shard_map/ppermute | solution.py:16
  89.2 6.4 %collective-permute-start.29 = (bf16[512,128]{1,0:T(8,128)(2,1)S(1)}, bf16[512,128]{1,0:T(8,128)(2,1)S(1)}, u32[]{:S(2)}, u32[]{:S(2)}) collective-permute-start(bf16[512,128]{1,0:T(8,128)(2,1)S(1)} %collective-permute-done.28.refs_6_), channel_id=1, source_target_pairs={{1,0},{0,1},{3,2},{2,3},{5,4},{4,5},{7,6},{6,7},{9,8},{8,9},{11,10... | collective-permute-start | bytes 393224 | tf_op jit(solution)/shard_map/ppermute | solution.py:16
  96.3 8.3 %collective-permute-start.32 = (bf16[512,128]{1,0:T(8,128)(2,1)S(1)}, bf16[512,128]{1,0:T(8,128)(2,1)S(1)}, u32[]{:S(2)}, u32[]{:S(2)}) collective-permute-start(bf16[512,128]{1,0:T(8,128)(2,1)S(1)} %get-tuple-element.184.refs_0_), channel_id=1, source_target_pairs={{12,0},{0,4},{4,8},{8,12},{13,1},{1,5},{5,9},{9,13},{14,2},{2,6},{... | collective-permute-start | bytes 393224 | tf_op jit(solution)/shard_map/ppermute | solution.py:16
  96.4 12.3 %collective-permute-start.31 = (bf16[512,128]{1,0:T(8,128)(2,1)S(1)}, bf16[512,128]{1,0:T(8,128)(2,1)S(1)}, u32[]{:S(2)}, u32[]{:S(2)}) collective-permute-start(bf16[512,128]{1,0:T(8,128)(2,1)S(1)} %get-tuple-element.184.refs_0_), channel_id=1, source_target_pairs={{8,0},{12,4},{0,8},{4,12},{9,1},{13,5},{1,9},{5,13},{10,2},{14,6},... | collective-permute-start | bytes 393224 | tf_op jit(solution)/shard_map/ppermute | solution.py:16
  98.6 10.1 %collective-permute-start.30 = (bf16[512,128]{1,0:T(8,128)(2,1)S(1)}, bf16[512,128]{1,0:T(8,128)(2,1)S(1)}, u32[]{:S(2)}, u32[]{:S(2)}) collective-permute-start(bf16[512,128]{1,0:T(8,128)(2,1)S(1)} %get-tuple-element.184.refs_0_), channel_id=1, source_target_pairs={{4,0},{8,4},{12,8},{0,12},{5,1},{9,5},{13,9},{1,13},{6,2},{10,6},{... | collective-permute-start | bytes 393224 | tf_op jit(solution)/shard_map/ppermute | solution.py:16
  100.1 8.7 %collective-permute-start.33 = (bf16[512,128]{1,0:T(8,128)(2,1)S(1)}, bf16[512,128]{1,0:T(8,128)(2,1)S(1)}, u32[]{:S(2)}, u32[]{:S(2)}) collective-permute-start(bf16[512,128]{1,0:T(8,128)(2,1)S(1)} %shard_map.183.refs_0_), channel_id=1, source_target_pairs={{1,0},{0,1},{3,2},{2,3},{5,4},{4,5},{7,6},{6,7},{9,8},{8,9},{11,10... | collective-permute-start | bytes 393224 | tf_op jit(solution)/shard_map/ppermute | solution.py:16
  100.8 8.0 %collective-permute-start.35 = (bf16[512,128]{1,0:T(8,128)(2,1)S(1)}, bf16[512,128]{1,0:T(8,128)(2,1)S(1)}, u32[]{:S(2)}, u32[]{:S(2)}) collective-permute-start(bf16[512,128]{1,0:T(8,128)(2,1)S(1)} %collective-permute-done.34.refs_2_), channel_id=1, source_target_pairs={{1,0},{0,1},{3,2},{2,3},{5,4},{4,5},{7,6},{6,7},{9,8},{8,9},{11,10... | collective-permute-start | bytes 393224 | tf_op jit(solution)/shard_map/ppermute | solution.py:16
  108.7 23.4 %collective-permute-start.41 = (bf16[2048,128]{1,0:T(8,128)(2,1)S(1)}, bf16[2048,128]{1,0:T(8,128)(2,1)S(1)}, u32[]{:S(2)}, u32[]{:S(2)}) collective-permute-start(bf16[2048,128]{1,0:T(8,128)(2,1)S(1)} %shard_map.182.mine), channel_id=1, source_target_pairs={{1,0},{0,1},{3,2},{2,3},{5,4},{4,5},{7,6},{6,7},{9,8},{8,9},{11,10... | collective-permute-start | bytes 1572872 | tf_op jit(solution)/shard_map/ppermute | solution.py:16
  111.9 13.5 %collective-permute-start.43 = (bf16[512,128]{1,0:T(8,128)(2,1)S(1)}, bf16[512,128]{1,0:T(8,128)(2,1)S(1)}, u32[]{:S(2)}, u32[]{:S(2)}) collective-permute-start(bf16[512,128]{1,0:T(8,128)(2,1)S(1)} %get-tuple-element.211.refs_4_), channel_id=1, source_target_pairs={{2,0},{0,2},{3,1},{1,3},{6,4},{4,6},{7,5},{5,7},{10,8},{8,10},{11,... | collective-permute-start | bytes 393224 | tf_op jit(solution)/shard_map/ppermute | solution.py:16
  113.9 6.8 %collective-permute-start.38 = (bf16[128,256]{1,0:T(8,128)(2,1)S(1)}, bf16[128,256]{1,0:T(8,128)(2,1)S(1)}, u32[]{:S(2)}, u32[]{:S(2)}) collective-permute-start(bf16[128,256]{1,0:T(8,128)(2,1)S(1)} %get-tuple-element.200), channel_id=1, source_target_pairs={{12,0},{0,4},{4,8},{8,12},{13,1},{1,5},{5,9},{9,13},{14,2},{2,6},{... | collective-permute-start | bytes 196616 | tf_op jit(solution)/shard_map/ppermute | solution.py:16
  116.3 6.7 %collective-permute-start.39 = (bf16[128,256]{1,0:T(8,128)(2,1)S(1)}, bf16[128,256]{1,0:T(8,128)(2,1)S(1)}, u32[]{:S(2)}, u32[]{:S(2)}) collective-permute-start(bf16[128,256]{1,0:T(8,128)(2,1)S(1)} %get-tuple-element.201), channel_id=1, source_target_pairs={{8,0},{12,4},{0,8},{4,12},{9,1},{13,5},{1,9},{5,13},{10,2},{14,6},... | collective-permute-start | bytes 196616 | tf_op jit(solution)/shard_map/ppermute | solution.py:16
  117.2 8.2 %collective-permute-start.40 = (bf16[128,256]{1,0:T(8,128)(2,1)S(1)}, bf16[128,256]{1,0:T(8,128)(2,1)S(1)}, u32[]{:S(2)}, u32[]{:S(2)}) collective-permute-start(bf16[128,256]{1,0:T(8,128)(2,1)S(1)} %get-tuple-element.202), channel_id=1, source_target_pairs={{4,0},{8,4},{12,8},{0,12},{5,1},{9,5},{13,9},{1,13},{6,2},{10,6},{... | collective-permute-start | bytes 196616 | tf_op jit(solution)/shard_map/ppermute | solution.py:16
  120.6 11.5 %collective-permute-start.42 = (bf16[512,128]{1,0:T(8,128)(2,1)S(1)}, bf16[512,128]{1,0:T(8,128)(2,1)S(1)}, u32[]{:S(2)}, u32[]{:S(2)}) collective-permute-start(bf16[512,128]{1,0:T(8,128)(2,1)S(1)} %get-tuple-element.211.refs_4_), channel_id=1, source_target_pairs={{1,0},{0,1},{3,2},{2,3},{5,4},{4,5},{7,6},{6,7},{9,8},{8,9},{11,10... | collective-permute-start | bytes 393224 | tf_op jit(solution)/shard_map/ppermute | solution.py:16
  125.4 6.8 %collective-permute-start.37 = (bf16[512,128]{1,0:T(8,128)(2,1)S(1)}, bf16[512,128]{1,0:T(8,128)(2,1)S(1)}, u32[]{:S(2)}, u32[]{:S(2)}) collective-permute-start(bf16[512,128]{1,0:T(8,128)(2,1)S(1)} %get-tuple-element.195), channel_id=1, source_target_pairs={{12,0},{0,4},{4,8},{8,12},{13,1},{1,5},{5,9},{9,13},{14,2},{2,6},{... | collective-permute-start | bytes 393224 | tf_op jit(solution)/shard_map/ppermute | solution.py:16
  125.4 6.8 %collective-permute-start.44 = (bf16[512,128]{1,0:T(8,128)(2,1)S(1)}, bf16[512,128]{1,0:T(8,128)(2,1)S(1)}, u32[]{:S(2)}, u32[]{:S(2)}) collective-permute-start(bf16[512,128]{1,0:T(8,128)(2,1)S(1)} %collective-permute-done.43.refs_6_), channel_id=1, source_target_pairs={{1,0},{0,1},{3,2},{2,3},{5,4},{4,5},{7,6},{6,7},{9,8},{8,9},{11,10... | collective-permute-start | bytes 393224 | tf_op jit(solution)/shard_map/ppermute | solution.py:16
  139.4 10.2 %collective-permute-start.50 = (bf16[512,128]{1,0:T(8,128)(2,1)S(1)}, bf16[512,128]{1,0:T(8,128)(2,1)S(1)}, u32[]{:S(2)}, u32[]{:S(2)}) collective-permute-start(bf16[512,128]{1,0:T(8,128)(2,1)S(1)} %get-tuple-element.215), channel_id=1, source_target_pairs={{12,0},{0,4},{4,8},{8,12},{13,1},{1,5},{5,9},{9,13},{14,2},{2,6},{... | collective-permute-start | bytes 393224 | tf_op jit(solution)/shard_map/ppermute | solution.py:16
  139.5 13.0 %collective-permute-start.49 = (bf16[512,128]{1,0:T(8,128)(2,1)S(1)}, bf16[512,128]{1,0:T(8,128)(2,1)S(1)}, u32[]{:S(2)}, u32[]{:S(2)}) collective-permute-start(bf16[512,128]{1,0:T(8,128)(2,1)S(1)} %get-tuple-element.215), channel_id=1, source_target_pairs={{8,0},{12,4},{0,8},{4,12},{9,1},{13,5},{1,9},{5,13},{10,2},{14,6},... | collective-permute-start | bytes 393224 | tf_op jit(solution)/shard_map/ppermute | solution.py:16
  140.6 11.8 %collective-permute-start.48 = (bf16[512,128]{1,0:T(8,128)(2,1)S(1)}, bf16[512,128]{1,0:T(8,128)(2,1)S(1)}, u32[]{:S(2)}, u32[]{:S(2)}) collective-permute-start(bf16[512,128]{1,0:T(8,128)(2,1)S(1)} %get-tuple-element.215), channel_id=1, source_target_pairs={{4,0},{8,4},{12,8},{0,12},{5,1},{9,5},{13,9},{1,13},{6,2},{10,6},{... | collective-permute-start | bytes 393224 | tf_op jit(solution)/shard_map/ppermute | solution.py:16
  152.5 12.0 %collective-permute-start.51 = (bf16[1536,128]{1,0:T(8,128)(2,1)S(1)}, bf16[1536,128]{1,0:T(8,128)(2,1)S(1)}, u32[]{:S(2)}, u32[]{:S(2)}) collective-permute-start(bf16[1536,128]{1,0:T(8,128)(2,1)S(1)} %shard_map.191.mine), channel_id=1, source_target_pairs={{1,0},{0,1},{3,2},{2,3},{5,4},{4,5},{7,6},{6,7},{9,8},{8,9},{11,10... | collective-permute-start | bytes 1179656 | tf_op jit(solution)/shard_map/ppermute | solution.py:16
  153.0 7.5 %collective-permute-start.52 = (bf16[192,256]{1,0:T(8,128)(2,1)S(1)}, bf16[192,256]{1,0:T(8,128)(2,1)S(1)}, u32[]{:S(2)}, u32[]{:S(2)}) collective-permute-start(bf16[192,256]{1,0:T(8,128)(2,1)S(1)} %get-tuple-element.230), channel_id=1, source_target_pairs={{12,0},{0,4},{4,8},{8,12},{13,1},{1,5},{5,9},{9,13},{14,2},{2,6},{... | collective-permute-start | bytes 294920 | tf_op jit(solution)/shard_map/ppermute | solution.py:16
  155.7 8.7 %collective-permute-start.53 = (bf16[192,256]{1,0:T(8,128)(2,1)S(1)}, bf16[192,256]{1,0:T(8,128)(2,1)S(1)}, u32[]{:S(2)}, u32[]{:S(2)}) collective-permute-start(bf16[192,256]{1,0:T(8,128)(2,1)S(1)} %get-tuple-element.231), channel_id=1, source_target_pairs={{8,0},{12,4},{0,8},{4,12},{9,1},{13,5},{1,9},{5,13},{10,2},{14,6},... | collective-permute-start | bytes 294920 | tf_op jit(solution)/shard_map/ppermute | solution.py:16
  156.3 8.1 %collective-permute-start.54 = (bf16[192,256]{1,0:T(8,128)(2,1)S(1)}, bf16[192,256]{1,0:T(8,128)(2,1)S(1)}, u32[]{:S(2)}, u32[]{:S(2)}) collective-permute-start(bf16[192,256]{1,0:T(8,128)(2,1)S(1)} %get-tuple-element.232), channel_id=1, source_target_pairs={{4,0},{8,4},{12,8},{0,12},{5,1},{9,5},{13,9},{1,13},{6,2},{10,6},{... | collective-permute-start | bytes 294920 | tf_op jit(solution)/shard_map/ppermute | solution.py:16
  158.1 11.4 %collective-permute-start.69 = (bf16[1536,128]{1,0:T(8,128)(2,1)S(1)}, bf16[1536,128]{1,0:T(8,128)(2,1)S(1)}, u32[]{:S(2)}, u32[]{:S(2)}) collective-permute-start(bf16[1536,128]{1,0:T(8,128)(2,1)S(1)} %shard_map.191.mine), channel_id=1, source_target_pairs={{2,0},{0,2},{3,1},{1,3},{6,4},{4,6},{7,5},{5,7},{10,8},{8,10},{11,... | collective-permute-start | bytes 1179656 | tf_op jit(solution)/shard_map/ppermute | solution.py:16
  169.5 35.6 %collective-permute-start.70 = (bf16[1536,128]{1,0:T(8,128)(2,1)S(1)}, bf16[1536,128]{1,0:T(8,128)(2,1)S(1)}, u32[]{:S(2)}, u32[]{:S(2)}) collective-permute-start(bf16[1536,128]{1,0:T(8,128)(2,1)S(1)} %collective-permute-done.69.refs_0_), channel_id=1, source_target_pairs={{1,0},{0,1},{3,2},{2,3},{5,4},{4,5},{7,6},{6,7},{9,8},{8,9},{11,10... | collective-permute-start | bytes 1179656 | tf_op jit(solution)/shard_map/ppermute | solution.py:16
  170.4 6.5 %collective-permute-start.55 = (bf16[128,256]{1,0:T(8,128)(2,1)S(1)}, bf16[128,256]{1,0:T(8,128)(2,1)S(1)}, u32[]{:S(2)}, u32[]{:S(2)}) collective-permute-start(bf16[128,256]{1,0:T(8,128)(2,1)S(1)} %get-tuple-element.237), channel_id=1, source_target_pairs={{12,0},{0,4},{4,8},{8,12},{13,1},{1,5},{5,9},{9,13},{14,2},{2,6},{... | collective-permute-start | bytes 196616 | tf_op jit(solution)/shard_map/ppermute | solution.py:16
  174.5 8.6 %collective-permute-start.57 = (bf16[128,256]{1,0:T(8,128)(2,1)S(1)}, bf16[128,256]{1,0:T(8,128)(2,1)S(1)}, u32[]{:S(2)}, u32[]{:S(2)}) collective-permute-start(bf16[128,256]{1,0:T(8,128)(2,1)S(1)} %get-tuple-element.239), channel_id=1, source_target_pairs={{4,0},{8,4},{12,8},{0,12},{5,1},{9,5},{13,9},{1,13},{6,2},{10,6},{... | collective-permute-start | bytes 196616 | tf_op jit(solution)/shard_map/ppermute | solution.py:16
  175.5 7.6 %collective-permute-start.59 = (bf16[64,256]{1,0:T(8,128)(2,1)S(1)}, bf16[64,256]{1,0:T(8,128)(2,1)S(1)}, u32[]{:S(2)}, u32[]{:S(2)}) collective-permute-start(bf16[64,256]{1,0:T(8,128)(2,1)S(1)} %get-tuple-element.243), channel_id=1, source_target_pairs={{12,0},{0,4},{4,8},{8,12},{13,1},{1,5},{5,9},{9,13},{14,2},{2,6},{... | collective-permute-start | bytes 98312 | tf_op jit(solution)/shard_map/ppermute | solution.py:16
  184.9 11.6 %collective-permute-start.67 = (bf16[512,256]{1,0:T(8,128)(2,1)S(1)}, bf16[512,256]{1,0:T(8,128)(2,1)S(1)}, u32[]{:S(2)}, u32[]{:S(2)}) collective-permute-start(bf16[512,256]{1,0:T(8,128)(2,1)S(1)} %shard_map.199.refs_0_), channel_id=1, source_target_pairs={{12,0},{0,4},{4,8},{8,12},{13,1},{1,5},{5,9},{9,13},{14,2},{2,6},{... | collective-permute-start | bytes 786440 | tf_op jit(solution)/shard_map/ppermute | solution.py:16
  185.0 19.6 %collective-permute-start.65 = (bf16[512,256]{1,0:T(8,128)(2,1)S(1)}, bf16[512,256]{1,0:T(8,128)(2,1)S(1)}, u32[]{:S(2)}, u32[]{:S(2)}) collective-permute-start(bf16[512,256]{1,0:T(8,128)(2,1)S(1)} %shard_map.199.refs_0_), channel_id=1, source_target_pairs={{8,0},{12,4},{0,8},{4,12},{9,1},{13,5},{1,9},{5,13},{10,2},{14,6},... | collective-permute-start | bytes 786440 | tf_op jit(solution)/shard_map/ppermute | solution.py:16
  189.8 14.8 %collective-permute-start.63 = (bf16[512,256]{1,0:T(8,128)(2,1)S(1)}, bf16[512,256]{1,0:T(8,128)(2,1)S(1)}, u32[]{:S(2)}, u32[]{:S(2)}) collective-permute-start(bf16[512,256]{1,0:T(8,128)(2,1)S(1)} %shard_map.199.refs_0_), channel_id=1, source_target_pairs={{4,0},{8,4},{12,8},{0,12},{5,1},{9,5},{13,9},{1,13},{6,2},{10,6},{... | collective-permute-start | bytes 786440 | tf_op jit(solution)/shard_map/ppermute | solution.py:16
  189.8 21.7 %collective-permute-start.62 = (bf16[512,256]{1,0:T(8,128)(2,1)S(1)}, bf16[512,256]{1,0:T(8,128)(2,1)S(1)}, u32[]{:S(2)}, u32[]{:S(2)}) collective-permute-start(bf16[512,256]{1,0:T(8,128)(2,1)S(1)} %shard_map.199.refs_0_), channel_id=1, source_target_pairs={{1,0},{0,1},{3,2},{2,3},{5,4},{4,5},{7,6},{6,7},{9,8},{8,9},{11,10... | collective-permute-start | bytes 786440 | tf_op jit(solution)/shard_map/ppermute | solution.py:16
  196.5 14.9 %collective-permute-start.68 = (bf16[512,256]{1,0:T(8,128)(2,1)S(1)}, bf16[512,256]{1,0:T(8,128)(2,1)S(1)}, u32[]{:S(2)}, u32[]{:S(2)}) collective-permute-start(bf16[512,256]{1,0:T(8,128)(2,1)S(1)} %collective-permute-done.67.refs_3_), channel_id=1, source_target_pairs={{1,0},{0,1},{3,2},{2,3},{5,4},{4,5},{7,6},{6,7},{9,8},{8,9},{11,10... | collective-permute-start | bytes 786440 | tf_op jit(solution)/shard_map/ppermute | solution.py:16
  204.6 6.9 %collective-permute-start.66 = (bf16[512,256]{1,0:T(8,128)(2,1)S(1)}, bf16[512,256]{1,0:T(8,128)(2,1)S(1)}, u32[]{:S(2)}, u32[]{:S(2)}) collective-permute-start(bf16[512,256]{1,0:T(8,128)(2,1)S(1)} %collective-permute-done.65.refs_2_), channel_id=1, source_target_pairs={{1,0},{0,1},{3,2},{2,3},{5,4},{4,5},{7,6},{6,7},{9,8},{8,9},{11,10... | collective-permute-start | bytes 786440 | tf_op jit(solution)/shard_map/ppermute | solution.py:16
  204.6 6.9 %collective-permute-start.64 = (bf16[512,256]{1,0:T(8,128)(2,1)S(1)}, bf16[512,256]{1,0:T(8,128)(2,1)S(1)}, u32[]{:S(2)}, u32[]{:S(2)}) collective-permute-start(bf16[512,256]{1,0:T(8,128)(2,1)S(1)} %collective-permute-done.63.refs_1_), channel_id=1, source_target_pairs={{1,0},{0,1},{3,2},{2,3},{5,4},{4,5},{7,6},{6,7},{9,8},{8,9},{11,10... | collective-permute-start | bytes 786440 | tf_op jit(solution)/shard_map/ppermute | solution.py:16
  (33 other events, 239.5 us)

commit v5 on v4

--- a/solution.py
+++ b/solution.py
@@ -465,6 +465,9 @@
     edge_flops = 6 * mesh_rows * mesh_rows * nbrs * part
     parts_count = 2 * chan_count
 
+    near = [k for k in range(1, faces) if k in (1, faces - 1)]
+    far = [k for k in range(1, faces) if k not in near]
+
     def join(keep, give):
         return run(join_body, (keep, shifted(give, "pipe", 1)), [(block, BF16)] * faces)
 
@@ -489,12 +492,13 @@
         spot_body, (links, shifted(links, "pipe", 1)),
         [((mesh_rows, 8), jnp.int32), ((1, nbrs * mesh_rows), jnp.int32)],
     )
+    state_part, spot, spot_row = tie((state_part, spot, spot_row))
     keep, give = run(
         on(sum_by_node, mesh_rows), (*ids, cotangent_late), sums, flops=sum_flops,
         vmem=grid_vmem, loads=(2,),
     )
     back_blocks = join(keep, give)
-    *parts, spot, spot_row = tie((*face_parts(state_part), spot, spot_row))
+    parts = face_parts(state_part)
 
     def edges(send_p, recv_p, below, above):
         return run(
@@ -507,16 +511,20 @@
         first_body, (w_send, w_recv, *parts),
         [(full, BF16), (block, BF16), (block, F32)], flops=4 * mesh_rows * wide * part,
     )
-    below, above, *back_blocks = tie((*neighbours(send_p), *back_blocks))
-    agg, slope_0 = edges(send_p, recv_p, below, above)
+    agg, slope_0 = edges(send_p, recv_p, *neighbours(send_p))
+    agg, *back_blocks = tie((agg, *back_blocks))
+    back_near = [shifted(back_blocks[k], "space", -k) for k in near]
+    outs = tie((*face_parts(agg), *back_near))
+    agg_parts, back_near = outs[:parts_count], outs[parts_count:]
     agg_0, state_1, send_p, recv_p = run(
-        next_body, (state_0, w_node, w_send, w_recv, *face_parts(agg)),
+        next_body, (state_0, w_node, w_send, w_recv, *agg_parts),
         [(full, BF16), (full, F32), (block, BF16), (block, F32)],
         flops=2 * mesh_rows * wide * wide,
     )
-    back_own = add([back_blocks[0], *over_faces(back_blocks, -1)])
-    below, above, *back_parts = tie((*neighbours(send_p), *face_parts(back_own)))
+    back_far = [shifted(back_blocks[k], "space", -k) for k in far]
+    below, above, *back_far = tie((*neighbours(send_p), *back_far))
     agg, slope_1 = edges(send_p, recv_p, below, above)
+    back_parts = face_parts(add([back_blocks[0], *back_near, *back_far]))
     back_outs = [(full, F32), (block, BF16), (block, BF16), (block, F32), (block, BF16)]
     back_scratch = [pltpu.VMEM((nbrs * mesh_rows, 2 * part), BF16)]
     agg_1, last_b, dec_part, dec_grad, grad_2, recv_grad, below, own, above = run(
@@ -538,10 +546,11 @@
         return [piece] + [shifted(piece, "space", k) for k in range(1, faces)]
 
     recv_parts = face_parts(recv_grad)
-    sums_a = weights((last_b, dec_grad, agg_1, grad_2), ((0, 1), (2, 3)))
     below, above = shifted(below, "space", 1), shifted(above, "space", -1)
     below, above, dec_part, *recv_parts = tie((below, above, dec_part, *recv_parts))
-    send_parts = face_parts(add([own, below, above]))
+    dec_near = [shifted(dec_part, "space", k) for k in near]
+    outs = tie((*face_parts(add([own, below, above])), *dec_near))
+    send_parts, dec_near = outs[:parts_count], outs[parts_count:]
     send_1, recv_1, grad_1, recv_grad, below, own, above = run(
         on(back_body, parts_count),
         (grad_2, w_send, w_recv, w_node, slope_0, spot, spot_row, *send_parts, *recv_parts),
@@ -550,14 +559,14 @@
     )
 
     recv_parts = face_parts(recv_grad)
-    sums_b = weights((state_1, send_1, recv_1, agg_0, grad_1), ((0, 1), (0, 2), (3, 4)))
-    dec_mine = stack(from_owners(dec_part))
+    below, above = shifted(below, "space", 1), shifted(above, "space", -1)
+    below, above, dec_last, *recv_parts = tie((below, above, dec_part, *recv_parts))
+    dec_far = [shifted(dec_last, "space", k) for k in far]
+    outs = tie((*face_parts(add([own, below, above])), *dec_far))
+    send_parts, dec_far = outs[:parts_count], outs[parts_count:]
+    dec_all = dict(zip(near + far, [*dec_near, *dec_far]))
+    dec_mine = stack([dec_part] + [dec_all[k] for k in range(1, faces)])
     dec_other = shifted(dec_mine, "pipe", 1)
-    below, above = shifted(below, "space", 1), shifted(above, "space", -1)
-    below, above, sums_a, dec_other, *recv_parts = tie(
-        (below, above, sums_a, dec_other, *recv_parts)
-    )
-    send_parts = face_parts(add([own, below, above]))
     send_0, recv_0, grad_0, enc_part, enc_all = run(
         on(last_body, parts_count, mix_scale), (grad_1, w_send, w_recv, *send_parts, *recv_parts),
         [(full, BF16), (full, BF16), (full, F32), (block, BF16), (full, BF16)],
@@ -565,7 +574,11 @@
     )
 
     enc_got = from_owners(enc_part)[1:]
-    sums_c = weights((state_0, send_0, recv_0), ((0, 1), (0, 2)))
+    sums_b = weights(
+        (state_1, send_1, recv_1, agg_0, grad_1, state_0, send_0, recv_0)
+        + (last_b, dec_grad, agg_1, grad_2),
+        ((0, 1), (0, 2), (3, 4), (5, 6), (5, 7), (8, 9), (10, 11)),
+    )
     grad_mesh, = run(pick_body, (grad_0,), [((mesh_rows, narrow), F32)], hbm=(0,))
     table = [pltpu.VMEM((mesh_all, narrow), BF16), pltpu.VMEM((1, grid_rows), jnp.int32)]
     mixed, slope_enc = run(
@@ -582,18 +595,17 @@
         scratch=table + [pltpu.VMEM((wide, narrow), F32)],
         flops=sum_flops + 2 * grid_rows * wide * narrow, vmem=grid_vmem,
     )
-    enc_grad, grad_keep, grad_give, sums_b = tie((enc_grad, grad_keep, grad_give, sums_b))
     sums_g = run(
         cores_body, (grad_keep, shifted(grad_give, "pipe", 1)),
         [((half // faces, narrow), BF16)] * faces, scratch=[pltpu.VMEM((half, narrow), F32)],
     )
+    *sums_g, sums_b = tie((*sums_g, sums_b))
     sums_g = add([sums_g[0], *over_faces(sums_g, -1)])
-    sums_all = (sums_a, sums_b, sums_c, sums_g)
+    sums_all = (sums_b, sums_g)
     reduced, = run(
         stack_all_body, sums_all, [((sum(a.shape[0] for a in sums_all), narrow), BF16)]
     )
     reduced = from_owners(reduced)
-    reduced_other = [shifted(piece, "pipe", 1) for piece in reduced]
     others = chan_count - 1
     pieces = face_parts(enc_mine)[2:]
     grad_grid, = run(
@@ -603,10 +615,11 @@
         scratch=[pltpu.VMEM((mesh_all, narrow * others), BF16), table[1]],
         flops=(sum_flops + 4 * grid_rows * narrow * narrow) * others, vmem=grid_vmem + 4, hbm=(0,),
     )
-    *reduced_other, grad_grid = tie((*reduced_other, grad_grid))
+    *reduced, grad_grid = tie((*reduced, grad_grid))
+    reduced_other = [shifted(piece, "pipe", 1) for piece in reduced]
     layer_shape = ((w_send.shape[0], wide, narrow), F32)
     places = (
-        ((3, None), (2, 1)), ((0, 1), (1, 1), (2, 0)), ((0, 0), (1, 0)), ((4, None),),
+        ((0, 1), (1, 1), (2, 0), (0, 0), (1, 0), (3, None), (2, 1)), ((4, None),),
     )
     grad_w_send, grad_w_recv, grad_w_node, grad_w_dec, grad_w_enc = run(
         on(write_body, places), (*reduced, *reduced_other),

time: 217 us -> 200 us (0.922)
  waiting for transfers between devices: 97 us -> 87.6 us
  starting transfers between devices: 71.4 us -> 64.2 us
    ppermute x71 -> x65, waiting for transfers between devices: 97 us -> 87.6 us  [shifted(): lax.ppermute(block, axis, [((i + distance) % count, i) for i in range(cou...]
    ppermute x71 -> x65, starting transfers between devices: 71.4 us -> 64.2 us  [shifted(): lax.ppermute(block, axis, [((i + distance) % count, i) for i in range(cou...]
    pallas_call x32 -> x28, Pallas kernels: 44.2 us -> 43.9 us  [run(): pl.pallas_call(body, out_shape=[jax.ShapeDtypeStruct(s, d) if i in hbm el...]
  transfers between devices with their start and end apart: 71 -> 65, of which waited for: 33 -> 36; matrix products, arithmetic and copies ran while one was open for 0% -> 0% of each run, Pallas kernels for 14% -> 14%
where the time goes in v5:
time: 200 us; the launch traced here: 197 us
  waiting for transfers between devices  87.6 us (44%)
  starting transfers between devices  64.2 us (32%)
  Pallas kernels  43.9 us (22%)
    ppermute x65, waiting for transfers between devices, shifted(): lax.ppermute(block, axis, [((i + distance) % count, i) for i in range(cou...  87.6 us
    ppermute x65, starting transfers between devices, shifted(): lax.ppermute(block, axis, [((i + distance) % count, i) for i in range(cou...  64.2 us
    pallas_call x28, Pallas kernels, run(): pl.pallas_call(body, out_shape=[jax.ShapeDtypeStruct(s, d) if i in hbm el...  43.9 us
  transfers between devices with their start and end apart: 65, of which 36 were waited for; matrix products, arithmetic and copies ran while one was open for 0% of the time, Pallas kernels for 14%

profile of v5, /device:TPU:0, one launch (start us, length us, event | category | flops | bytes accessed | tf_op | source)
XLA Modules:
  0.0 196.6 jit_solution(13090659376826954082)
XLA Ops:
  0.7 5.9 %shard_map.170 = (bf16[2048,128]{1,0:T(8,128)(2,1)S(1)}, bf16[2048,128]{1,0:T(8,128)(2,1)S(1)}) custom-call(bf16[2048,512]{1,0:T(8,128)(2,1)} %x.5, bf16[512,512]{1,0:T(8,128)(2,1)} %w.5, s32[1,2048]{1,0:T(1,128)} %bitcast.5, s32[1,2048]{1,0:T(1,128)} %bitcast.10), custom_call_target="tpu_custom_call" | custom-call | flops 2684354560 | tf_op jit(solution)/shard_map/pallas_call | solution.py:75
  8.8 3.0 %collective-permute-start.1 = (bf16[512,128]{1,0:T(8,128)(2,1)S(1)}, bf16[512,128]{1,0:T(8,128)(2,1)S(1)}, u32[]{:S(2)}, u32[]{:S(2)}) collective-permute-start(bf16[512,128]{1,0:T(8,128)(2,1)S(1)} %get-tuple-element.142), channel_id=1, source_target_pairs={{12,0},{0,4},{4,8},{8,12},{13,1},{1,5},{5,9},{9,13},{14,2},{2,6},{... | collective-permute-start | bytes 393224 | tf_op jit(solution)/shard_map/ppermute | solution.py:16
  11.8 2.6 %collective-permute-start.2 = (bf16[512,128]{1,0:T(8,128)(2,1)S(1)}, bf16[512,128]{1,0:T(8,128)(2,1)S(1)}, u32[]{:S(2)}, u32[]{:S(2)}) collective-permute-start(bf16[512,128]{1,0:T(8,128)(2,1)S(1)} %get-tuple-element.143), channel_id=1, source_target_pairs={{8,0},{12,4},{0,8},{4,12},{9,1},{13,5},{1,9},{5,13},{10,2},{14,6},... | collective-permute-start | bytes 393224 | tf_op jit(solution)/shard_map/ppermute | solution.py:16
  15.7 4.1 %shard_map.176 = (bf16[2048,128]{1,0:T(8,128)(2,1)S(1)}, bf16[2048,128]{1,0:T(8,128)(2,1)S(1)}) custom-call(s32[1,2048]{1,0:T(1,128)S(1)} %bitcast.6, s32[1,2048]{1,0:T(1,128)S(1)} %bitcast.11, bf16[2048,256]{1,0:T(8,128)(2,1)} %cotangent.1), custom_call_target="tpu_custom_call" | custom-call | flops 2147483648 | tf_op jit(solution)/shard_map/pallas_call | solution.py:75
  23.4 1.6 collective-permute-start.6
  25.0 3.8 %collective-permute-done.6.refs_2_ = bf16[512,128]{1,0:T(8,128)(2,1)S(1)} collective-permute-done((bf16[512,128]{1,0:T(8,128)(2,1)S(1)}, bf16[512,128]{1,0:T(8,128)(2,1)S(1)}, u32[]{:S(2)}, u32[]{:S(2)}) %collective-permute-start.6) | collective-permute-done | bytes 131104 | tf_op jit(solution)/shard_map/ppermute | solution.py:16
  30.7 4.0 %collective-permute-start.9 = (bf16[512,128]{1,0:T(8,128)(2,1)S(1)}, bf16[512,128]{1,0:T(8,128)(2,1)S(1)}, u32[]{:S(2)}, u32[]{:S(2)}) collective-permute-start(bf16[512,128]{1,0:T(8,128)(2,1)S(1)} %get-tuple-element.150.own), channel_id=1, source_target_pairs={{4,0},{8,4},{12,8},{0,12},{5,1},{9,5},{13,9},{1,13},{6,2},{10,6},{... | collective-permute-start | bytes 393224 | tf_op jit(solution)/shard_map/ppermute | solution.py:16
  34.8 3.8 %collective-permute-done.9.above = bf16[512,128]{1,0:T(8,128)(2,1)S(1)} collective-permute-done((bf16[512,128]{1,0:T(8,128)(2,1)S(1)}, bf16[512,128]{1,0:T(8,128)(2,1)S(1)}, u32[]{:S(2)}, u32[]{:S(2)}) %collective-permute-start.9) | collective-permute-done | bytes 131104 | tf_op jit(solution)/shard_map/ppermute | solution.py:16
  38.6 3.3 %collective-permute-done.8.below = bf16[512,128]{1,0:T(8,128)(2,1)S(1)} collective-permute-done((bf16[512,128]{1,0:T(8,128)(2,1)S(1)}, bf16[512,128]{1,0:T(8,128)(2,1)S(1)}, u32[]{:S(2)}, u32[]{:S(2)}) %collective-permute-start.8) | collective-permute-done | bytes 131104 | tf_op jit(solution)/shard_map/ppermute | solution.py:16
  41.9 1.8 shard_map.175
  43.7 1.6 collective-permute-start.12
  46.5 2.6 %collective-permute-start.15 = (bf16[512,128]{1,0:T(8,128)(2,1)S(1)}, bf16[512,128]{1,0:T(8,128)(2,1)S(1)}, u32[]{:S(2)}, u32[]{:S(2)}) collective-permute-start(bf16[512,128]{1,0:T(8,128)(2,1)S(1)} %get-tuple-element.163), channel_id=1, source_target_pairs={{4,0},{8,4},{12,8},{0,12},{5,1},{9,5},{13,9},{1,13},{6,2},{10,6},{... | collective-permute-start | bytes 393224 | tf_op jit(solution)/shard_map/ppermute | solution.py:16
  50.6 2.8 %collective-permute-done.14.refs_1_ = bf16[512,128]{1,0:T(8,128)(2,1)S(1)} collective-permute-done((bf16[512,128]{1,0:T(8,128)(2,1)S(1)}, bf16[512,128]{1,0:T(8,128)(2,1)S(1)}, u32[]{:S(2)}, u32[]{:S(2)}) %collective-permute-start.14) | collective-permute-done | bytes 131104 | tf_op jit(solution)/shard_map/ppermute | solution.py:16
  55.7 2.6 %collective-permute-start.17 = (bf16[512,128]{1,0:T(8,128)(2,1)S(1)}, bf16[512,128]{1,0:T(8,128)(2,1)S(1)}, u32[]{:S(2)}, u32[]{:S(2)}) collective-permute-start(bf16[512,128]{1,0:T(8,128)(2,1)S(1)} %get-tuple-element.169.own), channel_id=1, source_target_pairs={{4,0},{8,4},{12,8},{0,12},{5,1},{9,5},{13,9},{1,13},{6,2},{10,6},{... | collective-permute-start | bytes 393224 | tf_op jit(solution)/shard_map/ppermute | solution.py:16
  58.3 3.2 %collective-permute-done.18.refs_3_ = bf16[512,128]{1,0:T(8,128)(2,1)S(1)} collective-permute-done((bf16[512,128]{1,0:T(8,128)(2,1)S(1)}, bf16[512,128]{1,0:T(8,128)(2,1)S(1)}, u32[]{:S(2)}, u32[]{:S(2)}) %collective-permute-start.18) | collective-permute-done | bytes 131104 | tf_op jit(solution)/shard_map/ppermute | solution.py:16
  61.5 4.2 %collective-permute-done.17.above = bf16[512,128]{1,0:T(8,128)(2,1)S(1)} collective-permute-done((bf16[512,128]{1,0:T(8,128)(2,1)S(1)}, bf16[512,128]{1,0:T(8,128)(2,1)S(1)}, u32[]{:S(2)}, u32[]{:S(2)}) %collective-permute-start.17) | collective-permute-done | bytes 131104 | tf_op jit(solution)/shard_map/ppermute | solution.py:16
  66.4 1.8 shard_map.179
  71.1 2.2 %collective-permute-done.20.refs_2_ = bf16[512,128]{1,0:T(8,128)(2,1)S(1)} collective-permute-done((bf16[512,128]{1,0:T(8,128)(2,1)S(1)}, bf16[512,128]{1,0:T(8,128)(2,1)S(1)}, u32[]{:S(2)}, u32[]{:S(2)}) %collective-permute-start.20) | collective-permute-done | bytes 131104 | tf_op jit(solution)/shard_map/ppermute | solution.py:16
  74.6 3.5 %shard_map.181 = (bf16[512,512]{1,0:T(8,128)(2,1)S(1)}, bf16[512,512]{1,0:T(8,128)(2,1)S(1)}, bf16[512,128]{1,0:T(8,128)(2,1)S(1)}, bf16[512,512]{1,0:T(8,128)(2...) custom-call(f32[512,512]{1,0:T(8,128)S(1)} %get-tuple-element.168.st, ...), custom_call_target="tpu_custom_call" | custom-call | flops 2013265920 | tf_op jit(solution)/shard_map/pallas_call | solution.py:75
  78.1 1.6 collective-permute-start.28
  79.6 2.5 %collective-permute-start.25 = (bf16[512,128]{1,0:T(8,128)(2,1)S(1)}, bf16[512,128]{1,0:T(8,128)(2,1)S(1)}, u32[]{:S(2)}, u32[]{:S(2)}) collective-permute-start(bf16[512,128]{1,0:T(8,128)(2,1)S(1)} %get-tuple-element.181), channel_id=1, source_target_pairs={{4,0},{8,4},{12,8},{0,12},{5,1},{9,5},{13,9},{1,13},{6,2},{10,6},{... | collective-permute-start | bytes 393224 | tf_op jit(solution)/shard_map/ppermute | solution.py:16
  83.7 2.3 %collective-permute-done.25.refs_1_ = bf16[512,128]{1,0:T(8,128)(2,1)S(1)} collective-permute-done((bf16[512,128]{1,0:T(8,128)(2,1)S(1)}, bf16[512,128]{1,0:T(8,128)(2,1)S(1)}, u32[]{:S(2)}, u32[]{:S(2)}) %collective-permute-start.25) | collective-permute-done | bytes 131104 | tf_op jit(solution)/shard_map/ppermute | solution.py:16
  86.0 3.6 %collective-permute-done.26.refs_2_ = bf16[512,128]{1,0:T(8,128)(2,1)S(1)} collective-permute-done((bf16[512,128]{1,0:T(8,128)(2,1)S(1)}, bf16[512,128]{1,0:T(8,128)(2,1)S(1)}, u32[]{:S(2)}, u32[]{:S(2)}) %collective-permute-start.26) | collective-permute-done | bytes 131104 | tf_op jit(solution)/shard_map/ppermute | solution.py:16
  92.2 2.5 %collective-permute-start.33 = (bf16[512,128]{1,0:T(8,128)(2,1)S(1)}, bf16[512,128]{1,0:T(8,128)(2,1)S(1)}, u32[]{:S(2)}, u32[]{:S(2)}) collective-permute-start(bf16[512,128]{1,0:T(8,128)(2,1)S(1)} %get-tuple-element.206.refs_0_), channel_id=1, source_target_pairs={{4,0},{8,4},{12,8},{0,12},{5,1},{9,5},{13,9},{1,13},{6,2},{10,6},{... | collective-permute-start | bytes 393224 | tf_op jit(solution)/shard_map/ppermute | solution.py:16
  94.7 4.3 %collective-permute-done.34.refs_3_ = bf16[512,128]{1,0:T(8,128)(2,1)S(1)} collective-permute-done((bf16[512,128]{1,0:T(8,128)(2,1)S(1)}, bf16[512,128]{1,0:T(8,128)(2,1)S(1)}, u32[]{:S(2)}, u32[]{:S(2)}) %collective-permute-start.34) | collective-permute-done | bytes 131104 | tf_op jit(solution)/shard_map/ppermute | solution.py:16
  99.0 1.6 collective-permute-done.33.refs_1_
  100.7 3.0 %shard_map.183 = (bf16[512,512]{1,0:T(8,128)(2,1)S(1)}, bf16[512,512]{1,0:T(8,128)(2,1)S(1)}, f32[512,512]{1,0:T(8,128)S(1)}, bf16[512,128]{1,0:T(8,128)(2,1)S(1...) custom-call(f32[512,512]{1,0:T(8,128)S(1)} %get-tuple-element.190.grad.refs_11_, ...), custom_call_target="tpu_custom_call" | custom-call | flops 1744830464 | tf_op jit(solution)/shard_map/pallas_call | solution.py:75
  104.6 2.1 %collective-permute-start.35 = (bf16[512,128]{1,0:T(8,128)(2,1)S(1)}, bf16[512,128]{1,0:T(8,128)(2,1)S(1)}, u32[]{:S(2)}, u32[]{:S(2)}) collective-permute-start(bf16[512,128]{1,0:T(8,128)(2,1)S(1)} %get-tuple-element.201), channel_id=1, source_target_pairs={{4,0},{8,4},{12,8},{0,12},{5,1},{9,5},{13,9},{1,13},{6,2},{10,6},{... | collective-permute-start | bytes 393224 | tf_op jit(solution)/shard_map/ppermute | solution.py:16
  106.7 2.1 %collective-permute-done.38.refs_6_ = bf16[512,128]{1,0:T(8,128)(2,1)S(1)} collective-permute-done((bf16[512,128]{1,0:T(8,128)(2,1)S(1)}, bf16[512,128]{1,0:T(8,128)(2,1)S(1)}, u32[]{:S(2)}, u32[]{:S(2)}) %collective-permute-start.38) | collective-permute-done | bytes 131104 | tf_op jit(solution)/shard_map/ppermute | solution.py:16
  108.8 1.8 collective-permute-done.35.refs_1_
  110.6 3.6 %collective-permute-done.36.refs_2_ = bf16[512,128]{1,0:T(8,128)(2,1)S(1)} collective-permute-done((bf16[512,128]{1,0:T(8,128)(2,1)S(1)}, bf16[512,128]{1,0:T(8,128)(2,1)S(1)}, u32[]{:S(2)}, u32[]{:S(2)}) %collective-permute-start.36) | collective-permute-done | bytes 131104 | tf_op jit(solution)/shard_map/ppermute | solution.py:16
  116.5 2.7 %collective-permute-done.41.refs_2_ = bf16[512,128]{1,0:T(8,128)(2,1)S(1)} collective-permute-done((bf16[512,128]{1,0:T(8,128)(2,1)S(1)}, bf16[512,128]{1,0:T(8,128)(2,1)S(1)}, u32[]{:S(2)}, u32[]{:S(2)}) %collective-permute-start.41) | collective-permute-done | bytes 131104 | tf_op jit(solution)/shard_map/ppermute | solution.py:16
  119.2 5.8 %collective-permute-done.43.refs_2_ = bf16[512,128]{1,0:T(8,128)(2,1)S(1)} collective-permute-done((bf16[512,128]{1,0:T(8,128)(2,1)S(1)}, bf16[512,128]{1,0:T(8,128)(2,1)S(1)}, u32[]{:S(2)}, u32[]{:S(2)}) %collective-permute-start.43) | collective-permute-done | bytes 131104 | tf_op jit(solution)/shard_map/ppermute | solution.py:16
  126.1 2.3 %collective-permute-start.46 = (bf16[512,128]{1,0:T(8,128)(2,1)S(1)}, bf16[512,128]{1,0:T(8,128)(2,1)S(1)}, u32[]{:S(2)}, u32[]{:S(2)}) collective-permute-start(bf16[512,128]{1,0:T(8,128)(2,1)S(1)} %get-tuple-element.219), channel_id=1, source_target_pairs={{8,0},{12,4},{0,8},{4,12},{9,1},{13,5},{1,9},{5,13},{10,2},{14,6},... | collective-permute-start | bytes 393224 | tf_op jit(solution)/shard_map/ppermute | solution.py:16
  130.7 5.5 %shard_map.186 = (bf16[2048,256]{1,0:T(8,128)(2,1)}, bf16[2048,512]{1,0:T(8,128)(2,1)S(1)}) custom-call(bf16[2048,512]{1,0:T(8,128)(2,1)S(1)} %copy-done.5, bf16[512,512]{1,0:T(8,128)(2,1)S(1)} %copy-done.7, s32[1,2048]{1,0:T(1,128)S(1)} %bitcast.7, s32[1,2048]{1,0:T(1,128)S(1)} %bitcast.12, bf16[2048,128]{1,0:T(8,128)(2,1)S(1)} %shard_map.185.mine, ...), custom_call_target="tpu_custom_call" | custom-call | flops 3221225472 | tf_op jit(solution)/shard_map/pallas_call | solution.py:75
  136.2 2.8 %collective-permute-done.46.refs_1_ = bf16[512,128]{1,0:T(8,128)(2,1)S(1)} collective-permute-done((bf16[512,128]{1,0:T(8,128)(2,1)S(1)}, bf16[512,128]{1,0:T(8,128)(2,1)S(1)}, u32[]{:S(2)}, u32[]{:S(2)}) %collective-permute-start.46) | collective-permute-done | bytes 131104 | tf_op jit(solution)/shard_map/ppermute | solution.py:16
  140.8 3.0 %collective-permute-start.50 = (bf16[448,256]{1,0:T(8,128)(2,1)S(1)}, bf16[448,256]{1,0:T(8,128)(2,1)S(1)}, u32[]{:S(2)}, u32[]{:S(2)}) collective-permute-start(bf16[448,256]{1,0:T(8,128)(2,1)S(1)} %get-tuple-element.242), channel_id=1, source_target_pairs={{12,0},{0,4},{4,8},{8,12},{13,1},{1,5},{5,9},{9,13},{14,2},{2,6},{... | collective-permute-start | bytes 688136 | tf_op jit(solution)/shard_map/ppermute | solution.py:16
  144.4 1.8 collective-permute-start.52
  146.3 3.1 %collective-permute-done.59.refs_0_ = bf16[1536,128]{1,0:T(8,128)(2,1)S(1)} collective-permute-done((bf16[1536,128]{1,0:T(8,128)(2,1)S(1)}, bf16[1536,128]{1,0:T(8,128)(2,1)S(1)}, u32[]{:S(2)}, u32[]{:S(2)}) %collective-permute-start.59) | collective-permute-done | bytes 393248 | tf_op jit(solution)/shard_map/ppermute | solution.py:16
  149.4 5.0 %shard_map.190 = (bf16[2048,256]{1,0:T(8,128)(2,1)S(1)}, f32[256,256]{1,0:T(8,128)S(1)}, bf16[256,256]{1,0:T(8,128)(2,1)S(1)}) custom-call(bf16[2048,512]{1,0:T(8,128)(2,1)S(1)} %copy-done.5, s32[1,2048]{1,0:T(1,128)S(1)} %bitcast.8, s32[1,2048]{1,0:T(1,128)S(1)} %bitcast.13, bf16[2048,512]{1,0:T(8,128)(2,1)S(1)} %get-tuple-element.222.slope, ...), custom_call_target="tpu_custom_call" | custom-call | flops 2684354560 | tf_op jit(solution)/shard_map/pallas_call | solution.py:75
  154.9 5.7 %collective-permute-done.51.refs_2_ = bf16[448,256]{1,0:T(8,128)(2,1)S(1)} collective-permute-done((bf16[448,256]{1,0:T(8,128)(2,1)S(1)}, bf16[448,256]{1,0:T(8,128)(2,1)S(1)}, u32[]{:S(2)}, u32[]{:S(2)}) %collective-permute-start.51) | collective-permute-done | bytes 229408 | tf_op jit(solution)/shard_map/ppermute | solution.py:16
  160.8 5.5 %collective-permute-start.53 = (bf16[64,256]{1,0:T(8,128)(2,1)S(1)}, bf16[64,256]{1,0:T(8,128)(2,1)S(1)}, u32[]{:S(2)}, u32[]{:S(2)}) collective-permute-start(bf16[64,256]{1,0:T(8,128)(2,1)S(1)} %get-tuple-element.247), channel_id=1, source_target_pairs={{12,0},{0,4},{4,8},{8,12},{13,1},{1,5},{5,9},{9,13},{14,2},{2,6},{... | collective-permute-start | bytes 98312 | tf_op jit(solution)/shard_map/ppermute | solution.py:16
  166.3 1.7 collective-permute-start.54
  169.3 1.8 collective-permute-done.54.refs_2_
  172.1 3.0 %collective-permute-start.57 = (bf16[512,256]{1,0:T(8,128)(2,1)S(1)}, bf16[512,256]{1,0:T(8,128)(2,1)S(1)}, u32[]{:S(2)}, u32[]{:S(2)}) collective-permute-start(bf16[512,256]{1,0:T(8,128)(2,1)S(1)} %shard_map.195.refs_0_), channel_id=1, source_target_pairs={{8,0},{12,4},{0,8},{4,12},{9,1},{13,5},{1,9},{5,13},{10,2},{14,6},... | collective-permute-start | bytes 786440 | tf_op jit(solution)/shard_map/ppermute | solution.py:16
  176.1 6.3 %shard_map.196 = bf16[2048,256]{1,0:T(8,128)(2,1)} custom-call(s32[1,2048]{1,0:T(1,128)S(1)} %bitcast.9, s32[1,2048]{1,0:T(1,128)S(1)} %bitcast.14, bf16[2048,256]{1,0:T(8,128)(2,1)} %cotangent.1, bf16[2048,256]{1,0:T(8,128)(2,1)S(1)} %get-tuple-element.250.enc_grad, bf16[512,512]{1,0:T(8,128)(2,1)S(1)} %get-tuple-element.223.enc_all, ...), custom_call_target="tpu_custom_call" | custom-call | flops 2684354560 | tf_op jit(solution)/shard_map/pallas_call | solution.py:75
  183.2 8.5 %collective-permute-done.57.refs_2_ = bf16[512,256]{1,0:T(8,128)(2,1)S(1)} collective-permute-done((bf16[512,256]{1,0:T(8,128)(2,1)S(1)}, bf16[512,256]{1,0:T(8,128)(2,1)S(1)}, u32[]{:S(2)}, u32[]{:S(2)}) %collective-permute-start.57) | collective-permute-done | bytes 262176 | tf_op jit(solution)/shard_map/ppermute | solution.py:16
  194.4 2.3 %shard_map.197 = (f32[2,512,256]{2,1,0:T(8,128)}, f32[2,512,256]{2,1,0:T(8,128)}, f32[2,512,256]{2,1,0:T(8,128)}, f32[512,256]{1,0:T(8,128)}, f32[512,256]{1,0:T(8,128)}) custom-call(bf16[512,256]{1,0:T(8,128)(2,1)S(1)} %shard_map.195.refs_0_, bf16[512,256]{1,0:T(8,128)(2,1)S(1)} %collective-permute-done.56.refs_1_, ...), custom_call_target="tpu_custom_call" | custom-call | tf_op jit(solution)/shard_map/pallas_call | solution.py:75
  (130 shorter events, 39.7 us)
Async XLA Ops:
  8.8 13.2 %collective-permute-start.1 = (bf16[512,128]{1,0:T(8,128)(2,1)S(1)}, bf16[512,128]{1,0:T(8,128)(2,1)S(1)}, u32[]{:S(2)}, u32[]{:S(2)}) collective-permute-start(bf16[512,128]{1,0:T(8,128)(2,1)S(1)} %get-tuple-element.142), channel_id=1, source_target_pairs={{12,0},{0,4},{4,8},{8,12},{13,1},{1,5},{5,9},{9,13},{14,2},{2,6},{... | collective-permute-start | bytes 393224 | tf_op jit(solution)/shard_map/ppermute | solution.py:16
  11.8 11.5 %collective-permute-start.2 = (bf16[512,128]{1,0:T(8,128)(2,1)S(1)}, bf16[512,128]{1,0:T(8,128)(2,1)S(1)}, u32[]{:S(2)}, u32[]{:S(2)}) collective-permute-start(bf16[512,128]{1,0:T(8,128)(2,1)S(1)} %get-tuple-element.143), channel_id=1, source_target_pairs={{8,0},{12,4},{0,8},{4,12},{9,1},{13,5},{1,9},{5,13},{10,2},{14,6},... | collective-permute-start | bytes 393224 | tf_op jit(solution)/shard_map/ppermute | solution.py:16
  14.4 8.9 %collective-permute-start.3 = (bf16[512,128]{1,0:T(8,128)(2,1)S(1)}, bf16[512,128]{1,0:T(8,128)(2,1)S(1)}, u32[]{:S(2)}, u32[]{:S(2)}) collective-permute-start(bf16[512,128]{1,0:T(8,128)(2,1)S(1)} %get-tuple-element.144), channel_id=1, source_target_pairs={{4,0},{8,4},{12,8},{0,12},{5,1},{9,5},{13,9},{1,13},{6,2},{10,6},{... | collective-permute-start | bytes 393224 | tf_op jit(solution)/shard_map/ppermute | solution.py:16
  19.8 14.9 %collective-permute-start.10 = (bf16[2048,128]{1,0:T(8,128)(2,1)S(1)}, bf16[2048,128]{1,0:T(8,128)(2,1)S(1)}, u32[]{:S(2)}, u32[]{:S(2)}) collective-permute-start(bf16[2048,128]{1,0:T(8,128)(2,1)S(1)} %get-tuple-element.156), channel_id=1, source_target_pairs={{1,0},{0,1},{3,2},{2,3},{5,4},{4,5},{7,6},{6,7},{9,8},{8,9},{11,10... | collective-permute-start | bytes 1572872 | tf_op jit(solution)/shard_map/ppermute | solution.py:16
  23.4 5.4 %collective-permute-start.6 = (bf16[512,128]{1,0:T(8,128)(2,1)S(1)}, bf16[512,128]{1,0:T(8,128)(2,1)S(1)}, u32[]{:S(2)}, u32[]{:S(2)}) collective-permute-start(bf16[512,128]{1,0:T(8,128)(2,1)S(1)} %shard_map.172.refs_0_), channel_id=1, source_target_pairs={{2,0},{0,2},{3,1},{1,3},{6,4},{4,6},{7,5},{5,7},{10,8},{8,10},{11,... | collective-permute-start | bytes 393224 | tf_op jit(solution)/shard_map/ppermute | solution.py:16
  30.7 7.9 %collective-permute-start.9 = (bf16[512,128]{1,0:T(8,128)(2,1)S(1)}, bf16[512,128]{1,0:T(8,128)(2,1)S(1)}, u32[]{:S(2)}, u32[]{:S(2)}) collective-permute-start(bf16[512,128]{1,0:T(8,128)(2,1)S(1)} %get-tuple-element.150.own), channel_id=1, source_target_pairs={{4,0},{8,4},{12,8},{0,12},{5,1},{9,5},{13,9},{1,13},{6,2},{10,6},{... | collective-permute-start | bytes 393224 | tf_op jit(solution)/shard_map/ppermute | solution.py:16
  34.7 7.2 %collective-permute-start.8 = (bf16[512,128]{1,0:T(8,128)(2,1)S(1)}, bf16[512,128]{1,0:T(8,128)(2,1)S(1)}, u32[]{:S(2)}, u32[]{:S(2)}) collective-permute-start(bf16[512,128]{1,0:T(8,128)(2,1)S(1)} %get-tuple-element.150.own), channel_id=1, source_target_pairs={{12,0},{0,4},{4,8},{8,12},{13,1},{1,5},{5,9},{9,13},{14,2},{2,6},{... | collective-permute-start | bytes 393224 | tf_op jit(solution)/shard_map/ppermute | solution.py:16
  43.7 5.4 %collective-permute-start.12 = (bf16[512,128]{1,0:T(8,128)(2,1)S(1)}, bf16[512,128]{1,0:T(8,128)(2,1)S(1)}, u32[]{:S(2)}, u32[]{:S(2)}) collective-permute-start(bf16[512,128]{1,0:T(8,128)(2,1)S(1)} %get-tuple-element.164.refs_0_), channel_id=1, source_target_pairs={{2,0},{0,2},{3,1},{1,3},{6,4},{4,6},{7,5},{5,7},{10,8},{8,10},{11,... | collective-permute-start | bytes 393224 | tf_op jit(solution)/shard_map/ppermute | solution.py:16
  45.2 9.7 %collective-permute-start.11 = (bf16[512,128]{1,0:T(8,128)(2,1)S(1)}, bf16[512,128]{1,0:T(8,128)(2,1)S(1)}, u32[]{:S(2)}, u32[]{:S(2)}) collective-permute-start(bf16[512,128]{1,0:T(8,128)(2,1)S(1)} %get-tuple-element.164.refs_0_), channel_id=1, source_target_pairs={{1,0},{0,1},{3,2},{2,3},{5,4},{4,5},{7,6},{6,7},{9,8},{8,9},{11,10... | collective-permute-start | bytes 393224 | tf_op jit(solution)/shard_map/ppermute | solution.py:16
  45.2 8.1 %collective-permute-start.14 = (bf16[512,128]{1,0:T(8,128)(2,1)S(1)}, bf16[512,128]{1,0:T(8,128)(2,1)S(1)}, u32[]{:S(2)}, u32[]{:S(2)}) collective-permute-start(bf16[512,128]{1,0:T(8,128)(2,1)S(1)} %get-tuple-element.162), channel_id=1, source_target_pairs={{12,0},{0,4},{4,8},{8,12},{13,1},{1,5},{5,9},{9,13},{14,2},{2,6},{... | collective-permute-start | bytes 393224 | tf_op jit(solution)/shard_map/ppermute | solution.py:16
  46.5 8.4 %collective-permute-start.15 = (bf16[512,128]{1,0:T(8,128)(2,1)S(1)}, bf16[512,128]{1,0:T(8,128)(2,1)S(1)}, u32[]{:S(2)}, u32[]{:S(2)}) collective-permute-start(bf16[512,128]{1,0:T(8,128)(2,1)S(1)} %get-tuple-element.163), channel_id=1, source_target_pairs={{4,0},{8,4},{12,8},{0,12},{5,1},{9,5},{13,9},{1,13},{6,2},{10,6},{... | collective-permute-start | bytes 393224 | tf_op jit(solution)/shard_map/ppermute | solution.py:16
  49.1 5.8 %collective-permute-start.13 = (bf16[512,128]{1,0:T(8,128)(2,1)S(1)}, bf16[512,128]{1,0:T(8,128)(2,1)S(1)}, u32[]{:S(2)}, u32[]{:S(2)}) collective-permute-start(bf16[512,128]{1,0:T(8,128)(2,1)S(1)} %collective-permute-done.12.refs_2_), channel_id=1, source_target_pairs={{1,0},{0,1},{3,2},{2,3},{5,4},{4,5},{7,6},{6,7},{9,8},{8,9},{11,10... | collective-permute-start | bytes 393224 | tf_op jit(solution)/shard_map/ppermute | solution.py:16
  49.1 12.4 %collective-permute-start.18 = (bf16[512,128]{1,0:T(8,128)(2,1)S(1)}, bf16[512,128]{1,0:T(8,128)(2,1)S(1)}, u32[]{:S(2)}, u32[]{:S(2)}) collective-permute-start(bf16[512,128]{1,0:T(8,128)(2,1)S(1)} %get-tuple-element.170), channel_id=1, source_target_pairs={{8,0},{12,4},{0,8},{4,12},{9,1},{13,5},{1,9},{5,13},{10,2},{14,6},... | collective-permute-start | bytes 393224 | tf_op jit(solution)/shard_map/ppermute | solution.py:16
  55.7 10.0 %collective-permute-start.17 = (bf16[512,128]{1,0:T(8,128)(2,1)S(1)}, bf16[512,128]{1,0:T(8,128)(2,1)S(1)}, u32[]{:S(2)}, u32[]{:S(2)}) collective-permute-start(bf16[512,128]{1,0:T(8,128)(2,1)S(1)} %get-tuple-element.169.own), channel_id=1, source_target_pairs={{4,0},{8,4},{12,8},{0,12},{5,1},{9,5},{13,9},{1,13},{6,2},{10,6},{... | collective-permute-start | bytes 393224 | tf_op jit(solution)/shard_map/ppermute | solution.py:16
  58.3 7.4 %collective-permute-start.16 = (bf16[512,128]{1,0:T(8,128)(2,1)S(1)}, bf16[512,128]{1,0:T(8,128)(2,1)S(1)}, u32[]{:S(2)}, u32[]{:S(2)}) collective-permute-start(bf16[512,128]{1,0:T(8,128)(2,1)S(1)} %get-tuple-element.169.own), channel_id=1, source_target_pairs={{12,0},{0,4},{4,8},{8,12},{13,1},{1,5},{5,9},{9,13},{14,2},{2,6},{... | collective-permute-start | bytes 393224 | tf_op jit(solution)/shard_map/ppermute | solution.py:16
  65.8 5.3 %collective-permute-start.23 = (bf16[512,128]{1,0:T(8,128)(2,1)S(1)}, bf16[512,128]{1,0:T(8,128)(2,1)S(1)}, u32[]{:S(2)}, u32[]{:S(2)}) collective-permute-start(bf16[512,128]{1,0:T(8,128)(2,1)S(1)} %shard_map.180.refs_4_), channel_id=1, source_target_pairs={{2,0},{0,2},{3,1},{1,3},{6,4},{4,6},{7,5},{5,7},{10,8},{8,10},{11,... | collective-permute-start | bytes 393224 | tf_op jit(solution)/shard_map/ppermute | solution.py:16
  68.2 5.0 %collective-permute-start.20 = (bf16[512,128]{1,0:T(8,128)(2,1)S(1)}, bf16[512,128]{1,0:T(8,128)(2,1)S(1)}, u32[]{:S(2)}, u32[]{:S(2)}) collective-permute-start(bf16[512,128]{1,0:T(8,128)(2,1)S(1)} %get-tuple-element.176.refs_0_), channel_id=1, source_target_pairs={{2,0},{0,2},{3,1},{1,3},{6,4},{4,6},{7,5},{5,7},{10,8},{8,10},{11,... | collective-permute-start | bytes 393224 | tf_op jit(solution)/shard_map/ppermute | solution.py:16
  78.1 5.6 %collective-permute-start.28 = (bf16[512,128]{1,0:T(8,128)(2,1)S(1)}, bf16[512,128]{1,0:T(8,128)(2,1)S(1)}, u32[]{:S(2)}, u32[]{:S(2)}) collective-permute-start(bf16[512,128]{1,0:T(8,128)(2,1)S(1)} %get-tuple-element.196.refs_4_), channel_id=1, source_target_pairs={{2,0},{0,2},{3,1},{1,3},{6,4},{4,6},{7,5},{5,7},{10,8},{8,10},{11,... | collective-permute-start | bytes 393224 | tf_op jit(solution)/shard_map/ppermute | solution.py:16
  79.6 9.9 %collective-permute-start.27 = (bf16[512,128]{1,0:T(8,128)(2,1)S(1)}, bf16[512,128]{1,0:T(8,128)(2,1)S(1)}, u32[]{:S(2)}, u32[]{:S(2)}) collective-permute-start(bf16[512,128]{1,0:T(8,128)(2,1)S(1)} %get-tuple-element.196.refs_4_), channel_id=1, source_target_pairs={{1,0},{0,1},{3,2},{2,3},{5,4},{4,5},{7,6},{6,7},{9,8},{8,9},{11,10... | collective-permute-start | bytes 393224 | tf_op jit(solution)/shard_map/ppermute | solution.py:16
  79.6 6.4 %collective-permute-start.25 = (bf16[512,128]{1,0:T(8,128)(2,1)S(1)}, bf16[512,128]{1,0:T(8,128)(2,1)S(1)}, u32[]{:S(2)}, u32[]{:S(2)}) collective-permute-start(bf16[512,128]{1,0:T(8,128)(2,1)S(1)} %get-tuple-element.181), channel_id=1, source_target_pairs={{4,0},{8,4},{12,8},{0,12},{5,1},{9,5},{13,9},{1,13},{6,2},{10,6},{... | collective-permute-start | bytes 393224 | tf_op jit(solution)/shard_map/ppermute | solution.py:16
  82.1 7.4 %collective-permute-start.26 = (bf16[512,128]{1,0:T(8,128)(2,1)S(1)}, bf16[512,128]{1,0:T(8,128)(2,1)S(1)}, u32[]{:S(2)}, u32[]{:S(2)}) collective-permute-start(bf16[512,128]{1,0:T(8,128)(2,1)S(1)} %get-tuple-element.182), channel_id=1, source_target_pairs={{12,0},{0,4},{4,8},{8,12},{13,1},{1,5},{5,9},{9,13},{14,2},{2,6},{... | collective-permute-start | bytes 393224 | tf_op jit(solution)/shard_map/ppermute | solution.py:16
  83.7 5.9 %collective-permute-start.29 = (bf16[512,128]{1,0:T(8,128)(2,1)S(1)}, bf16[512,128]{1,0:T(8,128)(2,1)S(1)}, u32[]{:S(2)}, u32[]{:S(2)}) collective-permute-start(bf16[512,128]{1,0:T(8,128)(2,1)S(1)} %collective-permute-done.28.refs_6_), channel_id=1, source_target_pairs={{1,0},{0,1},{3,2},{2,3},{5,4},{4,5},{7,6},{6,7},{9,8},{8,9},{11,10... | collective-permute-start | bytes 393224 | tf_op jit(solution)/shard_map/ppermute | solution.py:16
  89.6 5.1 %collective-permute-start.31 = (bf16[512,128]{1,0:T(8,128)(2,1)S(1)}, bf16[512,128]{1,0:T(8,128)(2,1)S(1)}, u32[]{:S(2)}, u32[]{:S(2)}) collective-permute-start(bf16[512,128]{1,0:T(8,128)(2,1)S(1)} %shard_map.182.refs_0_), channel_id=1, source_target_pairs={{2,0},{0,2},{3,1},{1,3},{6,4},{4,6},{7,5},{5,7},{10,8},{8,10},{11,... | collective-permute-start | bytes 393224 | tf_op jit(solution)/shard_map/ppermute | solution.py:16
  90.9 8.1 %collective-permute-start.34 = (bf16[512,128]{1,0:T(8,128)(2,1)S(1)}, bf16[512,128]{1,0:T(8,128)(2,1)S(1)}, u32[]{:S(2)}, u32[]{:S(2)}) collective-permute-start(bf16[512,128]{1,0:T(8,128)(2,1)S(1)} %get-tuple-element.206.refs_0_), channel_id=1, source_target_pairs={{12,0},{0,4},{4,8},{8,12},{13,1},{1,5},{5,9},{9,13},{14,2},{2,6},{... | collective-permute-start | bytes 393224 | tf_op jit(solution)/shard_map/ppermute | solution.py:16
  92.2 8.4 %collective-permute-start.33 = (bf16[512,128]{1,0:T(8,128)(2,1)S(1)}, bf16[512,128]{1,0:T(8,128)(2,1)S(1)}, u32[]{:S(2)}, u32[]{:S(2)}) collective-permute-start(bf16[512,128]{1,0:T(8,128)(2,1)S(1)} %get-tuple-element.206.refs_0_), channel_id=1, source_target_pairs={{4,0},{8,4},{12,8},{0,12},{5,1},{9,5},{13,9},{1,13},{6,2},{10,6},{... | collective-permute-start | bytes 393224 | tf_op jit(solution)/shard_map/ppermute | solution.py:16
  94.7 5.9 %collective-permute-start.32 = (bf16[512,128]{1,0:T(8,128)(2,1)S(1)}, bf16[512,128]{1,0:T(8,128)(2,1)S(1)}, u32[]{:S(2)}, u32[]{:S(2)}) collective-permute-start(bf16[512,128]{1,0:T(8,128)(2,1)S(1)} %collective-permute-done.31.refs_2_), channel_id=1, source_target_pairs={{1,0},{0,1},{3,2},{2,3},{5,4},{4,5},{7,6},{6,7},{9,8},{8,9},{11,10... | collective-permute-start | bytes 393224 | tf_op jit(solution)/shard_map/ppermute | solution.py:16
  103.7 5.0 %collective-permute-start.38 = (bf16[512,128]{1,0:T(8,128)(2,1)S(1)}, bf16[512,128]{1,0:T(8,128)(2,1)S(1)}, u32[]{:S(2)}, u32[]{:S(2)}) collective-permute-start(bf16[512,128]{1,0:T(8,128)(2,1)S(1)} %get-tuple-element.215.refs_4_), channel_id=1, source_target_pairs={{2,0},{0,2},{3,1},{1,3},{6,4},{4,6},{7,5},{5,7},{10,8},{8,10},{11,... | collective-permute-start | bytes 393224 | tf_op jit(solution)/shard_map/ppermute | solution.py:16
  104.6 9.5 %collective-permute-start.37 = (bf16[512,128]{1,0:T(8,128)(2,1)S(1)}, bf16[512,128]{1,0:T(8,128)(2,1)S(1)}, u32[]{:S(2)}, u32[]{:S(2)}) collective-permute-start(bf16[512,128]{1,0:T(8,128)(2,1)S(1)} %get-tuple-element.215.refs_4_), channel_id=1, source_target_pairs={{1,0},{0,1},{3,2},{2,3},{5,4},{4,5},{7,6},{6,7},{9,8},{8,9},{11,10... | collective-permute-start | bytes 393224 | tf_op jit(solution)/shard_map/ppermute | solution.py:16
  104.6 5.9 %collective-permute-start.35 = (bf16[512,128]{1,0:T(8,128)(2,1)S(1)}, bf16[512,128]{1,0:T(8,128)(2,1)S(1)}, u32[]{:S(2)}, u32[]{:S(2)}) collective-permute-start(bf16[512,128]{1,0:T(8,128)(2,1)S(1)} %get-tuple-element.201), channel_id=1, source_target_pairs={{4,0},{8,4},{12,8},{0,12},{5,1},{9,5},{13,9},{1,13},{6,2},{10,6},{... | collective-permute-start | bytes 393224 | tf_op jit(solution)/shard_map/ppermute | solution.py:16
  106.7 7.4 %collective-permute-start.36 = (bf16[512,128]{1,0:T(8,128)(2,1)S(1)}, bf16[512,128]{1,0:T(8,128)(2,1)S(1)}, u32[]{:S(2)}, u32[]{:S(2)}) collective-permute-start(bf16[512,128]{1,0:T(8,128)(2,1)S(1)} %get-tuple-element.202), channel_id=1, source_target_pairs={{12,0},{0,4},{4,8},{8,12},{13,1},{1,5},{5,9},{9,13},{14,2},{2,6},{... | collective-permute-start | bytes 393224 | tf_op jit(solution)/shard_map/ppermute | solution.py:16
  108.8 5.4 %collective-permute-start.39 = (bf16[512,128]{1,0:T(8,128)(2,1)S(1)}, bf16[512,128]{1,0:T(8,128)(2,1)S(1)}, u32[]{:S(2)}, u32[]{:S(2)}) collective-permute-start(bf16[512,128]{1,0:T(8,128)(2,1)S(1)} %collective-permute-done.38.refs_6_), channel_id=1, source_target_pairs={{1,0},{0,1},{3,2},{2,3},{5,4},{4,5},{7,6},{6,7},{9,8},{8,9},{11,10... | collective-permute-start | bytes 393224 | tf_op jit(solution)/shard_map/ppermute | solution.py:16
  115.4 9.6 %collective-permute-start.43 = (bf16[512,128]{1,0:T(8,128)(2,1)S(1)}, bf16[512,128]{1,0:T(8,128)(2,1)S(1)}, u32[]{:S(2)}, u32[]{:S(2)}) collective-permute-start(bf16[512,128]{1,0:T(8,128)(2,1)S(1)} %get-tuple-element.206.refs_0_), channel_id=1, source_target_pairs={{8,0},{12,4},{0,8},{4,12},{9,1},{13,5},{1,9},{5,13},{10,2},{14,6},... | collective-permute-start | bytes 393224 | tf_op jit(solution)/shard_map/ppermute | solution.py:16
  119.2 5.9 %collective-permute-start.42 = (bf16[512,128]{1,0:T(8,128)(2,1)S(1)}, bf16[512,128]{1,0:T(8,128)(2,1)S(1)}, u32[]{:S(2)}, u32[]{:S(2)}) collective-permute-start(bf16[512,128]{1,0:T(8,128)(2,1)S(1)} %collective-permute-done.41.refs_2_), channel_id=1, source_target_pairs={{1,0},{0,1},{3,2},{2,3},{5,4},{4,5},{7,6},{6,7},{9,8},{8,9},{11,10... | collective-permute-start | bytes 393224 | tf_op jit(solution)/shard_map/ppermute | solution.py:16
  125.1 5.6 %collective-permute-start.44 = (bf16[2048,128]{1,0:T(8,128)(2,1)S(1)}, bf16[2048,128]{1,0:T(8,128)(2,1)S(1)}, u32[]{:S(2)}, u32[]{:S(2)}) collective-permute-start(bf16[2048,128]{1,0:T(8,128)(2,1)S(1)} %shard_map.185.mine), channel_id=1, source_target_pairs={{1,0},{0,1},{3,2},{2,3},{5,4},{4,5},{7,6},{6,7},{9,8},{8,9},{11,10... | collective-permute-start | bytes 1572872 | tf_op jit(solution)/shard_map/ppermute | solution.py:16
  126.0 10.2 %collective-permute-start.47 = (bf16[512,128]{1,0:T(8,128)(2,1)S(1)}, bf16[512,128]{1,0:T(8,128)(2,1)S(1)}, u32[]{:S(2)}, u32[]{:S(2)}) collective-permute-start(bf16[512,128]{1,0:T(8,128)(2,1)S(1)} %get-tuple-element.219), channel_id=1, source_target_pairs={{12,0},{0,4},{4,8},{8,12},{13,1},{1,5},{5,9},{9,13},{14,2},{2,6},{... | collective-permute-start | bytes 393224 | tf_op jit(solution)/shard_map/ppermute | solution.py:16
  126.1 12.9 %collective-permute-start.46 = (bf16[512,128]{1,0:T(8,128)(2,1)S(1)}, bf16[512,128]{1,0:T(8,128)(2,1)S(1)}, u32[]{:S(2)}, u32[]{:S(2)}) collective-permute-start(bf16[512,128]{1,0:T(8,128)(2,1)S(1)} %get-tuple-element.219), channel_id=1, source_target_pairs={{8,0},{12,4},{0,8},{4,12},{9,1},{13,5},{1,9},{5,13},{10,2},{14,6},... | collective-permute-start | bytes 393224 | tf_op jit(solution)/shard_map/ppermute | solution.py:16
  128.4 10.6 %collective-permute-start.45 = (bf16[512,128]{1,0:T(8,128)(2,1)S(1)}, bf16[512,128]{1,0:T(8,128)(2,1)S(1)}, u32[]{:S(2)}, u32[]{:S(2)}) collective-permute-start(bf16[512,128]{1,0:T(8,128)(2,1)S(1)} %get-tuple-element.219), channel_id=1, source_target_pairs={{4,0},{8,4},{12,8},{0,12},{5,1},{9,5},{13,9},{1,13},{6,2},{10,6},{... | collective-permute-start | bytes 393224 | tf_op jit(solution)/shard_map/ppermute | solution.py:16
  139.0 10.4 %collective-permute-start.59 = (bf16[1536,128]{1,0:T(8,128)(2,1)S(1)}, bf16[1536,128]{1,0:T(8,128)(2,1)S(1)}, u32[]{:S(2)}, u32[]{:S(2)}) collective-permute-start(bf16[1536,128]{1,0:T(8,128)(2,1)S(1)} %shard_map.189.mine), channel_id=1, source_target_pairs={{2,0},{0,2},{3,1},{1,3},{6,4},{4,6},{7,5},{5,7},{10,8},{8,10},{11,... | collective-permute-start | bytes 1179656 | tf_op jit(solution)/shard_map/ppermute | solution.py:16
  139.9 9.5 %collective-permute-start.48 = (bf16[1536,128]{1,0:T(8,128)(2,1)S(1)}, bf16[1536,128]{1,0:T(8,128)(2,1)S(1)}, u32[]{:S(2)}, u32[]{:S(2)}) collective-permute-start(bf16[1536,128]{1,0:T(8,128)(2,1)S(1)} %shard_map.189.mine), channel_id=1, source_target_pairs={{1,0},{0,1},{3,2},{2,3},{5,4},{4,5},{7,6},{6,7},{9,8},{8,9},{11,10... | collective-permute-start | bytes 1179656 | tf_op jit(solution)/shard_map/ppermute | solution.py:16
  140.8 14.1 %collective-permute-start.50 = (bf16[448,256]{1,0:T(8,128)(2,1)S(1)}, bf16[448,256]{1,0:T(8,128)(2,1)S(1)}, u32[]{:S(2)}, u32[]{:S(2)}) collective-permute-start(bf16[448,256]{1,0:T(8,128)(2,1)S(1)} %get-tuple-element.242), channel_id=1, source_target_pairs={{12,0},{0,4},{4,8},{8,12},{13,1},{1,5},{5,9},{9,13},{14,2},{2,6},{... | collective-permute-start | bytes 688136 | tf_op jit(solution)/shard_map/ppermute | solution.py:16
  143.8 16.8 %collective-permute-start.51 = (bf16[448,256]{1,0:T(8,128)(2,1)S(1)}, bf16[448,256]{1,0:T(8,128)(2,1)S(1)}, u32[]{:S(2)}, u32[]{:S(2)}) collective-permute-start(bf16[448,256]{1,0:T(8,128)(2,1)S(1)} %get-tuple-element.243), channel_id=1, source_target_pairs={{8,0},{12,4},{0,8},{4,12},{9,1},{13,5},{1,9},{5,13},{10,2},{14,6},... | collective-permute-start | bytes 688136 | tf_op jit(solution)/shard_map/ppermute | solution.py:16
  144.4 16.2 %collective-permute-start.52 = (bf16[448,256]{1,0:T(8,128)(2,1)S(1)}, bf16[448,256]{1,0:T(8,128)(2,1)S(1)}, u32[]{:S(2)}, u32[]{:S(2)}) collective-permute-start(bf16[448,256]{1,0:T(8,128)(2,1)S(1)} %get-tuple-element.244), channel_id=1, source_target_pairs={{4,0},{8,4},{12,8},{0,12},{5,1},{9,5},{13,9},{1,13},{6,2},{10,6},{... | collective-permute-start | bytes 688136 | tf_op jit(solution)/shard_map/ppermute | solution.py:16
  149.4 26.8 %collective-permute-start.60 = (bf16[1536,128]{1,0:T(8,128)(2,1)S(1)}, bf16[1536,128]{1,0:T(8,128)(2,1)S(1)}, u32[]{:S(2)}, u32[]{:S(2)}) collective-permute-start(bf16[1536,128]{1,0:T(8,128)(2,1)S(1)} %collective-permute-done.59.refs_0_), channel_id=1, source_target_pairs={{1,0},{0,1},{3,2},{2,3},{5,4},{4,5},{7,6},{6,7},{9,8},{8,9},{11,10... | collective-permute-start | bytes 1179656 | tf_op jit(solution)/shard_map/ppermute | solution.py:16
  154.4 6.4 %collective-permute-start.49 = (bf16[256,256]{1,0:T(8,128)(2,1)S(1)}, bf16[256,256]{1,0:T(8,128)(2,1)S(1)}, u32[]{:S(2)}, u32[]{:S(2)}) collective-permute-start(bf16[256,256]{1,0:T(8,128)(2,1)S(1)} %get-tuple-element.228), channel_id=1, source_target_pairs={{1,0},{0,1},{3,2},{2,3},{5,4},{4,5},{7,6},{6,7},{9,8},{8,9},{11,10... | collective-permute-start | bytes 393224 | tf_op jit(solution)/shard_map/ppermute | solution.py:16
  160.8 8.5 %collective-permute-start.53 = (bf16[64,256]{1,0:T(8,128)(2,1)S(1)}, bf16[64,256]{1,0:T(8,128)(2,1)S(1)}, u32[]{:S(2)}, u32[]{:S(2)}) collective-permute-start(bf16[64,256]{1,0:T(8,128)(2,1)S(1)} %get-tuple-element.247), channel_id=1, source_target_pairs={{12,0},{0,4},{4,8},{8,12},{13,1},{1,5},{5,9},{9,13},{14,2},{2,6},{... | collective-permute-start | bytes 98312 | tf_op jit(solution)/shard_map/ppermute | solution.py:16
  172.0 11.2 %collective-permute-start.58 = (bf16[512,256]{1,0:T(8,128)(2,1)S(1)}, bf16[512,256]{1,0:T(8,128)(2,1)S(1)}, u32[]{:S(2)}, u32[]{:S(2)}) collective-permute-start(bf16[512,256]{1,0:T(8,128)(2,1)S(1)} %shard_map.195.refs_0_), channel_id=1, source_target_pairs={{12,0},{0,4},{4,8},{8,12},{13,1},{1,5},{5,9},{9,13},{14,2},{2,6},{... | collective-permute-start | bytes 786440 | tf_op jit(solution)/shard_map/ppermute | solution.py:16
  172.1 19.6 %collective-permute-start.57 = (bf16[512,256]{1,0:T(8,128)(2,1)S(1)}, bf16[512,256]{1,0:T(8,128)(2,1)S(1)}, u32[]{:S(2)}, u32[]{:S(2)}) collective-permute-start(bf16[512,256]{1,0:T(8,128)(2,1)S(1)} %shard_map.195.refs_0_), channel_id=1, source_target_pairs={{8,0},{12,4},{0,8},{4,12},{9,1},{13,5},{1,9},{5,13},{10,2},{14,6},... | collective-permute-start | bytes 786440 | tf_op jit(solution)/shard_map/ppermute | solution.py:16
  175.1 16.6 %collective-permute-start.56 = (bf16[512,256]{1,0:T(8,128)(2,1)S(1)}, bf16[512,256]{1,0:T(8,128)(2,1)S(1)}, u32[]{:S(2)}, u32[]{:S(2)}) collective-permute-start(bf16[512,256]{1,0:T(8,128)(2,1)S(1)} %shard_map.195.refs_0_), channel_id=1, source_target_pairs={{4,0},{8,4},{12,8},{0,12},{5,1},{9,5},{13,9},{1,13},{6,2},{10,6},{... | collective-permute-start | bytes 786440 | tf_op jit(solution)/shard_map/ppermute | solution.py:16
  (27 other events, 179.4 us)

commit v6 on v5

--- a/solution.py
+++ b/solution.py
@@ -536,11 +536,10 @@
 
     def weights(args, kinds):
         rows = half * len(kinds)
-        pieces = run(
+        return run(
             on(weight_body, kinds), args, [((rows // faces, narrow), BF16)] * faces,
             scratch=[pltpu.VMEM((rows, narrow), BF16)], flops=2 * mesh_rows * rows * narrow,
         )
-        return add([pieces[0], *over_faces(pieces, -1)])
 
     def from_owners(piece):
         return [piece] + [shifted(piece, "space", k) for k in range(1, faces)]
@@ -574,7 +573,7 @@
     )
 
     enc_got = from_owners(enc_part)[1:]
-    sums_b = weights(
+    pieces_w = weights(
         (state_1, send_1, recv_1, agg_0, grad_1, state_0, send_0, recv_0)
         + (last_b, dec_grad, agg_1, grad_2),
         ((0, 1), (0, 2), (3, 4), (5, 6), (5, 7), (8, 9), (10, 11)),
@@ -586,7 +585,10 @@
         [((grid_rows, narrow), BF16), ((grid_rows, wide), BF16)], scratch=table, hbm=(0,),
         flops=sum_flops + 2 * grid_rows * wide * wide, vmem=grid_vmem,
     )
-    *enc_got, slope_enc, grad_mesh = tie((*enc_got, slope_enc, grad_mesh))
+    outs = tie((slope_enc, grad_mesh, *enc_got, *pieces_w))
+    slope_enc, grad_mesh = outs[:2]
+    enc_got, pieces_w = outs[2 : 1 + faces], outs[1 + faces :]
+    sums_b = add([pieces_w[0], *over_faces(pieces_w, -1)])
     enc_mine = stack(enc_got)
     enc_grad, grad_keep, grad_give = run(
         enc_own_body,

time: 200 us -> 199 us (level); the launches traced: 197 us -> 199 us
  waiting for transfers between devices: 87.6 us -> 95.2 us
  starting transfers between devices: 64.2 us -> 58 us
    ppermute x65, waiting for transfers between devices: 87.6 us -> 95.2 us  [shifted(): lax.ppermute(block, axis, [((i + distance) % count, i) for i in range(cou...]
    ppermute x65, starting transfers between devices: 64.2 us -> 58 us  [shifted(): lax.ppermute(block, axis, [((i + distance) % count, i) for i in range(cou...]
where the time goes in v6:
time: 199 us
  waiting for transfers between devices  95.2 us (48%)
  starting transfers between devices  58 us (29%)
  Pallas kernels  43.9 us (22%)
    ppermute x65, waiting for transfers between devices, shifted(): lax.ppermute(block, axis, [((i + distance) % count, i) for i in range(cou...  95.2 us
    ppermute x65, starting transfers between devices, shifted(): lax.ppermute(block, axis, [((i + distance) % count, i) for i in range(cou...  58 us
    pallas_call x28, Pallas kernels, run(): pl.pallas_call(body, out_shape=[jax.ShapeDtypeStruct(s, d) if i in hbm el...  43.9 us
  transfers between devices with their start and end apart: 65, of which 36 were waited for; matrix products, arithmetic and copies ran while one was open for 0% of the time, Pallas kernels for 14%

profile of v6, /device:TPU:0, one launch (start us, length us, event | category | flops | bytes accessed | tf_op | source)
XLA Modules:
  0.0 198.9 jit_solution(12701222922344394526)
XLA Ops:
  0.7 5.9 %shard_map.170 = (bf16[2048,128]{1,0:T(8,128)(2,1)S(1)}, bf16[2048,128]{1,0:T(8,128)(2,1)S(1)}) custom-call(bf16[2048,512]{1,0:T(8,128)(2,1)} %x.5, bf16[512,512]{1,0:T(8,128)(2,1)} %w.5, s32[1,2048]{1,0:T(1,128)} %bitcast.5, s32[1,2048]{1,0:T(1,128)} %bitcast.10), custom_call_target="tpu_custom_call" | custom-call | flops 2684354560 | tf_op jit(solution)/shard_map/pallas_call | solution.py:75
  7.1 1.5 collective-permute-done.got
  8.8 3.0 %collective-permute-start.1 = (bf16[512,128]{1,0:T(8,128)(2,1)S(1)}, bf16[512,128]{1,0:T(8,128)(2,1)S(1)}, u32[]{:S(2)}, u32[]{:S(2)}) collective-permute-start(bf16[512,128]{1,0:T(8,128)(2,1)S(1)} %get-tuple-element.146), channel_id=1, source_target_pairs={{12,0},{0,4},{4,8},{8,12},{13,1},{1,5},{5,9},{9,13},{14,2},{2,6},{... | collective-permute-start | bytes 393224 | tf_op jit(solution)/shard_map/ppermute | solution.py:16
  11.8 2.6 %collective-permute-start.2 = (bf16[512,128]{1,0:T(8,128)(2,1)S(1)}, bf16[512,128]{1,0:T(8,128)(2,1)S(1)}, u32[]{:S(2)}, u32[]{:S(2)}) collective-permute-start(bf16[512,128]{1,0:T(8,128)(2,1)S(1)} %get-tuple-element.147), channel_id=1, source_target_pairs={{8,0},{12,4},{0,8},{4,12},{9,1},{13,5},{1,9},{5,13},{10,2},{14,6},... | collective-permute-start | bytes 393224 | tf_op jit(solution)/shard_map/ppermute | solution.py:16
  15.7 4.1 %shard_map.176 = (bf16[2048,128]{1,0:T(8,128)(2,1)S(1)}, bf16[2048,128]{1,0:T(8,128)(2,1)S(1)}) custom-call(s32[1,2048]{1,0:T(1,128)S(1)} %bitcast.6, s32[1,2048]{1,0:T(1,128)S(1)} %bitcast.11, bf16[2048,256]{1,0:T(8,128)(2,1)} %cotangent.1), custom_call_target="tpu_custom_call" | custom-call | flops 2147483648 | tf_op jit(solution)/shard_map/pallas_call | solution.py:75
  23.4 1.6 collective-permute-start.6
  25.0 3.8 %collective-permute-done.6.refs_2_ = bf16[512,128]{1,0:T(8,128)(2,1)S(1)} collective-permute-done((bf16[512,128]{1,0:T(8,128)(2,1)S(1)}, bf16[512,128]{1,0:T(8,128)(2,1)S(1)}, u32[]{:S(2)}, u32[]{:S(2)}) %collective-permute-start.6) | collective-permute-done | bytes 131104 | tf_op jit(solution)/shard_map/ppermute | solution.py:16
  30.7 3.4 %collective-permute-start.8 = (bf16[512,128]{1,0:T(8,128)(2,1)S(1)}, bf16[512,128]{1,0:T(8,128)(2,1)S(1)}, u32[]{:S(2)}, u32[]{:S(2)}) collective-permute-start(bf16[512,128]{1,0:T(8,128)(2,1)S(1)} %get-tuple-element.154.own), channel_id=1, source_target_pairs={{12,0},{0,4},{4,8},{8,12},{13,1},{1,5},{5,9},{9,13},{14,2},{2,6},{... | collective-permute-start | bytes 393224 | tf_op jit(solution)/shard_map/ppermute | solution.py:16
  34.9 4.1 %collective-permute-done.8.below = bf16[512,128]{1,0:T(8,128)(2,1)S(1)} collective-permute-done((bf16[512,128]{1,0:T(8,128)(2,1)S(1)}, bf16[512,128]{1,0:T(8,128)(2,1)S(1)}, u32[]{:S(2)}, u32[]{:S(2)}) %collective-permute-start.8) | collective-permute-done | bytes 131104 | tf_op jit(solution)/shard_map/ppermute | solution.py:16
  39.0 2.3 %collective-permute-done.9.above = bf16[512,128]{1,0:T(8,128)(2,1)S(1)} collective-permute-done((bf16[512,128]{1,0:T(8,128)(2,1)S(1)}, bf16[512,128]{1,0:T(8,128)(2,1)S(1)}, u32[]{:S(2)}, u32[]{:S(2)}) %collective-permute-start.9) | collective-permute-done | bytes 131104 | tf_op jit(solution)/shard_map/ppermute | solution.py:16
  41.3 1.8 shard_map.175
  43.1 1.6 collective-permute-start.12
  45.3 3.3 %collective-permute-start.15 = (bf16[512,128]{1,0:T(8,128)(2,1)S(1)}, bf16[512,128]{1,0:T(8,128)(2,1)S(1)}, u32[]{:S(2)}, u32[]{:S(2)}) collective-permute-start(bf16[512,128]{1,0:T(8,128)(2,1)S(1)} %get-tuple-element.167), channel_id=1, source_target_pairs={{4,0},{8,4},{12,8},{0,12},{5,1},{9,5},{13,9},{1,13},{6,2},{10,6},{... | collective-permute-start | bytes 393224 | tf_op jit(solution)/shard_map/ppermute | solution.py:16
  48.8 4.0 %collective-permute-done.14.refs_1_ = bf16[512,128]{1,0:T(8,128)(2,1)S(1)} collective-permute-done((bf16[512,128]{1,0:T(8,128)(2,1)S(1)}, bf16[512,128]{1,0:T(8,128)(2,1)S(1)}, u32[]{:S(2)}, u32[]{:S(2)}) %collective-permute-start.14) | collective-permute-done | bytes 131104 | tf_op jit(solution)/shard_map/ppermute | solution.py:16
  54.5 2.5 %collective-permute-start.16 = (bf16[512,128]{1,0:T(8,128)(2,1)S(1)}, bf16[512,128]{1,0:T(8,128)(2,1)S(1)}, u32[]{:S(2)}, u32[]{:S(2)}) collective-permute-start(bf16[512,128]{1,0:T(8,128)(2,1)S(1)} %get-tuple-element.173.own), channel_id=1, source_target_pairs={{12,0},{0,4},{4,8},{8,12},{13,1},{1,5},{5,9},{9,13},{14,2},{2,6},{... | collective-permute-start | bytes 393224 | tf_op jit(solution)/shard_map/ppermute | solution.py:16
  58.3 5.4 %collective-permute-done.18.refs_3_ = bf16[512,128]{1,0:T(8,128)(2,1)S(1)} collective-permute-done((bf16[512,128]{1,0:T(8,128)(2,1)S(1)}, bf16[512,128]{1,0:T(8,128)(2,1)S(1)}, u32[]{:S(2)}, u32[]{:S(2)}) %collective-permute-start.18) | collective-permute-done | bytes 131104 | tf_op jit(solution)/shard_map/ppermute | solution.py:16
  63.7 2.4 %collective-permute-done.17.above = bf16[512,128]{1,0:T(8,128)(2,1)S(1)} collective-permute-done((bf16[512,128]{1,0:T(8,128)(2,1)S(1)}, bf16[512,128]{1,0:T(8,128)(2,1)S(1)}, u32[]{:S(2)}, u32[]{:S(2)}) %collective-permute-start.17) | collective-permute-done | bytes 131104 | tf_op jit(solution)/shard_map/ppermute | solution.py:16
  66.8 1.8 shard_map.179
  68.6 1.6 collective-permute-start.20
  70.7 1.6 collective-permute-done.23.refs_6_
  72.3 2.2 %collective-permute-done.20.refs_2_ = bf16[512,128]{1,0:T(8,128)(2,1)S(1)} collective-permute-done((bf16[512,128]{1,0:T(8,128)(2,1)S(1)}, bf16[512,128]{1,0:T(8,128)(2,1)S(1)}, u32[]{:S(2)}, u32[]{:S(2)}) %collective-permute-start.20) | collective-permute-done | bytes 131104 | tf_op jit(solution)/shard_map/ppermute | solution.py:16
  75.8 3.5 %shard_map.181 = (bf16[512,512]{1,0:T(8,128)(2,1)S(1)}, bf16[512,512]{1,0:T(8,128)(2,1)S(1)}, bf16[512,128]{1,0:T(8,128)(2,1)S(1)}, bf16[512,512]{1,0:T(8,128)(2...) custom-call(f32[512,512]{1,0:T(8,128)S(1)} %get-tuple-element.172.st, ...), custom_call_target="tpu_custom_call" | custom-call | flops 2013265920 | tf_op jit(solution)/shard_map/pallas_call | solution.py:75
  82.2 2.7 %collective-permute-done.28.refs_6_ = bf16[512,128]{1,0:T(8,128)(2,1)S(1)} collective-permute-done((bf16[512,128]{1,0:T(8,128)(2,1)S(1)}, bf16[512,128]{1,0:T(8,128)(2,1)S(1)}, u32[]{:S(2)}, u32[]{:S(2)}) %collective-permute-start.28) | collective-permute-done | bytes 131104 | tf_op jit(solution)/shard_map/ppermute | solution.py:16
  84.9 4.0 %collective-permute-done.25.refs_1_ = bf16[512,128]{1,0:T(8,128)(2,1)S(1)} collective-permute-done((bf16[512,128]{1,0:T(8,128)(2,1)S(1)}, bf16[512,128]{1,0:T(8,128)(2,1)S(1)}, u32[]{:S(2)}, u32[]{:S(2)}) %collective-permute-start.25) | collective-permute-done | bytes 131104 | tf_op jit(solution)/shard_map/ppermute | solution.py:16
  92.3 1.7 collective-permute-done.31.refs_2_
  94.0 2.1 %collective-permute-done.33.refs_1_ = bf16[512,128]{1,0:T(8,128)(2,1)S(1)} collective-permute-done((bf16[512,128]{1,0:T(8,128)(2,1)S(1)}, bf16[512,128]{1,0:T(8,128)(2,1)S(1)}, u32[]{:S(2)}, u32[]{:S(2)}) %collective-permute-start.33) | collective-permute-done | bytes 131104 | tf_op jit(solution)/shard_map/ppermute | solution.py:16
  96.2 3.7 %collective-permute-done.34.refs_3_ = bf16[512,128]{1,0:T(8,128)(2,1)S(1)} collective-permute-done((bf16[512,128]{1,0:T(8,128)(2,1)S(1)}, bf16[512,128]{1,0:T(8,128)(2,1)S(1)}, u32[]{:S(2)}, u32[]{:S(2)}) %collective-permute-start.34) | collective-permute-done | bytes 131104 | tf_op jit(solution)/shard_map/ppermute | solution.py:16
  99.9 3.0 %shard_map.183 = (bf16[512,512]{1,0:T(8,128)(2,1)S(1)}, bf16[512,512]{1,0:T(8,128)(2,1)S(1)}, f32[512,512]{1,0:T(8,128)S(1)}, bf16[512,128]{1,0:T(8,128)(2,1)S(1...) custom-call(f32[512,512]{1,0:T(8,128)S(1)} %get-tuple-element.194.grad.refs_11_, ...), custom_call_target="tpu_custom_call" | custom-call | flops 1744830464 | tf_op jit(solution)/shard_map/pallas_call | solution.py:75
  104.0 1.7 collective-permute-start.35
  106.0 2.2 %collective-permute-done.38.refs_6_ = bf16[512,128]{1,0:T(8,128)(2,1)S(1)} collective-permute-done((bf16[512,128]{1,0:T(8,128)(2,1)S(1)}, bf16[512,128]{1,0:T(8,128)(2,1)S(1)}, u32[]{:S(2)}, u32[]{:S(2)}) %collective-permute-start.38) | collective-permute-done | bytes 131104 | tf_op jit(solution)/shard_map/ppermute | solution.py:16
  108.2 1.7 collective-permute-done.35.refs_1_
  109.9 3.3 %collective-permute-done.36.refs_2_ = bf16[512,128]{1,0:T(8,128)(2,1)S(1)} collective-permute-done((bf16[512,128]{1,0:T(8,128)(2,1)S(1)}, bf16[512,128]{1,0:T(8,128)(2,1)S(1)}, u32[]{:S(2)}, u32[]{:S(2)}) %collective-permute-start.36) | collective-permute-done | bytes 131104 | tf_op jit(solution)/shard_map/ppermute | solution.py:16
  115.7 2.6 %collective-permute-done.41.refs_2_ = bf16[512,128]{1,0:T(8,128)(2,1)S(1)} collective-permute-done((bf16[512,128]{1,0:T(8,128)(2,1)S(1)}, bf16[512,128]{1,0:T(8,128)(2,1)S(1)}, u32[]{:S(2)}, u32[]{:S(2)}) %collective-permute-start.41) | collective-permute-done | bytes 131104 | tf_op jit(solution)/shard_map/ppermute | solution.py:16
  118.3 5.8 %collective-permute-done.43.refs_2_ = bf16[512,128]{1,0:T(8,128)(2,1)S(1)} collective-permute-done((bf16[512,128]{1,0:T(8,128)(2,1)S(1)}, bf16[512,128]{1,0:T(8,128)(2,1)S(1)}, u32[]{:S(2)}, u32[]{:S(2)}) %collective-permute-start.43) | collective-permute-done | bytes 131104 | tf_op jit(solution)/shard_map/ppermute | solution.py:16
  125.0 1.8 collective-permute-start.45
  130.0 5.5 %shard_map.186 = (bf16[2048,256]{1,0:T(8,128)(2,1)}, bf16[2048,512]{1,0:T(8,128)(2,1)S(1)}) custom-call(bf16[2048,512]{1,0:T(8,128)(2,1)S(1)} %copy-done.5, bf16[512,512]{1,0:T(8,128)(2,1)S(1)} %copy-done.7, s32[1,2048]{1,0:T(1,128)S(1)} %bitcast.7, s32[1,2048]{1,0:T(1,128)S(1)} %bitcast.12, bf16[2048,128]{1,0:T(8,128)(2,1)S(1)} %shard_map.185.mine, ...), custom_call_target="tpu_custom_call" | custom-call | flops 3221225472 | tf_op jit(solution)/shard_map/pallas_call | solution.py:75
  135.5 3.5 %collective-permute-done.46.refs_1_ = bf16[512,128]{1,0:T(8,128)(2,1)S(1)} collective-permute-done((bf16[512,128]{1,0:T(8,128)(2,1)S(1)}, bf16[512,128]{1,0:T(8,128)(2,1)S(1)}, u32[]{:S(2)}, u32[]{:S(2)}) %collective-permute-start.46) | collective-permute-done | bytes 131104 | tf_op jit(solution)/shard_map/ppermute | solution.py:16
  140.3 1.9 collective-permute-start.51
  142.2 2.9 %collective-permute-start.52 = (bf16[448,256]{1,0:T(8,128)(2,1)S(1)}, bf16[448,256]{1,0:T(8,128)(2,1)S(1)}, u32[]{:S(2)}, u32[]{:S(2)}) collective-permute-start(bf16[448,256]{1,0:T(8,128)(2,1)S(1)} %get-tuple-element.252), channel_id=1, source_target_pairs={{4,0},{8,4},{12,8},{0,12},{5,1},{9,5},{13,9},{1,13},{6,2},{10,6},{... | collective-permute-start | bytes 688136 | tf_op jit(solution)/shard_map/ppermute | solution.py:16
  145.1 4.6 %collective-permute-done.59.refs_0_ = bf16[1536,128]{1,0:T(8,128)(2,1)S(1)} collective-permute-done((bf16[1536,128]{1,0:T(8,128)(2,1)S(1)}, bf16[1536,128]{1,0:T(8,128)(2,1)S(1)}, u32[]{:S(2)}, u32[]{:S(2)}) %collective-permute-start.59) | collective-permute-done | bytes 393248 | tf_op jit(solution)/shard_map/ppermute | solution.py:16
  149.7 5.0 %shard_map.191 = (bf16[2048,256]{1,0:T(8,128)(2,1)S(1)}, f32[256,256]{1,0:T(8,128)S(1)}, bf16[256,256]{1,0:T(8,128)(2,1)S(1)}) custom-call(bf16[2048,512]{1,0:T(8,128)(2,1)S(1)} %copy-done.5, s32[1,2048]{1,0:T(1,128)S(1)} %bitcast.8, s32[1,2048]{1,0:T(1,128)S(1)} %bitcast.13, bf16[2048,512]{1,0:T(8,128)(2,1)S(1)} %get-tuple-element.238.slope, ...), custom_call_target="tpu_custom_call" | custom-call | flops 2684354560 | tf_op jit(solution)/shard_map/pallas_call | solution.py:75
  155.3 4.2 %collective-permute-done.51.refs_2_ = bf16[448,256]{1,0:T(8,128)(2,1)S(1)} collective-permute-done((bf16[448,256]{1,0:T(8,128)(2,1)S(1)}, bf16[448,256]{1,0:T(8,128)(2,1)S(1)}, u32[]{:S(2)}, u32[]{:S(2)}) %collective-permute-start.51) | collective-permute-done | bytes 229408 | tf_op jit(solution)/shard_map/ppermute | solution.py:16
  159.7 4.8 %collective-permute-start.53 = (bf16[64,256]{1,0:T(8,128)(2,1)S(1)}, bf16[64,256]{1,0:T(8,128)(2,1)S(1)}, u32[]{:S(2)}, u32[]{:S(2)}) collective-permute-start(bf16[64,256]{1,0:T(8,128)(2,1)S(1)} %get-tuple-element.255), channel_id=1, source_target_pairs={{12,0},{0,4},{4,8},{8,12},{13,1},{1,5},{5,9},{9,13},{14,2},{2,6},{... | collective-permute-start | bytes 98312 | tf_op jit(solution)/shard_map/ppermute | solution.py:16
  164.5 2.2 %collective-permute-start.54 = (bf16[64,256]{1,0:T(8,128)(2,1)S(1)}, bf16[64,256]{1,0:T(8,128)(2,1)S(1)}, u32[]{:S(2)}, u32[]{:S(2)}) collective-permute-start(bf16[64,256]{1,0:T(8,128)(2,1)S(1)} %get-tuple-element.256), channel_id=1, source_target_pairs={{8,0},{12,4},{0,8},{4,12},{9,1},{13,5},{1,9},{5,13},{10,2},{14,6},... | collective-permute-start | bytes 98312 | tf_op jit(solution)/shard_map/ppermute | solution.py:16
  170.6 2.2 %collective-permute-start.56 = (bf16[512,256]{1,0:T(8,128)(2,1)S(1)}, bf16[512,256]{1,0:T(8,128)(2,1)S(1)}, u32[]{:S(2)}, u32[]{:S(2)}) collective-permute-start(bf16[512,256]{1,0:T(8,128)(2,1)S(1)} %shard_map.195.refs_0_), channel_id=1, source_target_pairs={{4,0},{8,4},{12,8},{0,12},{5,1},{9,5},{13,9},{1,13},{6,2},{10,6},{... | collective-permute-start | bytes 786440 | tf_op jit(solution)/shard_map/ppermute | solution.py:16
  173.6 6.3 %shard_map.196 = bf16[2048,256]{1,0:T(8,128)(2,1)} custom-call(s32[1,2048]{1,0:T(1,128)S(1)} %bitcast.9, s32[1,2048]{1,0:T(1,128)S(1)} %bitcast.14, bf16[2048,256]{1,0:T(8,128)(2,1)} %cotangent.1, bf16[2048,256]{1,0:T(8,128)(2,1)S(1)} %get-tuple-element.258.enc_grad, bf16[512,512]{1,0:T(8,128)(2,1)S(1)} %get-tuple-element.239.enc_all, ...), custom_call_target="tpu_custom_call" | custom-call | flops 2684354560 | tf_op jit(solution)/shard_map/pallas_call | solution.py:75
  180.0 14.0 %collective-permute-done.57.refs_2_ = bf16[512,256]{1,0:T(8,128)(2,1)S(1)} collective-permute-done((bf16[512,256]{1,0:T(8,128)(2,1)S(1)}, bf16[512,256]{1,0:T(8,128)(2,1)S(1)}, u32[]{:S(2)}, u32[]{:S(2)}) %collective-permute-start.57) | collective-permute-done | bytes 262176 | tf_op jit(solution)/shard_map/ppermute | solution.py:16
  196.6 2.3 %shard_map.197 = (f32[2,512,256]{2,1,0:T(8,128)}, f32[2,512,256]{2,1,0:T(8,128)}, f32[2,512,256]{2,1,0:T(8,128)}, f32[512,256]{1,0:T(8,128)}, f32[512,256]{1,0:T(8,128)}) custom-call(bf16[512,256]{1,0:T(8,128)(2,1)S(1)} %shard_map.195.refs_0_, bf16[512,256]{1,0:T(8,128)(2,1)S(1)} %collective-permute-done.56.refs_1_, ...), custom_call_target="tpu_custom_call" | custom-call | tf_op jit(solution)/shard_map/pallas_call | solution.py:75
  (130 shorter events, 38.2 us)
Async XLA Ops:
  8.8 13.2 %collective-permute-start.1 = (bf16[512,128]{1,0:T(8,128)(2,1)S(1)}, bf16[512,128]{1,0:T(8,128)(2,1)S(1)}, u32[]{:S(2)}, u32[]{:S(2)}) collective-permute-start(bf16[512,128]{1,0:T(8,128)(2,1)S(1)} %get-tuple-element.146), channel_id=1, source_target_pairs={{12,0},{0,4},{4,8},{8,12},{13,1},{1,5},{5,9},{9,13},{14,2},{2,6},{... | collective-permute-start | bytes 393224 | tf_op jit(solution)/shard_map/ppermute | solution.py:16
  11.8 11.5 %collective-permute-start.2 = (bf16[512,128]{1,0:T(8,128)(2,1)S(1)}, bf16[512,128]{1,0:T(8,128)(2,1)S(1)}, u32[]{:S(2)}, u32[]{:S(2)}) collective-permute-start(bf16[512,128]{1,0:T(8,128)(2,1)S(1)} %get-tuple-element.147), channel_id=1, source_target_pairs={{8,0},{12,4},{0,8},{4,12},{9,1},{13,5},{1,9},{5,13},{10,2},{14,6},... | collective-permute-start | bytes 393224 | tf_op jit(solution)/shard_map/ppermute | solution.py:16
  14.4 8.9 %collective-permute-start.3 = (bf16[512,128]{1,0:T(8,128)(2,1)S(1)}, bf16[512,128]{1,0:T(8,128)(2,1)S(1)}, u32[]{:S(2)}, u32[]{:S(2)}) collective-permute-start(bf16[512,128]{1,0:T(8,128)(2,1)S(1)} %get-tuple-element.148), channel_id=1, source_target_pairs={{4,0},{8,4},{12,8},{0,12},{5,1},{9,5},{13,9},{1,13},{6,2},{10,6},{... | collective-permute-start | bytes 393224 | tf_op jit(solution)/shard_map/ppermute | solution.py:16
  19.8 15.0 %collective-permute-start.10 = (bf16[2048,128]{1,0:T(8,128)(2,1)S(1)}, bf16[2048,128]{1,0:T(8,128)(2,1)S(1)}, u32[]{:S(2)}, u32[]{:S(2)}) collective-permute-start(bf16[2048,128]{1,0:T(8,128)(2,1)S(1)} %get-tuple-element.160), channel_id=1, source_target_pairs={{1,0},{0,1},{3,2},{2,3},{5,4},{4,5},{7,6},{6,7},{9,8},{8,9},{11,10... | collective-permute-start | bytes 1572872 | tf_op jit(solution)/shard_map/ppermute | solution.py:16
  23.4 5.4 %collective-permute-start.6 = (bf16[512,128]{1,0:T(8,128)(2,1)S(1)}, bf16[512,128]{1,0:T(8,128)(2,1)S(1)}, u32[]{:S(2)}, u32[]{:S(2)}) collective-permute-start(bf16[512,128]{1,0:T(8,128)(2,1)S(1)} %shard_map.172.refs_0_), channel_id=1, source_target_pairs={{2,0},{0,2},{3,1},{1,3},{6,4},{4,6},{7,5},{5,7},{10,8},{8,10},{11,... | collective-permute-start | bytes 393224 | tf_op jit(solution)/shard_map/ppermute | solution.py:16
  30.7 8.3 %collective-permute-start.8 = (bf16[512,128]{1,0:T(8,128)(2,1)S(1)}, bf16[512,128]{1,0:T(8,128)(2,1)S(1)}, u32[]{:S(2)}, u32[]{:S(2)}) collective-permute-start(bf16[512,128]{1,0:T(8,128)(2,1)S(1)} %get-tuple-element.154.own), channel_id=1, source_target_pairs={{12,0},{0,4},{4,8},{8,12},{13,1},{1,5},{5,9},{9,13},{14,2},{2,6},{... | collective-permute-start | bytes 393224 | tf_op jit(solution)/shard_map/ppermute | solution.py:16
  34.1 7.2 %collective-permute-start.9 = (bf16[512,128]{1,0:T(8,128)(2,1)S(1)}, bf16[512,128]{1,0:T(8,128)(2,1)S(1)}, u32[]{:S(2)}, u32[]{:S(2)}) collective-permute-start(bf16[512,128]{1,0:T(8,128)(2,1)S(1)} %get-tuple-element.154.own), channel_id=1, source_target_pairs={{4,0},{8,4},{12,8},{0,12},{5,1},{9,5},{13,9},{1,13},{6,2},{10,6},{... | collective-permute-start | bytes 393224 | tf_op jit(solution)/shard_map/ppermute | solution.py:16
  43.1 5.4 %collective-permute-start.12 = (bf16[512,128]{1,0:T(8,128)(2,1)S(1)}, bf16[512,128]{1,0:T(8,128)(2,1)S(1)}, u32[]{:S(2)}, u32[]{:S(2)}) collective-permute-start(bf16[512,128]{1,0:T(8,128)(2,1)S(1)} %get-tuple-element.168.refs_0_), channel_id=1, source_target_pairs={{2,0},{0,2},{3,1},{1,3},{6,4},{4,6},{7,5},{5,7},{10,8},{8,10},{11,... | collective-permute-start | bytes 393224 | tf_op jit(solution)/shard_map/ppermute | solution.py:16
  44.7 8.1 %collective-permute-start.14 = (bf16[512,128]{1,0:T(8,128)(2,1)S(1)}, bf16[512,128]{1,0:T(8,128)(2,1)S(1)}, u32[]{:S(2)}, u32[]{:S(2)}) collective-permute-start(bf16[512,128]{1,0:T(8,128)(2,1)S(1)} %get-tuple-element.166), channel_id=1, source_target_pairs={{12,0},{0,4},{4,8},{8,12},{13,1},{1,5},{5,9},{9,13},{14,2},{2,6},{... | collective-permute-start | bytes 393224 | tf_op jit(solution)/shard_map/ppermute | solution.py:16
  45.3 8.4 %collective-permute-start.15 = (bf16[512,128]{1,0:T(8,128)(2,1)S(1)}, bf16[512,128]{1,0:T(8,128)(2,1)S(1)}, u32[]{:S(2)}, u32[]{:S(2)}) collective-permute-start(bf16[512,128]{1,0:T(8,128)(2,1)S(1)} %get-tuple-element.167), channel_id=1, source_target_pairs={{4,0},{8,4},{12,8},{0,12},{5,1},{9,5},{13,9},{1,13},{6,2},{10,6},{... | collective-permute-start | bytes 393224 | tf_op jit(solution)/shard_map/ppermute | solution.py:16
  48.6 5.1 %collective-permute-start.13 = (bf16[512,128]{1,0:T(8,128)(2,1)S(1)}, bf16[512,128]{1,0:T(8,128)(2,1)S(1)}, u32[]{:S(2)}, u32[]{:S(2)}) collective-permute-start(bf16[512,128]{1,0:T(8,128)(2,1)S(1)} %collective-permute-done.12.refs_2_), channel_id=1, source_target_pairs={{1,0},{0,1},{3,2},{2,3},{5,4},{4,5},{7,6},{6,7},{9,8},{8,9},{11,10... | collective-permute-start | bytes 393224 | tf_op jit(solution)/shard_map/ppermute | solution.py:16
  48.6 15.1 %collective-permute-start.18 = (bf16[512,128]{1,0:T(8,128)(2,1)S(1)}, bf16[512,128]{1,0:T(8,128)(2,1)S(1)}, u32[]{:S(2)}, u32[]{:S(2)}) collective-permute-start(bf16[512,128]{1,0:T(8,128)(2,1)S(1)} %get-tuple-element.174), channel_id=1, source_target_pairs={{8,0},{12,4},{0,8},{4,12},{9,1},{13,5},{1,9},{5,13},{10,2},{14,6},... | collective-permute-start | bytes 393224 | tf_op jit(solution)/shard_map/ppermute | solution.py:16
  54.5 9.2 %collective-permute-start.16 = (bf16[512,128]{1,0:T(8,128)(2,1)S(1)}, bf16[512,128]{1,0:T(8,128)(2,1)S(1)}, u32[]{:S(2)}, u32[]{:S(2)}) collective-permute-start(bf16[512,128]{1,0:T(8,128)(2,1)S(1)} %get-tuple-element.173.own), channel_id=1, source_target_pairs={{12,0},{0,4},{4,8},{8,12},{13,1},{1,5},{5,9},{9,13},{14,2},{2,6},{... | collective-permute-start | bytes 393224 | tf_op jit(solution)/shard_map/ppermute | solution.py:16
  57.0 9.1 %collective-permute-start.17 = (bf16[512,128]{1,0:T(8,128)(2,1)S(1)}, bf16[512,128]{1,0:T(8,128)(2,1)S(1)}, u32[]{:S(2)}, u32[]{:S(2)}) collective-permute-start(bf16[512,128]{1,0:T(8,128)(2,1)S(1)} %get-tuple-element.173.own), channel_id=1, source_target_pairs={{4,0},{8,4},{12,8},{0,12},{5,1},{9,5},{13,9},{1,13},{6,2},{10,6},{... | collective-permute-start | bytes 393224 | tf_op jit(solution)/shard_map/ppermute | solution.py:16
  66.2 6.1 %collective-permute-start.23 = (bf16[512,128]{1,0:T(8,128)(2,1)S(1)}, bf16[512,128]{1,0:T(8,128)(2,1)S(1)}, u32[]{:S(2)}, u32[]{:S(2)}) collective-permute-start(bf16[512,128]{1,0:T(8,128)(2,1)S(1)} %shard_map.180.refs_4_), channel_id=1, source_target_pairs={{2,0},{0,2},{3,1},{1,3},{6,4},{4,6},{7,5},{5,7},{10,8},{8,10},{11,... | collective-permute-start | bytes 393224 | tf_op jit(solution)/shard_map/ppermute | solution.py:16
  68.6 5.9 %collective-permute-start.20 = (bf16[512,128]{1,0:T(8,128)(2,1)S(1)}, bf16[512,128]{1,0:T(8,128)(2,1)S(1)}, u32[]{:S(2)}, u32[]{:S(2)}) collective-permute-start(bf16[512,128]{1,0:T(8,128)(2,1)S(1)} %get-tuple-element.180.refs_0_), channel_id=1, source_target_pairs={{2,0},{0,2},{3,1},{1,3},{6,4},{4,6},{7,5},{5,7},{10,8},{8,10},{11,... | collective-permute-start | bytes 393224 | tf_op jit(solution)/shard_map/ppermute | solution.py:16
  79.3 5.6 %collective-permute-start.28 = (bf16[512,128]{1,0:T(8,128)(2,1)S(1)}, bf16[512,128]{1,0:T(8,128)(2,1)S(1)}, u32[]{:S(2)}, u32[]{:S(2)}) collective-permute-start(bf16[512,128]{1,0:T(8,128)(2,1)S(1)} %get-tuple-element.200.refs_4_), channel_id=1, source_target_pairs={{2,0},{0,2},{3,1},{1,3},{6,4},{4,6},{7,5},{5,7},{10,8},{8,10},{11,... | collective-permute-start | bytes 393224 | tf_op jit(solution)/shard_map/ppermute | solution.py:16
  80.2 8.7 %collective-permute-start.27 = (bf16[512,128]{1,0:T(8,128)(2,1)S(1)}, bf16[512,128]{1,0:T(8,128)(2,1)S(1)}, u32[]{:S(2)}, u32[]{:S(2)}) collective-permute-start(bf16[512,128]{1,0:T(8,128)(2,1)S(1)} %get-tuple-element.200.refs_4_), channel_id=1, source_target_pairs={{1,0},{0,1},{3,2},{2,3},{5,4},{4,5},{7,6},{6,7},{9,8},{8,9},{11,10... | collective-permute-start | bytes 393224 | tf_op jit(solution)/shard_map/ppermute | solution.py:16
  80.2 8.7 %collective-permute-start.25 = (bf16[512,128]{1,0:T(8,128)(2,1)S(1)}, bf16[512,128]{1,0:T(8,128)(2,1)S(1)}, u32[]{:S(2)}, u32[]{:S(2)}) collective-permute-start(bf16[512,128]{1,0:T(8,128)(2,1)S(1)} %get-tuple-element.185), channel_id=1, source_target_pairs={{4,0},{8,4},{12,8},{0,12},{5,1},{9,5},{13,9},{1,13},{6,2},{10,6},{... | collective-permute-start | bytes 393224 | tf_op jit(solution)/shard_map/ppermute | solution.py:16
  81.1 7.8 %collective-permute-start.26 = (bf16[512,128]{1,0:T(8,128)(2,1)S(1)}, bf16[512,128]{1,0:T(8,128)(2,1)S(1)}, u32[]{:S(2)}, u32[]{:S(2)}) collective-permute-start(bf16[512,128]{1,0:T(8,128)(2,1)S(1)} %get-tuple-element.186), channel_id=1, source_target_pairs={{12,0},{0,4},{4,8},{8,12},{13,1},{1,5},{5,9},{9,13},{14,2},{2,6},{... | collective-permute-start | bytes 393224 | tf_op jit(solution)/shard_map/ppermute | solution.py:16
  89.0 5.0 %collective-permute-start.31 = (bf16[512,128]{1,0:T(8,128)(2,1)S(1)}, bf16[512,128]{1,0:T(8,128)(2,1)S(1)}, u32[]{:S(2)}, u32[]{:S(2)}) collective-permute-start(bf16[512,128]{1,0:T(8,128)(2,1)S(1)} %shard_map.182.refs_0_), channel_id=1, source_target_pairs={{2,0},{0,2},{3,1},{1,3},{6,4},{4,6},{7,5},{5,7},{10,8},{8,10},{11,... | collective-permute-start | bytes 393224 | tf_op jit(solution)/shard_map/ppermute | solution.py:16
  90.3 5.9 %collective-permute-start.33 = (bf16[512,128]{1,0:T(8,128)(2,1)S(1)}, bf16[512,128]{1,0:T(8,128)(2,1)S(1)}, u32[]{:S(2)}, u32[]{:S(2)}) collective-permute-start(bf16[512,128]{1,0:T(8,128)(2,1)S(1)} %get-tuple-element.210.refs_0_), channel_id=1, source_target_pairs={{4,0},{8,4},{12,8},{0,12},{5,1},{9,5},{13,9},{1,13},{6,2},{10,6},{... | collective-permute-start | bytes 393224 | tf_op jit(solution)/shard_map/ppermute | solution.py:16
  91.8 8.1 %collective-permute-start.34 = (bf16[512,128]{1,0:T(8,128)(2,1)S(1)}, bf16[512,128]{1,0:T(8,128)(2,1)S(1)}, u32[]{:S(2)}, u32[]{:S(2)}) collective-permute-start(bf16[512,128]{1,0:T(8,128)(2,1)S(1)} %get-tuple-element.210.refs_0_), channel_id=1, source_target_pairs={{12,0},{0,4},{4,8},{8,12},{13,1},{1,5},{5,9},{9,13},{14,2},{2,6},{... | collective-permute-start | bytes 393224 | tf_op jit(solution)/shard_map/ppermute | solution.py:16
  94.0 5.9 %collective-permute-start.32 = (bf16[512,128]{1,0:T(8,128)(2,1)S(1)}, bf16[512,128]{1,0:T(8,128)(2,1)S(1)}, u32[]{:S(2)}, u32[]{:S(2)}) collective-permute-start(bf16[512,128]{1,0:T(8,128)(2,1)S(1)} %collective-permute-done.31.refs_2_), channel_id=1, source_target_pairs={{1,0},{0,1},{3,2},{2,3},{5,4},{4,5},{7,6},{6,7},{9,8},{8,9},{11,10... | collective-permute-start | bytes 393224 | tf_op jit(solution)/shard_map/ppermute | solution.py:16
  103.0 5.2 %collective-permute-start.38 = (bf16[512,128]{1,0:T(8,128)(2,1)S(1)}, bf16[512,128]{1,0:T(8,128)(2,1)S(1)}, u32[]{:S(2)}, u32[]{:S(2)}) collective-permute-start(bf16[512,128]{1,0:T(8,128)(2,1)S(1)} %get-tuple-element.220.refs_4_), channel_id=1, source_target_pairs={{2,0},{0,2},{3,1},{1,3},{6,4},{4,6},{7,5},{5,7},{10,8},{8,10},{11,... | collective-permute-start | bytes 393224 | tf_op jit(solution)/shard_map/ppermute | solution.py:16
  104.0 9.2 %collective-permute-start.37 = (bf16[512,128]{1,0:T(8,128)(2,1)S(1)}, bf16[512,128]{1,0:T(8,128)(2,1)S(1)}, u32[]{:S(2)}, u32[]{:S(2)}) collective-permute-start(bf16[512,128]{1,0:T(8,128)(2,1)S(1)} %get-tuple-element.220.refs_4_), channel_id=1, source_target_pairs={{1,0},{0,1},{3,2},{2,3},{5,4},{4,5},{7,6},{6,7},{9,8},{8,9},{11,10... | collective-permute-start | bytes 393224 | tf_op jit(solution)/shard_map/ppermute | solution.py:16
  104.0 5.9 %collective-permute-start.35 = (bf16[512,128]{1,0:T(8,128)(2,1)S(1)}, bf16[512,128]{1,0:T(8,128)(2,1)S(1)}, u32[]{:S(2)}, u32[]{:S(2)}) collective-permute-start(bf16[512,128]{1,0:T(8,128)(2,1)S(1)} %get-tuple-element.205), channel_id=1, source_target_pairs={{4,0},{8,4},{12,8},{0,12},{5,1},{9,5},{13,9},{1,13},{6,2},{10,6},{... | collective-permute-start | bytes 393224 | tf_op jit(solution)/shard_map/ppermute | solution.py:16
  105.7 7.5 %collective-permute-start.36 = (bf16[512,128]{1,0:T(8,128)(2,1)S(1)}, bf16[512,128]{1,0:T(8,128)(2,1)S(1)}, u32[]{:S(2)}, u32[]{:S(2)}) collective-permute-start(bf16[512,128]{1,0:T(8,128)(2,1)S(1)} %get-tuple-element.206), channel_id=1, source_target_pairs={{12,0},{0,4},{4,8},{8,12},{13,1},{1,5},{5,9},{9,13},{14,2},{2,6},{... | collective-permute-start | bytes 393224 | tf_op jit(solution)/shard_map/ppermute | solution.py:16
  108.2 5.0 %collective-permute-start.39 = (bf16[512,128]{1,0:T(8,128)(2,1)S(1)}, bf16[512,128]{1,0:T(8,128)(2,1)S(1)}, u32[]{:S(2)}, u32[]{:S(2)}) collective-permute-start(bf16[512,128]{1,0:T(8,128)(2,1)S(1)} %collective-permute-done.38.refs_6_), channel_id=1, source_target_pairs={{1,0},{0,1},{3,2},{2,3},{5,4},{4,5},{7,6},{6,7},{9,8},{8,9},{11,10... | collective-permute-start | bytes 393224 | tf_op jit(solution)/shard_map/ppermute | solution.py:16
  113.2 5.0 %collective-permute-start.41 = (bf16[512,128]{1,0:T(8,128)(2,1)S(1)}, bf16[512,128]{1,0:T(8,128)(2,1)S(1)}, u32[]{:S(2)}, u32[]{:S(2)}) collective-permute-start(bf16[512,128]{1,0:T(8,128)(2,1)S(1)} %shard_map.184.refs_0_), channel_id=1, source_target_pairs={{2,0},{0,2},{3,1},{1,3},{6,4},{4,6},{7,5},{5,7},{10,8},{8,10},{11,... | collective-permute-start | bytes 393224 | tf_op jit(solution)/shard_map/ppermute | solution.py:16
  114.5 9.6 %collective-permute-start.43 = (bf16[512,128]{1,0:T(8,128)(2,1)S(1)}, bf16[512,128]{1,0:T(8,128)(2,1)S(1)}, u32[]{:S(2)}, u32[]{:S(2)}) collective-permute-start(bf16[512,128]{1,0:T(8,128)(2,1)S(1)} %get-tuple-element.210.refs_0_), channel_id=1, source_target_pairs={{8,0},{12,4},{0,8},{4,12},{9,1},{13,5},{1,9},{5,13},{10,2},{14,6},... | collective-permute-start | bytes 393224 | tf_op jit(solution)/shard_map/ppermute | solution.py:16
  118.3 5.9 %collective-permute-start.42 = (bf16[512,128]{1,0:T(8,128)(2,1)S(1)}, bf16[512,128]{1,0:T(8,128)(2,1)S(1)}, u32[]{:S(2)}, u32[]{:S(2)}) collective-permute-start(bf16[512,128]{1,0:T(8,128)(2,1)S(1)} %collective-permute-done.41.refs_2_), channel_id=1, source_target_pairs={{1,0},{0,1},{3,2},{2,3},{5,4},{4,5},{7,6},{6,7},{9,8},{8,9},{11,10... | collective-permute-start | bytes 393224 | tf_op jit(solution)/shard_map/ppermute | solution.py:16
  124.2 5.1 %collective-permute-start.44 = (bf16[2048,128]{1,0:T(8,128)(2,1)S(1)}, bf16[2048,128]{1,0:T(8,128)(2,1)S(1)}, u32[]{:S(2)}, u32[]{:S(2)}) collective-permute-start(bf16[2048,128]{1,0:T(8,128)(2,1)S(1)} %shard_map.185.mine), channel_id=1, source_target_pairs={{1,0},{0,1},{3,2},{2,3},{5,4},{4,5},{7,6},{6,7},{9,8},{8,9},{11,10... | collective-permute-start | bytes 1572872 | tf_op jit(solution)/shard_map/ppermute | solution.py:16
  125.0 10.4 %collective-permute-start.45 = (bf16[512,128]{1,0:T(8,128)(2,1)S(1)}, bf16[512,128]{1,0:T(8,128)(2,1)S(1)}, u32[]{:S(2)}, u32[]{:S(2)}) collective-permute-start(bf16[512,128]{1,0:T(8,128)(2,1)S(1)} %get-tuple-element.225), channel_id=1, source_target_pairs={{4,0},{8,4},{12,8},{0,12},{5,1},{9,5},{13,9},{1,13},{6,2},{10,6},{... | collective-permute-start | bytes 393224 | tf_op jit(solution)/shard_map/ppermute | solution.py:16
  126.8 12.1 %collective-permute-start.46 = (bf16[512,128]{1,0:T(8,128)(2,1)S(1)}, bf16[512,128]{1,0:T(8,128)(2,1)S(1)}, u32[]{:S(2)}, u32[]{:S(2)}) collective-permute-start(bf16[512,128]{1,0:T(8,128)(2,1)S(1)} %get-tuple-element.225), channel_id=1, source_target_pairs={{8,0},{12,4},{0,8},{4,12},{9,1},{13,5},{1,9},{5,13},{10,2},{14,6},... | collective-permute-start | bytes 393224 | tf_op jit(solution)/shard_map/ppermute | solution.py:16
  126.8 12.1 %collective-permute-start.47 = (bf16[512,128]{1,0:T(8,128)(2,1)S(1)}, bf16[512,128]{1,0:T(8,128)(2,1)S(1)}, u32[]{:S(2)}, u32[]{:S(2)}) collective-permute-start(bf16[512,128]{1,0:T(8,128)(2,1)S(1)} %get-tuple-element.225), channel_id=1, source_target_pairs={{12,0},{0,4},{4,8},{8,12},{13,1},{1,5},{5,9},{9,13},{14,2},{2,6},{... | collective-permute-start | bytes 393224 | tf_op jit(solution)/shard_map/ppermute | solution.py:16
  139.0 10.7 %collective-permute-start.59 = (bf16[1536,128]{1,0:T(8,128)(2,1)S(1)}, bf16[1536,128]{1,0:T(8,128)(2,1)S(1)}, u32[]{:S(2)}, u32[]{:S(2)}) collective-permute-start(bf16[1536,128]{1,0:T(8,128)(2,1)S(1)} %shard_map.190.mine), channel_id=1, source_target_pairs={{2,0},{0,2},{3,1},{1,3},{6,4},{4,6},{7,5},{5,7},{10,8},{8,10},{11,... | collective-permute-start | bytes 1179656 | tf_op jit(solution)/shard_map/ppermute | solution.py:16
  139.9 9.8 %collective-permute-start.48 = (bf16[1536,128]{1,0:T(8,128)(2,1)S(1)}, bf16[1536,128]{1,0:T(8,128)(2,1)S(1)}, u32[]{:S(2)}, u32[]{:S(2)}) collective-permute-start(bf16[1536,128]{1,0:T(8,128)(2,1)S(1)} %shard_map.190.mine), channel_id=1, source_target_pairs={{1,0},{0,1},{3,2},{2,3},{5,4},{4,5},{7,6},{6,7},{9,8},{8,9},{11,10... | collective-permute-start | bytes 1179656 | tf_op jit(solution)/shard_map/ppermute | solution.py:16
  139.9 15.4 %collective-permute-start.50 = (bf16[448,256]{1,0:T(8,128)(2,1)S(1)}, bf16[448,256]{1,0:T(8,128)(2,1)S(1)}, u32[]{:S(2)}, u32[]{:S(2)}) collective-permute-start(bf16[448,256]{1,0:T(8,128)(2,1)S(1)} %get-tuple-element.250), channel_id=1, source_target_pairs={{12,0},{0,4},{4,8},{8,12},{13,1},{1,5},{5,9},{9,13},{14,2},{2,6},{... | collective-permute-start | bytes 688136 | tf_op jit(solution)/shard_map/ppermute | solution.py:16
  140.3 19.2 %collective-permute-start.51 = (bf16[448,256]{1,0:T(8,128)(2,1)S(1)}, bf16[448,256]{1,0:T(8,128)(2,1)S(1)}, u32[]{:S(2)}, u32[]{:S(2)}) collective-permute-start(bf16[448,256]{1,0:T(8,128)(2,1)S(1)} %get-tuple-element.251), channel_id=1, source_target_pairs={{8,0},{12,4},{0,8},{4,12},{9,1},{13,5},{1,9},{5,13},{10,2},{14,6},... | collective-permute-start | bytes 688136 | tf_op jit(solution)/shard_map/ppermute | solution.py:16
  142.2 17.3 %collective-permute-start.52 = (bf16[448,256]{1,0:T(8,128)(2,1)S(1)}, bf16[448,256]{1,0:T(8,128)(2,1)S(1)}, u32[]{:S(2)}, u32[]{:S(2)}) collective-permute-start(bf16[448,256]{1,0:T(8,128)(2,1)S(1)} %get-tuple-element.252), channel_id=1, source_target_pairs={{4,0},{8,4},{12,8},{0,12},{5,1},{9,5},{13,9},{1,13},{6,2},{10,6},{... | collective-permute-start | bytes 688136 | tf_op jit(solution)/shard_map/ppermute | solution.py:16
  149.7 23.9 %collective-permute-start.60 = (bf16[1536,128]{1,0:T(8,128)(2,1)S(1)}, bf16[1536,128]{1,0:T(8,128)(2,1)S(1)}, u32[]{:S(2)}, u32[]{:S(2)}) collective-permute-start(bf16[1536,128]{1,0:T(8,128)(2,1)S(1)} %collective-permute-done.59.refs_0_), channel_id=1, source_target_pairs={{1,0},{0,1},{3,2},{2,3},{5,4},{4,5},{7,6},{6,7},{9,8},{8,9},{11,10... | collective-permute-start | bytes 1179656 | tf_op jit(solution)/shard_map/ppermute | solution.py:16
  154.7 4.9 %collective-permute-start.49 = (bf16[256,256]{1,0:T(8,128)(2,1)S(1)}, bf16[256,256]{1,0:T(8,128)(2,1)S(1)}, u32[]{:S(2)}, u32[]{:S(2)}) collective-permute-start(bf16[256,256]{1,0:T(8,128)(2,1)S(1)} %get-tuple-element.244), channel_id=1, source_target_pairs={{1,0},{0,1},{3,2},{2,3},{5,4},{4,5},{7,6},{6,7},{9,8},{8,9},{11,10... | collective-permute-start | bytes 393224 | tf_op jit(solution)/shard_map/ppermute | solution.py:16
  159.7 8.3 %collective-permute-start.53 = (bf16[64,256]{1,0:T(8,128)(2,1)S(1)}, bf16[64,256]{1,0:T(8,128)(2,1)S(1)}, u32[]{:S(2)}, u32[]{:S(2)}) collective-permute-start(bf16[64,256]{1,0:T(8,128)(2,1)S(1)} %get-tuple-element.255), channel_id=1, source_target_pairs={{12,0},{0,4},{4,8},{8,12},{13,1},{1,5},{5,9},{9,13},{14,2},{2,6},{... | collective-permute-start | bytes 98312 | tf_op jit(solution)/shard_map/ppermute | solution.py:16
  164.5 4.9 %collective-permute-start.54 = (bf16[64,256]{1,0:T(8,128)(2,1)S(1)}, bf16[64,256]{1,0:T(8,128)(2,1)S(1)}, u32[]{:S(2)}, u32[]{:S(2)}) collective-permute-start(bf16[64,256]{1,0:T(8,128)(2,1)S(1)} %get-tuple-element.256), channel_id=1, source_target_pairs={{8,0},{12,4},{0,8},{4,12},{9,1},{13,5},{1,9},{5,13},{10,2},{14,6},... | collective-permute-start | bytes 98312 | tf_op jit(solution)/shard_map/ppermute | solution.py:16
  170.6 9.3 %collective-permute-start.56 = (bf16[512,256]{1,0:T(8,128)(2,1)S(1)}, bf16[512,256]{1,0:T(8,128)(2,1)S(1)}, u32[]{:S(2)}, u32[]{:S(2)}) collective-permute-start(bf16[512,256]{1,0:T(8,128)(2,1)S(1)} %shard_map.195.refs_0_), channel_id=1, source_target_pairs={{4,0},{8,4},{12,8},{0,12},{5,1},{9,5},{13,9},{1,13},{6,2},{10,6},{... | collective-permute-start | bytes 786440 | tf_op jit(solution)/shard_map/ppermute | solution.py:16
  172.8 21.1 %collective-permute-start.57 = (bf16[512,256]{1,0:T(8,128)(2,1)S(1)}, bf16[512,256]{1,0:T(8,128)(2,1)S(1)}, u32[]{:S(2)}, u32[]{:S(2)}) collective-permute-start(bf16[512,256]{1,0:T(8,128)(2,1)S(1)} %shard_map.195.refs_0_), channel_id=1, source_target_pairs={{8,0},{12,4},{0,8},{4,12},{9,1},{13,5},{1,9},{5,13},{10,2},{14,6},... | collective-permute-start | bytes 786440 | tf_op jit(solution)/shard_map/ppermute | solution.py:16
  172.8 21.1 %collective-permute-start.58 = (bf16[512,256]{1,0:T(8,128)(2,1)S(1)}, bf16[512,256]{1,0:T(8,128)(2,1)S(1)}, u32[]{:S(2)}, u32[]{:S(2)}) collective-permute-start(bf16[512,256]{1,0:T(8,128)(2,1)S(1)} %shard_map.195.refs_0_), channel_id=1, source_target_pairs={{12,0},{0,4},{4,8},{8,12},{13,1},{1,5},{5,9},{9,13},{14,2},{2,6},{... | collective-permute-start | bytes 786440 | tf_op jit(solution)/shard_map/ppermute | solution.py:16
  (27 other events, 171.7 us)

commit v7 on v6

--- a/solution.py
+++ b/solution.py
@@ -391,8 +391,14 @@
 
 
 def cores_body(keep, got, *refs):
-    refs[-1][...] = keep[...] + got[...].astype(F32)
-    cut_by_face(refs[-1], refs[:-1])
+    count, table = len(refs) // 2, refs[-1]
+    face, size = lax.axis_index("space"), table.shape[0] // count
+    table[...] = keep[...] + got[...].astype(F32)
+    for k in range(count):
+        piece, out = refs[k], refs[count + k]
+        rows = piece.shape[0]
+        out[:rows, :] = piece[...]
+        out[rows:, :] = table[rows_at(lax.rem(face + k, count), size), :].astype(BF16)
 
 
 def stack_all_body(*refs):
@@ -454,6 +460,18 @@
             out += [mine, shifted(mine, "pipe", 1)]
         return out
 
+    def other_chans(block):
+        out = []
+        for j in range(1, chan_count):
+            for t in range(pipe_count):
+                route = [
+                    ((c + j) % chan_count * pipe_count + (p + t) % pipe_count, c * pipe_count + p)
+                    for c in range(chan_count)
+                    for p in range(pipe_count)
+                ]
+                out.append(lax.ppermute(block, FACE_AXES, route))
+        return out
+
     def add(parts, kind=BF16):
         return run(add_body, parts, [(parts[0].shape, kind)])[0]
 
@@ -574,10 +592,10 @@
 
     enc_got = from_owners(enc_part)[1:]
     pieces_w = weights(
-        (state_1, send_1, recv_1, agg_0, grad_1, state_0, send_0, recv_0)
-        + (last_b, dec_grad, agg_1, grad_2),
-        ((0, 1), (0, 2), (3, 4), (5, 6), (5, 7), (8, 9), (10, 11)),
-    )
+        (state_1, send_1, recv_1, agg_0, grad_1, last_b, dec_grad),
+        ((0, 1), (0, 2), (3, 4), (5, 6)),
+    )
+    pieces_c = weights((state_0, send_0, recv_0, agg_1, grad_2), ((0, 1), (0, 2), (3, 4)))
     grad_mesh, = run(pick_body, (grad_0,), [((mesh_rows, narrow), F32)], hbm=(0,))
     table = [pltpu.VMEM((mesh_all, narrow), BF16), pltpu.VMEM((1, grid_rows), jnp.int32)]
     mixed, slope_enc = run(
@@ -585,9 +603,10 @@
         [((grid_rows, narrow), BF16), ((grid_rows, wide), BF16)], scratch=table, hbm=(0,),
         flops=sum_flops + 2 * grid_rows * wide * wide, vmem=grid_vmem,
     )
-    outs = tie((slope_enc, grad_mesh, *enc_got, *pieces_w))
+    outs = tie((slope_enc, grad_mesh, *enc_got, *pieces_w, *pieces_c))
     slope_enc, grad_mesh = outs[:2]
-    enc_got, pieces_w = outs[2 : 1 + faces], outs[1 + faces :]
+    enc_got, pieces_w = outs[2 : 1 + faces], outs[1 + faces : 1 + 2 * faces]
+    pieces_c = outs[1 + 2 * faces :]
     sums_b = add([pieces_w[0], *over_faces(pieces_w, -1)])
     enc_mine = stack(enc_got)
     enc_grad, grad_keep, grad_give = run(
@@ -598,8 +617,8 @@
         flops=sum_flops + 2 * grid_rows * wide * narrow, vmem=grid_vmem,
     )
     sums_g = run(
-        cores_body, (grad_keep, shifted(grad_give, "pipe", 1)),
-        [((half // faces, narrow), BF16)] * faces, scratch=[pltpu.VMEM((half, narrow), F32)],
+        cores_body, (grad_keep, shifted(grad_give, "pipe", 1), *pieces_c),
+        [((pieces_c[0].shape[0] + half // faces, narrow), BF16)] * faces, scratch=[pltpu.VMEM((half, narrow), F32)],
     )
     *sums_g, sums_b = tie((*sums_g, sums_b))
     sums_g = add([sums_g[0], *over_faces(sums_g, -1)])
@@ -609,7 +628,7 @@
     )
     reduced = from_owners(reduced)
     others = chan_count - 1
-    pieces = face_parts(enc_mine)[2:]
+    pieces = other_chans(enc_mine)
     grad_grid, = run(
         on(enc_other_body, others),
         (*ids, cotangent, enc_grad, enc_all, slope_enc, w_enc, *pieces),
@@ -617,11 +636,13 @@
         scratch=[pltpu.VMEM((mesh_all, narrow * others), BF16), table[1]],
         flops=(sum_flops + 4 * grid_rows * narrow * narrow) * others, vmem=grid_vmem + 4, hbm=(0,),
     )
-    *reduced, grad_grid = tie((*reduced, grad_grid))
+    *reduced_far, grad_grid = tie((*(reduced[k] for k in far), grad_grid))
+    for k, piece in zip(far, reduced_far):
+        reduced[k] = piece
     reduced_other = [shifted(piece, "pipe", 1) for piece in reduced]
     layer_shape = ((w_send.shape[0], wide, narrow), F32)
     places = (
-        ((0, 1), (1, 1), (2, 0), (0, 0), (1, 0), (3, None), (2, 1)), ((4, None),),
+        ((0, 1), (1, 1), (2, 0), (3, None)), ((0, 0), (1, 0), (2, 1)), ((4, None),),
     )
     grad_w_send, grad_w_recv, grad_w_node, grad_w_dec, grad_w_enc = run(
         on(write_body, places), (*reduced, *reduced_other),

time: 199 us -> 198 us (level); the launches traced: 199 us -> 194 us
  waiting for transfers between devices: 95.2 us -> 84.1 us
  starting transfers between devices: 58 us -> 64.3 us
    ppermute x65 -> x63, waiting for transfers between devices: 95.2 us -> 84.1 us  [shifted(): lax.ppermute(block, axis, [((i + distance) % count, i) for i in range(cou...]
    ppermute x65 -> x63, starting transfers between devices: 58 us -> 62.2 us  [shifted(): lax.ppermute(block, axis, [((i + distance) % count, i) for i in range(cou...]
    ppermute x0 -> x2, starting transfers between devices: none -> 2.14 us  [other_chans(): out.append(lax.ppermute(block, FACE_AXES, route))]
    pallas_call x28 -> x29, Pallas kernels: 43.9 us -> 44.1 us  [run(): pl.pallas_call(body, out_shape=[jax.ShapeDtypeStruct(s, d) if i in hbm el...]
  transfers between devices with their start and end apart: 65 -> 65, of which waited for: 36 -> 32; matrix products, arithmetic and copies ran while one was open for 0% -> 0% of each run, Pallas kernels for 14% -> 14%
where the time goes in v7:
time: 198 us; the launch traced here: 194 us
  waiting for transfers between devices  84.1 us (42%)
  starting transfers between devices  64.3 us (32%)
  Pallas kernels  44.1 us (22%)
    ppermute x63, waiting for transfers between devices, shifted(): lax.ppermute(block, axis, [((i + distance) % count, i) for i in range(cou...  84.1 us
    ppermute x63, starting transfers between devices, shifted(): lax.ppermute(block, axis, [((i + distance) % count, i) for i in range(cou...  62.2 us
    pallas_call x29, Pallas kernels, run(): pl.pallas_call(body, out_shape=[jax.ShapeDtypeStruct(s, d) if i in hbm el...  44.1 us
  transfers between devices with their start and end apart: 65, of which 32 were waited for; matrix products, arithmetic and copies ran while one was open for 0% of the time, Pallas kernels for 14%

profile of v7, /device:TPU:0, one launch (start us, length us, event | category | flops | bytes accessed | tf_op | source)
XLA Modules:
  0.0 194.1 jit_solution(1600076915455624035)
XLA Ops:
  0.7 5.9 %shard_map.170 = (bf16[2048,128]{1,0:T(8,128)(2,1)S(1)}, bf16[2048,128]{1,0:T(8,128)(2,1)S(1)}) custom-call(bf16[2048,512]{1,0:T(8,128)(2,1)} %x.5, bf16[512,512]{1,0:T(8,128)(2,1)} %w.5, s32[1,2048]{1,0:T(1,128)} %bitcast.5, s32[1,2048]{1,0:T(1,128)} %bitcast.10), custom_call_target="tpu_custom_call" | custom-call | flops 2684354560 | tf_op jit(solution)/shard_map/pallas_call | solution.py:75
  8.8 3.0 %collective-permute-start.1 = (bf16[512,128]{1,0:T(8,128)(2,1)S(1)}, bf16[512,128]{1,0:T(8,128)(2,1)S(1)}, u32[]{:S(2)}, u32[]{:S(2)}) collective-permute-start(bf16[512,128]{1,0:T(8,128)(2,1)S(1)} %get-tuple-element.151), channel_id=1, source_target_pairs={{12,0},{0,4},{4,8},{8,12},{13,1},{1,5},{5,9},{9,13},{14,2},{2,6},{... | collective-permute-start | bytes 393224 | tf_op jit(solution)/shard_map/ppermute | solution.py:16
  11.8 2.6 %collective-permute-start.2 = (bf16[512,128]{1,0:T(8,128)(2,1)S(1)}, bf16[512,128]{1,0:T(8,128)(2,1)S(1)}, u32[]{:S(2)}, u32[]{:S(2)}) collective-permute-start(bf16[512,128]{1,0:T(8,128)(2,1)S(1)} %get-tuple-element.152), channel_id=1, source_target_pairs={{8,0},{12,4},{0,8},{4,12},{9,1},{13,5},{1,9},{5,13},{10,2},{14,6},... | collective-permute-start | bytes 393224 | tf_op jit(solution)/shard_map/ppermute | solution.py:16
  15.7 4.1 %shard_map.176 = (bf16[2048,128]{1,0:T(8,128)(2,1)S(1)}, bf16[2048,128]{1,0:T(8,128)(2,1)S(1)}) custom-call(s32[1,2048]{1,0:T(1,128)S(1)} %bitcast.6, s32[1,2048]{1,0:T(1,128)S(1)} %bitcast.11, bf16[2048,256]{1,0:T(8,128)(2,1)} %cotangent.1), custom_call_target="tpu_custom_call" | custom-call | flops 2147483648 | tf_op jit(solution)/shard_map/pallas_call | solution.py:75
  23.4 1.6 collective-permute-start.6
  25.0 3.8 %collective-permute-done.6.refs_2_ = bf16[512,128]{1,0:T(8,128)(2,1)S(1)} collective-permute-done((bf16[512,128]{1,0:T(8,128)(2,1)S(1)}, bf16[512,128]{1,0:T(8,128)(2,1)S(1)}, u32[]{:S(2)}, u32[]{:S(2)}) %collective-permute-start.6) | collective-permute-done | bytes 131104 | tf_op jit(solution)/shard_map/ppermute | solution.py:16
  30.7 4.0 %collective-permute-start.9 = (bf16[512,128]{1,0:T(8,128)(2,1)S(1)}, bf16[512,128]{1,0:T(8,128)(2,1)S(1)}, u32[]{:S(2)}, u32[]{:S(2)}) collective-permute-start(bf16[512,128]{1,0:T(8,128)(2,1)S(1)} %get-tuple-element.159.own), channel_id=1, source_target_pairs={{4,0},{8,4},{12,8},{0,12},{5,1},{9,5},{13,9},{1,13},{6,2},{10,6},{... | collective-permute-start | bytes 393224 | tf_op jit(solution)/shard_map/ppermute | solution.py:16
  34.8 3.8 %collective-permute-done.9.above = bf16[512,128]{1,0:T(8,128)(2,1)S(1)} collective-permute-done((bf16[512,128]{1,0:T(8,128)(2,1)S(1)}, bf16[512,128]{1,0:T(8,128)(2,1)S(1)}, u32[]{:S(2)}, u32[]{:S(2)}) %collective-permute-start.9) | collective-permute-done | bytes 131104 | tf_op jit(solution)/shard_map/ppermute | solution.py:16
  38.6 3.3 %collective-permute-done.8.below = bf16[512,128]{1,0:T(8,128)(2,1)S(1)} collective-permute-done((bf16[512,128]{1,0:T(8,128)(2,1)S(1)}, bf16[512,128]{1,0:T(8,128)(2,1)S(1)}, u32[]{:S(2)}, u32[]{:S(2)}) %collective-permute-start.8) | collective-permute-done | bytes 131104 | tf_op jit(solution)/shard_map/ppermute | solution.py:16
  41.9 1.8 shard_map.175
  43.7 1.6 collective-permute-start.12
  46.5 2.6 %collective-permute-start.15 = (bf16[512,128]{1,0:T(8,128)(2,1)S(1)}, bf16[512,128]{1,0:T(8,128)(2,1)S(1)}, u32[]{:S(2)}, u32[]{:S(2)}) collective-permute-start(bf16[512,128]{1,0:T(8,128)(2,1)S(1)} %get-tuple-element.172), channel_id=1, source_target_pairs={{4,0},{8,4},{12,8},{0,12},{5,1},{9,5},{13,9},{1,13},{6,2},{10,6},{... | collective-permute-start | bytes 393224 | tf_op jit(solution)/shard_map/ppermute | solution.py:16
  50.6 2.8 %collective-permute-done.14.refs_1_ = bf16[512,128]{1,0:T(8,128)(2,1)S(1)} collective-permute-done((bf16[512,128]{1,0:T(8,128)(2,1)S(1)}, bf16[512,128]{1,0:T(8,128)(2,1)S(1)}, u32[]{:S(2)}, u32[]{:S(2)}) %collective-permute-start.14) | collective-permute-done | bytes 131104 | tf_op jit(solution)/shard_map/ppermute | solution.py:16
  55.7 2.6 %collective-permute-start.17 = (bf16[512,128]{1,0:T(8,128)(2,1)S(1)}, bf16[512,128]{1,0:T(8,128)(2,1)S(1)}, u32[]{:S(2)}, u32[]{:S(2)}) collective-permute-start(bf16[512,128]{1,0:T(8,128)(2,1)S(1)} %get-tuple-element.178.own), channel_id=1, source_target_pairs={{4,0},{8,4},{12,8},{0,12},{5,1},{9,5},{13,9},{1,13},{6,2},{10,6},{... | collective-permute-start | bytes 393224 | tf_op jit(solution)/shard_map/ppermute | solution.py:16
  58.3 3.2 %collective-permute-done.18.refs_3_ = bf16[512,128]{1,0:T(8,128)(2,1)S(1)} collective-permute-done((bf16[512,128]{1,0:T(8,128)(2,1)S(1)}, bf16[512,128]{1,0:T(8,128)(2,1)S(1)}, u32[]{:S(2)}, u32[]{:S(2)}) %collective-permute-start.18) | collective-permute-done | bytes 131104 | tf_op jit(solution)/shard_map/ppermute | solution.py:16
  61.5 4.2 %collective-permute-done.17.above = bf16[512,128]{1,0:T(8,128)(2,1)S(1)} collective-permute-done((bf16[512,128]{1,0:T(8,128)(2,1)S(1)}, bf16[512,128]{1,0:T(8,128)(2,1)S(1)}, u32[]{:S(2)}, u32[]{:S(2)}) %collective-permute-start.17) | collective-permute-done | bytes 131104 | tf_op jit(solution)/shard_map/ppermute | solution.py:16
  66.4 1.8 shard_map.179
  71.0 2.2 %collective-permute-done.20.refs_2_ = bf16[512,128]{1,0:T(8,128)(2,1)S(1)} collective-permute-done((bf16[512,128]{1,0:T(8,128)(2,1)S(1)}, bf16[512,128]{1,0:T(8,128)(2,1)S(1)}, u32[]{:S(2)}, u32[]{:S(2)}) %collective-permute-start.20) | collective-permute-done | bytes 131104 | tf_op jit(solution)/shard_map/ppermute | solution.py:16
  74.5 3.5 %shard_map.181 = (bf16[512,512]{1,0:T(8,128)(2,1)S(1)}, bf16[512,512]{1,0:T(8,128)(2,1)S(1)}, bf16[512,128]{1,0:T(8,128)(2,1)S(1)}, bf16[512,512]{1,0:T(8,128)(2...) custom-call(f32[512,512]{1,0:T(8,128)S(1)} %get-tuple-element.177.st, ...), custom_call_target="tpu_custom_call" | custom-call | flops 2013265920 | tf_op jit(solution)/shard_map/pallas_call | solution.py:75
  79.6 2.5 %collective-permute-start.25 = (bf16[512,128]{1,0:T(8,128)(2,1)S(1)}, bf16[512,128]{1,0:T(8,128)(2,1)S(1)}, u32[]{:S(2)}, u32[]{:S(2)}) collective-permute-start(bf16[512,128]{1,0:T(8,128)(2,1)S(1)} %get-tuple-element.190), channel_id=1, source_target_pairs={{4,0},{8,4},{12,8},{0,12},{5,1},{9,5},{13,9},{1,13},{6,2},{10,6},{... | collective-permute-start | bytes 393224 | tf_op jit(solution)/shard_map/ppermute | solution.py:16
  83.7 2.3 %collective-permute-done.25.refs_1_ = bf16[512,128]{1,0:T(8,128)(2,1)S(1)} collective-permute-done((bf16[512,128]{1,0:T(8,128)(2,1)S(1)}, bf16[512,128]{1,0:T(8,128)(2,1)S(1)}, u32[]{:S(2)}, u32[]{:S(2)}) %collective-permute-start.25) | collective-permute-done | bytes 131104 | tf_op jit(solution)/shard_map/ppermute | solution.py:16
  86.0 3.6 %collective-permute-done.26.refs_2_ = bf16[512,128]{1,0:T(8,128)(2,1)S(1)} collective-permute-done((bf16[512,128]{1,0:T(8,128)(2,1)S(1)}, bf16[512,128]{1,0:T(8,128)(2,1)S(1)}, u32[]{:S(2)}, u32[]{:S(2)}) %collective-permute-start.26) | collective-permute-done | bytes 131104 | tf_op jit(solution)/shard_map/ppermute | solution.py:16
  92.2 2.5 %collective-permute-start.33 = (bf16[512,128]{1,0:T(8,128)(2,1)S(1)}, bf16[512,128]{1,0:T(8,128)(2,1)S(1)}, u32[]{:S(2)}, u32[]{:S(2)}) collective-permute-start(bf16[512,128]{1,0:T(8,128)(2,1)S(1)} %get-tuple-element.215.refs_0_), channel_id=1, source_target_pairs={{4,0},{8,4},{12,8},{0,12},{5,1},{9,5},{13,9},{1,13},{6,2},{10,6},{... | collective-permute-start | bytes 393224 | tf_op jit(solution)/shard_map/ppermute | solution.py:16
  94.7 4.3 %collective-permute-done.34.refs_3_ = bf16[512,128]{1,0:T(8,128)(2,1)S(1)} collective-permute-done((bf16[512,128]{1,0:T(8,128)(2,1)S(1)}, bf16[512,128]{1,0:T(8,128)(2,1)S(1)}, u32[]{:S(2)}, u32[]{:S(2)}) %collective-permute-start.34) | collective-permute-done | bytes 131104 | tf_op jit(solution)/shard_map/ppermute | solution.py:16
  99.0 1.6 collective-permute-done.33.refs_1_
  100.7 3.1 %shard_map.183 = (bf16[512,512]{1,0:T(8,128)(2,1)S(1)}, bf16[512,512]{1,0:T(8,128)(2,1)S(1)}, f32[512,512]{1,0:T(8,128)S(1)}, bf16[512,128]{1,0:T(8,128)(2,1)S(1...) custom-call(f32[512,512]{1,0:T(8,128)S(1)} %get-tuple-element.199.grad.refs_4_, ...), custom_call_target="tpu_custom_call" | custom-call | flops 1744830464 | tf_op jit(solution)/shard_map/pallas_call | solution.py:75
  104.6 2.1 %collective-permute-start.35 = (bf16[512,128]{1,0:T(8,128)(2,1)S(1)}, bf16[512,128]{1,0:T(8,128)(2,1)S(1)}, u32[]{:S(2)}, u32[]{:S(2)}) collective-permute-start(bf16[512,128]{1,0:T(8,128)(2,1)S(1)} %get-tuple-element.210), channel_id=1, source_target_pairs={{4,0},{8,4},{12,8},{0,12},{5,1},{9,5},{13,9},{1,13},{6,2},{10,6},{... | collective-permute-start | bytes 393224 | tf_op jit(solution)/shard_map/ppermute | solution.py:16
  106.7 2.1 %collective-permute-done.38.refs_6_ = bf16[512,128]{1,0:T(8,128)(2,1)S(1)} collective-permute-done((bf16[512,128]{1,0:T(8,128)(2,1)S(1)}, bf16[512,128]{1,0:T(8,128)(2,1)S(1)}, u32[]{:S(2)}, u32[]{:S(2)}) %collective-permute-start.38) | collective-permute-done | bytes 131104 | tf_op jit(solution)/shard_map/ppermute | solution.py:16
  108.8 1.8 collective-permute-done.35.refs_1_
  110.5 3.6 %collective-permute-done.36.refs_2_ = bf16[512,128]{1,0:T(8,128)(2,1)S(1)} collective-permute-done((bf16[512,128]{1,0:T(8,128)(2,1)S(1)}, bf16[512,128]{1,0:T(8,128)(2,1)S(1)}, u32[]{:S(2)}, u32[]{:S(2)}) %collective-permute-start.36) | collective-permute-done | bytes 131104 | tf_op jit(solution)/shard_map/ppermute | solution.py:16
  116.5 2.7 %collective-permute-done.41.refs_2_ = bf16[512,128]{1,0:T(8,128)(2,1)S(1)} collective-permute-done((bf16[512,128]{1,0:T(8,128)(2,1)S(1)}, bf16[512,128]{1,0:T(8,128)(2,1)S(1)}, u32[]{:S(2)}, u32[]{:S(2)}) %collective-permute-start.41) | collective-permute-done | bytes 131104 | tf_op jit(solution)/shard_map/ppermute | solution.py:16
  119.2 5.9 %collective-permute-done.43.refs_2_ = bf16[512,128]{1,0:T(8,128)(2,1)S(1)} collective-permute-done((bf16[512,128]{1,0:T(8,128)(2,1)S(1)}, bf16[512,128]{1,0:T(8,128)(2,1)S(1)}, u32[]{:S(2)}, u32[]{:S(2)}) %collective-permute-start.43) | collective-permute-done | bytes 131104 | tf_op jit(solution)/shard_map/ppermute | solution.py:16
  126.7 2.3 %collective-permute-start.46 = (bf16[512,128]{1,0:T(8,128)(2,1)S(1)}, bf16[512,128]{1,0:T(8,128)(2,1)S(1)}, u32[]{:S(2)}, u32[]{:S(2)}) collective-permute-start(bf16[512,128]{1,0:T(8,128)(2,1)S(1)} %get-tuple-element.230), channel_id=1, source_target_pairs={{8,0},{12,4},{0,8},{4,12},{9,1},{13,5},{1,9},{5,13},{10,2},{14,6},... | collective-permute-start | bytes 393224 | tf_op jit(solution)/shard_map/ppermute | solution.py:16
  132.3 5.5 %shard_map.186 = (bf16[2048,256]{1,0:T(8,128)(2,1)}, bf16[2048,512]{1,0:T(8,128)(2,1)S(1)}) custom-call(bf16[2048,512]{1,0:T(8,128)(2,1)S(1)} %copy-done.5, bf16[512,512]{1,0:T(8,128)(2,1)S(1)} %copy-done.7, s32[1,2048]{1,0:T(1,128)S(1)} %bitcast.7, s32[1,2048]{1,0:T(1,128)S(1)} %bitcast.12, bf16[2048,128]{1,0:T(8,128)(2,1)S(1)} %shard_map.185.mine, ...), custom_call_target="tpu_custom_call" | custom-call | flops 3221225472 | tf_op jit(solution)/shard_map/pallas_call | solution.py:75
  137.8 1.8 collective-permute-done.46.refs_1_
  141.8 3.0 %collective-permute-start.50 = (bf16[256,256]{1,0:T(8,128)(2,1)S(1)}, bf16[256,256]{1,0:T(8,128)(2,1)S(1)}, u32[]{:S(2)}, u32[]{:S(2)}) collective-permute-start(bf16[256,256]{1,0:T(8,128)(2,1)S(1)} %get-tuple-element.263), channel_id=1, source_target_pairs={{12,0},{0,4},{4,8},{8,12},{13,1},{1,5},{5,9},{9,13},{14,2},{2,6},{... | collective-permute-start | bytes 393224 | tf_op jit(solution)/shard_map/ppermute | solution.py:16
  145.4 1.7 collective-permute-start.52
  147.2 5.0 %shard_map.192 = (bf16[2048,256]{1,0:T(8,128)(2,1)S(1)}, f32[256,256]{1,0:T(8,128)S(1)}, bf16[256,256]{1,0:T(8,128)(2,1)S(1)}) custom-call(bf16[2048,512]{1,0:T(8,128)(2,1)S(1)} %copy-done.5, s32[1,2048]{1,0:T(1,128)S(1)} %bitcast.8, s32[1,2048]{1,0:T(1,128)S(1)} %bitcast.13, bf16[2048,512]{1,0:T(8,128)(2,1)S(1)} %get-tuple-element.247.slope, ...), custom_call_target="tpu_custom_call" | custom-call | flops 2684354560 | tf_op jit(solution)/shard_map/pallas_call | solution.py:75
  152.3 2.3 %collective-permute-done.51.refs_2_ = bf16[256,256]{1,0:T(8,128)(2,1)S(1)} collective-permute-done((bf16[256,256]{1,0:T(8,128)(2,1)S(1)}, bf16[256,256]{1,0:T(8,128)(2,1)S(1)}, u32[]{:S(2)}, u32[]{:S(2)}) %collective-permute-start.51) | collective-permute-done | bytes 131104 | tf_op jit(solution)/shard_map/ppermute | solution.py:16
  154.7 3.3 %collective-permute-start.53 = (bf16[256,256]{1,0:T(8,128)(2,1)S(1)}, bf16[256,256]{1,0:T(8,128)(2,1)S(1)}, u32[]{:S(2)}, u32[]{:S(2)}) collective-permute-start(bf16[256,256]{1,0:T(8,128)(2,1)S(1)} %get-tuple-element.268), channel_id=1, source_target_pairs={{12,0},{0,4},{4,8},{8,12},{13,1},{1,5},{5,9},{9,13},{14,2},{2,6},{... | collective-permute-start | bytes 393224 | tf_op jit(solution)/shard_map/ppermute | solution.py:16
  158.0 1.8 collective-permute-start.54
  160.5 3.0 %collective-permute-done.53.refs_1_ = bf16[256,256]{1,0:T(8,128)(2,1)S(1)} collective-permute-done((bf16[256,256]{1,0:T(8,128)(2,1)S(1)}, bf16[256,256]{1,0:T(8,128)(2,1)S(1)}, u32[]{:S(2)}, u32[]{:S(2)}) %collective-permute-start.53) | collective-permute-done | bytes 131104 | tf_op jit(solution)/shard_map/ppermute | solution.py:16
  163.5 4.5 %collective-permute-done.54.refs_2_ = bf16[256,256]{1,0:T(8,128)(2,1)S(1)} collective-permute-done((bf16[256,256]{1,0:T(8,128)(2,1)S(1)}, bf16[256,256]{1,0:T(8,128)(2,1)S(1)}, u32[]{:S(2)}, u32[]{:S(2)}) %collective-permute-start.54) | collective-permute-done | bytes 131104 | tf_op jit(solution)/shard_map/ppermute | solution.py:16
  168.0 2.3 %collective-permute-start.56 = (bf16[512,256]{1,0:T(8,128)(2,1)S(1)}, bf16[512,256]{1,0:T(8,128)(2,1)S(1)}, u32[]{:S(2)}, u32[]{:S(2)}) collective-permute-start(bf16[512,256]{1,0:T(8,128)(2,1)S(1)} %shard_map.196.refs_0_), channel_id=1, source_target_pairs={{8,0},{12,4},{0,8},{4,12},{9,1},{13,5},{1,9},{5,13},{10,2},{14,6},... | collective-permute-start | bytes 786440 | tf_op jit(solution)/shard_map/ppermute | solution.py:16
  170.3 2.9 %collective-permute-start.60 = (bf16[512,256]{1,0:T(8,128)(2,1)S(1)}, bf16[512,256]{1,0:T(8,128)(2,1)S(1)}, u32[]{:S(2)}, u32[]{:S(2)}) collective-permute-start(bf16[512,256]{1,0:T(8,128)(2,1)S(1)} %shard_map.196.refs_0_), channel_id=1, source_target_pairs={{12,0},{0,4},{4,8},{8,12},{13,1},{1,5},{5,9},{9,13},{14,2},{2,6},{... | collective-permute-start | bytes 786440 | tf_op jit(solution)/shard_map/ppermute | solution.py:16
  174.2 6.3 %shard_map.197 = bf16[2048,256]{1,0:T(8,128)(2,1)} custom-call(s32[1,2048]{1,0:T(1,128)S(1)} %bitcast.9, s32[1,2048]{1,0:T(1,128)S(1)} %bitcast.14, bf16[2048,256]{1,0:T(8,128)(2,1)} %cotangent.1, bf16[2048,256]{1,0:T(8,128)(2,1)S(1)} %get-tuple-element.271.enc_grad, bf16[512,512]{1,0:T(8,128)(2,1)S(1)} %get-tuple-element.248.enc_all, ...), custom_call_target="tpu_custom_call" | custom-call | flops 2684354560 | tf_op jit(solution)/shard_map/pallas_call | solution.py:75
  180.5 8.9 %collective-permute-done.56.refs_2_ = bf16[512,256]{1,0:T(8,128)(2,1)S(1)} collective-permute-done((bf16[512,256]{1,0:T(8,128)(2,1)S(1)}, bf16[512,256]{1,0:T(8,128)(2,1)S(1)}, u32[]{:S(2)}, u32[]{:S(2)}) %collective-permute-start.56) | collective-permute-done | bytes 262176 | tf_op jit(solution)/shard_map/ppermute | solution.py:16
  191.7 2.3 %shard_map.198 = (f32[2,512,256]{2,1,0:T(8,128)}, f32[2,512,256]{2,1,0:T(8,128)}, f32[2,512,256]{2,1,0:T(8,128)}, f32[512,256]{1,0:T(8,128)}, f32[512,256]{1,0:T(8,128)}) custom-call(bf16[512,256]{1,0:T(8,128)(2,1)S(1)} %shard_map.196.refs_0_, bf16[512,256]{1,0:T(8,128)(2,1)S(1)} %collective-permute-done.59.refs_1_, ...), custom_call_target="tpu_custom_call" | custom-call | tf_op jit(solution)/shard_map/pallas_call | solution.py:75
  (131 shorter events, 40.0 us)
Async XLA Ops:
  8.8 13.2 %collective-permute-start.1 = (bf16[512,128]{1,0:T(8,128)(2,1)S(1)}, bf16[512,128]{1,0:T(8,128)(2,1)S(1)}, u32[]{:S(2)}, u32[]{:S(2)}) collective-permute-start(bf16[512,128]{1,0:T(8,128)(2,1)S(1)} %get-tuple-element.151), channel_id=1, source_target_pairs={{12,0},{0,4},{4,8},{8,12},{13,1},{1,5},{5,9},{9,13},{14,2},{2,6},{... | collective-permute-start | bytes 393224 | tf_op jit(solution)/shard_map/ppermute | solution.py:16
  11.8 11.5 %collective-permute-start.2 = (bf16[512,128]{1,0:T(8,128)(2,1)S(1)}, bf16[512,128]{1,0:T(8,128)(2,1)S(1)}, u32[]{:S(2)}, u32[]{:S(2)}) collective-permute-start(bf16[512,128]{1,0:T(8,128)(2,1)S(1)} %get-tuple-element.152), channel_id=1, source_target_pairs={{8,0},{12,4},{0,8},{4,12},{9,1},{13,5},{1,9},{5,13},{10,2},{14,6},... | collective-permute-start | bytes 393224 | tf_op jit(solution)/shard_map/ppermute | solution.py:16
  14.4 8.9 %collective-permute-start.3 = (bf16[512,128]{1,0:T(8,128)(2,1)S(1)}, bf16[512,128]{1,0:T(8,128)(2,1)S(1)}, u32[]{:S(2)}, u32[]{:S(2)}) collective-permute-start(bf16[512,128]{1,0:T(8,128)(2,1)S(1)} %get-tuple-element.153), channel_id=1, source_target_pairs={{4,0},{8,4},{12,8},{0,12},{5,1},{9,5},{13,9},{1,13},{6,2},{10,6},{... | collective-permute-start | bytes 393224 | tf_op jit(solution)/shard_map/ppermute | solution.py:16
  19.8 14.9 %collective-permute-start.10 = (bf16[2048,128]{1,0:T(8,128)(2,1)S(1)}, bf16[2048,128]{1,0:T(8,128)(2,1)S(1)}, u32[]{:S(2)}, u32[]{:S(2)}) collective-permute-start(bf16[2048,128]{1,0:T(8,128)(2,1)S(1)} %get-tuple-element.165), channel_id=1, source_target_pairs={{1,0},{0,1},{3,2},{2,3},{5,4},{4,5},{7,6},{6,7},{9,8},{8,9},{11,10... | collective-permute-start | bytes 1572872 | tf_op jit(solution)/shard_map/ppermute | solution.py:16
  23.4 5.4 %collective-permute-start.6 = (bf16[512,128]{1,0:T(8,128)(2,1)S(1)}, bf16[512,128]{1,0:T(8,128)(2,1)S(1)}, u32[]{:S(2)}, u32[]{:S(2)}) collective-permute-start(bf16[512,128]{1,0:T(8,128)(2,1)S(1)} %shard_map.172.refs_0_), channel_id=1, source_target_pairs={{2,0},{0,2},{3,1},{1,3},{6,4},{4,6},{7,5},{5,7},{10,8},{8,10},{11,... | collective-permute-start | bytes 393224 | tf_op jit(solution)/shard_map/ppermute | solution.py:16
  30.7 7.9 %collective-permute-start.9 = (bf16[512,128]{1,0:T(8,128)(2,1)S(1)}, bf16[512,128]{1,0:T(8,128)(2,1)S(1)}, u32[]{:S(2)}, u32[]{:S(2)}) collective-permute-start(bf16[512,128]{1,0:T(8,128)(2,1)S(1)} %get-tuple-element.159.own), channel_id=1, source_target_pairs={{4,0},{8,4},{12,8},{0,12},{5,1},{9,5},{13,9},{1,13},{6,2},{10,6},{... | collective-permute-start | bytes 393224 | tf_op jit(solution)/shard_map/ppermute | solution.py:16
  34.7 7.2 %collective-permute-start.8 = (bf16[512,128]{1,0:T(8,128)(2,1)S(1)}, bf16[512,128]{1,0:T(8,128)(2,1)S(1)}, u32[]{:S(2)}, u32[]{:S(2)}) collective-permute-start(bf16[512,128]{1,0:T(8,128)(2,1)S(1)} %get-tuple-element.159.own), channel_id=1, source_target_pairs={{12,0},{0,4},{4,8},{8,12},{13,1},{1,5},{5,9},{9,13},{14,2},{2,6},{... | collective-permute-start | bytes 393224 | tf_op jit(solution)/shard_map/ppermute | solution.py:16
  43.7 5.4 %collective-permute-start.12 = (bf16[512,128]{1,0:T(8,128)(2,1)S(1)}, bf16[512,128]{1,0:T(8,128)(2,1)S(1)}, u32[]{:S(2)}, u32[]{:S(2)}) collective-permute-start(bf16[512,128]{1,0:T(8,128)(2,1)S(1)} %get-tuple-element.173.refs_0_), channel_id=1, source_target_pairs={{2,0},{0,2},{3,1},{1,3},{6,4},{4,6},{7,5},{5,7},{10,8},{8,10},{11,... | collective-permute-start | bytes 393224 | tf_op jit(solution)/shard_map/ppermute | solution.py:16
  45.2 9.7 %collective-permute-start.11 = (bf16[512,128]{1,0:T(8,128)(2,1)S(1)}, bf16[512,128]{1,0:T(8,128)(2,1)S(1)}, u32[]{:S(2)}, u32[]{:S(2)}) collective-permute-start(bf16[512,128]{1,0:T(8,128)(2,1)S(1)} %get-tuple-element.173.refs_0_), channel_id=1, source_target_pairs={{1,0},{0,1},{3,2},{2,3},{5,4},{4,5},{7,6},{6,7},{9,8},{8,9},{11,10... | collective-permute-start | bytes 393224 | tf_op jit(solution)/shard_map/ppermute | solution.py:16
  45.2 8.1 %collective-permute-start.14 = (bf16[512,128]{1,0:T(8,128)(2,1)S(1)}, bf16[512,128]{1,0:T(8,128)(2,1)S(1)}, u32[]{:S(2)}, u32[]{:S(2)}) collective-permute-start(bf16[512,128]{1,0:T(8,128)(2,1)S(1)} %get-tuple-element.171), channel_id=1, source_target_pairs={{12,0},{0,4},{4,8},{8,12},{13,1},{1,5},{5,9},{9,13},{14,2},{2,6},{... | collective-permute-start | bytes 393224 | tf_op jit(solution)/shard_map/ppermute | solution.py:16
  46.5 8.4 %collective-permute-start.15 = (bf16[512,128]{1,0:T(8,128)(2,1)S(1)}, bf16[512,128]{1,0:T(8,128)(2,1)S(1)}, u32[]{:S(2)}, u32[]{:S(2)}) collective-permute-start(bf16[512,128]{1,0:T(8,128)(2,1)S(1)} %get-tuple-element.172), channel_id=1, source_target_pairs={{4,0},{8,4},{12,8},{0,12},{5,1},{9,5},{13,9},{1,13},{6,2},{10,6},{... | collective-permute-start | bytes 393224 | tf_op jit(solution)/shard_map/ppermute | solution.py:16
  49.1 5.8 %collective-permute-start.13 = (bf16[512,128]{1,0:T(8,128)(2,1)S(1)}, bf16[512,128]{1,0:T(8,128)(2,1)S(1)}, u32[]{:S(2)}, u32[]{:S(2)}) collective-permute-start(bf16[512,128]{1,0:T(8,128)(2,1)S(1)} %collective-permute-done.12.refs_2_), channel_id=1, source_target_pairs={{1,0},{0,1},{3,2},{2,3},{5,4},{4,5},{7,6},{6,7},{9,8},{8,9},{11,10... | collective-permute-start | bytes 393224 | tf_op jit(solution)/shard_map/ppermute | solution.py:16
  49.1 12.4 %collective-permute-start.18 = (bf16[512,128]{1,0:T(8,128)(2,1)S(1)}, bf16[512,128]{1,0:T(8,128)(2,1)S(1)}, u32[]{:S(2)}, u32[]{:S(2)}) collective-permute-start(bf16[512,128]{1,0:T(8,128)(2,1)S(1)} %get-tuple-element.179), channel_id=1, source_target_pairs={{8,0},{12,4},{0,8},{4,12},{9,1},{13,5},{1,9},{5,13},{10,2},{14,6},... | collective-permute-start | bytes 393224 | tf_op jit(solution)/shard_map/ppermute | solution.py:16
  55.7 10.0 %collective-permute-start.17 = (bf16[512,128]{1,0:T(8,128)(2,1)S(1)}, bf16[512,128]{1,0:T(8,128)(2,1)S(1)}, u32[]{:S(2)}, u32[]{:S(2)}) collective-permute-start(bf16[512,128]{1,0:T(8,128)(2,1)S(1)} %get-tuple-element.178.own), channel_id=1, source_target_pairs={{4,0},{8,4},{12,8},{0,12},{5,1},{9,5},{13,9},{1,13},{6,2},{10,6},{... | collective-permute-start | bytes 393224 | tf_op jit(solution)/shard_map/ppermute | solution.py:16
  58.3 7.4 %collective-permute-start.16 = (bf16[512,128]{1,0:T(8,128)(2,1)S(1)}, bf16[512,128]{1,0:T(8,128)(2,1)S(1)}, u32[]{:S(2)}, u32[]{:S(2)}) collective-permute-start(bf16[512,128]{1,0:T(8,128)(2,1)S(1)} %get-tuple-element.178.own), channel_id=1, source_target_pairs={{12,0},{0,4},{4,8},{8,12},{13,1},{1,5},{5,9},{9,13},{14,2},{2,6},{... | collective-permute-start | bytes 393224 | tf_op jit(solution)/shard_map/ppermute | solution.py:16
  65.8 5.2 %collective-permute-start.23 = (bf16[512,128]{1,0:T(8,128)(2,1)S(1)}, bf16[512,128]{1,0:T(8,128)(2,1)S(1)}, u32[]{:S(2)}, u32[]{:S(2)}) collective-permute-start(bf16[512,128]{1,0:T(8,128)(2,1)S(1)} %shard_map.180.refs_4_), channel_id=1, source_target_pairs={{2,0},{0,2},{3,1},{1,3},{6,4},{4,6},{7,5},{5,7},{10,8},{8,10},{11,... | collective-permute-start | bytes 393224 | tf_op jit(solution)/shard_map/ppermute | solution.py:16
  78.0 5.6 %collective-permute-start.28 = (bf16[512,128]{1,0:T(8,128)(2,1)S(1)}, bf16[512,128]{1,0:T(8,128)(2,1)S(1)}, u32[]{:S(2)}, u32[]{:S(2)}) collective-permute-start(bf16[512,128]{1,0:T(8,128)(2,1)S(1)} %get-tuple-element.205.refs_4_), channel_id=1, source_target_pairs={{2,0},{0,2},{3,1},{1,3},{6,4},{4,6},{7,5},{5,7},{10,8},{8,10},{11,... | collective-permute-start | bytes 393224 | tf_op jit(solution)/shard_map/ppermute | solution.py:16
  79.6 9.9 %collective-permute-start.27 = (bf16[512,128]{1,0:T(8,128)(2,1)S(1)}, bf16[512,128]{1,0:T(8,128)(2,1)S(1)}, u32[]{:S(2)}, u32[]{:S(2)}) collective-permute-start(bf16[512,128]{1,0:T(8,128)(2,1)S(1)} %get-tuple-element.205.refs_4_), channel_id=1, source_target_pairs={{1,0},{0,1},{3,2},{2,3},{5,4},{4,5},{7,6},{6,7},{9,8},{8,9},{11,10... | collective-permute-start | bytes 393224 | tf_op jit(solution)/shard_map/ppermute | solution.py:16
  79.6 6.4 %collective-permute-start.25 = (bf16[512,128]{1,0:T(8,128)(2,1)S(1)}, bf16[512,128]{1,0:T(8,128)(2,1)S(1)}, u32[]{:S(2)}, u32[]{:S(2)}) collective-permute-start(bf16[512,128]{1,0:T(8,128)(2,1)S(1)} %get-tuple-element.190), channel_id=1, source_target_pairs={{4,0},{8,4},{12,8},{0,12},{5,1},{9,5},{13,9},{1,13},{6,2},{10,6},{... | collective-permute-start | bytes 393224 | tf_op jit(solution)/shard_map/ppermute | solution.py:16
  82.1 7.4 %collective-permute-start.26 = (bf16[512,128]{1,0:T(8,128)(2,1)S(1)}, bf16[512,128]{1,0:T(8,128)(2,1)S(1)}, u32[]{:S(2)}, u32[]{:S(2)}) collective-permute-start(bf16[512,128]{1,0:T(8,128)(2,1)S(1)} %get-tuple-element.191), channel_id=1, source_target_pairs={{12,0},{0,4},{4,8},{8,12},{13,1},{1,5},{5,9},{9,13},{14,2},{2,6},{... | collective-permute-start | bytes 393224 | tf_op jit(solution)/shard_map/ppermute | solution.py:16
  83.7 5.9 %collective-permute-start.29 = (bf16[512,128]{1,0:T(8,128)(2,1)S(1)}, bf16[512,128]{1,0:T(8,128)(2,1)S(1)}, u32[]{:S(2)}, u32[]{:S(2)}) collective-permute-start(bf16[512,128]{1,0:T(8,128)(2,1)S(1)} %collective-permute-done.28.refs_6_), channel_id=1, source_target_pairs={{1,0},{0,1},{3,2},{2,3},{5,4},{4,5},{7,6},{6,7},{9,8},{8,9},{11,10... | collective-permute-start | bytes 393224 | tf_op jit(solution)/shard_map/ppermute | solution.py:16
  89.6 5.1 %collective-permute-start.31 = (bf16[512,128]{1,0:T(8,128)(2,1)S(1)}, bf16[512,128]{1,0:T(8,128)(2,1)S(1)}, u32[]{:S(2)}, u32[]{:S(2)}) collective-permute-start(bf16[512,128]{1,0:T(8,128)(2,1)S(1)} %shard_map.182.refs_0_), channel_id=1, source_target_pairs={{2,0},{0,2},{3,1},{1,3},{6,4},{4,6},{7,5},{5,7},{10,8},{8,10},{11,... | collective-permute-start | bytes 393224 | tf_op jit(solution)/shard_map/ppermute | solution.py:16
  90.9 8.1 %collective-permute-start.34 = (bf16[512,128]{1,0:T(8,128)(2,1)S(1)}, bf16[512,128]{1,0:T(8,128)(2,1)S(1)}, u32[]{:S(2)}, u32[]{:S(2)}) collective-permute-start(bf16[512,128]{1,0:T(8,128)(2,1)S(1)} %get-tuple-element.215.refs_0_), channel_id=1, source_target_pairs={{12,0},{0,4},{4,8},{8,12},{13,1},{1,5},{5,9},{9,13},{14,2},{2,6},{... | collective-permute-start | bytes 393224 | tf_op jit(solution)/shard_map/ppermute | solution.py:16
  92.2 8.4 %collective-permute-start.33 = (bf16[512,128]{1,0:T(8,128)(2,1)S(1)}, bf16[512,128]{1,0:T(8,128)(2,1)S(1)}, u32[]{:S(2)}, u32[]{:S(2)}) collective-permute-start(bf16[512,128]{1,0:T(8,128)(2,1)S(1)} %get-tuple-element.215.refs_0_), channel_id=1, source_target_pairs={{4,0},{8,4},{12,8},{0,12},{5,1},{9,5},{13,9},{1,13},{6,2},{10,6},{... | collective-permute-start | bytes 393224 | tf_op jit(solution)/shard_map/ppermute | solution.py:16
  94.7 6.0 %collective-permute-start.32 = (bf16[512,128]{1,0:T(8,128)(2,1)S(1)}, bf16[512,128]{1,0:T(8,128)(2,1)S(1)}, u32[]{:S(2)}, u32[]{:S(2)}) collective-permute-start(bf16[512,128]{1,0:T(8,128)(2,1)S(1)} %collective-permute-done.31.refs_2_), channel_id=1, source_target_pairs={{1,0},{0,1},{3,2},{2,3},{5,4},{4,5},{7,6},{6,7},{9,8},{8,9},{11,10... | collective-permute-start | bytes 393224 | tf_op jit(solution)/shard_map/ppermute | solution.py:16
  104.6 9.5 %collective-permute-start.37 = (bf16[512,128]{1,0:T(8,128)(2,1)S(1)}, bf16[512,128]{1,0:T(8,128)(2,1)S(1)}, u32[]{:S(2)}, u32[]{:S(2)}) collective-permute-start(bf16[512,128]{1,0:T(8,128)(2,1)S(1)} %get-tuple-element.225.refs_4_), channel_id=1, source_target_pairs={{1,0},{0,1},{3,2},{2,3},{5,4},{4,5},{7,6},{6,7},{9,8},{8,9},{11,10... | collective-permute-start | bytes 393224 | tf_op jit(solution)/shard_map/ppermute | solution.py:16
  104.6 5.9 %collective-permute-start.35 = (bf16[512,128]{1,0:T(8,128)(2,1)S(1)}, bf16[512,128]{1,0:T(8,128)(2,1)S(1)}, u32[]{:S(2)}, u32[]{:S(2)}) collective-permute-start(bf16[512,128]{1,0:T(8,128)(2,1)S(1)} %get-tuple-element.210), channel_id=1, source_target_pairs={{4,0},{8,4},{12,8},{0,12},{5,1},{9,5},{13,9},{1,13},{6,2},{10,6},{... | collective-permute-start | bytes 393224 | tf_op jit(solution)/shard_map/ppermute | solution.py:16
  106.7 7.4 %collective-permute-start.36 = (bf16[512,128]{1,0:T(8,128)(2,1)S(1)}, bf16[512,128]{1,0:T(8,128)(2,1)S(1)}, u32[]{:S(2)}, u32[]{:S(2)}) collective-permute-start(bf16[512,128]{1,0:T(8,128)(2,1)S(1)} %get-tuple-element.211), channel_id=1, source_target_pairs={{12,0},{0,4},{4,8},{8,12},{13,1},{1,5},{5,9},{9,13},{14,2},{2,6},{... | collective-permute-start | bytes 393224 | tf_op jit(solution)/shard_map/ppermute | solution.py:16
  108.8 5.3 %collective-permute-start.39 = (bf16[512,128]{1,0:T(8,128)(2,1)S(1)}, bf16[512,128]{1,0:T(8,128)(2,1)S(1)}, u32[]{:S(2)}, u32[]{:S(2)}) collective-permute-start(bf16[512,128]{1,0:T(8,128)(2,1)S(1)} %collective-permute-done.38.refs_6_), channel_id=1, source_target_pairs={{1,0},{0,1},{3,2},{2,3},{5,4},{4,5},{7,6},{6,7},{9,8},{8,9},{11,10... | collective-permute-start | bytes 393224 | tf_op jit(solution)/shard_map/ppermute | solution.py:16
  115.5 9.6 %collective-permute-start.43 = (bf16[512,128]{1,0:T(8,128)(2,1)S(1)}, bf16[512,128]{1,0:T(8,128)(2,1)S(1)}, u32[]{:S(2)}, u32[]{:S(2)}) collective-permute-start(bf16[512,128]{1,0:T(8,128)(2,1)S(1)} %get-tuple-element.215.refs_0_), channel_id=1, source_target_pairs={{8,0},{12,4},{0,8},{4,12},{9,1},{13,5},{1,9},{5,13},{10,2},{14,6},... | collective-permute-start | bytes 393224 | tf_op jit(solution)/shard_map/ppermute | solution.py:16
  119.2 5.9 %collective-permute-start.42 = (bf16[512,128]{1,0:T(8,128)(2,1)S(1)}, bf16[512,128]{1,0:T(8,128)(2,1)S(1)}, u32[]{:S(2)}, u32[]{:S(2)}) collective-permute-start(bf16[512,128]{1,0:T(8,128)(2,1)S(1)} %collective-permute-done.41.refs_2_), channel_id=1, source_target_pairs={{1,0},{0,1},{3,2},{2,3},{5,4},{4,5},{7,6},{6,7},{9,8},{8,9},{11,10... | collective-permute-start | bytes 393224 | tf_op jit(solution)/shard_map/ppermute | solution.py:16
  125.1 6.8 %collective-permute-start.44 = (bf16[2048,128]{1,0:T(8,128)(2,1)S(1)}, bf16[2048,128]{1,0:T(8,128)(2,1)S(1)}, u32[]{:S(2)}, u32[]{:S(2)}) collective-permute-start(bf16[2048,128]{1,0:T(8,128)(2,1)S(1)} %shard_map.185.mine), channel_id=1, source_target_pairs={{1,0},{0,1},{3,2},{2,3},{5,4},{4,5},{7,6},{6,7},{9,8},{8,9},{11,10... | collective-permute-start | bytes 1572872 | tf_op jit(solution)/shard_map/ppermute | solution.py:16
  126.6 11.2 %collective-permute-start.47 = (bf16[512,128]{1,0:T(8,128)(2,1)S(1)}, bf16[512,128]{1,0:T(8,128)(2,1)S(1)}, u32[]{:S(2)}, u32[]{:S(2)}) collective-permute-start(bf16[512,128]{1,0:T(8,128)(2,1)S(1)} %get-tuple-element.230), channel_id=1, source_target_pairs={{12,0},{0,4},{4,8},{8,12},{13,1},{1,5},{5,9},{9,13},{14,2},{2,6},{... | collective-permute-start | bytes 393224 | tf_op jit(solution)/shard_map/ppermute | solution.py:16
  126.7 12.9 %collective-permute-start.46 = (bf16[512,128]{1,0:T(8,128)(2,1)S(1)}, bf16[512,128]{1,0:T(8,128)(2,1)S(1)}, u32[]{:S(2)}, u32[]{:S(2)}) collective-permute-start(bf16[512,128]{1,0:T(8,128)(2,1)S(1)} %get-tuple-element.230), channel_id=1, source_target_pairs={{8,0},{12,4},{0,8},{4,12},{9,1},{13,5},{1,9},{5,13},{10,2},{14,6},... | collective-permute-start | bytes 393224 | tf_op jit(solution)/shard_map/ppermute | solution.py:16
  129.0 10.6 %collective-permute-start.45 = (bf16[512,128]{1,0:T(8,128)(2,1)S(1)}, bf16[512,128]{1,0:T(8,128)(2,1)S(1)}, u32[]{:S(2)}, u32[]{:S(2)}) collective-permute-start(bf16[512,128]{1,0:T(8,128)(2,1)S(1)} %get-tuple-element.230), channel_id=1, source_target_pairs={{4,0},{8,4},{12,8},{0,12},{5,1},{9,5},{13,9},{1,13},{6,2},{10,6},{... | collective-permute-start | bytes 393224 | tf_op jit(solution)/shard_map/ppermute | solution.py:16
  139.6 5.8 %collective-permute-start.48 = (bf16[1536,128]{1,0:T(8,128)(2,1)S(1)}, bf16[1536,128]{1,0:T(8,128)(2,1)S(1)}, u32[]{:S(2)}, u32[]{:S(2)}) collective-permute-start(bf16[1536,128]{1,0:T(8,128)(2,1)S(1)} %shard_map.191.mine), channel_id=1, source_target_pairs={{1,0},{0,1},{3,2},{2,3},{5,4},{4,5},{7,6},{6,7},{9,8},{8,9},{11,10... | collective-permute-start | bytes 1179656 | tf_op jit(solution)/shard_map/ppermute | solution.py:16
  139.7 34.5 %collective-permute-start.58 = (bf16[1536,128]{1,0:T(8,128)(2,1)S(1)}, bf16[1536,128]{1,0:T(8,128)(2,1)S(1)}, u32[]{:S(2)}, u32[]{:S(2)}) collective-permute-start(bf16[1536,128]{1,0:T(8,128)(2,1)S(1)} %shard_map.191.mine), channel_id=1, source_target_pairs={{3,0},{2,1},{1,2},{0,3},{7,4},{6,5},{5,6},{4,7},{11,8},{10,9},{9,1... | collective-permute-start | bytes 1179656 | tf_op jit(solution)/shard_map/ppermute | solution.py:472
  140.6 33.6 %collective-permute-start.57 = (bf16[1536,128]{1,0:T(8,128)(2,1)S(1)}, bf16[1536,128]{1,0:T(8,128)(2,1)S(1)}, u32[]{:S(2)}, u32[]{:S(2)}) collective-permute-start(bf16[1536,128]{1,0:T(8,128)(2,1)S(1)} %shard_map.191.mine), channel_id=1, source_target_pairs={{2,0},{3,1},{0,2},{1,3},{6,4},{7,5},{4,6},{5,7},{10,8},{11,9},{8,1... | collective-permute-start | bytes 1179656 | tf_op jit(solution)/shard_map/ppermute | solution.py:472
  141.8 10.3 %collective-permute-start.50 = (bf16[256,256]{1,0:T(8,128)(2,1)S(1)}, bf16[256,256]{1,0:T(8,128)(2,1)S(1)}, u32[]{:S(2)}, u32[]{:S(2)}) collective-permute-start(bf16[256,256]{1,0:T(8,128)(2,1)S(1)} %get-tuple-element.263), channel_id=1, source_target_pairs={{12,0},{0,4},{4,8},{8,12},{13,1},{1,5},{5,9},{9,13},{14,2},{2,6},{... | collective-permute-start | bytes 393224 | tf_op jit(solution)/shard_map/ppermute | solution.py:16
  144.8 9.7 %collective-permute-start.51 = (bf16[256,256]{1,0:T(8,128)(2,1)S(1)}, bf16[256,256]{1,0:T(8,128)(2,1)S(1)}, u32[]{:S(2)}, u32[]{:S(2)}) collective-permute-start(bf16[256,256]{1,0:T(8,128)(2,1)S(1)} %get-tuple-element.264), channel_id=1, source_target_pairs={{8,0},{12,4},{0,8},{4,12},{9,1},{13,5},{1,9},{5,13},{10,2},{14,6},... | collective-permute-start | bytes 393224 | tf_op jit(solution)/shard_map/ppermute | solution.py:16
  145.4 9.1 %collective-permute-start.52 = (bf16[256,256]{1,0:T(8,128)(2,1)S(1)}, bf16[256,256]{1,0:T(8,128)(2,1)S(1)}, u32[]{:S(2)}, u32[]{:S(2)}) collective-permute-start(bf16[256,256]{1,0:T(8,128)(2,1)S(1)} %get-tuple-element.265), channel_id=1, source_target_pairs={{4,0},{8,4},{12,8},{0,12},{5,1},{9,5},{13,9},{1,13},{6,2},{10,6},{... | collective-permute-start | bytes 393224 | tf_op jit(solution)/shard_map/ppermute | solution.py:16
  154.7 8.8 %collective-permute-start.53 = (bf16[256,256]{1,0:T(8,128)(2,1)S(1)}, bf16[256,256]{1,0:T(8,128)(2,1)S(1)}, u32[]{:S(2)}, u32[]{:S(2)}) collective-permute-start(bf16[256,256]{1,0:T(8,128)(2,1)S(1)} %get-tuple-element.268), channel_id=1, source_target_pairs={{12,0},{0,4},{4,8},{8,12},{13,1},{1,5},{5,9},{9,13},{14,2},{2,6},{... | collective-permute-start | bytes 393224 | tf_op jit(solution)/shard_map/ppermute | solution.py:16
  158.0 9.9 %collective-permute-start.54 = (bf16[256,256]{1,0:T(8,128)(2,1)S(1)}, bf16[256,256]{1,0:T(8,128)(2,1)S(1)}, u32[]{:S(2)}, u32[]{:S(2)}) collective-permute-start(bf16[256,256]{1,0:T(8,128)(2,1)S(1)} %get-tuple-element.269), channel_id=1, source_target_pairs={{8,0},{12,4},{0,8},{4,12},{9,1},{13,5},{1,9},{5,13},{10,2},{14,6},... | collective-permute-start | bytes 393224 | tf_op jit(solution)/shard_map/ppermute | solution.py:16
  159.8 8.1 %collective-permute-start.55 = (bf16[256,256]{1,0:T(8,128)(2,1)S(1)}, bf16[256,256]{1,0:T(8,128)(2,1)S(1)}, u32[]{:S(2)}, u32[]{:S(2)}) collective-permute-start(bf16[256,256]{1,0:T(8,128)(2,1)S(1)} %get-tuple-element.270), channel_id=1, source_target_pairs={{4,0},{8,4},{12,8},{0,12},{5,1},{9,5},{13,9},{1,13},{6,2},{10,6},{... | collective-permute-start | bytes 393224 | tf_op jit(solution)/shard_map/ppermute | solution.py:16
  168.0 21.4 %collective-permute-start.56 = (bf16[512,256]{1,0:T(8,128)(2,1)S(1)}, bf16[512,256]{1,0:T(8,128)(2,1)S(1)}, u32[]{:S(2)}, u32[]{:S(2)}) collective-permute-start(bf16[512,256]{1,0:T(8,128)(2,1)S(1)} %shard_map.196.refs_0_), channel_id=1, source_target_pairs={{8,0},{12,4},{0,8},{4,12},{9,1},{13,5},{1,9},{5,13},{10,2},{14,6},... | collective-permute-start | bytes 786440 | tf_op jit(solution)/shard_map/ppermute | solution.py:16
  170.3 19.1 %collective-permute-start.60 = (bf16[512,256]{1,0:T(8,128)(2,1)S(1)}, bf16[512,256]{1,0:T(8,128)(2,1)S(1)}, u32[]{:S(2)}, u32[]{:S(2)}) collective-permute-start(bf16[512,256]{1,0:T(8,128)(2,1)S(1)} %shard_map.196.refs_0_), channel_id=1, source_target_pairs={{12,0},{0,4},{4,8},{8,12},{13,1},{1,5},{5,9},{9,13},{14,2},{2,6},{... | collective-permute-start | bytes 786440 | tf_op jit(solution)/shard_map/ppermute | solution.py:16
  173.2 16.2 %collective-permute-start.59 = (bf16[512,256]{1,0:T(8,128)(2,1)S(1)}, bf16[512,256]{1,0:T(8,128)(2,1)S(1)}, u32[]{:S(2)}, u32[]{:S(2)}) collective-permute-start(bf16[512,256]{1,0:T(8,128)(2,1)S(1)} %shard_map.196.refs_0_), channel_id=1, source_target_pairs={{4,0},{8,4},{12,8},{0,12},{5,1},{9,5},{13,9},{1,13},{6,2},{10,6},{... | collective-permute-start | bytes 786440 | tf_op jit(solution)/shard_map/ppermute | solution.py:16
  180.5 9.5 %collective-permute-start.61 = (bf16[512,256]{1,0:T(8,128)(2,1)S(1)}, bf16[512,256]{1,0:T(8,128)(2,1)S(1)}, u32[]{:S(2)}, u32[]{:S(2)}) collective-permute-start(bf16[512,256]{1,0:T(8,128)(2,1)S(1)} %shard_map.196.refs_0_), channel_id=1, source_target_pairs={{1,0},{0,1},{3,2},{2,3},{5,4},{4,5},{7,6},{6,7},{9,8},{8,9},{11,10... | collective-permute-start | bytes 786440 | tf_op jit(solution)/shard_map/ppermute | solution.py:16
  (27 other events, 173.6 us)
